TPU v7x, 32 devices: a whole 2x2x4 slice. The times are simulated.
32 devices in a mesh: shard: 8 (over z, y), help: 4 (over x, core).
Axes of the slice: x: 2, y: 2, z: 4, core: 2. Of those that a mesh axis runs over, the one named last changes fastest.
Arguments:
- queries: bfloat16 [8192, 768], P(('shard', 'help')), may hold values from -6 to 6
- probe_group: int32 [8192, 2], P(('shard', 'help')), may hold values from 0 to 7, all different within a row; in each aligned block of 256 rows (0 to 255, 256 to 511, ...) at most 128 rows name the same one
- probe_local: int32 [8192, 2], P(('shard', 'help')), may hold values from 0 to 3
- points: bfloat16 [32768, 768], P(('shard', 'help')), may hold values from -6 to 6
- point_cluster: int32 [8, 4096], P('shard'), may hold values from 0 to 3, never falling along the last dimension, each value on 1 to 3072 neighbouring positions
- test_matrix: bfloat16 [32, 32768], P(None, ('shard', 'help')), may hold values from -6 to 6
Outputs:
- sketch: float32 [32, 32768], P(None, ('shard', 'help'))
- regressor: float32 [32, 32, 768], P(('shard', 'help'))
Inputs may be any that keep to these rules, and one draw needn't show every extreme that they name: `probe_group`: A query's 2 groups differ. Among the 256 queries of one device (aligned blocks of rows), at most 128 pairs (q,k) name one group, and in some blocks one group is named exactly 128 times.
All inputs are finite; a program needn't handle non-finite values.
Results may differ from a plain program's by a relative error of at most 0.0037.
Values may be sent and summed in bfloat16 or wider, within the bound.
No kernel may reach another device: no remote copies, remote signals or barrier semaphores. Data moves between devices by JAX's collectives and lax.ppermute only.
A program may use at most 64 MiB of HBM per device.

v0:
```python
import jax
import jax.numpy as jnp
from jax import lax
from jax.sharding import PartitionSpec as P

PROBES = 2
CL_DEV = 1


def masked_scores(point_rows, point_ids, query_rows, query_ids):
    feature_width = point_rows.shape[1]
    block_rows = min(512, point_rows.shape[0])
    factor = feature_width ** (-0.5)

    def score_piece(pieces):
        piece_x, piece_ids = pieces
        product = (
            lax.dot_general(
                piece_x, query_rows, (((1,), (1,)), ((), ())), preferred_element_type=jnp.float32
            )
            * factor
        )
        return jnp.where(piece_ids[:, None] == query_ids[None, :], product, 0.0).astype(
            jnp.bfloat16
        )

    stacked = lax.map(
        score_piece,
        (point_rows.reshape(-1, block_rows, feature_width), point_ids.reshape(-1, block_rows)),
    )
    return stacked.reshape(point_rows.shape[0], query_rows.shape[0])


def pack_rows(source, target, member, groups, blocks, capacity, probes):
    feature_width = source.shape[1]
    row_total = target.shape[0]
    per_block = row_total // blocks
    labels = jnp.arange(groups, dtype=jnp.int32)
    onehot_dest = (
        (target[:, None] == labels[None, :]).astype(jnp.int32).reshape(blocks, per_block, groups)
    )
    ranking = jnp.sum((jnp.cumsum(onehot_dest, axis=1) - onehot_dest) * onehot_dest, axis=2)
    position = (
        target.reshape(blocks, per_block) * (blocks * capacity)
        + jnp.arange(blocks, dtype=jnp.int32)[:, None] * capacity
        + ranking
    )
    position = position.reshape(-1)
    copied_rows = jnp.repeat(source, probes, axis=0)
    filled = (
        jnp.zeros((groups * blocks * capacity, feature_width), jnp.bfloat16)
        .at[position]
        .set(copied_rows)
    )
    labelled = jnp.full((groups * blocks * capacity,), -1, jnp.int32).at[position].set(member)
    return (
        filled.reshape(groups, blocks * capacity, feature_width),
        labelled.reshape(groups, blocks * capacity),
    )


def count_labels(ids, labels):
    return jnp.sum((ids[None, :] == labels[:, None]).astype(jnp.float32), axis=1)


def shards(queries, probe_group, probe_local, points, point_cluster, test_matrix):
    groups = lax.axis_size("shard")
    helpers = lax.axis_size("help")
    helper = lax.axis_index("help")
    feature_width = queries.shape[1]
    per_device = queries.shape[0] * PROBES
    capacity = 2 * per_device // groups
    group_clusters = CL_DEV * helpers
    own_points = points.shape[0]
    group_ids = point_cluster[0]
    own_ids = lax.dynamic_slice_in_dim(group_ids, helper * own_points, own_points, 0)
    labels = jnp.arange(group_clusters, dtype=jnp.int32)
    resident = count_labels(group_ids, labels)
    peer_rows, peer_groups, peer_local = (
        lax.all_gather(queries, "help", axis=0, tiled=True),
        lax.all_gather(probe_group, "help", axis=0, tiled=True),
        lax.all_gather(probe_local, "help", axis=0, tiled=True),
    )
    outgoing, out_ids = pack_rows(
        peer_rows,
        peer_groups.reshape(-1),
        peer_local.reshape(-1),
        groups,
        helpers,
        capacity,
        PROBES,
    )
    query_pool, pool_ids = (
        lax.all_to_all(outgoing, "shard", split_axis=0, concat_axis=0, tiled=True),
        lax.all_to_all(out_ids, "shard", split_axis=0, concat_axis=0, tiled=True),
    )
    query_rows = query_pool.reshape(-1, feature_width)
    query_ids = pool_ids.reshape(-1)
    scores = masked_scores(points, own_ids, query_rows, query_ids)
    lifted = lax.psum(
        jnp.dot(test_matrix, scores, preferred_element_type=jnp.float32), "help"
    ).astype(jnp.bfloat16)
    product = lax.dot_general(
        lifted, scores, (((1,), (1,)), ((), ())), preferred_element_type=jnp.float32
    )
    queried = count_labels(query_ids, labels)
    factor = 1.0 / jnp.sqrt((queried + 1.0) * (queried + resident))
    own_hot = (own_ids[None, :] == labels[:, None]).astype(jnp.float32)
    sketch = product * jnp.sum(factor[:, None] * own_hot, axis=0)[None, :]
    rounded = sketch.astype(jnp.bfloat16)
    hot_rows = own_hot.astype(jnp.bfloat16)
    weighted = (hot_rows[:, None, :] * rounded[None, :, :]).reshape(
        CL_DEV * lax.axis_size("help") * rounded.shape[0], own_points
    )
    summed = jnp.dot(weighted, points, preferred_element_type=jnp.float32)
    partial_sum = lax.psum_scatter(
        summed.reshape(CL_DEV * lax.axis_size("help"), rounded.shape[0], feature_width),
        "help",
        scatter_dimension=0,
        tiled=True,
    )
    scale_own = lax.dynamic_slice_in_dim(1.0 / jnp.sqrt(resident), helper * CL_DEV, CL_DEV, 0)
    regressor = partial_sum * scale_own[:, None, None]
    return (sketch, regressor)


def solution(mesh):
    in_specs = (
        P(("shard", "help"), None),
        P(("shard", "help"), None),
        P(("shard", "help"), None),
        P(("shard", "help"), None),
        P("shard", None),
        P(None, ("shard", "help")),
    )
    out_specs = (P(None, ("shard", "help")), P(("shard", "help"), None, None))
    return jax.shard_map(shards, mesh=mesh, in_specs=in_specs, out_specs=out_specs, check_vma=False)
```

profile of v0, /device:TPU:0, one launch (start us, length us, event | category | flops | bytes accessed | tf_op | source)
XLA Modules:
  0.0 279.2 jit_solution(17911078598495910752)
XLA Ops:
  7.2 0.0 copy-start
  7.2 0.0 all-gather.2.cloned.1.call-start
  7.2 0.7 all-gather.2.cloned.1.call-update
  7.9 6.3 %all_gather.9 = s32[1024,2]{0,1:T(2,128)S(1)} all-gather(s32[256,2]{0,1:T(2,128)} %param.9), channel_id=1, replica_groups=mesh['shard'=8,'help'=4] {'help'}, dimensions={0}, use_global_device_ids=true | all-gather | bytes 10240 | tf_op jit(solution)/shard_map/all_gather | solution.py:81
  14.2 0.2 copy.17
  14.4 0.3 eq.96
  14.7 0.3 eq.92
  15.0 4.5 %reduce-window.6 = s32[4,8,4,128]{3,1,2,0:T(8,128)S(1)} reduce-window(s32[4,8,4,128]{3,1,2,0:T(8,128)S(1)} %fusion.15, s32[]{:T(128)} %constant.9.clone.1), window={size=1x1x1x128 pad=0_0x0_0x0_0x127_0}, to_apply=%region_0.0 | reduce-window | flops 2080768 | bytes 131076 | tf_op jit(solution)/shard_map/reduce-window
  19.5 0.4 slice_reduce_fusion
  20.0 0.1 fusion.14
  20.2 0.2 copy.16
  20.4 0.3 mul.85
  20.7 0.1 broadcast_bitcast_fusion
  20.8 5.5 %all_gather.10 = s32[1024,2]{0,1:T(2,128)S(1)} all-gather(s32[256,2]{0,1:T(2,128)} %param.10), channel_id=1, replica_groups=mesh['shard'=8,'help'=4] {'help'}, dimensions={0}, use_global_device_ids=true | all-gather | bytes 10240 | tf_op jit(solution)/shard_map/all_gather | solution.py:82
  26.3 0.2 copy.19
  26.6 0.3 reshape.158
  26.9 8.6 %scatter_custom_fusion = s32[4096]{0:T(1024)} fusion(s32[2048]{0:T(1024)S(1)} %bitcast.78, s32[2048]{0:T(1024)S(1)} %reshape.158, s32[]{:T(128)} %constant.20.clone.1), kind=kCustom, calls=%fused_computation.36 | custom fusion | bytes 16388 | tf_op jit(solution)/shard_map/scatter | solution.py:55
  35.5 6.1 %all-to-all-start = ((s32[8,1,512]{2,1,0:T(1,128)}), s32[8,1,512]{2,1,0:T(1,128)S(1)}, u32[]{:S(2)}, u32[]{:S(2)}) async-start(s32[8,1,512]{2,1,0:T(1,128)} %bitcast.6), calls=%async_computation | async-start | bytes 32768 | tf_op jit(solution)/shard_map/all_to_all | solution.py:95
  41.6 0.0 all-gather.2.cloned.1.call-done
  41.6 3.0 %broadcast_in_dim.20 = bf16[1024,2,768]{2,1,0:T(2,128)(2,1)S(1)} broadcast(bf16[1024,768]{1,0:T(8,128)(2,1)} %all-gather.2.cloned.1.call-done), dimensions={0,2} | broadcast | bytes 4718592 | tf_op jit(solution)/shard_map/broadcast_in_dim | solution.py:49
  44.6 2.7 reshape.166
  47.3 13.9 %scatter_custom_fusion.1 = bf16[4096,768]{1,0:T(8,128)(2,1)} fusion(s32[2048]{0:T(1024)S(1)} %bitcast.79, bf16[2048,768]{1,0:T(8,128)(2,1)} %reshape.166, bf16[]{:T(256)} %constant.22.clone.1), kind=kCustom, calls=%fused_computation.10 | custom fusion | bytes 6291968 | tf_op jit(solution)/shard_map/scatter | solution.py:53
  61.2 0.0 all-to-all-done
  61.2 0.0 copy-start.2
  61.2 0.0 copy-start.1
  61.2 6.1 %all-to-all-start.1 = ((bf16[8,512,768]{2,1,0:T(8,128)(2,1)}), bf16[8,512,768]{2,1,0:T(8,128)(2,1)}, u32[]{:S(2)}, u32[]{:S(2)}) async-start(bf16[8,512,768]{2,1,0:T(8,128)(2,1)} %bitcast.64), calls=%async_computation.1 | async-start | bytes 12582912 | tf_op jit(solution)/shard_map/all_to_all | solution.py:94
  67.4 0.2 reduce-scatter.2.cloned.1.call-start
  67.6 0.5 broadcast.100
  68.1 0.0 copy-done.2
  68.1 0.7 fusion.18
  68.8 0.1 convert_reduce_fusion
  69.0 0.1 convert_reduce_fusion.1
  69.1 0.1 select_reduce_fusion
  69.2 136.3 %all-to-all-done.1 = bf16[8,512,768]{2,1,0:T(8,128)(2,1)} async-done(((bf16[8,512,768]{2,1,0:T(8,128)(2,1)}), bf16[8,512,768]{2,1,0:T(8,128)(2,1)}, u32[]{:S(2)}, u32[]{:S(2)}) %all-to-all-start.1) | async-done | bytes 6291488 | tf_op jit(solution)/shard_map/all_to_all | solution.py:94
  205.5 0.0 copy-done.1
  205.5 15.7 %while.10 = (s32[]{:T(128)}, bf16[2,512,4096]{2,1,0:T(8,128)(2,1)}, s32[2,512]{1,0:T(2,128)S(1)}, s32[8,512]{1,0:T(8,128)S(1)}, bf16[2,512,768]{2,1,0:T(8,128)(2,1)S(1)}, /*index=5*/bf16[4096,768]{1,0:T(8,128)(2,1)}, s32[]{:T(128)}) while((s32[]{:T(128)}, bf16[2,512,4096]{2,1,0:T(8,128)(2,1)}, s32[2,512]{1,0:T(2,128)S(1)}, ...), condition=%wide.region_6.7_spmd, body=%wide.region_5.6_spmd.sunk | while | flops 3229614080 | bytes 11328601 | solution.py:27
  205.5 7.8 %fusion.31 = bf16[2,512,4096]{2,1,0:T(8,128)(2,1)} fusion(bf16[2,512,4096]{2,1,0:T(8,128)(2,1)} %get-tuple-element.98, s32[]{:T(128)S(6)} %copy.31, bf16[4096,768]{1,0:T(8,128)(2,1)} %get-tuple-element.109, s32[4096]{0:T(1024)S(1)} %bitcast.69, s32[512]{0:T(512)S(1)} %bitcast.71, bf16[2,512,768]{2,1,0:T(8,128)(2,1)S(1)} %get-tuple-element.108), kind=kOutput, calls=%fused_computation.4.clone.1 | convolution fusion | flops 3229614080 | bytes 11291648 | tf_op jit(solution)/shard_map/while/body/eval_jaxpr/dot_general | solution.py:18
  213.3 7.8 %fusion.31 = bf16[2,512,4096]{2,1,0:T(8,128)(2,1)} fusion(bf16[2,512,4096]{2,1,0:T(8,128)(2,1)} %get-tuple-element.98, s32[]{:T(128)S(6)} %copy.31, bf16[4096,768]{1,0:T(8,128)(2,1)} %get-tuple-element.109, s32[4096]{0:T(1024)S(1)} %bitcast.69, s32[512]{0:T(512)S(1)} %bitcast.71, bf16[2,512,768]{2,1,0:T(8,128)(2,1)S(1)} %get-tuple-element.108), kind=kOutput, calls=%fused_computation.4.clone.1 | convolution fusion | flops 3229614080 | bytes 11291648 | tf_op jit(solution)/shard_map/while/body/eval_jaxpr/dot_general | solution.py:18
  221.2 0.0 copy-done
  221.2 4.9 %convolution_bitcast_fusion = f32[32,4096]{1,0:T(8,128)S(1)} fusion(bf16[32,1024]{1,0:T(8,128)(2,1)S(1)} %copy-done, bf16[1024,4096]{1,0:T(8,128)(2,1)} %bitcast.62), kind=kOutput, calls=%fused_computation.9 | convolution fusion | flops 268435456 | bytes 8978432 | tf_op jit(solution)/shard_map/dot_general | solution.py:101
  226.1 16.3 %all-reduce.1 = bf16[32,4096]{1,0:T(8,128)(2,1)S(1)} all-reduce(f32[32,4096]{1,0:T(8,128)S(1)} %convolution_bitcast_fusion), channel_id=1, replica_groups=mesh['shard'=8,'help'=4] {'help'}, use_global_device_ids=true, to_apply=%region_7.8 | all-reduce | flops 131072 | bytes 786432 | tf_op jit(solution)/shard_map/psum | solution.py:100
  242.4 6.6 %fusion.20 = (bf16[32,1024]{1,0:T(8,128)(2,1)S(1)}, f32[32,1024]{1,0:T(8,128)}) fusion(f32[1024]{0:T(1024)S(1)} %select_reduce_fusion, bf16[32,4096]{1,0:T(8,128)(2,1)S(1)} %all-reduce.1, bf16[1024,4096]{1,0:T(8,128)(2,1)} %bitcast.63), kind=kOutput, calls=%fused_computation.45 | convolution fusion | flops 268500992 | bytes 8851456 | tf_op jit(solution)/shard_map/dot_general | solution.py:103
  249.0 1.1 fusion.7
  250.1 0.0 reduce-scatter.2.cloned.1.call-update
  250.2 0.6 dynamic_slice.15
  250.8 19.4 %reduce-scatter.2.cloned.1.call-done = f32[1,32,768]{2,1,0:T(8,128)} async-done(((f32[4,32,768]{2,1,0:T(8,128)}), f32[1,32,768]{2,1,0:T(8,128)}) %reduce-scatter.2.cloned.1.call-update) | async-done | bytes 98320 | tf_op jit(solution)/shard_map/reduce_scatter | solution.py:116
  270.2 2.2 broadcast_multiply_fusion
  (17 shorter events, 0.2 us)
Async XLA Ops:
  7.2 214.0 %copy-start = (bf16[32,1024]{1,0:T(8,128)(2,1)S(1)}, bf16[32,1024]{1,0:T(8,128)(2,1)}, u32[]{:S(2)}) copy-start(bf16[32,1024]{1,0:T(8,128)(2,1)} %param.13) | copy-start | bytes 196612
  7.2 34.4 %all-gather.2.cloned.1.call-start = ((), (), s32[]{:S(2)}) async-start(), calls=%async_computation.3 | async-start | bytes 1966080 | tf_op jit(solution)/shard_map/all_gather | solution.py:80
  35.5 25.8 %all-to-all-start = ((s32[8,1,512]{2,1,0:T(1,128)}), s32[8,1,512]{2,1,0:T(1,128)S(1)}, u32[]{:S(2)}, u32[]{:S(2)}) async-start(s32[8,1,512]{2,1,0:T(1,128)} %bitcast.6), calls=%async_computation | async-start | bytes 32768 | tf_op jit(solution)/shard_map/all_to_all | solution.py:95
  61.2 6.9 %copy-start.2 = (s32[1,4096]{1,0:T(1,128)S(1)}, s32[1,4096]{1,0:T(1,128)}, u32[]{:S(2)}) copy-start(s32[1,4096]{1,0:T(1,128)} %param.12) | copy-start | bytes 49156
  61.2 144.3 %copy-start.1 = (bf16[1024,768]{1,0:T(8,128)(2,1)S(1)}, bf16[1024,768]{1,0:T(8,128)(2,1)}, u32[]{:S(2)}) copy-start(bf16[1024,768]{1,0:T(8,128)(2,1)} %param.11) | copy-start | bytes 4718596
  61.2 144.2 %all-to-all-start.1 = ((bf16[8,512,768]{2,1,0:T(8,128)(2,1)}), bf16[8,512,768]{2,1,0:T(8,128)(2,1)}, u32[]{:S(2)}, u32[]{:S(2)}) async-start(bf16[8,512,768]{2,1,0:T(8,128)(2,1)} %bitcast.64), calls=%async_computation.1 | async-start | bytes 12582912 | tf_op jit(solution)/shard_map/all_to_all | solution.py:94
  67.4 202.8 %reduce-scatter.2.cloned.1.call-start = ((), (), s32[]{:S(2)}) async-start(), calls=%async_computation.4 | async-start | bytes 491520 | tf_op jit(solution)/shard_map/reduce_scatter | solution.py:116
Sparse Core Ops, SparseCore 0:
  9.6 22.3 all-gather.1
  250.3 19.8 reduce-scatter.1
where the time goes:
time: 280 us; the launch traced here: 279 us
  waiting for transfers between devices  156 us (56%)
  local copies, waits for them, and re-layouts  32.5 us (12%)
  matrix products  28.3 us (10%)
  blocking collectives  28.1 us (10%)
  between operations  14.2 us (5%)
  starting transfers between devices  12.5 us (4%)
  other arithmetic  7.27 us (3%)
    all_to_all x1, waiting for transfers between devices, shards(): lax.all_to_all(outgoing, 'shard', split_axis=0, concat_axis=0, tiled=True)  136 us
    reduce_scatter x1, waiting for transfers between devices, shards(): lax.psum_scatter(summed.reshape(CL_DEV * lax.axis_size('help'), rounded.s...  19.4 us
    psum x1, blocking collectives, shards(): lax.psum(jnp.dot(test_matrix, scores, preferred_element_type=jnp.float32)...  16.3 us
    dot_general x2, matrix products, score_piece(): lax.dot_general(piece_x, query_rows, (((1,), (1,)), ((), ())), preferred_...  15.6 us
    scatter x1, local copies, waits for them, and re-layouts, pack_rows(): filled = jnp.zeros((groups * blocks * capacity, feature_width), jnp.bfloa...  13.9 us
    scatter x1, local copies, waits for them, and re-layouts, pack_rows(): jnp.full((groups * blocks * capacity,), -1, jnp.int32).at[position]  8.62 us
    dot_general x1, matrix products, shards(): lax.dot_general(lifted, scores, (((1,), (1,)), ((), ())), preferred_eleme...  6.62 us
    all_gather x1, blocking collectives, shards(): lax.all_gather(probe_group, 'help', axis=0, tiled=True)  6.27 us
  transfers between devices with their start and end apart: 4, of which 2 were waited for; matrix products, arithmetic and copies ran while one was open for 13% of the time, Pallas kernels for 0%

commit v1 on v0

v1 whole, which is shorter than its diff:
```python
import functools

import jax
import jax.numpy as jnp
from jax import lax
from jax.experimental import pallas as pl
from jax.experimental.pallas import tpu as pltpu
from jax.sharding import PartitionSpec as P

F32 = jnp.float32
BF16 = jnp.bfloat16
LANES = 128
PARTIAL = BF16


def contract(a, b, dims):
    return lax.dot_general(a, b, (dims, ((), ())), preferred_element_type=F32)


def halves(value):
    high = value.astype(BF16)
    return high, (value - high.astype(F32)).astype(BF16)


def lift_kernel(helpers, ids_ref, test_ref, points_ref, own_ref, *send_refs):
    helper = lax.axis_index("help")
    count = points_ref.shape[0]
    ids = ids_ref[:, pl.ds(pl.multiple_of(helper * count, LANES), count)]
    test = test_ref[...]
    rows = [
        jnp.where(ids == (helper ^ d), test, jnp.zeros((), BF16)) for d in range(helpers)
    ]
    total = contract(jnp.concatenate(rows, axis=0), points_ref[...], ((1,), (0,)))
    rank = test.shape[0]
    own_ref[...] = total[:rank]
    for d in range(1, helpers):
        send_refs[d - 1][...] = total[d * rank : (d + 1) * rank].astype(send_refs[d - 1].dtype)


def score_kernel(groups, helpers, *refs):
    tests = refs[:groups]
    queries = refs[groups : groups + helpers]
    probes = refs[groups + helpers : groups + 2 * helpers]
    outs = refs[groups + 2 * helpers :]
    shard, helper = lax.axis_index("shard"), lax.axis_index("help")
    rank, width = tests[0].shape
    lifter = jnp.concatenate([t[...] for t in tests], axis=0)
    total = None
    tally = [None] * groups
    for q_ref, id_ref in zip(queries, probes):
        rows = q_ref[...]
        lifted = contract(lifter, rows, ((1,), (1,)))
        first, second = id_ref[0:1, :], id_ref[1:2, :]
        kept = []
        for d in range(groups):
            cluster = (shard ^ d) * helpers + helper
            hit = (first == cluster) | (second == cluster)
            kept.append(jnp.where(hit, lifted[d * rank : (d + 1) * rank], 0.0))
            here = jnp.sum(hit.astype(F32), axis=1, keepdims=True)
            tally[d] = here if tally[d] is None else tally[d] + here
        high, low = halves(jnp.concatenate(kept, axis=0))
        part = contract(high, rows, ((1,), (0,))) + contract(low, rows, ((1,), (0,)))
        total = part if total is None else total + part
    line = lax.broadcasted_iota(jnp.int32, (rank, LANES), 0)
    for d in range(groups):
        outs[d][:, :width] = total[d * rank : (d + 1) * rank].astype(BF16)
        many = jnp.floor(tally[d] * (1.0 / 256.0))
        rest = tally[d] - 256.0 * many
        outs[d][:, width:] = jnp.where(line == 0, many, jnp.where(line == 1, rest, 0.0)).astype(BF16)


def scale_kernel(groups, ids_ref, *refs):
    helper = lax.axis_index("help")
    parts, out_ref = refs[:groups], refs[groups]
    width = out_ref.shape[1]
    total = parts[0][...].astype(F32)
    for part in parts[1:]:
        total = total + part[...].astype(F32)
    queried = 256.0 * total[0:1, width : width + 1] + total[1:2, width : width + 1]
    resident = jnp.sum((ids_ref[...] == helper).astype(F32), axis=1, keepdims=True)
    factor = lax.rsqrt((queried + 1.0) * (queried + resident)) * (1.0 / width)
    out_ref[...] = (total[:, :width] * factor).astype(out_ref.dtype)


def sketch_kernel(helpers, ids_ref, points_ref, *refs):
    scaled = refs[:helpers]
    sketch_ref, own_ref, *send_refs = refs[helpers:]
    helper = lax.axis_index("help")
    count = points_ref.shape[0]
    rank = sketch_ref.shape[0]
    everyone = ids_ref[...]
    ids = ids_ref[:, pl.ds(pl.multiple_of(helper * count, LANES), count)]
    points = points_ref[...]
    product = contract(jnp.concatenate([s[...] for s in scaled], axis=0), points, ((1,), (1,)))
    sketch = jnp.zeros((rank, count), F32)
    for d in range(helpers):
        sketch = jnp.where(ids == (helper ^ d), product[d * rank : (d + 1) * rank], sketch)
    sketch_ref[...] = sketch
    rounded = sketch.astype(BF16)
    rows = [
        jnp.where(ids == (helper ^ d), rounded, jnp.zeros((), BF16)) for d in range(helpers)
    ]
    summed = contract(jnp.concatenate(rows, axis=0), points, ((1,), (0,)))
    for d in range(helpers):
        resident = jnp.sum((everyone == (helper ^ d)).astype(F32), axis=1, keepdims=True)
        block = summed[d * rank : (d + 1) * rank] * lax.rsqrt(resident)
        if d == 0:
            own_ref[...] = block
        else:
            send_refs[d - 1][...] = block.astype(send_refs[d - 1].dtype)


def swap(value, axis, d):
    size = lax.axis_size(axis)
    return lax.ppermute(value, axis, [(i, i ^ d) for i in range(size)])


def shards(queries, probe_group, probe_local, points, point_cluster, test_matrix):
    groups = lax.axis_size("shard")
    helpers = lax.axis_size("help")
    rank = test_matrix.shape[0]
    own_points, width = points.shape
    block = jax.ShapeDtypeStruct((rank, width), F32)
    sent = jax.ShapeDtypeStruct((rank, width), PARTIAL)
    params = pltpu.CompilerParams(vmem_limit_bytes=48 * 1024 * 1024)

    own, *out = pl.pallas_call(
        functools.partial(lift_kernel, helpers),
        out_shape=[block] + [sent] * (helpers - 1),
        compiler_params=params,
        name="lift",
    )(point_cluster, test_matrix, points)
    got = [swap(out[d - 1], "help", d) for d in range(1, helpers)]

    probes = (probe_group * helpers + probe_local).T
    peer_probes = [probes] + [swap(probes, "help", d) for d in range(1, helpers)]
    peer_rows = [queries] + [swap(queries, "help", d) for d in range(1, helpers)]

    lifter = own
    for part in got:
        lifter = lifter + part.astype(F32)
    lifter = lifter.astype(BF16)
    lifters = [lifter] + [swap(lifter, "shard", d) for d in range(1, groups)]

    moments = pl.pallas_call(
        functools.partial(score_kernel, groups, helpers),
        out_shape=[jax.ShapeDtypeStruct((rank, width + LANES), BF16)] * groups,
        compiler_params=params,
        name="score",
    )(*lifters, *peer_rows, *peer_probes)
    moments = [moments[0]] + [swap(moments[d], "shard", d) for d in range(1, groups)]

    scaled = pl.pallas_call(
        functools.partial(scale_kernel, groups),
        out_shape=jax.ShapeDtypeStruct((rank, width), BF16),
        compiler_params=params,
        name="scale",
    )(point_cluster, *moments)
    scaled = [scaled] + [swap(scaled, "help", d) for d in range(1, helpers)]

    sketch, own, *out = pl.pallas_call(
        functools.partial(sketch_kernel, helpers),
        out_shape=[jax.ShapeDtypeStruct((rank, own_points), F32), block] + [sent] * (helpers - 1),
        compiler_params=params,
        name="sketch",
    )(point_cluster, points, *scaled)
    regressor = own
    for d in range(1, helpers):
        regressor = regressor + swap(out[d - 1], "help", d).astype(F32)
    return sketch, regressor[None]


def solution(mesh):
    in_specs = (
        P(("shard", "help"), None),
        P(("shard", "help"), None),
        P(("shard", "help"), None),
        P(("shard", "help"), None),
        P("shard", None),
        P(None, ("shard", "help")),
    )
    out_specs = (P(None, ("shard", "help")), P(("shard", "help"), None, None))
    return jax.shard_map(shards, mesh=mesh, in_specs=in_specs, out_specs=out_specs, check_vma=False)
```

time: 280 us -> 81.7 us (0.29)
  waiting for transfers between devices: 156 us -> 33.5 us
  local copies, waits for them, and re-layouts: 32.5 us -> 2.98 us
  matrix products: 28.3 us -> 0 us
  blocking collectives: 28.1 us -> 0 us
  starting transfers between devices: 12.5 us -> 39.3 us
  between operations: 14.2 us -> 0.72 us
  other arithmetic: 7.27 us -> 0.69 us
  Pallas kernels: 0 us -> 4.36 us
    all_to_all x2 -> x0, waiting for transfers between devices: 136 us -> none  [the longest x1 136 us: shards(): lax.all_to_all(outgoing, 'shard', split_axis=0, concat_axis=0, tiled=True)]
    ppermute x0 -> x29, starting transfers between devices: none -> 39.3 us  [swap(): return lax.ppermute(value, axis, [(i, i ^ d) for i in range(size)])]
    ppermute x0 -> x29, waiting for transfers between devices: none -> 33.5 us  [swap(): return lax.ppermute(value, axis, [(i, i ^ d) for i in range(size)])]
    dot_general x5 -> x0, matrix products: 28.3 us -> none  [the longest x2 15.6 us: score_piece(): lax.dot_general(piece_x, query_rows, (((1,), (1,)), ((), ())), preferred_...]
    scatter x2 -> x0, local copies, waits for them, and re-layouts: 22.5 us -> none  [the longest x1 13.9 us: pack_rows(): filled = jnp.zeros((groups * blocks * capacity, feature_width), jnp.bfloa...]
    reduce_scatter x1 -> x0, waiting for transfers between devices: 19.4 us -> none  [shards(): lax.psum_scatter(summed.reshape(CL_DEV * lax.axis_size('help'), rounded.s...]
    psum x1 -> x0, blocking collectives: 16.3 us -> none  [shards(): lax.psum(jnp.dot(test_matrix, scores, preferred_element_type=jnp.float32)...]
    all_to_all x2 -> x0, starting transfers between devices: 12.2 us -> none  [the longest x1 6.11 us: shards(): lax.all_to_all(outgoing, 'shard', split_axis=0, concat_axis=0, tiled=True)]
  transfers between devices with their start and end apart: 4 -> 29, of which waited for: 2 -> 16; matrix products, arithmetic and copies ran while one was open for 13% -> 0% of each run, Pallas kernels for 0% -> 0%
where the time goes in v1:
time: 81.7 us; the launch traced here: 81.5 us
  starting transfers between devices  39.3 us (48%)
  waiting for transfers between devices  33.5 us (41%)
  Pallas kernels  4.36 us (5%)
  local copies, waits for them, and re-layouts  2.98 us (4%)
    ppermute x29, starting transfers between devices, swap(): return lax.ppermute(value, axis, [(i, i ^ d) for i in range(size)])  39.3 us
    ppermute x29, waiting for transfers between devices, swap(): return lax.ppermute(value, axis, [(i, i ^ d) for i in range(size)])  33.5 us
    unnamed x14, local copies, waits for them, and re-layouts  2.98 us
    pallas_call x1, Pallas kernels, shards(): pl.pallas_call(functools.partial(score_kernel, groups, helpers), out_shap...  2.26 us
  transfers between devices with their start and end apart: 29, of which 16 were waited for; matrix products, arithmetic and copies ran while one was open for 0% of the time, Pallas kernels for 0%

profile of v1, /device:TPU:0, one launch (start us, length us, event | category | flops | bytes accessed | tf_op | source)
XLA Modules:
  0.0 81.5 jit_solution(12955595505857659925)
XLA Ops:
  0.6 0.0 copy-start
  0.6 1.4 %copy-done = bf16[1024,768]{1,0:T(8,128)(2,1)S(1)} copy-done((bf16[1024,768]{1,0:T(8,128)(2,1)S(1)}, bf16[1024,768]{1,0:T(8,128)(2,1)}, u32[]{:S(2)}) %copy-start) | copy-done | bytes 1572888
  2.0 0.7 copy-done.3
  2.8 0.8 %copy-done.4 = bf16[32,1024]{1,0:T(8,128)(2,1)S(1)} copy-done((bf16[32,1024]{1,0:T(8,128)(2,1)S(1)}, bf16[32,1024]{1,0:T(8,128)(2,1)}, u32[]{:S(2)}) %copy-start.4) | copy-done | bytes 65560
  3.6 0.4 lift.1
  4.0 0.0 copy-start.1
  4.0 0.5 collective-permute-start
  4.5 2.6 %collective-permute-start.1 = (bf16[32,768]{1,0:T(8,128)(2,1)S(1)}, bf16[32,768]{1,0:T(8,128)(2,1)S(1)}, u32[]{:S(2)}, u32[]{:S(2)}) collective-permute-start(bf16[32,768]{1,0:T(8,128)(2,1)S(1)} %get-tuple-element.21), channel_id=1, source_target_pairs={{0,2},{1,3},{2,0},{3,1},{4,6},{5,7},{6,4},{7,5},{8,10},{9,11},{10,... | collective-permute-start | bytes 147464 | tf_op jit(solution)/shard_map/ppermute | solution.py:115
  7.1 0.1 collective-permute-start.2
  7.2 1.7 %collective-permute-start.11 = (bf16[256,768]{1,0:T(8,128)(2,1)S(1)}, bf16[256,768]{1,0:T(8,128)(2,1)S(1)}, u32[]{:S(2)}, u32[]{:S(2)}) collective-permute-start(bf16[256,768]{1,0:T(8,128)(2,1)S(1)} %copy-done.2), channel_id=1, source_target_pairs={{0,2},{1,3},{2,0},{3,1},{4,6},{5,7},{6,4},{7,5},{8,10},{9,11},{10,... | collective-permute-start | bytes 1179656 | tf_op jit(solution)/shard_map/ppermute | solution.py:115
  8.9 0.1 collective-permute-start.10
  8.9 0.0 collective-permute-done
  9.0 0.3 collective-permute-start.12
  9.3 0.1 collective-permute-done.1
  9.4 1.4 %collective-permute-done.2 = bf16[32,768]{1,0:T(8,128)(2,1)S(1)} collective-permute-done((bf16[32,768]{1,0:T(8,128)(2,1)S(1)}, bf16[32,768]{1,0:T(8,128)(2,1)S(1)}, u32[]{:S(2)}, u32[]{:S(2)}) %collective-permute-start.2) | collective-permute-done | bytes 49184 | tf_op jit(solution)/shard_map/ppermute | solution.py:115
  10.8 4.6 %collective-permute-start.9 = (bf16[32,768]{1,0:T(8,128)(2,1)S(1)}, bf16[32,768]{1,0:T(8,128)(2,1)S(1)}, u32[]{:S(2)}, u32[]{:S(2)}) collective-permute-start(bf16[32,768]{1,0:T(8,128)(2,1)S(1)} %add_convert_fusion.refs_0_), channel_id=1, source_target_pairs={{0,28},{4,24},{8,20},{12,16},{16,12},{20,8},{24,4},{28,0},{1,29},{... | collective-permute-start | bytes 147464 | tf_op jit(solution)/shard_map/ppermute | solution.py:115
  15.4 1.0 %collective-permute-start.15 = (s32[2,256]{1,0:T(2,128)S(1)}, s32[2,256]{1,0:T(2,128)S(1)}, u32[]{:S(2)}, u32[]{:S(2)}) collective-permute-start(s32[2,256]{1,0:T(2,128)S(1)} %add_bitcast_fusion.1.refs_12_), channel_id=1, source_target_pairs={{0,3},{1,2},{2,1},{3,0},{4,7},{5,6},{6,5},{7,4},{8,11},{9,10},{10,... | collective-permute-start | bytes 6152 | tf_op jit(solution)/shard_map/ppermute | solution.py:115
  16.5 11.2 %collective-permute-done.15.refs_15_ = s32[2,256]{1,0:T(2,128)S(1)} collective-permute-done((s32[2,256]{1,0:T(2,128)S(1)}, s32[2,256]{1,0:T(2,128)S(1)}, u32[]{:S(2)}, u32[]{:S(2)}) %collective-permute-start.15) | collective-permute-done | bytes 2080 | tf_op jit(solution)/shard_map/ppermute | solution.py:115
  27.7 1.1 %collective-permute-start.14 = (s32[2,256]{1,0:T(2,128)S(1)}, s32[2,256]{1,0:T(2,128)S(1)}, u32[]{:S(2)}, u32[]{:S(2)}) collective-permute-start(s32[2,256]{1,0:T(2,128)S(1)} %add_bitcast_fusion.1.refs_12_), channel_id=1, source_target_pairs={{0,2},{1,3},{2,0},{3,1},{4,6},{5,7},{6,4},{7,5},{8,10},{9,11},{10,... | collective-permute-start | bytes 6152 | tf_op jit(solution)/shard_map/ppermute | solution.py:115
  28.7 2.5 %collective-permute-done.14.refs_14_ = s32[2,256]{1,0:T(2,128)S(1)} collective-permute-done((s32[2,256]{1,0:T(2,128)S(1)}, s32[2,256]{1,0:T(2,128)S(1)}, u32[]{:S(2)}, u32[]{:S(2)}) %collective-permute-start.14) | collective-permute-done | bytes 2080 | tf_op jit(solution)/shard_map/ppermute | solution.py:115
  31.3 0.0 collective-permute-start.13
  31.3 1.2 %collective-permute-done.13.refs_13_ = s32[2,256]{1,0:T(2,128)S(1)} collective-permute-done((s32[2,256]{1,0:T(2,128)S(1)}, s32[2,256]{1,0:T(2,128)S(1)}, u32[]{:S(2)}, u32[]{:S(2)}) %collective-permute-start.13) | collective-permute-done | bytes 2080 | tf_op jit(solution)/shard_map/ppermute | solution.py:115
  32.4 3.6 %collective-permute-start.8 = (bf16[32,768]{1,0:T(8,128)(2,1)S(1)}, bf16[32,768]{1,0:T(8,128)(2,1)S(1)}, u32[]{:S(2)}, u32[]{:S(2)}) collective-permute-start(bf16[32,768]{1,0:T(8,128)(2,1)S(1)} %add_convert_fusion.refs_0_), channel_id=1, source_target_pairs={{0,24},{4,28},{8,16},{12,20},{16,8},{20,12},{24,0},{28,4},{1,25},{... | collective-permute-start | bytes 147464 | tf_op jit(solution)/shard_map/ppermute | solution.py:115
  36.0 0.0 collective-permute-done.9.refs_7_
  36.0 0.4 collective-permute-start.7
  36.4 1.9 %collective-permute-done.8.refs_6_ = bf16[32,768]{1,0:T(8,128)(2,1)S(1)} collective-permute-done((bf16[32,768]{1,0:T(8,128)(2,1)S(1)}, bf16[32,768]{1,0:T(8,128)(2,1)S(1)}, u32[]{:S(2)}, u32[]{:S(2)}) %collective-permute-start.8) | collective-permute-done | bytes 49184 | tf_op jit(solution)/shard_map/ppermute | solution.py:115
  38.4 1.5 %collective-permute-start.6 = (bf16[32,768]{1,0:T(8,128)(2,1)S(1)}, bf16[32,768]{1,0:T(8,128)(2,1)S(1)}, u32[]{:S(2)}, u32[]{:S(2)}) collective-permute-start(bf16[32,768]{1,0:T(8,128)(2,1)S(1)} %add_convert_fusion.refs_0_), channel_id=1, source_target_pairs={{0,16},{4,20},{8,24},{12,28},{16,0},{20,4},{24,8},{28,12},{1,17},{... | collective-permute-start | bytes 147464 | tf_op jit(solution)/shard_map/ppermute | solution.py:115
  39.9 2.0 %collective-permute-done.7.refs_5_ = bf16[32,768]{1,0:T(8,128)(2,1)S(1)} collective-permute-done((bf16[32,768]{1,0:T(8,128)(2,1)S(1)}, bf16[32,768]{1,0:T(8,128)(2,1)S(1)}, u32[]{:S(2)}, u32[]{:S(2)}) %collective-permute-start.7) | collective-permute-done | bytes 49184 | tf_op jit(solution)/shard_map/ppermute | solution.py:115
  41.9 1.9 %collective-permute-start.5 = (bf16[32,768]{1,0:T(8,128)(2,1)S(1)}, bf16[32,768]{1,0:T(8,128)(2,1)S(1)}, u32[]{:S(2)}, u32[]{:S(2)}) collective-permute-start(bf16[32,768]{1,0:T(8,128)(2,1)S(1)} %add_convert_fusion.refs_0_), channel_id=1, source_target_pairs={{0,12},{4,8},{8,4},{12,0},{16,28},{20,24},{24,20},{28,16},{1,13},{... | collective-permute-start | bytes 147464 | tf_op jit(solution)/shard_map/ppermute | solution.py:115
  43.8 0.0 collective-permute-done.6.refs_4_
  43.8 2.1 %collective-permute-start.4 = (bf16[32,768]{1,0:T(8,128)(2,1)S(1)}, bf16[32,768]{1,0:T(8,128)(2,1)S(1)}, u32[]{:S(2)}, u32[]{:S(2)}) collective-permute-start(bf16[32,768]{1,0:T(8,128)(2,1)S(1)} %add_convert_fusion.refs_0_), channel_id=1, source_target_pairs={{0,8},{4,12},{8,0},{12,4},{16,24},{20,28},{24,16},{28,20},{1,9},{5... | collective-permute-start | bytes 147464 | tf_op jit(solution)/shard_map/ppermute | solution.py:115
  45.9 1.0 %collective-permute-done.5.refs_3_ = bf16[32,768]{1,0:T(8,128)(2,1)S(1)} collective-permute-done((bf16[32,768]{1,0:T(8,128)(2,1)S(1)}, bf16[32,768]{1,0:T(8,128)(2,1)S(1)}, u32[]{:S(2)}, u32[]{:S(2)}) %collective-permute-start.5) | collective-permute-done | bytes 49184 | tf_op jit(solution)/shard_map/ppermute | solution.py:115
  46.9 2.6 %collective-permute-start.3 = (bf16[32,768]{1,0:T(8,128)(2,1)S(1)}, bf16[32,768]{1,0:T(8,128)(2,1)S(1)}, u32[]{:S(2)}, u32[]{:S(2)}) collective-permute-start(bf16[32,768]{1,0:T(8,128)(2,1)S(1)} %add_convert_fusion.refs_0_), channel_id=1, source_target_pairs={{0,4},{4,0},{8,12},{12,8},{16,20},{20,16},{24,28},{28,24},{1,5},{5... | collective-permute-start | bytes 147464 | tf_op jit(solution)/shard_map/ppermute | solution.py:115
  49.5 0.0 collective-permute-done.4.refs_2_
  49.5 2.1 %collective-permute-done.3.refs_1_ = bf16[32,768]{1,0:T(8,128)(2,1)S(1)} collective-permute-done((bf16[32,768]{1,0:T(8,128)(2,1)S(1)}, bf16[32,768]{1,0:T(8,128)(2,1)S(1)}, u32[]{:S(2)}, u32[]{:S(2)}) %collective-permute-start.3) | collective-permute-done | bytes 49184 | tf_op jit(solution)/shard_map/ppermute | solution.py:115
  51.6 0.0 collective-permute-done.11.refs_10_
  51.6 0.0 collective-permute-done.10.refs_9_
  51.6 0.0 collective-permute-done.12.refs_11_
  51.6 2.3 %score.1 = (bf16[32,896]{1,0:T(8,128)(2,1)S(1)}, bf16[32,896]{1,0:T(8,128)(2,1)S(1)}, bf16[32,896]{1,0:T(8,128)(2,1)S(1)}, bf16[32,896]{1,0:T(8,128)(2,1)S(1)}, ...) custom-call(bf16[32,768]{1,0:T(8,128)(2,1)S(1)} %add_convert_fusion., ...), custom_call_target="tpu_custom_call" | custom-call | tf_op jit(solution)/shard_map/score/pallas_call | solution.py:145
  53.8 2.1 %collective-permute-start.16 = (bf16[32,896]{1,0:T(8,128)(2,1)S(1)}, bf16[32,896]{1,0:T(8,128)(2,1)S(1)}, u32[]{:S(2)}, u32[]{:S(2)}) collective-permute-start(bf16[32,896]{1,0:T(8,128)(2,1)S(1)} %get-tuple-element.24), channel_id=1, source_target_pairs={{0,4},{4,0},{8,12},{12,8},{16,20},{20,16},{24,28},{28,24},{1,5},{5... | collective-permute-start | bytes 172040 | tf_op jit(solution)/shard_map/ppermute | solution.py:115
  55.9 0.0 collective-permute-start.17
  55.9 1.5 %collective-permute-start.18 = (bf16[32,896]{1,0:T(8,128)(2,1)S(1)}, bf16[32,896]{1,0:T(8,128)(2,1)S(1)}, u32[]{:S(2)}, u32[]{:S(2)}) collective-permute-start(bf16[32,896]{1,0:T(8,128)(2,1)S(1)} %get-tuple-element.26), channel_id=1, source_target_pairs={{0,12},{4,8},{8,4},{12,0},{16,28},{20,24},{24,20},{28,16},{1,13},{... | collective-permute-start | bytes 172040 | tf_op jit(solution)/shard_map/ppermute | solution.py:115
  57.5 1.0 %collective-permute-start.19 = (bf16[32,896]{1,0:T(8,128)(2,1)S(1)}, bf16[32,896]{1,0:T(8,128)(2,1)S(1)}, u32[]{:S(2)}, u32[]{:S(2)}) collective-permute-start(bf16[32,896]{1,0:T(8,128)(2,1)S(1)} %get-tuple-element.27), channel_id=1, source_target_pairs={{0,16},{4,20},{8,24},{12,28},{16,0},{20,4},{24,8},{28,12},{1,17},{... | collective-permute-start | bytes 172040 | tf_op jit(solution)/shard_map/ppermute | solution.py:115
  58.4 3.4 %collective-permute-start.20 = (bf16[32,896]{1,0:T(8,128)(2,1)S(1)}, bf16[32,896]{1,0:T(8,128)(2,1)S(1)}, u32[]{:S(2)}, u32[]{:S(2)}) collective-permute-start(bf16[32,896]{1,0:T(8,128)(2,1)S(1)} %get-tuple-element.28), channel_id=1, source_target_pairs={{0,20},{4,16},{8,28},{12,24},{16,4},{20,0},{24,12},{28,8},{1,21},{... | collective-permute-start | bytes 172040 | tf_op jit(solution)/shard_map/ppermute | solution.py:115
  61.8 0.0 collective-permute-done.16.refs_1_
  61.8 0.8 collective-permute-start.21
  62.6 0.0 collective-permute-done.17.refs_2_
  62.6 2.5 %collective-permute-start.22 = (bf16[32,896]{1,0:T(8,128)(2,1)S(1)}, bf16[32,896]{1,0:T(8,128)(2,1)S(1)}, u32[]{:S(2)}, u32[]{:S(2)}) collective-permute-start(bf16[32,896]{1,0:T(8,128)(2,1)S(1)} %get-tuple-element.30), channel_id=1, source_target_pairs={{0,28},{4,24},{8,20},{12,16},{16,12},{20,8},{24,4},{28,0},{1,29},{... | collective-permute-start | bytes 172040 | tf_op jit(solution)/shard_map/ppermute | solution.py:115
  65.1 0.1 collective-permute-done.20.refs_5_
  65.2 2.5 %collective-permute-done.21.refs_6_ = bf16[32,896]{1,0:T(8,128)(2,1)S(1)} collective-permute-done((bf16[32,896]{1,0:T(8,128)(2,1)S(1)}, bf16[32,896]{1,0:T(8,128)(2,1)S(1)}, u32[]{:S(2)}, u32[]{:S(2)}) %collective-permute-start.21) | collective-permute-done | bytes 57376 | tf_op jit(solution)/shard_map/ppermute | solution.py:115
  67.8 1.7 %collective-permute-done.22.refs_7_ = bf16[32,896]{1,0:T(8,128)(2,1)S(1)} collective-permute-done((bf16[32,896]{1,0:T(8,128)(2,1)S(1)}, bf16[32,896]{1,0:T(8,128)(2,1)S(1)}, u32[]{:S(2)}, u32[]{:S(2)}) %collective-permute-start.22) | collective-permute-done | bytes 57376 | tf_op jit(solution)/shard_map/ppermute | solution.py:115
  69.5 0.2 scale.1.refs_0_
  69.7 0.1 collective-permute-start.25
  69.8 1.1 %collective-permute-start.24 = (bf16[32,768]{1,0:T(8,128)(2,1)S(1)}, bf16[32,768]{1,0:T(8,128)(2,1)S(1)}, u32[]{:S(2)}, u32[]{:S(2)}) collective-permute-start(bf16[32,768]{1,0:T(8,128)(2,1)S(1)} %scale.1.refs_0_), channel_id=1, source_target_pairs={{0,2},{1,3},{2,0},{3,1},{4,6},{5,7},{6,4},{7,5},{8,10},{9,11},{10,... | collective-permute-start | bytes 147464 | tf_op jit(solution)/shard_map/ppermute | solution.py:115
  70.9 0.7 collective-permute-start.23
  71.6 1.9 %collective-permute-done.25.refs_3_ = bf16[32,768]{1,0:T(8,128)(2,1)S(1)} collective-permute-done((bf16[32,768]{1,0:T(8,128)(2,1)S(1)}, bf16[32,768]{1,0:T(8,128)(2,1)S(1)}, u32[]{:S(2)}, u32[]{:S(2)}) %collective-permute-start.25) | collective-permute-done | bytes 49184 | tf_op jit(solution)/shard_map/ppermute | solution.py:115
  73.5 0.9 %collective-permute-done.24.refs_2_ = bf16[32,768]{1,0:T(8,128)(2,1)S(1)} collective-permute-done((bf16[32,768]{1,0:T(8,128)(2,1)S(1)}, bf16[32,768]{1,0:T(8,128)(2,1)S(1)}, u32[]{:S(2)}, u32[]{:S(2)}) %collective-permute-start.24) | collective-permute-done | bytes 49184 | tf_op jit(solution)/shard_map/ppermute | solution.py:115
  74.4 1.5 %sketch.1 = (f32[32,1024]{1,0:T(8,128)}, f32[32,768]{1,0:T(8,128)S(1)}, bf16[32,768]{1,0:T(8,128)(2,1)S(1)}, bf16[32,768]{1,0:T(8,128)(2,1)S(1)}, bf16[32,768]{1,0:T(8,128)(2,1)S(1)}) custom-call(s32[1,4096]{1,0:T(1,128)S(1)} %copy-done.3, bf16[1024,768]{1,0:T(8,128)(2,1)S(1)} %copy-done.1, bf16[32,768]{1,0:T(8,128)(2,1)S(1)} %scale.1.refs_0_, ...), custom_call_target="tpu_custom_call" | custom-call | tf_op jit(solution)/shard_map/sketch/pallas_call | solution.py:161
  75.9 0.1 collective-permute-start.26
  76.0 1.1 %collective-permute-start.27 = (bf16[32,768]{1,0:T(8,128)(2,1)S(1)}, bf16[32,768]{1,0:T(8,128)(2,1)S(1)}, u32[]{:S(2)}, u32[]{:S(2)}) collective-permute-start(bf16[32,768]{1,0:T(8,128)(2,1)S(1)} %get-tuple-element.34), channel_id=1, source_target_pairs={{0,2},{1,3},{2,0},{3,1},{4,6},{5,7},{6,4},{7,5},{8,10},{9,11},{10,... | collective-permute-start | bytes 147464 | tf_op jit(solution)/shard_map/ppermute | solution.py:115
  77.1 0.7 collective-permute-start.28
  77.8 2.3 %collective-permute-done.27 = bf16[32,768]{1,0:T(8,128)(2,1)S(1)} collective-permute-done((bf16[32,768]{1,0:T(8,128)(2,1)S(1)}, bf16[32,768]{1,0:T(8,128)(2,1)S(1)}, u32[]{:S(2)}, u32[]{:S(2)}) %collective-permute-start.27) | collective-permute-done | bytes 49184 | tf_op jit(solution)/shard_map/ppermute | solution.py:115
  80.1 0.7 collective-permute-done.28
  80.8 0.7 add_bitcast_fusion
  (15 shorter events, 0.1 us)
Async XLA Ops:
  0.6 1.4 %copy-start = (bf16[1024,768]{1,0:T(8,128)(2,1)S(1)}, bf16[1024,768]{1,0:T(8,128)(2,1)}, u32[]{:S(2)}) copy-start(bf16[1024,768]{1,0:T(8,128)(2,1)} %points_ref.3) | copy-start | bytes 4718596
  2.0 0.7 copy-start.3
  2.8 0.8 %copy-start.4 = (bf16[32,1024]{1,0:T(8,128)(2,1)S(1)}, bf16[32,1024]{1,0:T(8,128)(2,1)}, u32[]{:S(2)}) copy-start(bf16[32,1024]{1,0:T(8,128)(2,1)} %test_ref.1) | copy-start | bytes 196612
  3.6 3.6 %copy-start.2 = (bf16[256,768]{1,0:T(8,128)(2,1)S(1)}, bf16[256,768]{1,0:T(8,128)(2,1)}, u32[]{:S(2)}) copy-start(bf16[256,768]{1,0:T(8,128)(2,1)} %refs_8_.1) | copy-start | bytes 1179652
  3.6 11.8 %copy-start.5 = (s32[256,2]{0,1:T(2,128)S(1)}, s32[256,2]{0,1:T(2,128)}, u32[]{:S(2)}) copy-start(s32[256,2]{0,1:T(2,128)} %param.8) | copy-start | bytes 6148
  3.6 11.8 %copy-start.6 = (s32[256,2]{0,1:T(2,128)S(1)}, s32[256,2]{0,1:T(2,128)}, u32[]{:S(2)}) copy-start(s32[256,2]{0,1:T(2,128)} %param.7) | copy-start | bytes 6148
  4.0 70.4 %copy-start.1 = (bf16[1024,768]{1,0:T(8,128)(2,1)S(1)}, bf16[1024,768]{1,0:T(8,128)(2,1)}, u32[]{:S(2)}) copy-start(bf16[1024,768]{1,0:T(8,128)(2,1)} %points_ref.3) | copy-start | bytes 4718596
  4.0 4.9 %collective-permute-start = (bf16[32,768]{1,0:T(8,128)(2,1)S(1)}, bf16[32,768]{1,0:T(8,128)(2,1)S(1)}, u32[]{:S(2)}, u32[]{:S(2)}) collective-permute-start(bf16[32,768]{1,0:T(8,128)(2,1)S(1)} %get-tuple-element.20), channel_id=1, source_target_pairs={{0,1},{1,0},{2,3},{3,2},{4,5},{5,4},{6,7},{7,6},{8,9},{9,8},{10,11... | collective-permute-start | bytes 147464 | tf_op jit(solution)/shard_map/ppermute | solution.py:115
  4.5 4.9 %collective-permute-start.1 = (bf16[32,768]{1,0:T(8,128)(2,1)S(1)}, bf16[32,768]{1,0:T(8,128)(2,1)S(1)}, u32[]{:S(2)}, u32[]{:S(2)}) collective-permute-start(bf16[32,768]{1,0:T(8,128)(2,1)S(1)} %get-tuple-element.21), channel_id=1, source_target_pairs={{0,2},{1,3},{2,0},{3,1},{4,6},{5,7},{6,4},{7,5},{8,10},{9,11},{10,... | collective-permute-start | bytes 147464 | tf_op jit(solution)/shard_map/ppermute | solution.py:115
  7.1 3.7 %collective-permute-start.2 = (bf16[32,768]{1,0:T(8,128)(2,1)S(1)}, bf16[32,768]{1,0:T(8,128)(2,1)S(1)}, u32[]{:S(2)}, u32[]{:S(2)}) collective-permute-start(bf16[32,768]{1,0:T(8,128)(2,1)S(1)} %get-tuple-element.22), channel_id=1, source_target_pairs={{0,3},{1,2},{2,1},{3,0},{4,7},{5,6},{6,5},{7,4},{8,11},{9,10},{10,... | collective-permute-start | bytes 147464 | tf_op jit(solution)/shard_map/ppermute | solution.py:115
  7.2 44.4 %collective-permute-start.11 = (bf16[256,768]{1,0:T(8,128)(2,1)S(1)}, bf16[256,768]{1,0:T(8,128)(2,1)S(1)}, u32[]{:S(2)}, u32[]{:S(2)}) collective-permute-start(bf16[256,768]{1,0:T(8,128)(2,1)S(1)} %copy-done.2), channel_id=1, source_target_pairs={{0,2},{1,3},{2,0},{3,1},{4,6},{5,7},{6,4},{7,5},{8,10},{9,11},{10,... | collective-permute-start | bytes 1179656 | tf_op jit(solution)/shard_map/ppermute | solution.py:115
  8.9 42.7 %collective-permute-start.10 = (bf16[256,768]{1,0:T(8,128)(2,1)S(1)}, bf16[256,768]{1,0:T(8,128)(2,1)S(1)}, u32[]{:S(2)}, u32[]{:S(2)}) collective-permute-start(bf16[256,768]{1,0:T(8,128)(2,1)S(1)} %copy-done.2), channel_id=1, source_target_pairs={{0,1},{1,0},{2,3},{3,2},{4,5},{5,4},{6,7},{7,6},{8,9},{9,8},{10,11... | collective-permute-start | bytes 1179656 | tf_op jit(solution)/shard_map/ppermute | solution.py:115
  9.0 42.6 %collective-permute-start.12 = (bf16[256,768]{1,0:T(8,128)(2,1)S(1)}, bf16[256,768]{1,0:T(8,128)(2,1)S(1)}, u32[]{:S(2)}, u32[]{:S(2)}) collective-permute-start(bf16[256,768]{1,0:T(8,128)(2,1)S(1)} %copy-done.2), channel_id=1, source_target_pairs={{0,3},{1,2},{2,1},{3,0},{4,7},{5,6},{6,5},{7,4},{8,11},{9,10},{10,... | collective-permute-start | bytes 1179656 | tf_op jit(solution)/shard_map/ppermute | solution.py:115
  10.8 25.2 %collective-permute-start.9 = (bf16[32,768]{1,0:T(8,128)(2,1)S(1)}, bf16[32,768]{1,0:T(8,128)(2,1)S(1)}, u32[]{:S(2)}, u32[]{:S(2)}) collective-permute-start(bf16[32,768]{1,0:T(8,128)(2,1)S(1)} %add_convert_fusion.refs_0_), channel_id=1, source_target_pairs={{0,28},{4,24},{8,20},{12,16},{16,12},{20,8},{24,4},{28,0},{1,29},{... | collective-permute-start | bytes 147464 | tf_op jit(solution)/shard_map/ppermute | solution.py:115
  15.4 12.2 %collective-permute-start.15 = (s32[2,256]{1,0:T(2,128)S(1)}, s32[2,256]{1,0:T(2,128)S(1)}, u32[]{:S(2)}, u32[]{:S(2)}) collective-permute-start(s32[2,256]{1,0:T(2,128)S(1)} %add_bitcast_fusion.1.refs_12_), channel_id=1, source_target_pairs={{0,3},{1,2},{2,1},{3,0},{4,7},{5,6},{6,5},{7,4},{8,11},{9,10},{10,... | collective-permute-start | bytes 6152 | tf_op jit(solution)/shard_map/ppermute | solution.py:115
  27.7 3.6 %collective-permute-start.14 = (s32[2,256]{1,0:T(2,128)S(1)}, s32[2,256]{1,0:T(2,128)S(1)}, u32[]{:S(2)}, u32[]{:S(2)}) collective-permute-start(s32[2,256]{1,0:T(2,128)S(1)} %add_bitcast_fusion.1.refs_12_), channel_id=1, source_target_pairs={{0,2},{1,3},{2,0},{3,1},{4,6},{5,7},{6,4},{7,5},{8,10},{9,11},{10,... | collective-permute-start | bytes 6152 | tf_op jit(solution)/shard_map/ppermute | solution.py:115
  31.3 1.2 %collective-permute-start.13 = (s32[2,256]{1,0:T(2,128)S(1)}, s32[2,256]{1,0:T(2,128)S(1)}, u32[]{:S(2)}, u32[]{:S(2)}) collective-permute-start(s32[2,256]{1,0:T(2,128)S(1)} %add_bitcast_fusion.1.refs_12_), channel_id=1, source_target_pairs={{0,1},{1,0},{2,3},{3,2},{4,5},{5,4},{6,7},{7,6},{8,9},{9,8},{10,11... | collective-permute-start | bytes 6152 | tf_op jit(solution)/shard_map/ppermute | solution.py:115
  32.4 5.9 %collective-permute-start.8 = (bf16[32,768]{1,0:T(8,128)(2,1)S(1)}, bf16[32,768]{1,0:T(8,128)(2,1)S(1)}, u32[]{:S(2)}, u32[]{:S(2)}) collective-permute-start(bf16[32,768]{1,0:T(8,128)(2,1)S(1)} %add_convert_fusion.refs_0_), channel_id=1, source_target_pairs={{0,24},{4,28},{8,16},{12,20},{16,8},{20,12},{24,0},{28,4},{1,25},{... | collective-permute-start | bytes 147464 | tf_op jit(solution)/shard_map/ppermute | solution.py:115
  36.0 5.9 %collective-permute-start.7 = (bf16[32,768]{1,0:T(8,128)(2,1)S(1)}, bf16[32,768]{1,0:T(8,128)(2,1)S(1)}, u32[]{:S(2)}, u32[]{:S(2)}) collective-permute-start(bf16[32,768]{1,0:T(8,128)(2,1)S(1)} %add_convert_fusion.refs_0_), channel_id=1, source_target_pairs={{0,20},{4,16},{8,28},{12,24},{16,4},{20,0},{24,12},{28,8},{1,21},{... | collective-permute-start | bytes 147464 | tf_op jit(solution)/shard_map/ppermute | solution.py:115
  38.4 5.4 %collective-permute-start.6 = (bf16[32,768]{1,0:T(8,128)(2,1)S(1)}, bf16[32,768]{1,0:T(8,128)(2,1)S(1)}, u32[]{:S(2)}, u32[]{:S(2)}) collective-permute-start(bf16[32,768]{1,0:T(8,128)(2,1)S(1)} %add_convert_fusion.refs_0_), channel_id=1, source_target_pairs={{0,16},{4,20},{8,24},{12,28},{16,0},{20,4},{24,8},{28,12},{1,17},{... | collective-permute-start | bytes 147464 | tf_op jit(solution)/shard_map/ppermute | solution.py:115
  41.9 5.0 %collective-permute-start.5 = (bf16[32,768]{1,0:T(8,128)(2,1)S(1)}, bf16[32,768]{1,0:T(8,128)(2,1)S(1)}, u32[]{:S(2)}, u32[]{:S(2)}) collective-permute-start(bf16[32,768]{1,0:T(8,128)(2,1)S(1)} %add_convert_fusion.refs_0_), channel_id=1, source_target_pairs={{0,12},{4,8},{8,4},{12,0},{16,28},{20,24},{24,20},{28,16},{1,13},{... | collective-permute-start | bytes 147464 | tf_op jit(solution)/shard_map/ppermute | solution.py:115
  43.8 5.7 %collective-permute-start.4 = (bf16[32,768]{1,0:T(8,128)(2,1)S(1)}, bf16[32,768]{1,0:T(8,128)(2,1)S(1)}, u32[]{:S(2)}, u32[]{:S(2)}) collective-permute-start(bf16[32,768]{1,0:T(8,128)(2,1)S(1)} %add_convert_fusion.refs_0_), channel_id=1, source_target_pairs={{0,8},{4,12},{8,0},{12,4},{16,24},{20,28},{24,16},{28,20},{1,9},{5... | collective-permute-start | bytes 147464 | tf_op jit(solution)/shard_map/ppermute | solution.py:115
  46.9 4.7 %collective-permute-start.3 = (bf16[32,768]{1,0:T(8,128)(2,1)S(1)}, bf16[32,768]{1,0:T(8,128)(2,1)S(1)}, u32[]{:S(2)}, u32[]{:S(2)}) collective-permute-start(bf16[32,768]{1,0:T(8,128)(2,1)S(1)} %add_convert_fusion.refs_0_), channel_id=1, source_target_pairs={{0,4},{4,0},{8,12},{12,8},{16,20},{20,16},{24,28},{28,24},{1,5},{5... | collective-permute-start | bytes 147464 | tf_op jit(solution)/shard_map/ppermute | solution.py:115
  53.8 7.9 %collective-permute-start.16 = (bf16[32,896]{1,0:T(8,128)(2,1)S(1)}, bf16[32,896]{1,0:T(8,128)(2,1)S(1)}, u32[]{:S(2)}, u32[]{:S(2)}) collective-permute-start(bf16[32,896]{1,0:T(8,128)(2,1)S(1)} %get-tuple-element.24), channel_id=1, source_target_pairs={{0,4},{4,0},{8,12},{12,8},{16,20},{20,16},{24,28},{28,24},{1,5},{5... | collective-permute-start | bytes 172040 | tf_op jit(solution)/shard_map/ppermute | solution.py:115
  55.9 6.7 %collective-permute-start.17 = (bf16[32,896]{1,0:T(8,128)(2,1)S(1)}, bf16[32,896]{1,0:T(8,128)(2,1)S(1)}, u32[]{:S(2)}, u32[]{:S(2)}) collective-permute-start(bf16[32,896]{1,0:T(8,128)(2,1)S(1)} %get-tuple-element.25), channel_id=1, source_target_pairs={{0,8},{4,12},{8,0},{12,4},{16,24},{20,28},{24,16},{28,20},{1,9},{5... | collective-permute-start | bytes 172040 | tf_op jit(solution)/shard_map/ppermute | solution.py:115
  55.9 9.2 %collective-permute-start.18 = (bf16[32,896]{1,0:T(8,128)(2,1)S(1)}, bf16[32,896]{1,0:T(8,128)(2,1)S(1)}, u32[]{:S(2)}, u32[]{:S(2)}) collective-permute-start(bf16[32,896]{1,0:T(8,128)(2,1)S(1)} %get-tuple-element.26), channel_id=1, source_target_pairs={{0,12},{4,8},{8,4},{12,0},{16,28},{20,24},{24,20},{28,16},{1,13},{... | collective-permute-start | bytes 172040 | tf_op jit(solution)/shard_map/ppermute | solution.py:115
  57.5 7.7 %collective-permute-start.19 = (bf16[32,896]{1,0:T(8,128)(2,1)S(1)}, bf16[32,896]{1,0:T(8,128)(2,1)S(1)}, u32[]{:S(2)}, u32[]{:S(2)}) collective-permute-start(bf16[32,896]{1,0:T(8,128)(2,1)S(1)} %get-tuple-element.27), channel_id=1, source_target_pairs={{0,16},{4,20},{8,24},{12,28},{16,0},{20,4},{24,8},{28,12},{1,17},{... | collective-permute-start | bytes 172040 | tf_op jit(solution)/shard_map/ppermute | solution.py:115
  58.4 6.8 %collective-permute-start.20 = (bf16[32,896]{1,0:T(8,128)(2,1)S(1)}, bf16[32,896]{1,0:T(8,128)(2,1)S(1)}, u32[]{:S(2)}, u32[]{:S(2)}) collective-permute-start(bf16[32,896]{1,0:T(8,128)(2,1)S(1)} %get-tuple-element.28), channel_id=1, source_target_pairs={{0,20},{4,16},{8,28},{12,24},{16,4},{20,0},{24,12},{28,8},{1,21},{... | collective-permute-start | bytes 172040 | tf_op jit(solution)/shard_map/ppermute | solution.py:115
  61.8 6.0 %collective-permute-start.21 = (bf16[32,896]{1,0:T(8,128)(2,1)S(1)}, bf16[32,896]{1,0:T(8,128)(2,1)S(1)}, u32[]{:S(2)}, u32[]{:S(2)}) collective-permute-start(bf16[32,896]{1,0:T(8,128)(2,1)S(1)} %get-tuple-element.29), channel_id=1, source_target_pairs={{0,24},{4,28},{8,16},{12,20},{16,8},{20,12},{24,0},{28,4},{1,25},{... | collective-permute-start | bytes 172040 | tf_op jit(solution)/shard_map/ppermute | solution.py:115
  62.6 6.9 %collective-permute-start.22 = (bf16[32,896]{1,0:T(8,128)(2,1)S(1)}, bf16[32,896]{1,0:T(8,128)(2,1)S(1)}, u32[]{:S(2)}, u32[]{:S(2)}) collective-permute-start(bf16[32,896]{1,0:T(8,128)(2,1)S(1)} %get-tuple-element.30), channel_id=1, source_target_pairs={{0,28},{4,24},{8,20},{12,16},{16,12},{20,8},{24,4},{28,0},{1,29},{... | collective-permute-start | bytes 172040 | tf_op jit(solution)/shard_map/ppermute | solution.py:115
  69.7 3.8 %collective-permute-start.25 = (bf16[32,768]{1,0:T(8,128)(2,1)S(1)}, bf16[32,768]{1,0:T(8,128)(2,1)S(1)}, u32[]{:S(2)}, u32[]{:S(2)}) collective-permute-start(bf16[32,768]{1,0:T(8,128)(2,1)S(1)} %scale.1.refs_0_), channel_id=1, source_target_pairs={{0,3},{1,2},{2,1},{3,0},{4,7},{5,6},{6,5},{7,4},{8,11},{9,10},{10,... | collective-permute-start | bytes 147464 | tf_op jit(solution)/shard_map/ppermute | solution.py:115
  69.8 4.6 %collective-permute-start.24 = (bf16[32,768]{1,0:T(8,128)(2,1)S(1)}, bf16[32,768]{1,0:T(8,128)(2,1)S(1)}, u32[]{:S(2)}, u32[]{:S(2)}) collective-permute-start(bf16[32,768]{1,0:T(8,128)(2,1)S(1)} %scale.1.refs_0_), channel_id=1, source_target_pairs={{0,2},{1,3},{2,0},{3,1},{4,6},{5,7},{6,4},{7,5},{8,10},{9,11},{10,... | collective-permute-start | bytes 147464 | tf_op jit(solution)/shard_map/ppermute | solution.py:115
  70.9 3.5 %collective-permute-start.23 = (bf16[32,768]{1,0:T(8,128)(2,1)S(1)}, bf16[32,768]{1,0:T(8,128)(2,1)S(1)}, u32[]{:S(2)}, u32[]{:S(2)}) collective-permute-start(bf16[32,768]{1,0:T(8,128)(2,1)S(1)} %scale.1.refs_0_), channel_id=1, source_target_pairs={{0,1},{1,0},{2,3},{3,2},{4,5},{5,4},{6,7},{7,6},{8,9},{9,8},{10,11... | collective-permute-start | bytes 147464 | tf_op jit(solution)/shard_map/ppermute | solution.py:115
  75.9 1.9 %collective-permute-start.26 = (bf16[32,768]{1,0:T(8,128)(2,1)S(1)}, bf16[32,768]{1,0:T(8,128)(2,1)S(1)}, u32[]{:S(2)}, u32[]{:S(2)}) collective-permute-start(bf16[32,768]{1,0:T(8,128)(2,1)S(1)} %get-tuple-element.33), channel_id=1, source_target_pairs={{0,1},{1,0},{2,3},{3,2},{4,5},{5,4},{6,7},{7,6},{8,9},{9,8},{10,11... | collective-permute-start | bytes 147464 | tf_op jit(solution)/shard_map/ppermute | solution.py:115
  76.0 4.1 %collective-permute-start.27 = (bf16[32,768]{1,0:T(8,128)(2,1)S(1)}, bf16[32,768]{1,0:T(8,128)(2,1)S(1)}, u32[]{:S(2)}, u32[]{:S(2)}) collective-permute-start(bf16[32,768]{1,0:T(8,128)(2,1)S(1)} %get-tuple-element.34), channel_id=1, source_target_pairs={{0,2},{1,3},{2,0},{3,1},{4,6},{5,7},{6,4},{7,5},{8,10},{9,11},{10,... | collective-permute-start | bytes 147464 | tf_op jit(solution)/shard_map/ppermute | solution.py:115
  77.1 3.7 %collective-permute-start.28 = (bf16[32,768]{1,0:T(8,128)(2,1)S(1)}, bf16[32,768]{1,0:T(8,128)(2,1)S(1)}, u32[]{:S(2)}, u32[]{:S(2)}) collective-permute-start(bf16[32,768]{1,0:T(8,128)(2,1)S(1)} %get-tuple-element.35), channel_id=1, source_target_pairs={{0,3},{1,2},{2,1},{3,0},{4,7},{5,6},{6,5},{7,4},{8,11},{9,10},{10,... | collective-permute-start | bytes 147464 | tf_op jit(solution)/shard_map/ppermute | solution.py:115

commit v2 on v1

v2 whole, which is shorter than its diff:
```python
import functools

import jax
import jax.numpy as jnp
from jax import lax
from jax.experimental import pallas as pl
from jax.experimental.pallas import tpu as pltpu
from jax.sharding import PartitionSpec as P

F32 = jnp.float32
BF16 = jnp.bfloat16
LANES = 128
TILE = 16
INNER = 2
CHUNKS = 4
FIRST = 60

HBM = pl.BlockSpec(memory_space=pltpu.HBM)
PARAMS = pltpu.CompilerParams(vmem_limit_bytes=32 * 1024 * 1024)


def contract(a, b, dims):
    return lax.dot_general(a, b, (dims, ((), ())), preferred_element_type=F32)


def halves(value):
    high = value.astype(BF16)
    return high, (value - high.astype(F32)).astype(BF16)


def lift_kernel(helpers, rows_hbm, group_hbm, local_hbm, ids_hbm, test_hbm, points_hbm, packed_ref, own_ref, *refs):
    send_refs = refs[: helpers - 1]
    mark_ref, resident_ref, group_ref, local_ref, ids_ref, test_ref, points_ref, sems = refs[helpers - 1 :]
    helper = lax.axis_index("help")
    asked, width = rows_hbm.shape
    rank, count = test_ref.shape
    piece = count // CHUNKS
    pairs = [(ids_hbm, ids_ref), (test_hbm, test_ref)]
    for k in range(CHUNKS):
        part = pl.ds(k * piece, piece)
        pairs.append((points_hbm.at[part], points_ref.at[part]))
    pairs += [(group_hbm, group_ref), (local_hbm, local_ref), (rows_hbm, packed_ref.at[pl.ds(0, asked)])]
    copies = [pltpu.make_async_copy(*pair, sems.at[k]) for k, pair in enumerate(pairs)]
    for copy in copies:
        copy.start()
    copies[0].wait()
    everyone = ids_ref[...]
    mark = ids_ref[:, pl.ds(pl.multiple_of(helper * count, LANES), count)] ^ helper
    mark_ref[...] = mark
    for d in range(helpers):
        many = jnp.sum((everyone == (helper ^ d)).astype(F32), axis=1, keepdims=True)
        resident_ref[d : d + 1, :] = jnp.broadcast_to(many, (1, LANES))
    copies[1].wait()
    test = test_ref[...]
    rows = jnp.concatenate([jnp.where(mark == d, test, jnp.zeros((), BF16)) for d in range(helpers)], axis=0)
    total = None
    for k in range(CHUNKS):
        copies[2 + k].wait()
        part = slice(k * piece, (k + 1) * piece)
        more = contract(rows[:, part], points_ref[part, :], ((1,), (0,)))
        total = more if total is None else total + more
    own_ref[...] = total[:rank]
    for d in range(1, helpers):
        send_refs[d - 1][...] = total[d * rank : (d + 1) * rank].astype(BF16)
    copies[-3].wait()
    copies[-2].wait()
    cluster = (group_ref[...] * helpers + local_ref[...]).astype(F32)
    spare = jnp.zeros((1, width - 2 * asked), F32)
    line = jnp.concatenate([cluster[0:1], cluster[1:2], spare], axis=1)
    packed_ref[asked:, :] = jnp.broadcast_to(line, (TILE, width)).astype(BF16)
    copies[-1].wait()


def score_kernel(planes, helpers, blocks, mine_ref, theirs_ref, *refs):
    queries, rest = refs[:blocks], refs[blocks:]
    shard, helper = lax.axis_index("shard"), lax.axis_index("help")
    span, width = mine_ref.shape
    rank = span // planes
    count = queries[0].shape[0] - TILE
    lifter = jnp.concatenate([mine_ref[...], theirs_ref[...]], axis=0)
    clusters = [
        ((shard ^ (INNER * d)) * helpers + (helper ^ side)).astype(F32) for side in (0, 1) for d in range(planes)
    ]
    total, tally = None, [None] * len(clusters)
    for q_ref in queries:
        rows = q_ref[:count, :]
        line = q_ref[count : count + TILE, :][0:1].astype(F32)
        first, second = line[:, :count], line[:, count : 2 * count]
        lifted = contract(lifter, rows, ((1,), (1,)))
        kept = []
        for k, cluster in enumerate(clusters):
            hit = (first == cluster) | (second == cluster)
            kept.append(jnp.where(hit, lifted[k * rank : (k + 1) * rank], 0.0))
            here = hit.astype(F32)
            tally[k] = here if tally[k] is None else tally[k] + here
        high, low = halves(jnp.concatenate(kept, axis=0))
        part = contract(high, rows, ((1,), (0,))) + contract(low, rows, ((1,), (0,)))
        total = part if total is None else total + part
    named = jnp.concatenate(
        [jnp.broadcast_to(jnp.sum(t, axis=1, keepdims=True), (rank, LANES)) for t in tally], axis=0
    )
    if len(rest) == 1:
        rest[0][:, :width] = total
        rest[0][:, width:] = named
    else:
        before, *outs = rest
        for side, out in enumerate(outs):
            part = slice(side * span, (side + 1) * span)
            out[:, :width] = before[part, :width] + total[part]
            out[:, width:] = before[part, width:] + named[part]


def fold_kernel(planes, mine_ref, theirs_ref, own_ref, *send_refs):
    rank, wide = own_ref.shape
    width = wide - LANES
    line = lax.broadcasted_iota(jnp.int32, (rank, LANES), 0)
    for d in range(planes):
        part = slice(d * rank, (d + 1) * rank)
        total = mine_ref[part, :] + theirs_ref[part, :]
        if d == 0:
            own_ref[...] = total
        else:
            many = jnp.floor(total[:, width:] * (1.0 / 256.0))
            rest = total[:, width:] - 256.0 * many
            send_refs[d - 1][:, :width] = total[:, :width].astype(BF16)
            send_refs[d - 1][:, width:] = jnp.where(line == 0, many, jnp.where(line == 1, rest, 0.0)).astype(BF16)


def scale_kernel(resident_ref, own_ref, *refs):
    *parts, out_ref = refs
    width = out_ref.shape[1]
    total = own_ref[:, :width]
    queried = own_ref[0:1, width : width + 1]
    for part in parts:
        total = total + part[:, :width].astype(F32)
        tile = part[:, width:].astype(F32)
        queried = queried + 256.0 * tile[0:1, 0:1] + tile[1:2, 0:1]
    resident = resident_ref[0:1, 0:1]
    factor = lax.rsqrt((queried + 1.0) * (queried + resident)) * (1.0 / width)
    out_ref[...] = (total * factor).astype(out_ref.dtype)


def sketch_kernel(helpers, mark_ref, resident_ref, points_ref, *refs):
    scaled = refs[:helpers]
    sketch_ref, own_ref, *send_refs = refs[helpers:]
    rank, count = sketch_ref.shape
    mark = mark_ref[...]
    points = points_ref[...]
    product = contract(jnp.concatenate([s[...] for s in scaled], axis=0), points, ((1,), (1,)))
    sketch = product[:rank]
    for d in range(1, helpers):
        sketch = jnp.where(mark == d, product[d * rank : (d + 1) * rank], sketch)
    sketch_ref[...] = sketch
    rounded = sketch.astype(BF16)
    rows = [jnp.where(mark == d, rounded, jnp.zeros((), BF16)) for d in range(helpers)]
    summed = contract(jnp.concatenate(rows, axis=0), points, ((1,), (0,)))
    for d in range(helpers):
        block = summed[d * rank : (d + 1) * rank] * lax.rsqrt(resident_ref[d : d + 1, 0:1])
        if d == 0:
            own_ref[...] = block
        else:
            send_refs[d - 1][...] = block.astype(BF16)


def swap(value, axis, d):
    return lax.ppermute(value, axis, [(i, i ^ d) for i in range(lax.axis_size(axis))])


def pool_queries(packed, lifter, groups, helpers):
    index = range(groups * helpers)
    one = [(i, i ^ (2 if i % 2 == 0 else helpers)) for i in index]
    two = [(i, i ^ (helpers if i % 2 == 0 else 2)) for i in index]
    both = ("shard", "help")
    near = lax.ppermute(packed, both, one)
    far = lax.ppermute(packed, both, two)
    near, far, _ = lax.optimization_barrier((near, far, lifter))
    return near, far, lax.ppermute(near, both, two)


def shards(queries, probe_group, probe_local, points, point_cluster, test_matrix):
    groups = lax.axis_size("shard")
    helpers = lax.axis_size("help")
    planes = groups // INNER
    count = queries.shape[0]
    rank = test_matrix.shape[0]
    own_points, width = points.shape
    block = jax.ShapeDtypeStruct((rank, width), F32)
    sent = jax.ShapeDtypeStruct((rank, width), BF16)

    packed, own, *out, mark, resident = pl.pallas_call(
        functools.partial(lift_kernel, helpers),
        out_shape=[jax.ShapeDtypeStruct((count + TILE, width), BF16), block]
        + [sent] * (helpers - 1)
        + [jax.ShapeDtypeStruct((1, own_points), jnp.int32), jax.ShapeDtypeStruct((8, LANES), F32)],
        in_specs=[HBM] * 6,
        scratch_shapes=[
            pltpu.VMEM((2, count), jnp.int32),
            pltpu.VMEM((2, count), jnp.int32),
            pltpu.VMEM(point_cluster.shape, jnp.int32),
            pltpu.VMEM(test_matrix.shape, BF16),
            pltpu.VMEM(points.shape, BF16),
            pltpu.SemaphoreType.DMA((5 + CHUNKS,)),
        ],
        compiler_params=pltpu.CompilerParams(vmem_limit_bytes=FIRST << 20),
        name="lift",
    )(queries, probe_group.T, probe_local.T, point_cluster, test_matrix, points)
    lifter = own
    for d in range(1, helpers):
        lifter = lifter + swap(out[d - 1], "help", d).astype(F32)
    lifter = lifter.astype(BF16)
    lifters = [lifter] + [swap(lifter, "shard", INNER * d) for d in range(1, planes)]
    near, far, across = pool_queries(packed, lifters[1], groups, helpers)
    mine = jnp.concatenate(lifters, axis=0)
    theirs = swap(mine, "help", 1)

    wide = width + LANES
    begun = pl.pallas_call(
        functools.partial(score_kernel, planes, helpers, 3),
        out_shape=jax.ShapeDtypeStruct((2 * planes * rank, wide), F32),
        compiler_params=PARAMS,
        name="score",
    )(mine, theirs, packed, near, far)
    moments, passed = pl.pallas_call(
        functools.partial(score_kernel, planes, helpers, 1),
        out_shape=[jax.ShapeDtypeStruct((planes * rank, wide), F32)] * 2,
        compiler_params=PARAMS,
        name="score_last",
    )(mine, theirs, across, begun)
    folded = pl.pallas_call(
        functools.partial(fold_kernel, planes),
        out_shape=[jax.ShapeDtypeStruct((rank, wide), F32)]
        + [jax.ShapeDtypeStruct((rank, wide), BF16)] * (planes - 1),
        compiler_params=PARAMS,
        name="fold",
    )(moments, swap(passed, "help", 1))
    moments = [folded[0]] + [swap(folded[d], "shard", INNER * d) for d in range(1, planes)]

    scaled = pl.pallas_call(
        scale_kernel,
        out_shape=sent,
        compiler_params=PARAMS,
        name="scale",
    )(resident, *moments)
    scaled = [scaled] + [swap(scaled, "help", d) for d in range(1, helpers)]

    sketch, own, *out = pl.pallas_call(
        functools.partial(sketch_kernel, helpers),
        out_shape=[jax.ShapeDtypeStruct((rank, own_points), F32), block] + [sent] * (helpers - 1),
        compiler_params=PARAMS,
        name="sketch",
    )(mark, resident, points, *scaled)
    regressor = own
    for d in range(1, helpers):
        regressor = regressor + swap(out[d - 1], "help", d).astype(F32)
    return sketch, regressor[None]


def solution(mesh):
    in_specs = (
        P(("shard", "help"), None),
        P(("shard", "help"), None),
        P(("shard", "help"), None),
        P(("shard", "help"), None),
        P("shard", None),
        P(None, ("shard", "help")),
    )
    out_specs = (P(None, ("shard", "help")), P(("shard", "help"), None, None))
    return jax.shard_map(shards, mesh=mesh, in_specs=in_specs, out_specs=out_specs, check_vma=False)
```

time: 81.7 us -> 60.9 us (0.75)
  starting transfers between devices: 39.3 us -> 22.2 us
  waiting for transfers between devices: 33.5 us -> 28.1 us
  Pallas kernels: 4.36 us -> 6.99 us
  local copies, waits for them, and re-layouts: 2.98 us -> 1.02 us
  other arithmetic: 0.69 us -> 1.6 us
    ppermute x29 -> x20, starting transfers between devices: 39.3 us -> 22.2 us  [the longest x17 15.9 us: swap(): lax.ppermute(value, axis, [(i, i ^ d) for i in range(lax.axis_size(axis))])]
    ppermute x29 -> x20, waiting for transfers between devices: 33.5 us -> 28.1 us  [the longest x17 28.1 us: swap(): lax.ppermute(value, axis, [(i, i ^ d) for i in range(lax.axis_size(axis))])]
    pallas_call x3 -> x5, Pallas kernels: 2.84 us -> 5.46 us  [the longest x1 2.7 us: shards(): pl.pallas_call(functools.partial(lift_kernel, helpers), out_shape=[jax.Sh...]
    unnamed x14 -> x8, local copies, waits for them, and re-layouts: 2.98 us -> 1.02 us
    convert_element_type x1, other arithmetic: 0.02 us -> 0.92 us  [shards(): lifter = lifter.astype(BF16)]
  transfers between devices with their start and end apart: 29 -> 20, of which waited for: 16 -> 12; matrix products, arithmetic and copies ran while one was open for 0% -> 2% of each run, Pallas kernels for 0% -> 3%
where the time goes in v2:
time: 60.9 us; the launch traced here: 60.6 us
  waiting for transfers between devices  28.1 us (46%)
  starting transfers between devices  22.2 us (36%)
  Pallas kernels  6.99 us (11%)
  other arithmetic  1.6 us (3%)
  local copies, waits for them, and re-layouts  1.02 us (2%)
  between operations  0.75 us (1%)
    ppermute x17, waiting for transfers between devices, swap(): lax.ppermute(value, axis, [(i, i ^ d) for i in range(lax.axis_size(axis))])  28.1 us
    ppermute x17, starting transfers between devices, swap(): lax.ppermute(value, axis, [(i, i ^ d) for i in range(lax.axis_size(axis))])  15.9 us
    ppermute x1, starting transfers between devices, pool_queries(): far = lax.ppermute(packed, both, two)  3.03 us
    pallas_call x1, Pallas kernels, shards(): pl.pallas_call(functools.partial(lift_kernel, helpers), out_shape=[jax.Sh...  2.7 us
    pallas_call x1, Pallas kernels, shards(): pl.pallas_call(functools.partial(score_kernel, planes, helpers, 3), out_s...  1.81 us
    ppermute x1, starting transfers between devices, pool_queries(): return (near, far, lax.ppermute(near, both, two))  1.77 us
    pallas_call x1, Pallas kernels, shards(): pl.pallas_call(functools.partial(sketch_kernel, helpers), out_shape=[jax....  1.53 us
    ppermute x1, starting transfers between devices, pool_queries(): near = lax.ppermute(packed, both, one)  1.49 us
  transfers between devices with their start and end apart: 20, of which 12 were waited for; matrix products, arithmetic and copies ran while one was open for 2% of the time, Pallas kernels for 3%

profile of v2, /device:TPU:0, one launch (start us, length us, event | category | flops | bytes accessed | tf_op | source)
XLA Modules:
  0.0 60.6 jit_solution(14931927678267807334)
XLA Ops:
  0.6 2.7 %lift.1 = (bf16[272,768]{1,0:T(8,128)(2,1)}, f32[32,768]{1,0:T(8,128)}, bf16[32,768]{1,0:T(8,128)(2,1)}, bf16[32,768]{1,0:T(8,128)(2,1)}, bf16[32,768]{1,0:T(8,1...) custom-call(bf16[256,768]{1,0:T(8,128)(2,1)} %rows_hbm.1, s32[2,256]{1,0:T(2,128)} %bitcast.4, s32[2,256]{1,0:T(2,128)} %bitcast.5, ...), custom_call_target="tpu_custom_call" | custom-call | tf_op jit(solution)/shard_map/lift/pallas_call | solution.py:190
  3.3 3.0 %collective-permute-start.8 = (bf16[272,768]{1,0:T(8,128)(2,1)}, bf16[272,768]{1,0:T(8,128)(2,1)S(1)}, u32[]{:S(2)}, u32[]{:S(2)}) collective-permute-start(bf16[272,768]{1,0:T(8,128)(2,1)} %get-tuple-element.28.refs_0_), channel_id=1, source_target_pairs={{0,4},{1,3},{2,6},{3,1},{4,0},{5,7},{6,2},{7,5},{8,12},{9,11},{10,... | collective-permute-start | bytes 1253384 | tf_op jit(solution)/shard_map/ppermute | solution.py:175
  6.4 1.5 %collective-permute-start.7 = (bf16[272,768]{1,0:T(8,128)(2,1)}, bf16[272,768]{1,0:T(8,128)(2,1)S(1)}, u32[]{:S(2)}, u32[]{:S(2)}) collective-permute-start(bf16[272,768]{1,0:T(8,128)(2,1)} %get-tuple-element.28.refs_0_), channel_id=1, source_target_pairs={{0,2},{1,5},{2,0},{3,7},{4,6},{5,1},{6,4},{7,3},{8,10},{9,13},{10,... | collective-permute-start | bytes 1253384 | tf_op jit(solution)/shard_map/ppermute | solution.py:174
  7.9 0.0 collective-permute-start
  7.9 0.5 collective-permute-start.1
  8.4 1.3 %collective-permute-start.2 = (bf16[32,768]{1,0:T(8,128)(2,1)}, bf16[32,768]{1,0:T(8,128)(2,1)S(1)}, u32[]{:S(2)}, u32[]{:S(2)}) collective-permute-start(bf16[32,768]{1,0:T(8,128)(2,1)} %get-tuple-element.27), channel_id=1, source_target_pairs={{0,3},{1,2},{2,1},{3,0},{4,7},{5,6},{6,5},{7,4},{8,11},{9,10},{10,... | collective-permute-start | bytes 147464 | tf_op jit(solution)/shard_map/ppermute | solution.py:166
  9.7 0.0 collective-permute-done
  9.7 8.0 %collective-permute-done.1 = bf16[32,768]{1,0:T(8,128)(2,1)S(1)} collective-permute-done((bf16[32,768]{1,0:T(8,128)(2,1)}, bf16[32,768]{1,0:T(8,128)(2,1)S(1)}, u32[]{:S(2)}, u32[]{:S(2)}) %collective-permute-start.1) | collective-permute-done | bytes 49184 | tf_op jit(solution)/shard_map/ppermute | solution.py:166
  17.8 0.0 collective-permute-done.2
  17.8 0.9 %add_convert_fusion = bf16[32,768]{1,0:T(8,128)(2,1)S(1)} fusion(bf16[32,768]{1,0:T(8,128)(2,1)S(1)} %collective-permute-done.2, bf16[32,768]{1,0:T(8,128)(2,1)S(1)} %collective-permute-done.1, f32[32,768]{1,0:T(8,128)} %get-tuple-element.24, bf16[32,768]{1,0:T(8,128)(2,1)S(1)} %collective-permute-done), kind=kLoop, calls=%fused_computation.2 | loop fusion | flops 172032 | bytes 294912 | tf_op jit(solution)/shard_map/convert_element_type | solution.py:210
  18.7 1.9 %collective-permute-start.3 = (bf16[32,768]{1,0:T(8,128)(2,1)S(1)}, bf16[32,768]{1,0:T(8,128)(2,1)S(1)}, u32[]{:S(2)}, u32[]{:S(2)}) collective-permute-start(bf16[32,768]{1,0:T(8,128)(2,1)S(1)} %add_convert_fusion), channel_id=1, source_target_pairs={{0,8},{4,12},{8,0},{12,4},{16,24},{20,28},{24,16},{28,20},{1,9},{5... | collective-permute-start | bytes 147464 | tf_op jit(solution)/shard_map/ppermute | solution.py:166
  20.6 2.3 %collective-permute-done.3 = bf16[32,768]{1,0:T(8,128)(2,1)S(1)} collective-permute-done((bf16[32,768]{1,0:T(8,128)(2,1)S(1)}, bf16[32,768]{1,0:T(8,128)(2,1)S(1)}, u32[]{:S(2)}, u32[]{:S(2)}) %collective-permute-start.3) | collective-permute-done | bytes 49184 | tf_op jit(solution)/shard_map/ppermute | solution.py:166
  22.9 0.0 collective-permute-done.8.refs_2_
  22.9 0.0 collective-permute-done.7.refs_1_
  22.9 1.8 %collective-permute-start.9 = (bf16[272,768]{1,0:T(8,128)(2,1)S(1)}, bf16[272,768]{1,0:T(8,128)(2,1)S(1)}, u32[]{:S(2)}, u32[]{:S(2)}) collective-permute-start(bf16[272,768]{1,0:T(8,128)(2,1)S(1)} %collective-permute-done.7.refs_1_), channel_id=1, source_target_pairs={{0,4},{1,3},{2,6},{3,1},{4,0},{5,7},{6,2},{7,5},{8,12},{9,11},{10,... | collective-permute-start | bytes 1253384 | tf_op jit(solution)/shard_map/ppermute | solution.py:177
  24.6 3.6 %collective-permute-start.5 = (bf16[32,768]{1,0:T(8,128)(2,1)S(1)}, bf16[32,768]{1,0:T(8,128)(2,1)S(1)}, u32[]{:S(2)}, u32[]{:S(2)}) collective-permute-start(bf16[32,768]{1,0:T(8,128)(2,1)S(1)} %add_convert_fusion), channel_id=1, source_target_pairs={{0,24},{4,28},{8,16},{12,20},{16,8},{20,12},{24,0},{28,4},{1,25},{... | collective-permute-start | bytes 147464 | tf_op jit(solution)/shard_map/ppermute | solution.py:166
  28.2 0.0 collective-permute-start.4
  28.2 2.3 %collective-permute-done.5 = bf16[32,768]{1,0:T(8,128)(2,1)S(1)} collective-permute-done((bf16[32,768]{1,0:T(8,128)(2,1)S(1)}, bf16[32,768]{1,0:T(8,128)(2,1)S(1)}, u32[]{:S(2)}, u32[]{:S(2)}) %collective-permute-start.5) | collective-permute-done | bytes 49184 | tf_op jit(solution)/shard_map/ppermute | solution.py:166
  30.5 2.7 %collective-permute-done.4 = bf16[32,768]{1,0:T(8,128)(2,1)S(1)} collective-permute-done((bf16[32,768]{1,0:T(8,128)(2,1)S(1)}, bf16[32,768]{1,0:T(8,128)(2,1)S(1)}, u32[]{:S(2)}, u32[]{:S(2)}) %collective-permute-start.4) | collective-permute-done | bytes 49184 | tf_op jit(solution)/shard_map/ppermute | solution.py:166
  33.2 0.1 collective-permute-start.6
  33.3 1.4 %collective-permute-done.6.theirs_ref = bf16[128,768]{1,0:T(8,128)(2,1)S(1)} collective-permute-done((bf16[128,768]{1,0:T(8,128)(2,1)S(1)}, bf16[128,768]{1,0:T(8,128)(2,1)S(1)}, u32[]{:S(2)}, u32[]{:S(2)}) %collective-permute-start.6) | collective-permute-done | bytes 196640 | tf_op jit(solution)/shard_map/ppermute | solution.py:166
  34.7 0.0 copy-start.1
  34.7 1.0 %copy-done.1 = bf16[272,768]{1,0:T(8,128)(2,1)S(1)} copy-done((bf16[272,768]{1,0:T(8,128)(2,1)S(1)}, bf16[272,768]{1,0:T(8,128)(2,1)}, u32[]{:S(2)}) %copy-start.1) | copy-done | bytes 417816
  35.7 1.8 %score.1.refs_1_ = f32[256,896]{1,0:T(8,128)S(1)} custom-call(bf16[128,768]{1,0:T(8,128)(2,1)S(1)} %pad_maximum_fusion.mine_ref, bf16[128,768]{1,0:T(8,128)(2,1)S(1)} %collective-permute-done.6.theirs_ref, bf16[272,768]{1,0:T(8,128)(2,1)S(1)} %copy-done.1, bf16[272,768]{1,0:T(8,128)(2,1)S(1)} %collective-permute-done.7.refs_1_, ...), custom_call_target="tpu_custom_call" | custom-call | tf_op jit(solution)/shard_map/score/pallas_call | solution.py:217
  37.6 0.0 copy-start.2
  37.6 0.0 copy-start
  37.6 0.0 copy-start.3
  37.6 0.0 collective-permute-done.9.refs_0_
  37.6 0.8 %score_last.1 = (f32[128,896]{1,0:T(8,128)S(1)}, f32[128,896]{1,0:T(8,128)S(1)}) custom-call(bf16[128,768]{1,0:T(8,128)(2,1)S(1)} %pad_maximum_fusion.mine_ref, bf16[128,768]{1,0:T(8,128)(2,1)S(1)} %collective-permute-done.6.theirs_ref, bf16[272,768]{1,0:T(8,128)(2,1)S(1)} %collective-permute-done.9.refs_0_, f32[256,896]{1,0:T(8,128)S(1)} %score.1.refs_1_), custom_call_target="tpu_custom_call" | custom-call | tf_op jit(solution)/shard_map/score_last/pallas_call | solution.py:223
  38.4 0.2 collective-permute-start.10
  38.6 1.7 %collective-permute-done.10.theirs_ref = f32[128,896]{1,0:T(8,128)S(1)} collective-permute-done((f32[128,896]{1,0:T(8,128)S(1)}, f32[128,896]{1,0:T(8,128)S(1)}, u32[]{:S(2)}, u32[]{:S(2)}) %collective-permute-start.10) | collective-permute-done | bytes 458784 | tf_op jit(solution)/shard_map/ppermute | solution.py:166
  40.3 0.1 fold.1
  40.4 0.1 collective-permute-start.11
  40.4 1.5 %collective-permute-start.12 = (bf16[32,896]{1,0:T(8,128)(2,1)S(1)}, bf16[32,896]{1,0:T(8,128)(2,1)S(1)}, u32[]{:S(2)}, u32[]{:S(2)}) collective-permute-start(bf16[32,896]{1,0:T(8,128)(2,1)S(1)} %get-tuple-element.35), channel_id=1, source_target_pairs={{0,16},{4,20},{8,24},{12,28},{16,0},{20,4},{24,8},{28,12},{1,17},{... | collective-permute-start | bytes 172040 | tf_op jit(solution)/shard_map/ppermute | solution.py:166
  41.9 2.9 %collective-permute-start.13 = (bf16[32,896]{1,0:T(8,128)(2,1)S(1)}, bf16[32,896]{1,0:T(8,128)(2,1)S(1)}, u32[]{:S(2)}, u32[]{:S(2)}) collective-permute-start(bf16[32,896]{1,0:T(8,128)(2,1)S(1)} %get-tuple-element.36), channel_id=1, source_target_pairs={{0,24},{4,28},{8,16},{12,20},{16,8},{20,12},{24,0},{28,4},{1,25},{... | collective-permute-start | bytes 172040 | tf_op jit(solution)/shard_map/ppermute | solution.py:166
  44.8 0.6 %collective-permute-done.11.refs_0_ = bf16[32,896]{1,0:T(8,128)(2,1)S(1)} collective-permute-done((bf16[32,896]{1,0:T(8,128)(2,1)S(1)}, bf16[32,896]{1,0:T(8,128)(2,1)S(1)}, u32[]{:S(2)}, u32[]{:S(2)}) %collective-permute-start.11) | collective-permute-done | bytes 57376 | tf_op jit(solution)/shard_map/ppermute | solution.py:166
  45.4 3.0 %collective-permute-done.12.refs_1_ = bf16[32,896]{1,0:T(8,128)(2,1)S(1)} collective-permute-done((bf16[32,896]{1,0:T(8,128)(2,1)S(1)}, bf16[32,896]{1,0:T(8,128)(2,1)S(1)}, u32[]{:S(2)}, u32[]{:S(2)}) %collective-permute-start.12) | collective-permute-done | bytes 57376 | tf_op jit(solution)/shard_map/ppermute | solution.py:166
  48.4 0.0 collective-permute-done.13.refs_2_
  48.5 0.0 copy-done.2
  48.5 0.1 scale.1.refs_0_
  48.5 0.1 collective-permute-start.16
  48.6 1.6 %collective-permute-start.15 = (bf16[32,768]{1,0:T(8,128)(2,1)S(1)}, bf16[32,768]{1,0:T(8,128)(2,1)S(1)}, u32[]{:S(2)}, u32[]{:S(2)}) collective-permute-start(bf16[32,768]{1,0:T(8,128)(2,1)S(1)} %scale.1.refs_0_), channel_id=1, source_target_pairs={{0,2},{1,3},{2,0},{3,1},{4,6},{5,7},{6,4},{7,5},{8,10},{9,11},{10,... | collective-permute-start | bytes 147464 | tf_op jit(solution)/shard_map/ppermute | solution.py:166
  50.2 0.3 collective-permute-start.14
  50.5 2.1 %collective-permute-done.16.refs_3_ = bf16[32,768]{1,0:T(8,128)(2,1)S(1)} collective-permute-done((bf16[32,768]{1,0:T(8,128)(2,1)S(1)}, bf16[32,768]{1,0:T(8,128)(2,1)S(1)}, u32[]{:S(2)}, u32[]{:S(2)}) %collective-permute-start.16) | collective-permute-done | bytes 49184 | tf_op jit(solution)/shard_map/ppermute | solution.py:166
  52.6 0.9 %collective-permute-done.15.refs_2_ = bf16[32,768]{1,0:T(8,128)(2,1)S(1)} collective-permute-done((bf16[32,768]{1,0:T(8,128)(2,1)S(1)}, bf16[32,768]{1,0:T(8,128)(2,1)S(1)}, u32[]{:S(2)}, u32[]{:S(2)}) %collective-permute-start.15) | collective-permute-done | bytes 49184 | tf_op jit(solution)/shard_map/ppermute | solution.py:166
  53.5 0.0 collective-permute-done.14.refs_1_
  53.5 0.0 copy-done
  53.5 0.0 copy-done.3
  53.5 1.5 %sketch.1 = (f32[32,1024]{1,0:T(8,128)}, f32[32,768]{1,0:T(8,128)S(1)}, bf16[32,768]{1,0:T(8,128)(2,1)S(1)}, bf16[32,768]{1,0:T(8,128)(2,1)S(1)}, bf16[32,768]{1,0:T(8,128)(2,1)S(1)}) custom-call(s32[1,1024]{1,0:T(1,128)S(1)} %copy-done.3, f32[8,128]{1,0:T(8,128)S(1)} %copy-done.2, bf16[1024,768]{1,0:T(8,128)(2,1)S(1)} %copy-done, ...), custom_call_target="tpu_custom_call" | custom-call | tf_op jit(solution)/shard_map/sketch/pallas_call | solution.py:246
  55.1 0.1 collective-permute-start.17
  55.2 1.1 %collective-permute-start.18 = (bf16[32,768]{1,0:T(8,128)(2,1)S(1)}, bf16[32,768]{1,0:T(8,128)(2,1)S(1)}, u32[]{:S(2)}, u32[]{:S(2)}) collective-permute-start(bf16[32,768]{1,0:T(8,128)(2,1)S(1)} %get-tuple-element.40), channel_id=1, source_target_pairs={{0,2},{1,3},{2,0},{3,1},{4,6},{5,7},{6,4},{7,5},{8,10},{9,11},{10,... | collective-permute-start | bytes 147464 | tf_op jit(solution)/shard_map/ppermute | solution.py:166
  56.2 0.7 %collective-permute-start.19 = (bf16[32,768]{1,0:T(8,128)(2,1)S(1)}, bf16[32,768]{1,0:T(8,128)(2,1)S(1)}, u32[]{:S(2)}, u32[]{:S(2)}) collective-permute-start(bf16[32,768]{1,0:T(8,128)(2,1)S(1)} %get-tuple-element.41), channel_id=1, source_target_pairs={{0,3},{1,2},{2,1},{3,0},{4,7},{5,6},{6,5},{7,4},{8,11},{9,10},{10,... | collective-permute-start | bytes 147464 | tf_op jit(solution)/shard_map/ppermute | solution.py:166
  57.0 0.0 collective-permute-done.17
  57.0 2.4 %collective-permute-done.18 = bf16[32,768]{1,0:T(8,128)(2,1)S(1)} collective-permute-done((bf16[32,768]{1,0:T(8,128)(2,1)S(1)}, bf16[32,768]{1,0:T(8,128)(2,1)S(1)}, u32[]{:S(2)}, u32[]{:S(2)}) %collective-permute-start.18) | collective-permute-done | bytes 49184 | tf_op jit(solution)/shard_map/ppermute | solution.py:166
  59.4 0.6 collective-permute-done.19
  60.0 0.7 %add_bitcast_fusion = f32[1,32,768]{2,1,0:T(8,128)} fusion(bf16[32,768]{1,0:T(8,128)(2,1)S(1)} %collective-permute-done.19, bf16[32,768]{1,0:T(8,128)(2,1)S(1)} %collective-permute-done.18, f32[32,768]{1,0:T(8,128)S(1)} %get-tuple-element.38, bf16[32,768]{1,0:T(8,128)(2,1)S(1)} %collective-permute-done.17), kind=kLoop, calls=%fused_computation.1 | loop fusion | flops 147456 | bytes 344064 | tf_op jit(solution)/shard_map/broadcast_in_dim | solution.py:255
  (1 shorter events, 0.0 us)
Async XLA Ops:
  3.3 19.5 %collective-permute-start.8 = (bf16[272,768]{1,0:T(8,128)(2,1)}, bf16[272,768]{1,0:T(8,128)(2,1)S(1)}, u32[]{:S(2)}, u32[]{:S(2)}) collective-permute-start(bf16[272,768]{1,0:T(8,128)(2,1)} %get-tuple-element.28.refs_0_), channel_id=1, source_target_pairs={{0,4},{1,3},{2,6},{3,1},{4,0},{5,7},{6,2},{7,5},{8,12},{9,11},{10,... | collective-permute-start | bytes 1253384 | tf_op jit(solution)/shard_map/ppermute | solution.py:175
  6.4 16.5 %collective-permute-start.7 = (bf16[272,768]{1,0:T(8,128)(2,1)}, bf16[272,768]{1,0:T(8,128)(2,1)S(1)}, u32[]{:S(2)}, u32[]{:S(2)}) collective-permute-start(bf16[272,768]{1,0:T(8,128)(2,1)} %get-tuple-element.28.refs_0_), channel_id=1, source_target_pairs={{0,2},{1,5},{2,0},{3,7},{4,6},{5,1},{6,4},{7,3},{8,10},{9,13},{10,... | collective-permute-start | bytes 1253384 | tf_op jit(solution)/shard_map/ppermute | solution.py:174
  7.9 1.9 %collective-permute-start = (bf16[32,768]{1,0:T(8,128)(2,1)}, bf16[32,768]{1,0:T(8,128)(2,1)S(1)}, u32[]{:S(2)}, u32[]{:S(2)}) collective-permute-start(bf16[32,768]{1,0:T(8,128)(2,1)} %get-tuple-element.25), channel_id=1, source_target_pairs={{0,1},{1,0},{2,3},{3,2},{4,5},{5,4},{6,7},{7,6},{8,9},{9,8},{10,11... | collective-permute-start | bytes 147464 | tf_op jit(solution)/shard_map/ppermute | solution.py:166
  7.9 9.9 %collective-permute-start.1 = (bf16[32,768]{1,0:T(8,128)(2,1)}, bf16[32,768]{1,0:T(8,128)(2,1)S(1)}, u32[]{:S(2)}, u32[]{:S(2)}) collective-permute-start(bf16[32,768]{1,0:T(8,128)(2,1)} %get-tuple-element.26), channel_id=1, source_target_pairs={{0,2},{1,3},{2,0},{3,1},{4,6},{5,7},{6,4},{7,5},{8,10},{9,11},{10,... | collective-permute-start | bytes 147464 | tf_op jit(solution)/shard_map/ppermute | solution.py:166
  8.4 9.4 %collective-permute-start.2 = (bf16[32,768]{1,0:T(8,128)(2,1)}, bf16[32,768]{1,0:T(8,128)(2,1)S(1)}, u32[]{:S(2)}, u32[]{:S(2)}) collective-permute-start(bf16[32,768]{1,0:T(8,128)(2,1)} %get-tuple-element.27), channel_id=1, source_target_pairs={{0,3},{1,2},{2,1},{3,0},{4,7},{5,6},{6,5},{7,4},{8,11},{9,10},{10,... | collective-permute-start | bytes 147464 | tf_op jit(solution)/shard_map/ppermute | solution.py:166
  18.7 4.2 %collective-permute-start.3 = (bf16[32,768]{1,0:T(8,128)(2,1)S(1)}, bf16[32,768]{1,0:T(8,128)(2,1)S(1)}, u32[]{:S(2)}, u32[]{:S(2)}) collective-permute-start(bf16[32,768]{1,0:T(8,128)(2,1)S(1)} %add_convert_fusion), channel_id=1, source_target_pairs={{0,8},{4,12},{8,0},{12,4},{16,24},{20,28},{24,16},{28,20},{1,9},{5... | collective-permute-start | bytes 147464 | tf_op jit(solution)/shard_map/ppermute | solution.py:166
  22.9 14.7 %collective-permute-start.9 = (bf16[272,768]{1,0:T(8,128)(2,1)S(1)}, bf16[272,768]{1,0:T(8,128)(2,1)S(1)}, u32[]{:S(2)}, u32[]{:S(2)}) collective-permute-start(bf16[272,768]{1,0:T(8,128)(2,1)S(1)} %collective-permute-done.7.refs_1_), channel_id=1, source_target_pairs={{0,4},{1,3},{2,6},{3,1},{4,0},{5,7},{6,2},{7,5},{8,12},{9,11},{10,... | collective-permute-start | bytes 1253384 | tf_op jit(solution)/shard_map/ppermute | solution.py:177
  24.6 5.9 %collective-permute-start.5 = (bf16[32,768]{1,0:T(8,128)(2,1)S(1)}, bf16[32,768]{1,0:T(8,128)(2,1)S(1)}, u32[]{:S(2)}, u32[]{:S(2)}) collective-permute-start(bf16[32,768]{1,0:T(8,128)(2,1)S(1)} %add_convert_fusion), channel_id=1, source_target_pairs={{0,24},{4,28},{8,16},{12,20},{16,8},{20,12},{24,0},{28,4},{1,25},{... | collective-permute-start | bytes 147464 | tf_op jit(solution)/shard_map/ppermute | solution.py:166
  28.2 5.0 %collective-permute-start.4 = (bf16[32,768]{1,0:T(8,128)(2,1)S(1)}, bf16[32,768]{1,0:T(8,128)(2,1)S(1)}, u32[]{:S(2)}, u32[]{:S(2)}) collective-permute-start(bf16[32,768]{1,0:T(8,128)(2,1)S(1)} %add_convert_fusion), channel_id=1, source_target_pairs={{0,16},{4,20},{8,24},{12,28},{16,0},{20,4},{24,8},{28,12},{1,17},{... | collective-permute-start | bytes 147464 | tf_op jit(solution)/shard_map/ppermute | solution.py:166
  33.2 1.5 %collective-permute-start.6 = (bf16[128,768]{1,0:T(8,128)(2,1)S(1)}, bf16[128,768]{1,0:T(8,128)(2,1)S(1)}, u32[]{:S(2)}, u32[]{:S(2)}) collective-permute-start(bf16[128,768]{1,0:T(8,128)(2,1)S(1)} %pad_maximum_fusion.mine_ref), channel_id=1, source_target_pairs={{0,1},{1,0},{2,3},{3,2},{4,5},{5,4},{6,7},{7,6},{8,9},{9,8},{10,11... | collective-permute-start | bytes 589832 | tf_op jit(solution)/shard_map/ppermute | solution.py:166
  34.7 1.0 %copy-start.1 = (bf16[272,768]{1,0:T(8,128)(2,1)S(1)}, bf16[272,768]{1,0:T(8,128)(2,1)}, u32[]{:S(2)}) copy-start(bf16[272,768]{1,0:T(8,128)(2,1)} %get-tuple-element.28.refs_0_) | copy-start | bytes 1253380
  37.6 10.9 %copy-start.2 = (f32[8,128]{1,0:T(8,128)S(1)}, f32[8,128]{1,0:T(8,128)}, u32[]{:S(2)}) copy-start(f32[8,128]{1,0:T(8,128)} %get-tuple-element.23.resident_ref) | copy-start | bytes 12292
  37.6 15.9 %copy-start = (bf16[1024,768]{1,0:T(8,128)(2,1)S(1)}, bf16[1024,768]{1,0:T(8,128)(2,1)}, u32[]{:S(2)}) copy-start(bf16[1024,768]{1,0:T(8,128)(2,1)} %points_ref.1) | copy-start | bytes 4718596
  37.6 15.9 %copy-start.3 = (s32[1,1024]{1,0:T(1,128)S(1)}, s32[1,1024]{1,0:T(1,128)}, u32[]{:S(2)}) copy-start(s32[1,1024]{1,0:T(1,128)} %get-tuple-element.22.mark_ref) | copy-start | bytes 12292
  38.4 1.9 %collective-permute-start.10 = (f32[128,896]{1,0:T(8,128)S(1)}, f32[128,896]{1,0:T(8,128)S(1)}, u32[]{:S(2)}, u32[]{:S(2)}) collective-permute-start(f32[128,896]{1,0:T(8,128)S(1)} %get-tuple-element.32), channel_id=1, source_target_pairs={{0,1},{1,0},{2,3},{3,2},{4,5},{5,4},{6,7},{7,6},{8,9},{9,8},{10,11... | collective-permute-start | bytes 1376264 | tf_op jit(solution)/shard_map/ppermute | solution.py:166
  40.4 5.1 %collective-permute-start.11 = (bf16[32,896]{1,0:T(8,128)(2,1)S(1)}, bf16[32,896]{1,0:T(8,128)(2,1)S(1)}, u32[]{:S(2)}, u32[]{:S(2)}) collective-permute-start(bf16[32,896]{1,0:T(8,128)(2,1)S(1)} %get-tuple-element.34), channel_id=1, source_target_pairs={{0,8},{4,12},{8,0},{12,4},{16,24},{20,28},{24,16},{28,20},{1,9},{5... | collective-permute-start | bytes 172040 | tf_op jit(solution)/shard_map/ppermute | solution.py:166
  40.4 8.0 %collective-permute-start.12 = (bf16[32,896]{1,0:T(8,128)(2,1)S(1)}, bf16[32,896]{1,0:T(8,128)(2,1)S(1)}, u32[]{:S(2)}, u32[]{:S(2)}) collective-permute-start(bf16[32,896]{1,0:T(8,128)(2,1)S(1)} %get-tuple-element.35), channel_id=1, source_target_pairs={{0,16},{4,20},{8,24},{12,28},{16,0},{20,4},{24,8},{28,12},{1,17},{... | collective-permute-start | bytes 172040 | tf_op jit(solution)/shard_map/ppermute | solution.py:166
  41.9 6.5 %collective-permute-start.13 = (bf16[32,896]{1,0:T(8,128)(2,1)S(1)}, bf16[32,896]{1,0:T(8,128)(2,1)S(1)}, u32[]{:S(2)}, u32[]{:S(2)}) collective-permute-start(bf16[32,896]{1,0:T(8,128)(2,1)S(1)} %get-tuple-element.36), channel_id=1, source_target_pairs={{0,24},{4,28},{8,16},{12,20},{16,8},{20,12},{24,0},{28,4},{1,25},{... | collective-permute-start | bytes 172040 | tf_op jit(solution)/shard_map/ppermute | solution.py:166
  48.5 4.1 %collective-permute-start.16 = (bf16[32,768]{1,0:T(8,128)(2,1)S(1)}, bf16[32,768]{1,0:T(8,128)(2,1)S(1)}, u32[]{:S(2)}, u32[]{:S(2)}) collective-permute-start(bf16[32,768]{1,0:T(8,128)(2,1)S(1)} %scale.1.refs_0_), channel_id=1, source_target_pairs={{0,3},{1,2},{2,1},{3,0},{4,7},{5,6},{6,5},{7,4},{8,11},{9,10},{10,... | collective-permute-start | bytes 147464 | tf_op jit(solution)/shard_map/ppermute | solution.py:166
  48.6 4.9 %collective-permute-start.15 = (bf16[32,768]{1,0:T(8,128)(2,1)S(1)}, bf16[32,768]{1,0:T(8,128)(2,1)S(1)}, u32[]{:S(2)}, u32[]{:S(2)}) collective-permute-start(bf16[32,768]{1,0:T(8,128)(2,1)S(1)} %scale.1.refs_0_), channel_id=1, source_target_pairs={{0,2},{1,3},{2,0},{3,1},{4,6},{5,7},{6,4},{7,5},{8,10},{9,11},{10,... | collective-permute-start | bytes 147464 | tf_op jit(solution)/shard_map/ppermute | solution.py:166
  50.2 3.3 %collective-permute-start.14 = (bf16[32,768]{1,0:T(8,128)(2,1)S(1)}, bf16[32,768]{1,0:T(8,128)(2,1)S(1)}, u32[]{:S(2)}, u32[]{:S(2)}) collective-permute-start(bf16[32,768]{1,0:T(8,128)(2,1)S(1)} %scale.1.refs_0_), channel_id=1, source_target_pairs={{0,1},{1,0},{2,3},{3,2},{4,5},{5,4},{6,7},{7,6},{8,9},{9,8},{10,11... | collective-permute-start | bytes 147464 | tf_op jit(solution)/shard_map/ppermute | solution.py:166
  55.1 1.9 %collective-permute-start.17 = (bf16[32,768]{1,0:T(8,128)(2,1)S(1)}, bf16[32,768]{1,0:T(8,128)(2,1)S(1)}, u32[]{:S(2)}, u32[]{:S(2)}) collective-permute-start(bf16[32,768]{1,0:T(8,128)(2,1)S(1)} %get-tuple-element.39), channel_id=1, source_target_pairs={{0,1},{1,0},{2,3},{3,2},{4,5},{5,4},{6,7},{7,6},{8,9},{9,8},{10,11... | collective-permute-start | bytes 147464 | tf_op jit(solution)/shard_map/ppermute | solution.py:166
  55.2 4.2 %collective-permute-start.18 = (bf16[32,768]{1,0:T(8,128)(2,1)S(1)}, bf16[32,768]{1,0:T(8,128)(2,1)S(1)}, u32[]{:S(2)}, u32[]{:S(2)}) collective-permute-start(bf16[32,768]{1,0:T(8,128)(2,1)S(1)} %get-tuple-element.40), channel_id=1, source_target_pairs={{0,2},{1,3},{2,0},{3,1},{4,6},{5,7},{6,4},{7,5},{8,10},{9,11},{10,... | collective-permute-start | bytes 147464 | tf_op jit(solution)/shard_map/ppermute | solution.py:166
  56.2 3.7 %collective-permute-start.19 = (bf16[32,768]{1,0:T(8,128)(2,1)S(1)}, bf16[32,768]{1,0:T(8,128)(2,1)S(1)}, u32[]{:S(2)}, u32[]{:S(2)}) collective-permute-start(bf16[32,768]{1,0:T(8,128)(2,1)S(1)} %get-tuple-element.41), channel_id=1, source_target_pairs={{0,3},{1,2},{2,1},{3,0},{4,7},{5,6},{6,5},{7,4},{8,11},{9,10},{10,... | collective-permute-start | bytes 147464 | tf_op jit(solution)/shard_map/ppermute | solution.py:166

commit v3 on v2

v3 whole, which is shorter than its diff:
```python
import functools

import jax
import jax.numpy as jnp
from jax import lax
from jax.experimental import pallas as pl
from jax.experimental.pallas import tpu as pltpu
from jax.sharding import PartitionSpec as P

F32 = jnp.float32
BF16 = jnp.bfloat16
LANES = 128
TILE = 16
INNER = 2
CHUNKS = 4
FIRST = 60

ANY = pl.BlockSpec(memory_space=pl.ANY)
HBM = pl.BlockSpec(memory_space=pltpu.HBM)
PARAMS = pltpu.CompilerParams(vmem_limit_bytes=32 * 1024 * 1024)


def contract(a, b, dims):
    return lax.dot_general(a, b, (dims, ((), ())), preferred_element_type=F32)


def halves(value):
    high = value.astype(BF16)
    return high, (value - high.astype(F32)).astype(BF16)


def slabs(ref, rows, width):
    return jnp.concatenate([ref[k * rows : (k + 1) * rows, :] for k in range(width // LANES)], axis=1)


def order(helpers):
    return [*range(0, helpers, 2), *range(1, helpers, 2)]


def lift_kernel(helpers, *refs):
    rows_hbm, group_hbm, local_hbm, ids_hbm, test_hbm, points_hbm = refs[:6]
    packed_ref, keep_ref, pass_ref, mark_ref, resident_ref = refs[6:11]
    group_ref, local_ref, ids_ref, test_ref, points_ref, sems = refs[11:]
    helper = lax.axis_index("help")
    asked, width = rows_hbm.shape
    rank, count = test_ref.shape
    piece = count // CHUNKS
    pairs = [(ids_hbm, ids_ref), (test_hbm, test_ref)]
    for k in range(CHUNKS):
        part = pl.ds(k * piece, piece)
        pairs.append((points_hbm.at[part], points_ref.at[part]))
    pairs += [(group_hbm, group_ref), (local_hbm, local_ref)]
    for k in range(width // LANES):
        pairs.append((rows_hbm.at[:, pl.ds(k * LANES, LANES)], packed_ref.at[pl.ds(k * asked, asked)]))
    copies = [pltpu.make_async_copy(*pair, sems.at[k]) for k, pair in enumerate(pairs)]
    for copy in copies:
        copy.start()
    copies[0].wait()
    everyone = ids_ref[...]
    mark = ids_ref[:, pl.ds(pl.multiple_of(helper * count, LANES), count)] ^ helper
    mark_ref[...] = mark
    for d in range(helpers):
        many = jnp.sum((everyone == (helper ^ d)).astype(F32), axis=1, keepdims=True)
        resident_ref[d : d + 1, :] = jnp.broadcast_to(many, (1, LANES))
    copies[1].wait()
    test = test_ref[...]
    offsets = order(helpers)
    rows = jnp.concatenate([jnp.where(mark == d, test, jnp.zeros((), BF16)) for d in offsets], axis=0)
    total = None
    for k in range(CHUNKS):
        copies[2 + k].wait()
        part = slice(k * piece, (k + 1) * piece)
        more = contract(rows[:, part], points_ref[part, :], ((1,), (0,)))
        total = more if total is None else total + more
    keep_ref[...] = total[: keep_ref.shape[0]]
    pass_ref[...] = total[keep_ref.shape[0] :]
    for copy in copies[2 + CHUNKS :]:
        copy.wait()
    cluster = (group_ref[...] * helpers + local_ref[...]).astype(F32)
    line = [cluster[k : k + 1, j : j + LANES] for k in (0, 1) for j in range(0, asked, LANES)]
    line.append(jnp.zeros((TILE - len(line), LANES), F32))
    packed_ref[asked * width // LANES :, :] = jnp.concatenate(line, axis=0).astype(BF16)


def gate_kernel(*refs):
    pass


def gate(value, *others):
    return pl.pallas_call(
        gate_kernel,
        out_shape=jax.ShapeDtypeStruct(value.shape, value.dtype),
        in_specs=[ANY] * (1 + len(others)),
        out_specs=ANY,
        input_output_aliases={0: 0},
        cost_estimate=pl.CostEstimate(flops=10**10, bytes_accessed=10**7, transcendentals=0),
        name="gate",
    )(value, *others)


def score_kernel(planes, helpers, blocks, mine_ref, theirs_ref, *refs):
    queries, rest = refs[:blocks], refs[blocks:]
    shard, helper = lax.axis_index("shard"), lax.axis_index("help")
    span, width = mine_ref.shape
    rank = span // planes
    count = (queries[0].shape[0] - TILE) * LANES // width
    pieces = count // LANES
    lifter = jnp.concatenate([mine_ref[...], theirs_ref[...]], axis=0)
    clusters = [
        ((shard ^ (INNER * d)) * helpers + (helper ^ side)).astype(F32) for side in (0, 1) for d in range(planes)
    ]
    total, tally = None, [None] * len(clusters)
    for q_ref in queries:
        rows = slabs(q_ref, count, width)
        tile = q_ref[count * width // LANES :, :].astype(F32)
        first, second = (
            jnp.concatenate([tile[k * pieces + j : k * pieces + j + 1] for j in range(pieces)], axis=1) for k in (0, 1)
        )
        lifted = contract(lifter, rows, ((1,), (1,)))
        kept = []
        for k, cluster in enumerate(clusters):
            hit = (first == cluster) | (second == cluster)
            kept.append(jnp.where(hit, lifted[k * rank : (k + 1) * rank], 0.0))
            here = hit.astype(F32)
            tally[k] = here if tally[k] is None else tally[k] + here
        high, low = halves(jnp.concatenate(kept, axis=0))
        part = contract(high, rows, ((1,), (0,))) + contract(low, rows, ((1,), (0,)))
        total = part if total is None else total + part
    named = jnp.concatenate(
        [jnp.broadcast_to(jnp.sum(t, axis=1, keepdims=True), (rank, LANES)) for t in tally], axis=0
    )
    if len(rest) == 1:
        rest[0][:, :width] = total
        rest[0][:, width:] = named
    else:
        before, *outs = rest
        for side, out in enumerate(outs):
            part = slice(side * span, (side + 1) * span)
            out[:, :width] = before[part, :width] + total[part]
            out[:, width:] = before[part, width:] + named[part]


def fold_kernel(planes, mine_ref, theirs_ref, own_ref, *send_refs):
    rank, wide = own_ref.shape
    width = wide - LANES
    line = lax.broadcasted_iota(jnp.int32, (TILE, LANES), 0)
    for d in range(planes):
        part = slice(d * rank, (d + 1) * rank)
        total = mine_ref[part, :] + theirs_ref[part, :]
        if d == 0:
            own_ref[...] = total
        else:
            ref = send_refs[d - 1]
            for k in range(width // LANES):
                ref[k * rank : (k + 1) * rank, :] = total[:, k * LANES : (k + 1) * LANES].astype(BF16)
            named = total[:TILE, width:]
            many = jnp.floor(named * (1.0 / 256.0))
            rest = named - 256.0 * many
            ref[rank * width // LANES :, :] = jnp.where(line == 0, many, jnp.where(line == 1, rest, 0.0)).astype(BF16)


def scale_kernel(resident_ref, own_ref, *refs):
    *parts, out_ref = refs
    rank, width = out_ref.shape
    total = own_ref[:, :width]
    queried = own_ref[0:1, width : width + 1]
    for part in parts:
        total = total + slabs(part, rank, width).astype(F32)
        tile = part[rank * width // LANES :, :].astype(F32)
        queried = queried + 256.0 * tile[0:1, 0:1] + tile[1:2, 0:1]
    resident = resident_ref[0:1, 0:1]
    factor = lax.rsqrt((queried + 1.0) * (queried + resident)) * (1.0 / width)
    out_ref[...] = (total * factor).astype(out_ref.dtype)


def sketch_kernel(helpers, mark_ref, resident_ref, points_ref, mine_ref, theirs_ref, sketch_ref, keep_ref, pass_ref):
    rank, count = sketch_ref.shape
    offsets = order(helpers)
    mark = mark_ref[...]
    points = points_ref[...]
    product = contract(jnp.concatenate([mine_ref[...], theirs_ref[...]], axis=0), points, ((1,), (1,)))
    sketch = product[:rank]
    for k, d in enumerate(offsets[1:], 1):
        sketch = jnp.where(mark == d, product[k * rank : (k + 1) * rank], sketch)
    sketch_ref[...] = sketch
    rounded = sketch.astype(BF16)
    rows = [jnp.where(mark == d, rounded, jnp.zeros((), BF16)) for d in offsets]
    summed = contract(jnp.concatenate(rows, axis=0), points, ((1,), (0,)))
    blocks = [
        summed[k * rank : (k + 1) * rank] * lax.rsqrt(resident_ref[d : d + 1, 0:1]) for k, d in enumerate(offsets)
    ]
    kept = helpers // 2
    keep_ref[...] = jnp.concatenate(blocks[:kept], axis=0)
    pass_ref[...] = jnp.concatenate(blocks[kept:], axis=0)


def swap(value, axis, d):
    return lax.ppermute(value, axis, [(i, i ^ d) for i in range(lax.axis_size(axis))])


def gather_to_owner(keep, passed, rank, helpers):
    both = keep + swap(passed, "help", 1)
    blocks = [both[k * rank : (k + 1) * rank] for k in range(helpers // 2)]
    sent = [block.astype(BF16) for block in blocks[1:]]
    return blocks[0], [swap(block, "help", 2 * k) for k, block in enumerate(sent, 1)], sent


def shards(queries, probe_group, probe_local, points, point_cluster, test_matrix):
    groups = lax.axis_size("shard")
    helpers = lax.axis_size("help")
    planes = groups // INNER
    count = queries.shape[0]
    rank = test_matrix.shape[0]
    own_points, width = points.shape
    kept = jax.ShapeDtypeStruct((helpers // 2 * rank, width), F32)

    packed, keep, passed, mark, resident = pl.pallas_call(
        functools.partial(lift_kernel, helpers),
        out_shape=[
            jax.ShapeDtypeStruct((count * width // LANES + TILE, LANES), BF16),
            kept,
            kept,
            jax.ShapeDtypeStruct((1, own_points), jnp.int32),
            jax.ShapeDtypeStruct((8, LANES), F32),
        ],
        in_specs=[HBM] * 6,
        scratch_shapes=[
            pltpu.VMEM((2, count), jnp.int32),
            pltpu.VMEM((2, count), jnp.int32),
            pltpu.VMEM(point_cluster.shape, jnp.int32),
            pltpu.VMEM(test_matrix.shape, BF16),
            pltpu.VMEM(points.shape, BF16),
            pltpu.SemaphoreType.DMA((4 + CHUNKS + width // LANES,)),
        ],
        compiler_params=pltpu.CompilerParams(vmem_limit_bytes=FIRST << 20),
        name="lift",
    )(queries, probe_group.T, probe_local.T, point_cluster, test_matrix, points)
    own, others, leaving = gather_to_owner(keep, passed, rank, helpers)

    index, axes = range(groups * helpers), ("shard", "help")
    one = [(i, i ^ (2 if i % 2 == 0 else helpers)) for i in index]
    two = [(i, i ^ (helpers if i % 2 == 0 else 2)) for i in index]
    packed = gate(packed, *leaving)
    near = lax.ppermute(packed, axes, one)
    far = lax.ppermute(packed, axes, two)

    for part in others:
        own = own + part.astype(F32)
    lifter = own.astype(BF16)
    lifters = [lifter] + [swap(lifter, "shard", INNER * d) for d in range(1, planes)]
    near = gate(near, lifter)
    across = lax.ppermute(near, axes, two)
    mine = jnp.concatenate(lifters, axis=0)
    theirs = swap(mine, "help", 1)

    wide = width + LANES
    begun = pl.pallas_call(
        functools.partial(score_kernel, planes, helpers, 3),
        out_shape=jax.ShapeDtypeStruct((2 * planes * rank, wide), F32),
        compiler_params=PARAMS,
        name="score",
    )(mine, theirs, packed, near, far)
    moments, passed = pl.pallas_call(
        functools.partial(score_kernel, planes, helpers, 1),
        out_shape=[jax.ShapeDtypeStruct((planes * rank, wide), F32)] * 2,
        compiler_params=PARAMS,
        name="score_last",
    )(mine, theirs, across, begun)
    folded = pl.pallas_call(
        functools.partial(fold_kernel, planes),
        out_shape=[jax.ShapeDtypeStruct((rank, wide), F32)]
        + [jax.ShapeDtypeStruct((rank * width // LANES + TILE, LANES), BF16)] * (planes - 1),
        compiler_params=PARAMS,
        name="fold",
    )(moments, swap(passed, "help", 1))
    moments = [folded[0]] + [swap(folded[d], "shard", INNER * d) for d in range(1, planes)]

    scaled = pl.pallas_call(
        scale_kernel,
        out_shape=jax.ShapeDtypeStruct((rank, width), BF16),
        compiler_params=PARAMS,
        name="scale",
    )(resident, *moments)
    scaled = jnp.concatenate([scaled] + [swap(scaled, "help", d) for d in range(2, helpers, 2)], axis=0)

    sketch, keep, passed = pl.pallas_call(
        functools.partial(sketch_kernel, helpers),
        out_shape=[jax.ShapeDtypeStruct((rank, own_points), F32), kept, kept],
        compiler_params=PARAMS,
        name="sketch",
    )(mark, resident, points, scaled, swap(scaled, "help", 1))
    regressor, others, _ = gather_to_owner(keep, passed, rank, helpers)
    for part in others:
        regressor = regressor + part.astype(F32)
    return sketch, regressor[None]


def solution(mesh):
    in_specs = (
        P(("shard", "help"), None),
        P(("shard", "help"), None),
        P(("shard", "help"), None),
        P(("shard", "help"), None),
        P("shard", None),
        P(None, ("shard", "help")),
    )
    out_specs = (P(None, ("shard", "help")), P(("shard", "help"), None, None))
    return jax.shard_map(shards, mesh=mesh, in_specs=in_specs, out_specs=out_specs, check_vma=False)
```

time: 60.9 us -> 61.4 us (level)
  local copies, waits for them, and re-layouts: 1.02 us -> 2.42 us
  starting transfers between devices: 22.2 us -> 21.4 us
  waiting for transfers between devices: 28.1 us -> 27.3 us
  other arithmetic: 1.6 us -> 2.28 us
    add x0 -> x2, other arithmetic: none -> 0.97 us  [gather_to_owner(): both = keep + swap(passed, 'help', 1)]
    ppermute x17 -> x14, starting transfers between devices: 15.9 us -> 14.9 us  [swap(): lax.ppermute(value, axis, [(i, i ^ d) for i in range(lax.axis_size(axis))])]
    ppermute x17 -> x14, waiting for transfers between devices: 28.1 us -> 27.3 us  [swap(): lax.ppermute(value, axis, [(i, i ^ d) for i in range(lax.axis_size(axis))])]
    unnamed x8 -> x16, local copies, waits for them, and re-layouts: 1.02 us -> 1.79 us
    slice x0 -> x2, local copies, waits for them, and re-layouts: none -> 0.63 us  [gather_to_owner(): blocks = [both[k * rank:(k + 1) * rank] for k in range(helpers // 2)]]
  transfers between devices with their start and end apart: 20 -> 17, of which waited for: 12 -> 13; matrix products, arithmetic and copies ran while one was open for 2% -> 1% of each run, Pallas kernels for 3% -> 3%
where the time goes in v3:
time: 61.4 us; the launch traced here: 61.1 us
  waiting for transfers between devices  27.3 us (44%)
  starting transfers between devices  21.4 us (35%)
  Pallas kernels  6.93 us (11%)
  local copies, waits for them, and re-layouts  2.42 us (4%)
  other arithmetic  2.28 us (4%)
  between operations  0.76 us (1%)
    ppermute x14, waiting for transfers between devices, swap(): lax.ppermute(value, axis, [(i, i ^ d) for i in range(lax.axis_size(axis))])  27.3 us
    ppermute x14, starting transfers between devices, swap(): lax.ppermute(value, axis, [(i, i ^ d) for i in range(lax.axis_size(axis))])  14.9 us
    ppermute x1, starting transfers between devices, shards(): near = lax.ppermute(packed, axes, one)  2.86 us
    pallas_call x1, Pallas kernels, shards(): pl.pallas_call(functools.partial(lift_kernel, helpers), out_shape=[jax.Sh...  2.81 us
    ppermute x1, starting transfers between devices, shards(): across = lax.ppermute(near, axes, two)  2.07 us
    pallas_call x1, Pallas kernels, shards(): pl.pallas_call(functools.partial(score_kernel, planes, helpers, 3), out_s...  1.81 us
    unnamed x16, local copies, waits for them, and re-layouts  1.79 us
    ppermute x1, starting transfers between devices, shards(): far = lax.ppermute(packed, axes, two)  1.55 us
  transfers between devices with their start and end apart: 17, of which 13 were waited for; matrix products, arithmetic and copies ran while one was open for 1% of the time, Pallas kernels for 3%

profile of v3, /device:TPU:0, one launch (start us, length us, event | category | flops | bytes accessed | tf_op | source)
XLA Modules:
  0.0 61.1 jit_solution(8773453916615555285)
XLA Ops:
  0.6 2.8 %lift.1 = (bf16[1552,128]{1,0:T(8,128)(2,1)}, f32[64,768]{1,0:T(8,128)}, f32[64,768]{1,0:T(8,128)}, s32[1,1024]{1,0:T(1,128)}, f32[8,128]{1,0:T(8,128)}) custom-call(bf16[256,768]{1,0:T(8,128)(2,1)} %refs_0_.1, s32[2,256]{1,0:T(2,128)} %bitcast.4, s32[2,256]{1,0:T(2,128)} %bitcast.5, s32[1,4096]{1,0:T(1,128)} %refs_3_.1, bf16[32,1024]{1,0:T(8,128)(2,1)} %refs_4_.1, ...), custom_call_target="tpu_custom_call" | custom-call | tf_op jit(solution)/shard_map/lift/pallas_call | solution.py:217
  3.4 0.5 collective-permute-start
  4.0 1.3 %collective-permute-done = f32[64,768]{1,0:T(8,128)S(1)} collective-permute-done((f32[64,768]{1,0:T(8,128)}, f32[64,768]{1,0:T(8,128)S(1)}, u32[]{:S(2)}, u32[]{:S(2)}) %collective-permute-start) | collective-permute-done | bytes 196640 | tf_op jit(solution)/shard_map/ppermute | solution.py:198
  5.3 0.9 %add.12 = f32[64,768]{1,0:T(8,128)S(1)} add(f32[64,768]{1,0:T(8,128)} %get-tuple-element.18, f32[64,768]{1,0:T(8,128)S(1)} %collective-permute-done) | non-fusion elementwise | flops 49152 | bytes 589824 | tf_op jit(solution)/shard_map/add | solution.py:202
  6.2 0.6 %slice.31.refs_1_ = bf16[32,768]{1,0:T(8,128)(2,1)} slice(f32[64,768]{1,0:T(8,128)S(1)} %add.12), slice={[32:64], [0:768]} | slice | bytes 98304 | tf_op jit(solution)/shard_map/slice | solution.py:203
  6.8 0.0 copy-start.7
  6.8 2.9 %collective-permute-start.6 = (bf16[1552,128]{1,0:T(8,128)(2,1)}, bf16[1552,128]{1,0:T(8,128)(2,1)S(1)}, u32[]{:S(2)}, u32[]{:S(2)}) collective-permute-start(bf16[1552,128]{1,0:T(8,128)(2,1)} %gate.2.refs_0_), channel_id=1, source_target_pairs={{0,2},{1,5},{2,0},{3,7},{4,6},{5,1},{6,4},{7,3},{8,10},{9,13},{10,... | collective-permute-start | bytes 1191944 | tf_op jit(solution)/shard_map/ppermute | solution.py:244
  9.7 0.0 copy-done.7
  9.7 0.8 %collective-permute-start.1 = (bf16[32,768]{1,0:T(8,128)(2,1)S(1)}, bf16[32,768]{1,0:T(8,128)(2,1)S(1)}, u32[]{:S(2)}, u32[]{:S(2)}) collective-permute-start(bf16[32,768]{1,0:T(8,128)(2,1)S(1)} %copy-done.7), channel_id=1, source_target_pairs={{0,2},{1,3},{2,0},{3,1},{4,6},{5,7},{6,4},{7,5},{8,10},{9,11},{10,... | collective-permute-start | bytes 147464 | tf_op jit(solution)/shard_map/ppermute | solution.py:198
  10.5 1.5 %collective-permute-start.8 = (bf16[1552,128]{1,0:T(8,128)(2,1)}, bf16[1552,128]{1,0:T(8,128)(2,1)S(1)}, u32[]{:S(2)}, u32[]{:S(2)}) collective-permute-start(bf16[1552,128]{1,0:T(8,128)(2,1)} %gate.2.refs_0_), channel_id=1, source_target_pairs={{0,4},{1,3},{2,6},{3,1},{4,0},{5,7},{6,2},{7,5},{8,12},{9,11},{10,... | collective-permute-start | bytes 1191944 | tf_op jit(solution)/shard_map/ppermute | solution.py:245
  12.0 8.3 %collective-permute-done.1 = bf16[32,768]{1,0:T(8,128)(2,1)S(1)} collective-permute-done((bf16[32,768]{1,0:T(8,128)(2,1)S(1)}, bf16[32,768]{1,0:T(8,128)(2,1)S(1)}, u32[]{:S(2)}, u32[]{:S(2)}) %collective-permute-start.1) | collective-permute-done | bytes 49184 | tf_op jit(solution)/shard_map/ppermute | solution.py:198
  20.4 0.6 %fusion.1.refs_1_ = bf16[32,768]{1,0:T(8,128)(2,1)} fusion(f32[64,768]{1,0:T(8,128)S(1)} %add.12, bf16[32,768]{1,0:T(8,128)(2,1)S(1)} %collective-permute-done.1), kind=kLoop, calls=%fused_computation.6 | loop fusion | flops 73728 | bytes 196608 | tf_op jit(solution)/shard_map/convert_element_type | solution.py:249
  21.0 0.0 copy-start.6
  21.0 0.0 copy-start.3
  21.0 0.0 collective-permute-done.6.refs_0_
  21.0 0.0 copy-start.1
  21.0 0.8 %copy-done.1 = bf16[1552,128]{1,0:T(8,128)(2,1)} copy-done((bf16[1552,128]{1,0:T(8,128)(2,1)}, bf16[1552,128]{1,0:T(8,128)(2,1)S(1)}, u32[]{:S(2)}) %copy-start.1) | copy-done | bytes 397336
  21.8 2.1 %collective-permute-start.7 = (bf16[1552,128]{1,0:T(8,128)(2,1)}, bf16[1552,128]{1,0:T(8,128)(2,1)S(1)}, u32[]{:S(2)}, u32[]{:S(2)}) collective-permute-start(bf16[1552,128]{1,0:T(8,128)(2,1)} %gate.3.refs_1_), channel_id=1, source_target_pairs={{0,4},{1,3},{2,6},{3,1},{4,0},{5,7},{6,2},{7,5},{8,12},{9,11},{10,... | collective-permute-start | bytes 1191944 | tf_op jit(solution)/shard_map/ppermute | solution.py:252
  23.8 0.0 copy-done.6
  23.8 3.6 %collective-permute-start.4 = (bf16[32,768]{1,0:T(8,128)(2,1)S(1)}, bf16[32,768]{1,0:T(8,128)(2,1)S(1)}, u32[]{:S(2)}, u32[]{:S(2)}) collective-permute-start(bf16[32,768]{1,0:T(8,128)(2,1)S(1)} %copy-done.6), channel_id=1, source_target_pairs={{0,24},{4,28},{8,16},{12,20},{16,8},{20,12},{24,0},{28,4},{1,25},{... | collective-permute-start | bytes 147464 | tf_op jit(solution)/shard_map/ppermute | solution.py:198
  27.4 0.0 collective-permute-start.3
  27.4 0.8 %collective-permute-start.2 = (bf16[32,768]{1,0:T(8,128)(2,1)S(1)}, bf16[32,768]{1,0:T(8,128)(2,1)S(1)}, u32[]{:S(2)}, u32[]{:S(2)}) collective-permute-start(bf16[32,768]{1,0:T(8,128)(2,1)S(1)} %copy-done.6), channel_id=1, source_target_pairs={{0,8},{4,12},{8,0},{12,4},{16,24},{20,28},{24,16},{28,20},{1,9},{5... | collective-permute-start | bytes 147464 | tf_op jit(solution)/shard_map/ppermute | solution.py:198
  28.2 1.5 %collective-permute-done.4 = bf16[32,768]{1,0:T(8,128)(2,1)S(1)} collective-permute-done((bf16[32,768]{1,0:T(8,128)(2,1)S(1)}, bf16[32,768]{1,0:T(8,128)(2,1)S(1)}, u32[]{:S(2)}, u32[]{:S(2)}) %collective-permute-start.4) | collective-permute-done | bytes 49184 | tf_op jit(solution)/shard_map/ppermute | solution.py:198
  29.7 2.7 %collective-permute-done.3 = bf16[32,768]{1,0:T(8,128)(2,1)S(1)} collective-permute-done((bf16[32,768]{1,0:T(8,128)(2,1)S(1)}, bf16[32,768]{1,0:T(8,128)(2,1)S(1)}, u32[]{:S(2)}, u32[]{:S(2)}) %collective-permute-start.3) | collective-permute-done | bytes 49184 | tf_op jit(solution)/shard_map/ppermute | solution.py:198
  32.4 0.0 collective-permute-done.2
  32.4 0.1 collective-permute-start.5
  32.5 1.4 %collective-permute-done.5.theirs_ref = bf16[128,768]{1,0:T(8,128)(2,1)S(1)} collective-permute-done((bf16[128,768]{1,0:T(8,128)(2,1)S(1)}, bf16[128,768]{1,0:T(8,128)(2,1)S(1)}, u32[]{:S(2)}, u32[]{:S(2)}) %collective-permute-start.5) | collective-permute-done | bytes 196640 | tf_op jit(solution)/shard_map/ppermute | solution.py:198
  34.0 0.0 collective-permute-done.8.refs_2_
  34.0 0.0 copy-done.3
  34.0 0.0 copy-start.2
  34.0 1.0 %copy-done.2 = bf16[1552,128]{1,0:T(8,128)(2,1)S(1)} copy-done((bf16[1552,128]{1,0:T(8,128)(2,1)S(1)}, bf16[1552,128]{1,0:T(8,128)(2,1)}, u32[]{:S(2)}) %copy-start.2) | copy-done | bytes 397336
  35.0 1.8 %score.1.refs_1_ = f32[256,896]{1,0:T(8,128)S(1)} custom-call(bf16[128,768]{1,0:T(8,128)(2,1)S(1)} %pad_maximum_fusion.mine_ref, bf16[128,768]{1,0:T(8,128)(2,1)S(1)} %collective-permute-done.5.theirs_ref, bf16[1552,128]{1,0:T(8,128)(2,1)S(1)} %copy-done.3, bf16[1552,128]{1,0:T(8,128)(2,1)S(1)} %copy-done.2, bf16[1552,128]{1,0:T(8,128)(2,1)S(1)} %collective-permute-done.8.refs_2_), custom_call_target="tpu_custom_call" | custom-call | tf_op jit(solution)/shard_map/score/pallas_call | solution.py:257
  36.8 0.0 copy-start.4
  36.8 0.0 copy-start
  36.8 0.0 copy-start.5
  36.8 0.0 collective-permute-done.7.refs_0_
  36.8 0.8 %score_last.1 = (f32[128,896]{1,0:T(8,128)S(1)}, f32[128,896]{1,0:T(8,128)S(1)}) custom-call(bf16[128,768]{1,0:T(8,128)(2,1)S(1)} %pad_maximum_fusion.mine_ref, bf16[128,768]{1,0:T(8,128)(2,1)S(1)} %collective-permute-done.5.theirs_ref, bf16[1552,128]{1,0:T(8,128)(2,1)S(1)} %collective-permute-done.7.refs_0_, f32[256,896]{1,0:T(8,128)S(1)} %score.1.refs_1_), custom_call_target="tpu_custom_call" | custom-call | tf_op jit(solution)/shard_map/score_last/pallas_call | solution.py:263
  37.6 0.2 collective-permute-start.9
  37.8 1.7 %collective-permute-done.9.theirs_ref = f32[128,896]{1,0:T(8,128)S(1)} collective-permute-done((f32[128,896]{1,0:T(8,128)S(1)}, f32[128,896]{1,0:T(8,128)S(1)}, u32[]{:S(2)}, u32[]{:S(2)}) %collective-permute-start.9) | collective-permute-done | bytes 458784 | tf_op jit(solution)/shard_map/ppermute | solution.py:198
  39.6 0.2 collective-permute-start.10
  39.8 2.0 %collective-permute-start.11 = (bf16[208,128]{1,0:T(8,128)(2,1)S(1)}, bf16[208,128]{1,0:T(8,128)(2,1)S(1)}, u32[]{:S(2)}, u32[]{:S(2)}) collective-permute-start(bf16[208,128]{1,0:T(8,128)(2,1)S(1)} %get-tuple-element.25), channel_id=1, source_target_pairs={{0,16},{4,20},{8,24},{12,28},{16,0},{20,4},{24,8},{28,12},{1,17},{... | collective-permute-start | bytes 159752 | tf_op jit(solution)/shard_map/ppermute | solution.py:198
  41.7 2.3 %collective-permute-start.12 = (bf16[208,128]{1,0:T(8,128)(2,1)S(1)}, bf16[208,128]{1,0:T(8,128)(2,1)S(1)}, u32[]{:S(2)}, u32[]{:S(2)}) collective-permute-start(bf16[208,128]{1,0:T(8,128)(2,1)S(1)} %get-tuple-element.26), channel_id=1, source_target_pairs={{0,24},{4,28},{8,16},{12,20},{16,8},{20,12},{24,0},{28,4},{1,25},{... | collective-permute-start | bytes 159752 | tf_op jit(solution)/shard_map/ppermute | solution.py:198
  44.0 0.6 %collective-permute-done.10.refs_0_ = bf16[208,128]{1,0:T(8,128)(2,1)S(1)} collective-permute-done((bf16[208,128]{1,0:T(8,128)(2,1)S(1)}, bf16[208,128]{1,0:T(8,128)(2,1)S(1)}, u32[]{:S(2)}, u32[]{:S(2)}) %collective-permute-start.10) | collective-permute-done | bytes 53280 | tf_op jit(solution)/shard_map/ppermute | solution.py:198
  44.6 0.8 %collective-permute-done.11.refs_1_ = bf16[208,128]{1,0:T(8,128)(2,1)S(1)} collective-permute-done((bf16[208,128]{1,0:T(8,128)(2,1)S(1)}, bf16[208,128]{1,0:T(8,128)(2,1)S(1)}, u32[]{:S(2)}, u32[]{:S(2)}) %collective-permute-start.11) | collective-permute-done | bytes 53280 | tf_op jit(solution)/shard_map/ppermute | solution.py:198
  45.4 2.3 %collective-permute-done.12.refs_2_ = bf16[208,128]{1,0:T(8,128)(2,1)S(1)} collective-permute-done((bf16[208,128]{1,0:T(8,128)(2,1)S(1)}, bf16[208,128]{1,0:T(8,128)(2,1)S(1)}, u32[]{:S(2)}, u32[]{:S(2)}) %collective-permute-start.12) | collective-permute-done | bytes 53280 | tf_op jit(solution)/shard_map/ppermute | solution.py:198
  47.7 0.0 copy-done.4
  47.7 0.1 scale.1
  47.8 2.2 %collective-permute-start.13 = (bf16[32,768]{1,0:T(8,128)(2,1)S(1)}, bf16[32,768]{1,0:T(8,128)(2,1)S(1)}, u32[]{:S(2)}, u32[]{:S(2)}) collective-permute-start(bf16[32,768]{1,0:T(8,128)(2,1)S(1)} %scale.1), channel_id=1, source_target_pairs={{0,2},{1,3},{2,0},{3,1},{4,6},{5,7},{6,4},{7,5},{8,10},{9,11},{10,... | collective-permute-start | bytes 147464 | tf_op jit(solution)/shard_map/ppermute | solution.py:198
  50.0 2.1 %collective-permute-done.13 = bf16[32,768]{1,0:T(8,128)(2,1)S(1)} collective-permute-done((bf16[32,768]{1,0:T(8,128)(2,1)S(1)}, bf16[32,768]{1,0:T(8,128)(2,1)S(1)}, u32[]{:S(2)}, u32[]{:S(2)}) %collective-permute-start.13) | collective-permute-done | bytes 49184 | tf_op jit(solution)/shard_map/ppermute | solution.py:198
  52.1 0.1 collective-permute-start.14
  52.2 1.3 %collective-permute-done.14.theirs_ref = bf16[64,768]{1,0:T(8,128)(2,1)S(1)} collective-permute-done((bf16[64,768]{1,0:T(8,128)(2,1)S(1)}, bf16[64,768]{1,0:T(8,128)(2,1)S(1)}, u32[]{:S(2)}, u32[]{:S(2)}) %collective-permute-start.14) | collective-permute-done | bytes 98336 | tf_op jit(solution)/shard_map/ppermute | solution.py:198
  53.4 0.0 copy-done
  53.4 0.0 copy-done.5
  53.4 1.4 %sketch.1 = (f32[32,1024]{1,0:T(8,128)}, f32[64,768]{1,0:T(8,128)S(1)}, f32[64,768]{1,0:T(8,128)S(1)}) custom-call(s32[1,1024]{1,0:T(1,128)S(1)} %copy-done.5, f32[8,128]{1,0:T(8,128)S(1)} %copy-done.4, bf16[1024,768]{1,0:T(8,128)(2,1)S(1)} %copy-done, bf16[64,768]{1,0:T(8,128)(2,1)S(1)} %pad_maximum_fusion.1.mine_ref, ...), custom_call_target="tpu_custom_call" | custom-call | tf_op jit(solution)/shard_map/sketch/pallas_call | solution.py:286
  54.8 0.1 collective-permute-start.15
  55.0 1.3 %collective-permute-done.15 = f32[64,768]{1,0:T(8,128)S(1)} collective-permute-done((f32[64,768]{1,0:T(8,128)S(1)}, f32[64,768]{1,0:T(8,128)S(1)}, u32[]{:S(2)}, u32[]{:S(2)}) %collective-permute-start.15) | collective-permute-done | bytes 196640 | tf_op jit(solution)/shard_map/ppermute | solution.py:198
  56.3 2.1 %collective-permute-start.16 = (bf16[32,768]{1,0:T(8,128)(2,1)S(1)}, bf16[32,768]{1,0:T(8,128)(2,1)S(1)}, u32[]{:S(2)}, u32[]{:S(2)}) collective-permute-start(bf16[32,768]{1,0:T(8,128)(2,1)S(1)} %slice.30), channel_id=1, source_target_pairs={{0,2},{1,3},{2,0},{3,1},{4,6},{5,7},{6,4},{7,5},{8,10},{9,11},{10,... | collective-permute-start | bytes 147464 | tf_op jit(solution)/shard_map/ppermute | solution.py:198
  58.4 2.1 %collective-permute-done.16 = bf16[32,768]{1,0:T(8,128)(2,1)S(1)} collective-permute-done((bf16[32,768]{1,0:T(8,128)(2,1)S(1)}, bf16[32,768]{1,0:T(8,128)(2,1)S(1)}, u32[]{:S(2)}, u32[]{:S(2)}) %collective-permute-start.16) | collective-permute-done | bytes 49184 | tf_op jit(solution)/shard_map/ppermute | solution.py:198
  60.5 0.7 %fusion = f32[1,32,768]{2,1,0:T(8,128)} fusion(f32[64,768]{1,0:T(8,128)S(1)} %add.14, bf16[32,768]{1,0:T(8,128)(2,1)S(1)} %collective-permute-done.16), kind=kLoop, calls=%fused_computation.3 | loop fusion | flops 49152 | bytes 245760 | tf_op jit(solution)/shard_map/broadcast_in_dim | solution.py:295
  (7 shorter events, 0.1 us)
Async XLA Ops:
  3.4 1.8 %collective-permute-start = (f32[64,768]{1,0:T(8,128)}, f32[64,768]{1,0:T(8,128)S(1)}, u32[]{:S(2)}, u32[]{:S(2)}) collective-permute-start(f32[64,768]{1,0:T(8,128)} %get-tuple-element.19), channel_id=1, source_target_pairs={{0,1},{1,0},{2,3},{3,2},{4,5},{5,4},{6,7},{7,6},{8,9},{9,8},{10,11... | collective-permute-start | bytes 589832 | tf_op jit(solution)/shard_map/ppermute | solution.py:198
  6.8 2.9 %copy-start.7 = (bf16[32,768]{1,0:T(8,128)(2,1)S(1)}, bf16[32,768]{1,0:T(8,128)(2,1)}, u32[]{:S(2)}) copy-start(bf16[32,768]{1,0:T(8,128)(2,1)} %slice.31.refs_1_) | copy-start | bytes 147460
  6.8 14.2 %collective-permute-start.6 = (bf16[1552,128]{1,0:T(8,128)(2,1)}, bf16[1552,128]{1,0:T(8,128)(2,1)S(1)}, u32[]{:S(2)}, u32[]{:S(2)}) collective-permute-start(bf16[1552,128]{1,0:T(8,128)(2,1)} %gate.2.refs_0_), channel_id=1, source_target_pairs={{0,2},{1,5},{2,0},{3,7},{4,6},{5,1},{6,4},{7,3},{8,10},{9,13},{10,... | collective-permute-start | bytes 1191944 | tf_op jit(solution)/shard_map/ppermute | solution.py:244
  9.7 10.7 %collective-permute-start.1 = (bf16[32,768]{1,0:T(8,128)(2,1)S(1)}, bf16[32,768]{1,0:T(8,128)(2,1)S(1)}, u32[]{:S(2)}, u32[]{:S(2)}) collective-permute-start(bf16[32,768]{1,0:T(8,128)(2,1)S(1)} %copy-done.7), channel_id=1, source_target_pairs={{0,2},{1,3},{2,0},{3,1},{4,6},{5,7},{6,4},{7,5},{8,10},{9,11},{10,... | collective-permute-start | bytes 147464 | tf_op jit(solution)/shard_map/ppermute | solution.py:198
  10.5 23.5 %collective-permute-start.8 = (bf16[1552,128]{1,0:T(8,128)(2,1)}, bf16[1552,128]{1,0:T(8,128)(2,1)S(1)}, u32[]{:S(2)}, u32[]{:S(2)}) collective-permute-start(bf16[1552,128]{1,0:T(8,128)(2,1)} %gate.2.refs_0_), channel_id=1, source_target_pairs={{0,4},{1,3},{2,6},{3,1},{4,0},{5,7},{6,2},{7,5},{8,12},{9,11},{10,... | collective-permute-start | bytes 1191944 | tf_op jit(solution)/shard_map/ppermute | solution.py:245
  21.0 2.8 %copy-start.6 = (bf16[32,768]{1,0:T(8,128)(2,1)S(1)}, bf16[32,768]{1,0:T(8,128)(2,1)}, u32[]{:S(2)}) copy-start(bf16[32,768]{1,0:T(8,128)(2,1)} %fusion.1.refs_1_) | copy-start | bytes 147460
  21.0 13.0 %copy-start.3 = (bf16[1552,128]{1,0:T(8,128)(2,1)S(1)}, bf16[1552,128]{1,0:T(8,128)(2,1)}, u32[]{:S(2)}) copy-start(bf16[1552,128]{1,0:T(8,128)(2,1)} %gate.2.refs_0_) | copy-start | bytes 1191940
  21.0 0.8 %copy-start.1 = (bf16[1552,128]{1,0:T(8,128)(2,1)}, bf16[1552,128]{1,0:T(8,128)(2,1)S(1)}, u32[]{:S(2)}) copy-start(bf16[1552,128]{1,0:T(8,128)(2,1)S(1)} %collective-permute-done.6.refs_0_) | copy-start | bytes 1191940
  21.8 15.1 %collective-permute-start.7 = (bf16[1552,128]{1,0:T(8,128)(2,1)}, bf16[1552,128]{1,0:T(8,128)(2,1)S(1)}, u32[]{:S(2)}, u32[]{:S(2)}) collective-permute-start(bf16[1552,128]{1,0:T(8,128)(2,1)} %gate.3.refs_1_), channel_id=1, source_target_pairs={{0,4},{1,3},{2,6},{3,1},{4,0},{5,7},{6,2},{7,5},{8,12},{9,11},{10,... | collective-permute-start | bytes 1191944 | tf_op jit(solution)/shard_map/ppermute | solution.py:252
  23.8 5.9 %collective-permute-start.4 = (bf16[32,768]{1,0:T(8,128)(2,1)S(1)}, bf16[32,768]{1,0:T(8,128)(2,1)S(1)}, u32[]{:S(2)}, u32[]{:S(2)}) collective-permute-start(bf16[32,768]{1,0:T(8,128)(2,1)S(1)} %copy-done.6), channel_id=1, source_target_pairs={{0,24},{4,28},{8,16},{12,20},{16,8},{20,12},{24,0},{28,4},{1,25},{... | collective-permute-start | bytes 147464 | tf_op jit(solution)/shard_map/ppermute | solution.py:198
  27.4 5.0 %collective-permute-start.3 = (bf16[32,768]{1,0:T(8,128)(2,1)S(1)}, bf16[32,768]{1,0:T(8,128)(2,1)S(1)}, u32[]{:S(2)}, u32[]{:S(2)}) collective-permute-start(bf16[32,768]{1,0:T(8,128)(2,1)S(1)} %copy-done.6), channel_id=1, source_target_pairs={{0,16},{4,20},{8,24},{12,28},{16,0},{20,4},{24,8},{28,12},{1,17},{... | collective-permute-start | bytes 147464 | tf_op jit(solution)/shard_map/ppermute | solution.py:198
  27.4 5.0 %collective-permute-start.2 = (bf16[32,768]{1,0:T(8,128)(2,1)S(1)}, bf16[32,768]{1,0:T(8,128)(2,1)S(1)}, u32[]{:S(2)}, u32[]{:S(2)}) collective-permute-start(bf16[32,768]{1,0:T(8,128)(2,1)S(1)} %copy-done.6), channel_id=1, source_target_pairs={{0,8},{4,12},{8,0},{12,4},{16,24},{20,28},{24,16},{28,20},{1,9},{5... | collective-permute-start | bytes 147464 | tf_op jit(solution)/shard_map/ppermute | solution.py:198
  32.4 1.5 %collective-permute-start.5 = (bf16[128,768]{1,0:T(8,128)(2,1)S(1)}, bf16[128,768]{1,0:T(8,128)(2,1)S(1)}, u32[]{:S(2)}, u32[]{:S(2)}) collective-permute-start(bf16[128,768]{1,0:T(8,128)(2,1)S(1)} %pad_maximum_fusion.mine_ref), channel_id=1, source_target_pairs={{0,1},{1,0},{2,3},{3,2},{4,5},{5,4},{6,7},{7,6},{8,9},{9,8},{10,11... | collective-permute-start | bytes 589832 | tf_op jit(solution)/shard_map/ppermute | solution.py:198
  34.0 1.0 %copy-start.2 = (bf16[1552,128]{1,0:T(8,128)(2,1)S(1)}, bf16[1552,128]{1,0:T(8,128)(2,1)}, u32[]{:S(2)}) copy-start(bf16[1552,128]{1,0:T(8,128)(2,1)} %gate.3.refs_1_) | copy-start | bytes 1191940
  36.8 10.9 %copy-start.4 = (f32[8,128]{1,0:T(8,128)S(1)}, f32[8,128]{1,0:T(8,128)}, u32[]{:S(2)}) copy-start(f32[8,128]{1,0:T(8,128)} %get-tuple-element.17.resident_ref) | copy-start | bytes 12292
  36.8 16.7 %copy-start = (bf16[1024,768]{1,0:T(8,128)(2,1)S(1)}, bf16[1024,768]{1,0:T(8,128)(2,1)}, u32[]{:S(2)}) copy-start(bf16[1024,768]{1,0:T(8,128)(2,1)} %points_ref.1) | copy-start | bytes 4718596
  36.8 16.6 %copy-start.5 = (s32[1,1024]{1,0:T(1,128)S(1)}, s32[1,1024]{1,0:T(1,128)}, u32[]{:S(2)}) copy-start(s32[1,1024]{1,0:T(1,128)} %get-tuple-element.16.mark_ref) | copy-start | bytes 12292
  37.6 1.9 %collective-permute-start.9 = (f32[128,896]{1,0:T(8,128)S(1)}, f32[128,896]{1,0:T(8,128)S(1)}, u32[]{:S(2)}, u32[]{:S(2)}) collective-permute-start(f32[128,896]{1,0:T(8,128)S(1)} %get-tuple-element.22), channel_id=1, source_target_pairs={{0,1},{1,0},{2,3},{3,2},{4,5},{5,4},{6,7},{7,6},{8,9},{9,8},{10,11... | collective-permute-start | bytes 1376264 | tf_op jit(solution)/shard_map/ppermute | solution.py:198
  39.6 5.1 %collective-permute-start.10 = (bf16[208,128]{1,0:T(8,128)(2,1)S(1)}, bf16[208,128]{1,0:T(8,128)(2,1)S(1)}, u32[]{:S(2)}, u32[]{:S(2)}) collective-permute-start(bf16[208,128]{1,0:T(8,128)(2,1)S(1)} %get-tuple-element.24), channel_id=1, source_target_pairs={{0,8},{4,12},{8,0},{12,4},{16,24},{20,28},{24,16},{28,20},{1,9},{5... | collective-permute-start | bytes 159752 | tf_op jit(solution)/shard_map/ppermute | solution.py:198
  39.8 5.6 %collective-permute-start.11 = (bf16[208,128]{1,0:T(8,128)(2,1)S(1)}, bf16[208,128]{1,0:T(8,128)(2,1)S(1)}, u32[]{:S(2)}, u32[]{:S(2)}) collective-permute-start(bf16[208,128]{1,0:T(8,128)(2,1)S(1)} %get-tuple-element.25), channel_id=1, source_target_pairs={{0,16},{4,20},{8,24},{12,28},{16,0},{20,4},{24,8},{28,12},{1,17},{... | collective-permute-start | bytes 159752 | tf_op jit(solution)/shard_map/ppermute | solution.py:198
  41.7 6.0 %collective-permute-start.12 = (bf16[208,128]{1,0:T(8,128)(2,1)S(1)}, bf16[208,128]{1,0:T(8,128)(2,1)S(1)}, u32[]{:S(2)}, u32[]{:S(2)}) collective-permute-start(bf16[208,128]{1,0:T(8,128)(2,1)S(1)} %get-tuple-element.26), channel_id=1, source_target_pairs={{0,24},{4,28},{8,16},{12,20},{16,8},{20,12},{24,0},{28,4},{1,25},{... | collective-permute-start | bytes 159752 | tf_op jit(solution)/shard_map/ppermute | solution.py:198
  47.8 4.3 %collective-permute-start.13 = (bf16[32,768]{1,0:T(8,128)(2,1)S(1)}, bf16[32,768]{1,0:T(8,128)(2,1)S(1)}, u32[]{:S(2)}, u32[]{:S(2)}) collective-permute-start(bf16[32,768]{1,0:T(8,128)(2,1)S(1)} %scale.1), channel_id=1, source_target_pairs={{0,2},{1,3},{2,0},{3,1},{4,6},{5,7},{6,4},{7,5},{8,10},{9,11},{10,... | collective-permute-start | bytes 147464 | tf_op jit(solution)/shard_map/ppermute | solution.py:198
  52.1 1.4 %collective-permute-start.14 = (bf16[64,768]{1,0:T(8,128)(2,1)S(1)}, bf16[64,768]{1,0:T(8,128)(2,1)S(1)}, u32[]{:S(2)}, u32[]{:S(2)}) collective-permute-start(bf16[64,768]{1,0:T(8,128)(2,1)S(1)} %pad_maximum_fusion.1.mine_ref), channel_id=1, source_target_pairs={{0,1},{1,0},{2,3},{3,2},{4,5},{5,4},{6,7},{7,6},{8,9},{9,8},{10,11... | collective-permute-start | bytes 294920 | tf_op jit(solution)/shard_map/ppermute | solution.py:198
  54.8 1.4 %collective-permute-start.15 = (f32[64,768]{1,0:T(8,128)S(1)}, f32[64,768]{1,0:T(8,128)S(1)}, u32[]{:S(2)}, u32[]{:S(2)}) collective-permute-start(f32[64,768]{1,0:T(8,128)S(1)} %get-tuple-element.29), channel_id=1, source_target_pairs={{0,1},{1,0},{2,3},{3,2},{4,5},{5,4},{6,7},{7,6},{8,9},{9,8},{10,11... | collective-permute-start | bytes 589832 | tf_op jit(solution)/shard_map/ppermute | solution.py:198
  56.3 4.2 %collective-permute-start.16 = (bf16[32,768]{1,0:T(8,128)(2,1)S(1)}, bf16[32,768]{1,0:T(8,128)(2,1)S(1)}, u32[]{:S(2)}, u32[]{:S(2)}) collective-permute-start(bf16[32,768]{1,0:T(8,128)(2,1)S(1)} %slice.30), channel_id=1, source_target_pairs={{0,2},{1,3},{2,0},{3,1},{4,6},{5,7},{6,4},{7,5},{8,10},{9,11},{10,... | collective-permute-start | bytes 147464 | tf_op jit(solution)/shard_map/ppermute | solution.py:198

commit v4 on v3

--- a/solution.py
+++ b/solution.py
@@ -11,11 +11,12 @@
 BF16 = jnp.bfloat16
 LANES = 128
 TILE = 16
+CHUNKS = 4
 INNER = 2
-CHUNKS = 4
 FIRST = 60
 
 ANY = pl.BlockSpec(memory_space=pl.ANY)
+VMEM = pl.BlockSpec(memory_space=pltpu.VMEM)
 HBM = pl.BlockSpec(memory_space=pltpu.HBM)
 PARAMS = pltpu.CompilerParams(vmem_limit_bytes=32 * 1024 * 1024)
 
@@ -82,6 +83,14 @@
     packed_ref[asked * width // LANES :, :] = jnp.concatenate(line, axis=0).astype(BF16)
 
 
+def join_kernel(keep_ref, got_ref, own_ref, *send_refs):
+    rank = own_ref.shape[0]
+    own_ref[...] = keep_ref[:rank, :] + got_ref[:rank, :]
+    for k, ref in enumerate(send_refs, 1):
+        part = slice(k * rank, (k + 1) * rank)
+        ref[...] = (keep_ref[part, :] + got_ref[part, :]).astype(BF16)
+
+
 def gate_kernel(*refs):
     pass
 
@@ -173,36 +182,26 @@
     out_ref[...] = (total * factor).astype(out_ref.dtype)
 
 
-def sketch_kernel(helpers, mark_ref, resident_ref, points_ref, mine_ref, theirs_ref, sketch_ref, keep_ref, pass_ref):
+def sketch_kernel(helpers, mark_ref, resident_ref, points_ref, *refs):
+    scaled, sketch_ref, outs = refs[:helpers], refs[helpers], refs[helpers + 1 :]
     rank, count = sketch_ref.shape
-    offsets = order(helpers)
     mark = mark_ref[...]
     points = points_ref[...]
-    product = contract(jnp.concatenate([mine_ref[...], theirs_ref[...]], axis=0), points, ((1,), (1,)))
+    product = contract(jnp.concatenate([s[...] for s in scaled], axis=0), points, ((1,), (1,)))
     sketch = product[:rank]
-    for k, d in enumerate(offsets[1:], 1):
-        sketch = jnp.where(mark == d, product[k * rank : (k + 1) * rank], sketch)
+    for d in range(1, helpers):
+        sketch = jnp.where(mark == d, product[d * rank : (d + 1) * rank], sketch)
     sketch_ref[...] = sketch
     rounded = sketch.astype(BF16)
-    rows = [jnp.where(mark == d, rounded, jnp.zeros((), BF16)) for d in offsets]
+    rows = [jnp.where(mark == d, rounded, jnp.zeros((), BF16)) for d in range(helpers)]
     summed = contract(jnp.concatenate(rows, axis=0), points, ((1,), (0,)))
-    blocks = [
-        summed[k * rank : (k + 1) * rank] * lax.rsqrt(resident_ref[d : d + 1, 0:1]) for k, d in enumerate(offsets)
-    ]
-    kept = helpers // 2
-    keep_ref[...] = jnp.concatenate(blocks[:kept], axis=0)
-    pass_ref[...] = jnp.concatenate(blocks[kept:], axis=0)
+    for d, out in enumerate(outs):
+        block = summed[d * rank : (d + 1) * rank] * lax.rsqrt(resident_ref[d : d + 1, 0:1])
+        out[...] = block.astype(out.dtype)
 
 
 def swap(value, axis, d):
     return lax.ppermute(value, axis, [(i, i ^ d) for i in range(lax.axis_size(axis))])
-
-
-def gather_to_owner(keep, passed, rank, helpers):
-    both = keep + swap(passed, "help", 1)
-    blocks = [both[k * rank : (k + 1) * rank] for k in range(helpers // 2)]
-    sent = [block.astype(BF16) for block in blocks[1:]]
-    return blocks[0], [swap(block, "help", 2 * k) for k, block in enumerate(sent, 1)], sent
 
 
 def shards(queries, probe_group, probe_local, points, point_cluster, test_matrix):
@@ -235,23 +234,25 @@
         compiler_params=pltpu.CompilerParams(vmem_limit_bytes=FIRST << 20),
         name="lift",
     )(queries, probe_group.T, probe_local.T, point_cluster, test_matrix, points)
-    own, others, leaving = gather_to_owner(keep, passed, rank, helpers)
+    own, *leaving = pl.pallas_call(
+        join_kernel,
+        out_shape=[jax.ShapeDtypeStruct((rank, width), F32)]
+        + [jax.ShapeDtypeStruct((rank, width), BF16)] * (helpers // 2 - 1),
+        compiler_params=PARAMS,
+        name="join",
+    )(keep, swap(passed, "help", 1))
+    for k, part in enumerate(leaving, 1):
+        own = own + swap(part, "help", 2 * k).astype(F32)
+    lifter = own.astype(BF16)
+    mine = jnp.concatenate([lifter] + [swap(lifter, "shard", INNER * d) for d in range(1, planes)], axis=0)
+    theirs = swap(mine, "help", 1)
 
     index, axes = range(groups * helpers), ("shard", "help")
     one = [(i, i ^ (2 if i % 2 == 0 else helpers)) for i in index]
     two = [(i, i ^ (helpers if i % 2 == 0 else 2)) for i in index]
-    packed = gate(packed, *leaving)
-    near = lax.ppermute(packed, axes, one)
     far = lax.ppermute(packed, axes, two)
-
-    for part in others:
-        own = own + part.astype(F32)
-    lifter = own.astype(BF16)
-    lifters = [lifter] + [swap(lifter, "shard", INNER * d) for d in range(1, planes)]
-    near = gate(near, lifter)
+    near = gate(lax.ppermute(packed, axes, one), mine)
     across = lax.ppermute(near, axes, two)
-    mine = jnp.concatenate(lifters, axis=0)
-    theirs = swap(mine, "help", 1)
 
     wide = width + LANES
     begun = pl.pallas_call(
@@ -281,17 +282,18 @@
         compiler_params=PARAMS,
         name="scale",
     )(resident, *moments)
-    scaled = jnp.concatenate([scaled] + [swap(scaled, "help", d) for d in range(2, helpers, 2)], axis=0)
-
-    sketch, keep, passed = pl.pallas_call(
+    scaled = [scaled] + [swap(scaled, "help", d) for d in range(1, helpers)]
+
+    block = jax.ShapeDtypeStruct((rank, width), F32)
+    sent = jax.ShapeDtypeStruct((rank, width), BF16)
+    sketch, regressor, *parts = pl.pallas_call(
         functools.partial(sketch_kernel, helpers),
-        out_shape=[jax.ShapeDtypeStruct((rank, own_points), F32), kept, kept],
+        out_shape=[jax.ShapeDtypeStruct((rank, own_points), F32), block, block] + [sent] * (helpers - 2),
         compiler_params=PARAMS,
         name="sketch",
-    )(mark, resident, points, scaled, swap(scaled, "help", 1))
-    regressor, others, _ = gather_to_owner(keep, passed, rank, helpers)
-    for part in others:
-        regressor = regressor + part.astype(F32)
+    )(mark, resident, points, *scaled)
+    for d, part in enumerate(parts, 1):
+        regressor = regressor + swap(part, "help", d).astype(F32)
     return sketch, regressor[None]
 
 

time: 61.4 us -> 53.8 us (0.88)
  waiting for transfers between devices: 27.3 us -> 21.8 us
  starting transfers between devices: 21.4 us -> 19.9 us
  other arithmetic: 2.28 us -> 1.38 us
    ppermute x14 -> x16, waiting for transfers between devices: 27.3 us -> 18.9 us  [swap(): lax.ppermute(value, axis, [(i, i ^ d) for i in range(lax.axis_size(axis))])]
    ppermute x1, starting transfers between devices: 2.86 us -> 0.08 us  [shards(): near = gate(lax.ppermute(packed, axes, one), mine)]
    ppermute x1, waiting for transfers between devices: 0.01 us -> 2.21 us  [shards(): across = lax.ppermute(near, axes, two)]
    ppermute x14 -> x16, starting transfers between devices: 14.9 us -> 16.6 us  [swap(): lax.ppermute(value, axis, [(i, i ^ d) for i in range(lax.axis_size(axis))])]
    add x2 -> x0, other arithmetic: 0.97 us -> none  [gather_to_owner(): both = keep + swap(passed, 'help', 1)]
    unnamed x16, local copies, waits for them, and re-layouts: 1.79 us -> 2.71 us
    concatenate x2 -> x1, other arithmetic: 0.02 us -> 0.7 us  [shards(): jnp.concatenate([lifter] + [swap(lifter, 'shard', INNER * d) for d in ran...]
    ppermute x1, waiting for transfers between devices: 0.01 us -> 0.68 us  [shards(): far = lax.ppermute(packed, axes, two)]
  transfers between devices with their start and end apart: 17 -> 19, of which waited for: 13 -> 15; matrix products, arithmetic and copies ran while one was open for 1% -> 1% of each run, Pallas kernels for 3% -> 3%
where the time goes in v4:
time: 53.8 us; the launch traced here: 53.6 us
  waiting for transfers between devices  21.8 us (41%)
  starting transfers between devices  19.9 us (37%)
  Pallas kernels  7.09 us (13%)
  local copies, waits for them, and re-layouts  2.71 us (5%)
  other arithmetic  1.38 us (3%)
  between operations  0.74 us (1%)
    ppermute x16, waiting for transfers between devices, swap(): lax.ppermute(value, axis, [(i, i ^ d) for i in range(lax.axis_size(axis))])  18.9 us
    ppermute x16, starting transfers between devices, swap(): lax.ppermute(value, axis, [(i, i ^ d) for i in range(lax.axis_size(axis))])  16.6 us
    pallas_call x1, Pallas kernels, shards(): pl.pallas_call(functools.partial(lift_kernel, helpers), out_shape=[jax.Sh...  2.81 us
    unnamed x16, local copies, waits for them, and re-layouts  2.71 us
    ppermute x1, waiting for transfers between devices, shards(): across = lax.ppermute(near, axes, two)  2.21 us
    pallas_call x1, Pallas kernels, shards(): pl.pallas_call(functools.partial(score_kernel, planes, helpers, 3), out_s...  1.81 us
    ppermute x1, starting transfers between devices, shards(): far = lax.ppermute(packed, axes, two)  1.66 us
    pallas_call x1, Pallas kernels, shards(): pl.pallas_call(functools.partial(sketch_kernel, helpers), out_shape=[jax....  1.53 us
  transfers between devices with their start and end apart: 19, of which 15 were waited for; matrix products, arithmetic and copies ran while one was open for 1% of the time, Pallas kernels for 3%

profile of v4, /device:TPU:0, one launch (start us, length us, event | category | flops | bytes accessed | tf_op | source)
XLA Modules:
  0.0 53.6 jit_solution(9027600417155443563)
XLA Ops:
  0.6 2.8 %lift.1 = (bf16[1552,128]{1,0:T(8,128)(2,1)}, f32[64,768]{1,0:T(8,128)}, f32[64,768]{1,0:T(8,128)}, s32[1,1024]{1,0:T(1,128)}, f32[8,128]{1,0:T(8,128)}) custom-call(bf16[256,768]{1,0:T(8,128)(2,1)} %refs_0_.1, s32[2,256]{1,0:T(2,128)} %bitcast.4, s32[2,256]{1,0:T(2,128)} %bitcast.5, s32[1,4096]{1,0:T(1,128)} %refs_3_.1, bf16[32,1024]{1,0:T(8,128)(2,1)} %refs_4_.1, ...), custom_call_target="tpu_custom_call" | custom-call | tf_op jit(solution)/shard_map/lift/pallas_call | solution.py:216
  3.4 0.5 collective-permute-start
  4.0 1.3 %collective-permute-done.got_ref = f32[64,768]{1,0:T(8,128)S(1)} collective-permute-done((f32[64,768]{1,0:T(8,128)}, f32[64,768]{1,0:T(8,128)S(1)}, u32[]{:S(2)}, u32[]{:S(2)}) %collective-permute-start) | collective-permute-done | bytes 196640 | tf_op jit(solution)/shard_map/ppermute | solution.py:204
  5.2 0.0 copy-start.5
  5.2 0.9 %copy-done.5 = f32[64,768]{1,0:T(8,128)S(1)} copy-done((f32[64,768]{1,0:T(8,128)S(1)}, f32[64,768]{1,0:T(8,128)}, u32[]{:S(2)}) %copy-start.5) | copy-done | bytes 196632
  6.2 2.9 %collective-permute-start.1 = (bf16[32,768]{1,0:T(8,128)(2,1)S(1)}, bf16[32,768]{1,0:T(8,128)(2,1)S(1)}, u32[]{:S(2)}, u32[]{:S(2)}) collective-permute-start(bf16[32,768]{1,0:T(8,128)(2,1)S(1)} %get-tuple-element.25), channel_id=1, source_target_pairs={{0,2},{1,3},{2,0},{3,1},{4,6},{5,7},{6,4},{7,5},{8,10},{9,11},{10,... | collective-permute-start | bytes 147464 | tf_op jit(solution)/shard_map/ppermute | solution.py:204
  9.1 0.1 collective-permute-start.6
  9.2 2.0 %collective-permute-done.1 = bf16[32,768]{1,0:T(8,128)(2,1)S(1)} collective-permute-done((bf16[32,768]{1,0:T(8,128)(2,1)S(1)}, bf16[32,768]{1,0:T(8,128)(2,1)S(1)}, u32[]{:S(2)}, u32[]{:S(2)}) %collective-permute-start.1) | collective-permute-done | bytes 49184 | tf_op jit(solution)/shard_map/ppermute | solution.py:204
  11.2 4.2 %collective-permute-start.4 = (bf16[32,768]{1,0:T(8,128)(2,1)S(1)}, bf16[32,768]{1,0:T(8,128)(2,1)S(1)}, u32[]{:S(2)}, u32[]{:S(2)}) collective-permute-start(bf16[32,768]{1,0:T(8,128)(2,1)S(1)} %add_convert_fusion), channel_id=1, source_target_pairs={{0,24},{4,28},{8,16},{12,20},{16,8},{20,12},{24,0},{28,4},{1,25},{... | collective-permute-start | bytes 147464 | tf_op jit(solution)/shard_map/ppermute | solution.py:204
  15.4 0.0 collective-permute-start.3
  15.4 0.6 %collective-permute-start.2 = (bf16[32,768]{1,0:T(8,128)(2,1)S(1)}, bf16[32,768]{1,0:T(8,128)(2,1)S(1)}, u32[]{:S(2)}, u32[]{:S(2)}) collective-permute-start(bf16[32,768]{1,0:T(8,128)(2,1)S(1)} %add_convert_fusion), channel_id=1, source_target_pairs={{0,8},{4,12},{8,0},{12,4},{16,24},{20,28},{24,16},{28,20},{1,9},{5... | collective-permute-start | bytes 147464 | tf_op jit(solution)/shard_map/ppermute | solution.py:204
  16.0 1.7 %collective-permute-start.8 = (bf16[1552,128]{1,0:T(8,128)(2,1)}, bf16[1552,128]{1,0:T(8,128)(2,1)S(1)}, u32[]{:S(2)}, u32[]{:S(2)}) collective-permute-start(bf16[1552,128]{1,0:T(8,128)(2,1)} %get-tuple-element.26.refs_0_), channel_id=1, source_target_pairs={{0,4},{1,3},{2,6},{3,1},{4,0},{5,7},{6,2},{7,5},{8,12},{9,11},{10,... | collective-permute-start | bytes 1191944 | tf_op jit(solution)/shard_map/ppermute | solution.py:253
  17.7 0.1 collective-permute-done.4
  17.8 2.6 %collective-permute-done.3 = bf16[32,768]{1,0:T(8,128)(2,1)S(1)} collective-permute-done((bf16[32,768]{1,0:T(8,128)(2,1)S(1)}, bf16[32,768]{1,0:T(8,128)(2,1)S(1)}, u32[]{:S(2)}, u32[]{:S(2)}) %collective-permute-start.3) | collective-permute-done | bytes 49184 | tf_op jit(solution)/shard_map/ppermute | solution.py:204
  20.4 0.0 collective-permute-done.2
  20.4 0.7 %pad_maximum_fusion.refs_1_.mine_ref = bf16[128,768]{1,0:T(8,128)(2,1)} fusion(bf16[32,768]{1,0:T(8,128)(2,1)S(1)} %collective-permute-done.4, bf16[32,768]{1,0:T(8,128)(2,1)S(1)} %collective-permute-done.3, bf16[32,768]{1,0:T(8,128)(2,1)S(1)} %collective-permute-done.2, bf16[32,768]{1,0:T(8,128)(2,1)S(1)} %add_convert_fusion), kind=kLoop, calls=%fused_computation | loop fusion | flops 786432 | bytes 393216 | tf_op jit(solution)/shard_map/concatenate | solution.py:247
  21.1 0.0 copy-start.1
  21.1 0.0 copy-start.2
  21.1 0.0 collective-permute-done.6.refs_0_
  21.1 0.0 copy-start.3
  21.1 0.8 %copy-done.3 = bf16[1552,128]{1,0:T(8,128)(2,1)} copy-done((bf16[1552,128]{1,0:T(8,128)(2,1)}, bf16[1552,128]{1,0:T(8,128)(2,1)S(1)}, u32[]{:S(2)}) %copy-start.3) | copy-done | bytes 397336
  21.9 1.5 %collective-permute-start.7 = (bf16[1552,128]{1,0:T(8,128)(2,1)}, bf16[1552,128]{1,0:T(8,128)(2,1)S(1)}, u32[]{:S(2)}, u32[]{:S(2)}) collective-permute-start(bf16[1552,128]{1,0:T(8,128)(2,1)} %gate.1.refs_1_), channel_id=1, source_target_pairs={{0,4},{1,3},{2,6},{3,1},{4,0},{5,7},{6,2},{7,5},{8,12},{9,11},{10,... | collective-permute-start | bytes 1191944 | tf_op jit(solution)/shard_map/ppermute | solution.py:255
  23.4 0.0 copy-done.1
  23.4 0.0 collective-permute-start.5
  23.4 0.7 %collective-permute-done.8.refs_2_ = bf16[1552,128]{1,0:T(8,128)(2,1)S(1)} collective-permute-done((bf16[1552,128]{1,0:T(8,128)(2,1)}, bf16[1552,128]{1,0:T(8,128)(2,1)S(1)}, u32[]{:S(2)}, u32[]{:S(2)}) %collective-permute-start.8) | collective-permute-done | bytes 397344 | tf_op jit(solution)/shard_map/ppermute | solution.py:253
  24.1 0.8 %collective-permute-done.5.theirs_ref = bf16[128,768]{1,0:T(8,128)(2,1)S(1)} collective-permute-done((bf16[128,768]{1,0:T(8,128)(2,1)S(1)}, bf16[128,768]{1,0:T(8,128)(2,1)S(1)}, u32[]{:S(2)}, u32[]{:S(2)}) %collective-permute-start.5) | collective-permute-done | bytes 196640 | tf_op jit(solution)/shard_map/ppermute | solution.py:204
  24.8 0.0 copy-done.2
  24.8 0.0 copy-start.4
  24.8 1.0 %copy-done.4 = bf16[1552,128]{1,0:T(8,128)(2,1)S(1)} copy-done((bf16[1552,128]{1,0:T(8,128)(2,1)S(1)}, bf16[1552,128]{1,0:T(8,128)(2,1)}, u32[]{:S(2)}) %copy-start.4) | copy-done | bytes 397336
  25.8 1.8 %score.1.refs_1_ = f32[256,896]{1,0:T(8,128)S(1)} custom-call(bf16[128,768]{1,0:T(8,128)(2,1)S(1)} %copy-done.1, bf16[128,768]{1,0:T(8,128)(2,1)S(1)} %collective-permute-done.5.theirs_ref, bf16[1552,128]{1,0:T(8,128)(2,1)S(1)} %copy-done.2, bf16[1552,128]{1,0:T(8,128)(2,1)S(1)} %copy-done.4, bf16[1552,128]{1,0:T(8,128)(2,1)S(1)} %collective-permute-done.8.refs_2_), custom_call_target="tpu_custom_call" | custom-call | tf_op jit(solution)/shard_map/score/pallas_call | solution.py:258
  27.7 0.0 copy-start.6
  27.7 0.0 copy-start
  27.7 0.0 copy-start.7
  27.7 2.2 %collective-permute-done.7.refs_0_ = bf16[1552,128]{1,0:T(8,128)(2,1)S(1)} collective-permute-done((bf16[1552,128]{1,0:T(8,128)(2,1)}, bf16[1552,128]{1,0:T(8,128)(2,1)S(1)}, u32[]{:S(2)}, u32[]{:S(2)}) %collective-permute-start.7) | collective-permute-done | bytes 397344 | tf_op jit(solution)/shard_map/ppermute | solution.py:255
  29.9 0.8 %score_last.1 = (f32[128,896]{1,0:T(8,128)S(1)}, f32[128,896]{1,0:T(8,128)S(1)}) custom-call(bf16[128,768]{1,0:T(8,128)(2,1)S(1)} %copy-done.1, bf16[128,768]{1,0:T(8,128)(2,1)S(1)} %collective-permute-done.5.theirs_ref, bf16[1552,128]{1,0:T(8,128)(2,1)S(1)} %collective-permute-done.7.refs_0_, f32[256,896]{1,0:T(8,128)S(1)} %score.1.refs_1_), custom_call_target="tpu_custom_call" | custom-call | tf_op jit(solution)/shard_map/score_last/pallas_call | solution.py:264
  30.7 0.1 collective-permute-start.9
  30.8 1.8 %collective-permute-done.9.theirs_ref = f32[128,896]{1,0:T(8,128)S(1)} collective-permute-done((f32[128,896]{1,0:T(8,128)S(1)}, f32[128,896]{1,0:T(8,128)S(1)}, u32[]{:S(2)}, u32[]{:S(2)}) %collective-permute-start.9) | collective-permute-done | bytes 458784 | tf_op jit(solution)/shard_map/ppermute | solution.py:204
  32.6 0.3 collective-permute-start.10
  32.9 2.5 %collective-permute-start.11 = (bf16[208,128]{1,0:T(8,128)(2,1)S(1)}, bf16[208,128]{1,0:T(8,128)(2,1)S(1)}, u32[]{:S(2)}, u32[]{:S(2)}) collective-permute-start(bf16[208,128]{1,0:T(8,128)(2,1)S(1)} %get-tuple-element.31), channel_id=1, source_target_pairs={{0,16},{4,20},{8,24},{12,28},{16,0},{20,4},{24,8},{28,12},{1,17},{... | collective-permute-start | bytes 159752 | tf_op jit(solution)/shard_map/ppermute | solution.py:204
  35.4 1.6 %collective-permute-start.12 = (bf16[208,128]{1,0:T(8,128)(2,1)S(1)}, bf16[208,128]{1,0:T(8,128)(2,1)S(1)}, u32[]{:S(2)}, u32[]{:S(2)}) collective-permute-start(bf16[208,128]{1,0:T(8,128)(2,1)S(1)} %get-tuple-element.32), channel_id=1, source_target_pairs={{0,24},{4,28},{8,16},{12,20},{16,8},{20,12},{24,0},{28,4},{1,25},{... | collective-permute-start | bytes 159752 | tf_op jit(solution)/shard_map/ppermute | solution.py:204
  37.1 0.6 %collective-permute-done.10.refs_0_ = bf16[208,128]{1,0:T(8,128)(2,1)S(1)} collective-permute-done((bf16[208,128]{1,0:T(8,128)(2,1)S(1)}, bf16[208,128]{1,0:T(8,128)(2,1)S(1)}, u32[]{:S(2)}, u32[]{:S(2)}) %collective-permute-start.10) | collective-permute-done | bytes 53280 | tf_op jit(solution)/shard_map/ppermute | solution.py:204
  37.7 0.9 %collective-permute-done.11.refs_1_ = bf16[208,128]{1,0:T(8,128)(2,1)S(1)} collective-permute-done((bf16[208,128]{1,0:T(8,128)(2,1)S(1)}, bf16[208,128]{1,0:T(8,128)(2,1)S(1)}, u32[]{:S(2)}, u32[]{:S(2)}) %collective-permute-start.11) | collective-permute-done | bytes 53280 | tf_op jit(solution)/shard_map/ppermute | solution.py:204
  38.6 2.8 %collective-permute-done.12.refs_2_ = bf16[208,128]{1,0:T(8,128)(2,1)S(1)} collective-permute-done((bf16[208,128]{1,0:T(8,128)(2,1)S(1)}, bf16[208,128]{1,0:T(8,128)(2,1)S(1)}, u32[]{:S(2)}, u32[]{:S(2)}) %collective-permute-start.12) | collective-permute-done | bytes 53280 | tf_op jit(solution)/shard_map/ppermute | solution.py:204
  41.4 0.0 copy-done.6
  41.4 0.1 scale.1.refs_0_
  41.5 0.1 collective-permute-start.15
  41.5 1.6 %collective-permute-start.14 = (bf16[32,768]{1,0:T(8,128)(2,1)S(1)}, bf16[32,768]{1,0:T(8,128)(2,1)S(1)}, u32[]{:S(2)}, u32[]{:S(2)}) collective-permute-start(bf16[32,768]{1,0:T(8,128)(2,1)S(1)} %scale.1.refs_0_), channel_id=1, source_target_pairs={{0,2},{1,3},{2,0},{3,1},{4,6},{5,7},{6,4},{7,5},{8,10},{9,11},{10,... | collective-permute-start | bytes 147464 | tf_op jit(solution)/shard_map/ppermute | solution.py:204
  43.1 0.3 collective-permute-start.13
  43.4 2.1 %collective-permute-done.15.refs_3_ = bf16[32,768]{1,0:T(8,128)(2,1)S(1)} collective-permute-done((bf16[32,768]{1,0:T(8,128)(2,1)S(1)}, bf16[32,768]{1,0:T(8,128)(2,1)S(1)}, u32[]{:S(2)}, u32[]{:S(2)}) %collective-permute-start.15) | collective-permute-done | bytes 49184 | tf_op jit(solution)/shard_map/ppermute | solution.py:204
  45.5 0.9 %collective-permute-done.14.refs_2_ = bf16[32,768]{1,0:T(8,128)(2,1)S(1)} collective-permute-done((bf16[32,768]{1,0:T(8,128)(2,1)S(1)}, bf16[32,768]{1,0:T(8,128)(2,1)S(1)}, u32[]{:S(2)}, u32[]{:S(2)}) %collective-permute-start.14) | collective-permute-done | bytes 49184 | tf_op jit(solution)/shard_map/ppermute | solution.py:204
  46.4 0.0 collective-permute-done.13.refs_1_
  46.4 0.0 copy-done
  46.5 0.0 copy-done.7
  46.5 1.5 %sketch.1 = (f32[32,1024]{1,0:T(8,128)}, f32[32,768]{1,0:T(8,128)S(1)}, f32[32,768]{1,0:T(8,128)S(1)}, bf16[32,768]{1,0:T(8,128)(2,1)S(1)}, bf16[32,768]{1,0:T(8,128)(2,1)S(1)}) custom-call(s32[1,1024]{1,0:T(1,128)S(1)} %copy-done.7, f32[8,128]{1,0:T(8,128)S(1)} %copy-done.6, bf16[1024,768]{1,0:T(8,128)(2,1)S(1)} %copy-done, ...), custom_call_target="tpu_custom_call" | custom-call | tf_op jit(solution)/shard_map/sketch/pallas_call | solution.py:289
  48.0 0.1 collective-permute-start.16
  48.1 1.1 %collective-permute-start.17 = (bf16[32,768]{1,0:T(8,128)(2,1)S(1)}, bf16[32,768]{1,0:T(8,128)(2,1)S(1)}, u32[]{:S(2)}, u32[]{:S(2)}) collective-permute-start(bf16[32,768]{1,0:T(8,128)(2,1)S(1)} %get-tuple-element.36), channel_id=1, source_target_pairs={{0,2},{1,3},{2,0},{3,1},{4,6},{5,7},{6,4},{7,5},{8,10},{9,11},{10,... | collective-permute-start | bytes 147464 | tf_op jit(solution)/shard_map/ppermute | solution.py:204
  49.2 0.7 %collective-permute-start.18 = (bf16[32,768]{1,0:T(8,128)(2,1)S(1)}, bf16[32,768]{1,0:T(8,128)(2,1)S(1)}, u32[]{:S(2)}, u32[]{:S(2)}) collective-permute-start(bf16[32,768]{1,0:T(8,128)(2,1)S(1)} %get-tuple-element.37), channel_id=1, source_target_pairs={{0,3},{1,2},{2,1},{3,0},{4,7},{5,6},{6,5},{7,4},{8,11},{9,10},{10,... | collective-permute-start | bytes 147464 | tf_op jit(solution)/shard_map/ppermute | solution.py:204
  49.9 2.4 %collective-permute-done.17 = bf16[32,768]{1,0:T(8,128)(2,1)S(1)} collective-permute-done((bf16[32,768]{1,0:T(8,128)(2,1)S(1)}, bf16[32,768]{1,0:T(8,128)(2,1)S(1)}, u32[]{:S(2)}, u32[]{:S(2)}) %collective-permute-start.17) | collective-permute-done | bytes 49184 | tf_op jit(solution)/shard_map/ppermute | solution.py:204
  52.3 0.6 %collective-permute-done.18 = bf16[32,768]{1,0:T(8,128)(2,1)S(1)} collective-permute-done((bf16[32,768]{1,0:T(8,128)(2,1)S(1)}, bf16[32,768]{1,0:T(8,128)(2,1)S(1)}, u32[]{:S(2)}, u32[]{:S(2)}) %collective-permute-start.18) | collective-permute-done | bytes 49184 | tf_op jit(solution)/shard_map/ppermute | solution.py:204
  52.9 0.0 collective-permute-done.16
  52.9 0.7 %add_bitcast_fusion = f32[1,32,768]{2,1,0:T(8,128)} fusion(bf16[32,768]{1,0:T(8,128)(2,1)S(1)} %collective-permute-done.18, bf16[32,768]{1,0:T(8,128)(2,1)S(1)} %collective-permute-done.17, f32[32,768]{1,0:T(8,128)S(1)} %get-tuple-element.34, f32[32,768]{1,0:T(8,128)S(1)} %collective-permute-done.16), kind=kLoop, calls=%fused_computation.1 | loop fusion | flops 122880 | bytes 393216 | tf_op jit(solution)/shard_map/broadcast_in_dim | solution.py:297
  (4 shorter events, 0.1 us)
Async XLA Ops:
  3.4 1.8 %collective-permute-start = (f32[64,768]{1,0:T(8,128)}, f32[64,768]{1,0:T(8,128)S(1)}, u32[]{:S(2)}, u32[]{:S(2)}) collective-permute-start(f32[64,768]{1,0:T(8,128)} %get-tuple-element.23), channel_id=1, source_target_pairs={{0,1},{1,0},{2,3},{3,2},{4,5},{5,4},{6,7},{7,6},{8,9},{9,8},{10,11... | collective-permute-start | bytes 589832 | tf_op jit(solution)/shard_map/ppermute | solution.py:204
  5.2 0.9 %copy-start.5 = (f32[64,768]{1,0:T(8,128)S(1)}, f32[64,768]{1,0:T(8,128)}, u32[]{:S(2)}) copy-start(f32[64,768]{1,0:T(8,128)} %get-tuple-element.22.keep_ref) | copy-start | bytes 589828
  6.2 5.0 %collective-permute-start.1 = (bf16[32,768]{1,0:T(8,128)(2,1)S(1)}, bf16[32,768]{1,0:T(8,128)(2,1)S(1)}, u32[]{:S(2)}, u32[]{:S(2)}) collective-permute-start(bf16[32,768]{1,0:T(8,128)(2,1)S(1)} %get-tuple-element.25), channel_id=1, source_target_pairs={{0,2},{1,3},{2,0},{3,1},{4,6},{5,7},{6,4},{7,5},{8,10},{9,11},{10,... | collective-permute-start | bytes 147464 | tf_op jit(solution)/shard_map/ppermute | solution.py:204
  9.1 12.0 %collective-permute-start.6 = (bf16[1552,128]{1,0:T(8,128)(2,1)}, bf16[1552,128]{1,0:T(8,128)(2,1)S(1)}, u32[]{:S(2)}, u32[]{:S(2)}) collective-permute-start(bf16[1552,128]{1,0:T(8,128)(2,1)} %get-tuple-element.26.refs_0_), channel_id=1, source_target_pairs={{0,2},{1,5},{2,0},{3,7},{4,6},{5,1},{6,4},{7,3},{8,10},{9,13},{10,... | collective-permute-start | bytes 1191944 | tf_op jit(solution)/shard_map/ppermute | solution.py:254
  11.2 6.6 %collective-permute-start.4 = (bf16[32,768]{1,0:T(8,128)(2,1)S(1)}, bf16[32,768]{1,0:T(8,128)(2,1)S(1)}, u32[]{:S(2)}, u32[]{:S(2)}) collective-permute-start(bf16[32,768]{1,0:T(8,128)(2,1)S(1)} %add_convert_fusion), channel_id=1, source_target_pairs={{0,24},{4,28},{8,16},{12,20},{16,8},{20,12},{24,0},{28,4},{1,25},{... | collective-permute-start | bytes 147464 | tf_op jit(solution)/shard_map/ppermute | solution.py:204
  15.4 5.0 %collective-permute-start.3 = (bf16[32,768]{1,0:T(8,128)(2,1)S(1)}, bf16[32,768]{1,0:T(8,128)(2,1)S(1)}, u32[]{:S(2)}, u32[]{:S(2)}) collective-permute-start(bf16[32,768]{1,0:T(8,128)(2,1)S(1)} %add_convert_fusion), channel_id=1, source_target_pairs={{0,16},{4,20},{8,24},{12,28},{16,0},{20,4},{24,8},{28,12},{1,17},{... | collective-permute-start | bytes 147464 | tf_op jit(solution)/shard_map/ppermute | solution.py:204
  15.4 5.0 %collective-permute-start.2 = (bf16[32,768]{1,0:T(8,128)(2,1)S(1)}, bf16[32,768]{1,0:T(8,128)(2,1)S(1)}, u32[]{:S(2)}, u32[]{:S(2)}) collective-permute-start(bf16[32,768]{1,0:T(8,128)(2,1)S(1)} %add_convert_fusion), channel_id=1, source_target_pairs={{0,8},{4,12},{8,0},{12,4},{16,24},{20,28},{24,16},{28,20},{1,9},{5... | collective-permute-start | bytes 147464 | tf_op jit(solution)/shard_map/ppermute | solution.py:204
  16.0 8.0 %collective-permute-start.8 = (bf16[1552,128]{1,0:T(8,128)(2,1)}, bf16[1552,128]{1,0:T(8,128)(2,1)S(1)}, u32[]{:S(2)}, u32[]{:S(2)}) collective-permute-start(bf16[1552,128]{1,0:T(8,128)(2,1)} %get-tuple-element.26.refs_0_), channel_id=1, source_target_pairs={{0,4},{1,3},{2,6},{3,1},{4,0},{5,7},{6,2},{7,5},{8,12},{9,11},{10,... | collective-permute-start | bytes 1191944 | tf_op jit(solution)/shard_map/ppermute | solution.py:253
  21.1 2.3 %copy-start.1 = (bf16[128,768]{1,0:T(8,128)(2,1)S(1)}, bf16[128,768]{1,0:T(8,128)(2,1)}, u32[]{:S(2)}) copy-start(bf16[128,768]{1,0:T(8,128)(2,1)} %pad_maximum_fusion.refs_1_.mine_ref) | copy-start | bytes 589828
  21.1 3.7 %copy-start.2 = (bf16[1552,128]{1,0:T(8,128)(2,1)S(1)}, bf16[1552,128]{1,0:T(8,128)(2,1)}, u32[]{:S(2)}) copy-start(bf16[1552,128]{1,0:T(8,128)(2,1)} %get-tuple-element.26.refs_0_) | copy-start | bytes 1191940
  21.1 0.8 %copy-start.3 = (bf16[1552,128]{1,0:T(8,128)(2,1)}, bf16[1552,128]{1,0:T(8,128)(2,1)S(1)}, u32[]{:S(2)}) copy-start(bf16[1552,128]{1,0:T(8,128)(2,1)S(1)} %collective-permute-done.6.refs_0_) | copy-start | bytes 1191940
  21.9 8.0 %collective-permute-start.7 = (bf16[1552,128]{1,0:T(8,128)(2,1)}, bf16[1552,128]{1,0:T(8,128)(2,1)S(1)}, u32[]{:S(2)}, u32[]{:S(2)}) collective-permute-start(bf16[1552,128]{1,0:T(8,128)(2,1)} %gate.1.refs_1_), channel_id=1, source_target_pairs={{0,4},{1,3},{2,6},{3,1},{4,0},{5,7},{6,2},{7,5},{8,12},{9,11},{10,... | collective-permute-start | bytes 1191944 | tf_op jit(solution)/shard_map/ppermute | solution.py:255
  23.4 1.4 %collective-permute-start.5 = (bf16[128,768]{1,0:T(8,128)(2,1)S(1)}, bf16[128,768]{1,0:T(8,128)(2,1)S(1)}, u32[]{:S(2)}, u32[]{:S(2)}) collective-permute-start(bf16[128,768]{1,0:T(8,128)(2,1)S(1)} %copy-done.1), channel_id=1, source_target_pairs={{0,1},{1,0},{2,3},{3,2},{4,5},{5,4},{6,7},{7,6},{8,9},{9,8},{10,11... | collective-permute-start | bytes 589832 | tf_op jit(solution)/shard_map/ppermute | solution.py:204
  24.8 1.0 %copy-start.4 = (bf16[1552,128]{1,0:T(8,128)(2,1)S(1)}, bf16[1552,128]{1,0:T(8,128)(2,1)}, u32[]{:S(2)}) copy-start(bf16[1552,128]{1,0:T(8,128)(2,1)} %gate.1.refs_1_) | copy-start | bytes 1191940
  27.7 13.7 %copy-start.6 = (f32[8,128]{1,0:T(8,128)S(1)}, f32[8,128]{1,0:T(8,128)}, u32[]{:S(2)}) copy-start(f32[8,128]{1,0:T(8,128)} %get-tuple-element.21.resident_ref) | copy-start | bytes 12292
  27.7 18.8 %copy-start = (bf16[1024,768]{1,0:T(8,128)(2,1)S(1)}, bf16[1024,768]{1,0:T(8,128)(2,1)}, u32[]{:S(2)}) copy-start(bf16[1024,768]{1,0:T(8,128)(2,1)} %points_ref.1) | copy-start | bytes 4718596
  27.7 18.8 %copy-start.7 = (s32[1,1024]{1,0:T(1,128)S(1)}, s32[1,1024]{1,0:T(1,128)}, u32[]{:S(2)}) copy-start(s32[1,1024]{1,0:T(1,128)} %get-tuple-element.20.mark_ref) | copy-start | bytes 12292
  30.7 1.9 %collective-permute-start.9 = (f32[128,896]{1,0:T(8,128)S(1)}, f32[128,896]{1,0:T(8,128)S(1)}, u32[]{:S(2)}, u32[]{:S(2)}) collective-permute-start(f32[128,896]{1,0:T(8,128)S(1)} %get-tuple-element.28), channel_id=1, source_target_pairs={{0,1},{1,0},{2,3},{3,2},{4,5},{5,4},{6,7},{7,6},{8,9},{9,8},{10,11... | collective-permute-start | bytes 1376264 | tf_op jit(solution)/shard_map/ppermute | solution.py:204
  32.6 5.0 %collective-permute-start.10 = (bf16[208,128]{1,0:T(8,128)(2,1)S(1)}, bf16[208,128]{1,0:T(8,128)(2,1)S(1)}, u32[]{:S(2)}, u32[]{:S(2)}) collective-permute-start(bf16[208,128]{1,0:T(8,128)(2,1)S(1)} %get-tuple-element.30), channel_id=1, source_target_pairs={{0,8},{4,12},{8,0},{12,4},{16,24},{20,28},{24,16},{28,20},{1,9},{5... | collective-permute-start | bytes 159752 | tf_op jit(solution)/shard_map/ppermute | solution.py:204
  32.9 5.7 %collective-permute-start.11 = (bf16[208,128]{1,0:T(8,128)(2,1)S(1)}, bf16[208,128]{1,0:T(8,128)(2,1)S(1)}, u32[]{:S(2)}, u32[]{:S(2)}) collective-permute-start(bf16[208,128]{1,0:T(8,128)(2,1)S(1)} %get-tuple-element.31), channel_id=1, source_target_pairs={{0,16},{4,20},{8,24},{12,28},{16,0},{20,4},{24,8},{28,12},{1,17},{... | collective-permute-start | bytes 159752 | tf_op jit(solution)/shard_map/ppermute | solution.py:204
  35.4 5.9 %collective-permute-start.12 = (bf16[208,128]{1,0:T(8,128)(2,1)S(1)}, bf16[208,128]{1,0:T(8,128)(2,1)S(1)}, u32[]{:S(2)}, u32[]{:S(2)}) collective-permute-start(bf16[208,128]{1,0:T(8,128)(2,1)S(1)} %get-tuple-element.32), channel_id=1, source_target_pairs={{0,24},{4,28},{8,16},{12,20},{16,8},{20,12},{24,0},{28,4},{1,25},{... | collective-permute-start | bytes 159752 | tf_op jit(solution)/shard_map/ppermute | solution.py:204
  41.5 4.1 %collective-permute-start.15 = (bf16[32,768]{1,0:T(8,128)(2,1)S(1)}, bf16[32,768]{1,0:T(8,128)(2,1)S(1)}, u32[]{:S(2)}, u32[]{:S(2)}) collective-permute-start(bf16[32,768]{1,0:T(8,128)(2,1)S(1)} %scale.1.refs_0_), channel_id=1, source_target_pairs={{0,3},{1,2},{2,1},{3,0},{4,7},{5,6},{6,5},{7,4},{8,11},{9,10},{10,... | collective-permute-start | bytes 147464 | tf_op jit(solution)/shard_map/ppermute | solution.py:204
  41.5 4.9 %collective-permute-start.14 = (bf16[32,768]{1,0:T(8,128)(2,1)S(1)}, bf16[32,768]{1,0:T(8,128)(2,1)S(1)}, u32[]{:S(2)}, u32[]{:S(2)}) collective-permute-start(bf16[32,768]{1,0:T(8,128)(2,1)S(1)} %scale.1.refs_0_), channel_id=1, source_target_pairs={{0,2},{1,3},{2,0},{3,1},{4,6},{5,7},{6,4},{7,5},{8,10},{9,11},{10,... | collective-permute-start | bytes 147464 | tf_op jit(solution)/shard_map/ppermute | solution.py:204
  43.1 3.3 %collective-permute-start.13 = (bf16[32,768]{1,0:T(8,128)(2,1)S(1)}, bf16[32,768]{1,0:T(8,128)(2,1)S(1)}, u32[]{:S(2)}, u32[]{:S(2)}) collective-permute-start(bf16[32,768]{1,0:T(8,128)(2,1)S(1)} %scale.1.refs_0_), channel_id=1, source_target_pairs={{0,1},{1,0},{2,3},{3,2},{4,5},{5,4},{6,7},{7,6},{8,9},{9,8},{10,11... | collective-permute-start | bytes 147464 | tf_op jit(solution)/shard_map/ppermute | solution.py:204
  48.0 4.9 %collective-permute-start.16 = (f32[32,768]{1,0:T(8,128)S(1)}, f32[32,768]{1,0:T(8,128)S(1)}, u32[]{:S(2)}, u32[]{:S(2)}) collective-permute-start(f32[32,768]{1,0:T(8,128)S(1)} %get-tuple-element.35), channel_id=1, source_target_pairs={{0,1},{1,0},{2,3},{3,2},{4,5},{5,4},{6,7},{7,6},{8,9},{9,8},{10,11... | collective-permute-start | bytes 294920 | tf_op jit(solution)/shard_map/ppermute | solution.py:204
  48.1 4.2 %collective-permute-start.17 = (bf16[32,768]{1,0:T(8,128)(2,1)S(1)}, bf16[32,768]{1,0:T(8,128)(2,1)S(1)}, u32[]{:S(2)}, u32[]{:S(2)}) collective-permute-start(bf16[32,768]{1,0:T(8,128)(2,1)S(1)} %get-tuple-element.36), channel_id=1, source_target_pairs={{0,2},{1,3},{2,0},{3,1},{4,6},{5,7},{6,4},{7,5},{8,10},{9,11},{10,... | collective-permute-start | bytes 147464 | tf_op jit(solution)/shard_map/ppermute | solution.py:204
  49.2 3.7 %collective-permute-start.18 = (bf16[32,768]{1,0:T(8,128)(2,1)S(1)}, bf16[32,768]{1,0:T(8,128)(2,1)S(1)}, u32[]{:S(2)}, u32[]{:S(2)}) collective-permute-start(bf16[32,768]{1,0:T(8,128)(2,1)S(1)} %get-tuple-element.37), channel_id=1, source_target_pairs={{0,3},{1,2},{2,1},{3,0},{4,7},{5,6},{6,5},{7,4},{8,11},{9,10},{10,... | collective-permute-start | bytes 147464 | tf_op jit(solution)/shard_map/ppermute | solution.py:204

commit v5 on v4

--- a/solution.py
+++ b/solution.py
@@ -95,16 +95,16 @@
     pass
 
 
-def gate(value, *others):
+def gate(values, *others):
     return pl.pallas_call(
         gate_kernel,
-        out_shape=jax.ShapeDtypeStruct(value.shape, value.dtype),
-        in_specs=[ANY] * (1 + len(others)),
-        out_specs=ANY,
-        input_output_aliases={0: 0},
-        cost_estimate=pl.CostEstimate(flops=10**10, bytes_accessed=10**7, transcendentals=0),
+        out_shape=[jax.ShapeDtypeStruct(value.shape, value.dtype) for value in values],
+        in_specs=[ANY] * (len(values) + len(others)),
+        out_specs=[ANY] * len(values),
+        input_output_aliases={k: k for k in range(len(values))},
+        compiler_params=pltpu.CompilerParams(vmem_limit_bytes=1 << 20),
         name="gate",
-    )(value, *others)
+    )(*values, *others)
 
 
 def score_kernel(planes, helpers, blocks, mine_ref, theirs_ref, *refs):
@@ -250,8 +250,7 @@
     index, axes = range(groups * helpers), ("shard", "help")
     one = [(i, i ^ (2 if i % 2 == 0 else helpers)) for i in index]
     two = [(i, i ^ (helpers if i % 2 == 0 else 2)) for i in index]
-    far = lax.ppermute(packed, axes, two)
-    near = gate(lax.ppermute(packed, axes, one), mine)
+    near, far = gate([lax.ppermute(packed, axes, turn) for turn in (one, two)], mine)
     across = lax.ppermute(near, axes, two)
 
     wide = width + LANES

time: 53.8 us -> 53.7 us (level)
  waiting for transfers between devices: 21.8 us -> 23.7 us
  local copies, waits for them, and re-layouts: 2.71 us -> 0.95 us
  other arithmetic: 1.38 us -> 0.69 us
    ppermute x16, waiting for transfers between devices: 18.9 us -> 20.8 us  [swap(): lax.ppermute(value, axis, [(i, i ^ d) for i in range(lax.axis_size(axis))])]
    unnamed x16 -> x10, local copies, waits for them, and re-layouts: 2.71 us -> 0.95 us
    ppermute x1, waiting for transfers between devices: 2.21 us -> 2.96 us  [shards(): across = lax.ppermute(near, axes, two)]
    concatenate x1, other arithmetic: 0.7 us -> 0.01 us  [shards(): jnp.concatenate([lifter] + [swap(lifter, 'shard', INNER * d) for d in ran...]
    ppermute x2, waiting for transfers between devices: 0.68 us -> 0.01 us  [shards(): lax.ppermute(packed, axes, turn)]
  transfers between devices with their start and end apart: 19 -> 19, of which waited for: 15 -> 13; matrix products, arithmetic and copies ran while one was open for 1% -> 0% of each run, Pallas kernels for 3% -> 3%
where the time goes in v5:
time: 53.7 us; the launch traced here: 53.5 us
  waiting for transfers between devices  23.7 us (44%)
  starting transfers between devices  20.2 us (38%)
  Pallas kernels  7.12 us (13%)
  local copies, waits for them, and re-layouts  0.95 us (2%)
  between operations  0.76 us (1%)
  other arithmetic  0.69 us (1%)
    ppermute x16, waiting for transfers between devices, swap(): lax.ppermute(value, axis, [(i, i ^ d) for i in range(lax.axis_size(axis))])  20.8 us
    ppermute x16, starting transfers between devices, swap(): lax.ppermute(value, axis, [(i, i ^ d) for i in range(lax.axis_size(axis))])  16.5 us
    ppermute x1, waiting for transfers between devices, shards(): across = lax.ppermute(near, axes, two)  2.96 us
    pallas_call x1, Pallas kernels, shards(): pl.pallas_call(functools.partial(lift_kernel, helpers), out_shape=[jax.Sh...  2.82 us
    ppermute x2, starting transfers between devices, shards(): lax.ppermute(packed, axes, turn)  2.05 us
    pallas_call x1, Pallas kernels, shards(): pl.pallas_call(functools.partial(score_kernel, planes, helpers, 3), out_s...  1.81 us
    ppermute x1, starting transfers between devices, shards(): across = lax.ppermute(near, axes, two)  1.63 us
    pallas_call x1, Pallas kernels, shards(): pl.pallas_call(functools.partial(sketch_kernel, helpers), out_shape=[jax....  1.52 us
  transfers between devices with their start and end apart: 19, of which 13 were waited for; matrix products, arithmetic and copies ran while one was open for 0% of the time, Pallas kernels for 3%

profile of v5, /device:TPU:0, one launch (start us, length us, event | category | flops | bytes accessed | tf_op | source)
XLA Modules:
  0.0 53.5 jit_solution(17305167879672356874)
XLA Ops:
  0.6 2.8 %lift.1 = (bf16[1552,128]{1,0:T(8,128)(2,1)}, f32[64,768]{1,0:T(8,128)}, f32[64,768]{1,0:T(8,128)}, s32[1,1024]{1,0:T(1,128)}, f32[8,128]{1,0:T(8,128)}) custom-call(bf16[256,768]{1,0:T(8,128)(2,1)} %refs_0_.1, s32[2,256]{1,0:T(2,128)} %bitcast.4, s32[2,256]{1,0:T(2,128)} %bitcast.5, s32[1,4096]{1,0:T(1,128)} %refs_3_.1, bf16[32,1024]{1,0:T(8,128)(2,1)} %refs_4_.1, ...), custom_call_target="tpu_custom_call" | custom-call | tf_op jit(solution)/shard_map/lift/pallas_call | solution.py:216
  3.5 0.0 copy-start.1
  3.5 0.5 collective-permute-start
  4.0 1.3 %collective-permute-done.got_ref = f32[64,768]{1,0:T(8,128)S(1)} collective-permute-done((f32[64,768]{1,0:T(8,128)}, f32[64,768]{1,0:T(8,128)S(1)}, u32[]{:S(2)}, u32[]{:S(2)}) %collective-permute-start) | collective-permute-done | bytes 196640 | tf_op jit(solution)/shard_map/ppermute | solution.py:204
  5.3 0.0 copy-start.2
  5.3 0.9 %copy-done.2 = f32[64,768]{1,0:T(8,128)S(1)} copy-done((f32[64,768]{1,0:T(8,128)S(1)}, f32[64,768]{1,0:T(8,128)}, u32[]{:S(2)}) %copy-start.2) | copy-done | bytes 196632
  6.2 2.9 %collective-permute-start.1 = (bf16[32,768]{1,0:T(8,128)(2,1)S(1)}, bf16[32,768]{1,0:T(8,128)(2,1)S(1)}, u32[]{:S(2)}, u32[]{:S(2)}) collective-permute-start(bf16[32,768]{1,0:T(8,128)(2,1)S(1)} %get-tuple-element.27), channel_id=1, source_target_pairs={{0,2},{1,3},{2,0},{3,1},{4,6},{5,7},{6,4},{7,5},{8,10},{9,11},{10,... | collective-permute-start | bytes 147464 | tf_op jit(solution)/shard_map/ppermute | solution.py:204
  9.1 1.5 %collective-permute-start.7 = (bf16[1552,128]{1,0:T(8,128)(2,1)}, bf16[1552,128]{1,0:T(8,128)(2,1)S(1)}, u32[]{:S(2)}, u32[]{:S(2)}) collective-permute-start(bf16[1552,128]{1,0:T(8,128)(2,1)} %get-tuple-element.28.refs_0_), channel_id=1, source_target_pairs={{0,4},{1,3},{2,6},{3,1},{4,0},{5,7},{6,2},{7,5},{8,12},{9,11},{10,... | collective-permute-start | bytes 1191944 | tf_op jit(solution)/shard_map/ppermute | solution.py:253
  10.7 0.5 collective-permute-start.6
  11.2 0.1 collective-permute-done.1
  11.3 4.2 %collective-permute-start.4 = (bf16[32,768]{1,0:T(8,128)(2,1)S(1)}, bf16[32,768]{1,0:T(8,128)(2,1)S(1)}, u32[]{:S(2)}, u32[]{:S(2)}) collective-permute-start(bf16[32,768]{1,0:T(8,128)(2,1)S(1)} %add_convert_fusion), channel_id=1, source_target_pairs={{0,24},{4,28},{8,16},{12,20},{16,8},{20,12},{24,0},{28,4},{1,25},{... | collective-permute-start | bytes 147464 | tf_op jit(solution)/shard_map/ppermute | solution.py:204
  15.4 0.0 collective-permute-start.3
  15.4 0.6 %collective-permute-start.2 = (bf16[32,768]{1,0:T(8,128)(2,1)S(1)}, bf16[32,768]{1,0:T(8,128)(2,1)S(1)}, u32[]{:S(2)}, u32[]{:S(2)}) collective-permute-start(bf16[32,768]{1,0:T(8,128)(2,1)S(1)} %add_convert_fusion), channel_id=1, source_target_pairs={{0,8},{4,12},{8,0},{12,4},{16,24},{20,28},{24,16},{28,20},{1,9},{5... | collective-permute-start | bytes 147464 | tf_op jit(solution)/shard_map/ppermute | solution.py:204
  16.1 1.7 %collective-permute-done.4 = bf16[32,768]{1,0:T(8,128)(2,1)S(1)} collective-permute-done((bf16[32,768]{1,0:T(8,128)(2,1)S(1)}, bf16[32,768]{1,0:T(8,128)(2,1)S(1)}, u32[]{:S(2)}, u32[]{:S(2)}) %collective-permute-start.4) | collective-permute-done | bytes 49184 | tf_op jit(solution)/shard_map/ppermute | solution.py:204
  17.8 2.6 %collective-permute-done.3 = bf16[32,768]{1,0:T(8,128)(2,1)S(1)} collective-permute-done((bf16[32,768]{1,0:T(8,128)(2,1)S(1)}, bf16[32,768]{1,0:T(8,128)(2,1)S(1)}, u32[]{:S(2)}, u32[]{:S(2)}) %collective-permute-start.3) | collective-permute-done | bytes 49184 | tf_op jit(solution)/shard_map/ppermute | solution.py:204
  20.4 0.0 collective-permute-done.2
  20.4 0.0 collective-permute-done.7.refs_1_
  20.5 0.0 collective-permute-done.6.refs_0_
  20.5 1.6 %collective-permute-start.8 = (bf16[1552,128]{1,0:T(8,128)(2,1)S(1)}, bf16[1552,128]{1,0:T(8,128)(2,1)S(1)}, u32[]{:S(2)}, u32[]{:S(2)}) collective-permute-start(bf16[1552,128]{1,0:T(8,128)(2,1)S(1)} %get-tuple-element.29.refs_1_), channel_id=1, source_target_pairs={{0,4},{1,3},{2,6},{3,1},{4,0},{5,7},{6,2},{7,5},{8,12},{9,11},{10,... | collective-permute-start | bytes 1191944 | tf_op jit(solution)/shard_map/ppermute | solution.py:254
  22.1 0.0 collective-permute-start.5
  22.1 1.4 %collective-permute-done.5.theirs_ref = bf16[128,768]{1,0:T(8,128)(2,1)S(1)} collective-permute-done((bf16[128,768]{1,0:T(8,128)(2,1)S(1)}, bf16[128,768]{1,0:T(8,128)(2,1)S(1)}, u32[]{:S(2)}, u32[]{:S(2)}) %collective-permute-start.5) | collective-permute-done | bytes 196640 | tf_op jit(solution)/shard_map/ppermute | solution.py:204
  23.5 0.0 copy-done.1
  23.5 1.8 %score.1.refs_1_ = f32[256,896]{1,0:T(8,128)S(1)} custom-call(bf16[128,768]{1,0:T(8,128)(2,1)S(1)} %pad_maximum_fusion.refs_2_.mine_ref, bf16[128,768]{1,0:T(8,128)(2,1)S(1)} %collective-permute-done.5.theirs_ref, bf16[1552,128]{1,0:T(8,128)(2,1)S(1)} %copy-done.1, bf16[1552,128]{1,0:T(8,128)(2,1)S(1)} %get-tuple-element.29.refs_1_, ...), custom_call_target="tpu_custom_call" | custom-call | tf_op jit(solution)/shard_map/score/pallas_call | solution.py:257
  25.4 0.0 copy-start.3
  25.4 0.0 copy-start
  25.4 0.0 copy-start.4
  25.4 3.0 %collective-permute-done.8.refs_0_ = bf16[1552,128]{1,0:T(8,128)(2,1)S(1)} collective-permute-done((bf16[1552,128]{1,0:T(8,128)(2,1)S(1)}, bf16[1552,128]{1,0:T(8,128)(2,1)S(1)}, u32[]{:S(2)}, u32[]{:S(2)}) %collective-permute-start.8) | collective-permute-done | bytes 397344 | tf_op jit(solution)/shard_map/ppermute | solution.py:254
  28.4 0.8 %score_last.1 = (f32[128,896]{1,0:T(8,128)S(1)}, f32[128,896]{1,0:T(8,128)S(1)}) custom-call(bf16[128,768]{1,0:T(8,128)(2,1)S(1)} %pad_maximum_fusion.refs_2_.mine_ref, bf16[128,768]{1,0:T(8,128)(2,1)S(1)} %collective-permute-done.5.theirs_ref, bf16[1552,128]{1,0:T(8,128)(2,1)S(1)} %collective-permute-done.8.refs_0_, f32[256,896]{1,0:T(8,128)S(1)} %score.1.refs_1_), custom_call_target="tpu_custom_call" | custom-call | tf_op jit(solution)/shard_map/score_last/pallas_call | solution.py:263
  29.2 0.1 collective-permute-start.9
  29.2 1.8 %collective-permute-done.9.theirs_ref = f32[128,896]{1,0:T(8,128)S(1)} collective-permute-done((f32[128,896]{1,0:T(8,128)S(1)}, f32[128,896]{1,0:T(8,128)S(1)}, u32[]{:S(2)}, u32[]{:S(2)}) %collective-permute-start.9) | collective-permute-done | bytes 458784 | tf_op jit(solution)/shard_map/ppermute | solution.py:204
  31.1 0.1 fold.1
  31.1 1.7 %collective-permute-start.10 = (bf16[208,128]{1,0:T(8,128)(2,1)S(1)}, bf16[208,128]{1,0:T(8,128)(2,1)S(1)}, u32[]{:S(2)}, u32[]{:S(2)}) collective-permute-start(bf16[208,128]{1,0:T(8,128)(2,1)S(1)} %get-tuple-element.34), channel_id=1, source_target_pairs={{0,8},{4,12},{8,0},{12,4},{16,24},{20,28},{24,16},{28,20},{1,9},{5... | collective-permute-start | bytes 159752 | tf_op jit(solution)/shard_map/ppermute | solution.py:204
  32.8 2.6 %collective-permute-start.11 = (bf16[208,128]{1,0:T(8,128)(2,1)S(1)}, bf16[208,128]{1,0:T(8,128)(2,1)S(1)}, u32[]{:S(2)}, u32[]{:S(2)}) collective-permute-start(bf16[208,128]{1,0:T(8,128)(2,1)S(1)} %get-tuple-element.35), channel_id=1, source_target_pairs={{0,16},{4,20},{8,24},{12,28},{16,0},{20,4},{24,8},{28,12},{1,17},{... | collective-permute-start | bytes 159752 | tf_op jit(solution)/shard_map/ppermute | solution.py:204
  35.4 0.2 collective-permute-start.12
  35.6 0.0 collective-permute-done.10.refs_0_
  35.6 3.4 %collective-permute-done.11.refs_1_ = bf16[208,128]{1,0:T(8,128)(2,1)S(1)} collective-permute-done((bf16[208,128]{1,0:T(8,128)(2,1)S(1)}, bf16[208,128]{1,0:T(8,128)(2,1)S(1)}, u32[]{:S(2)}, u32[]{:S(2)}) %collective-permute-start.11) | collective-permute-done | bytes 53280 | tf_op jit(solution)/shard_map/ppermute | solution.py:204
  39.0 2.3 %collective-permute-done.12.refs_2_ = bf16[208,128]{1,0:T(8,128)(2,1)S(1)} collective-permute-done((bf16[208,128]{1,0:T(8,128)(2,1)S(1)}, bf16[208,128]{1,0:T(8,128)(2,1)S(1)}, u32[]{:S(2)}, u32[]{:S(2)}) %collective-permute-start.12) | collective-permute-done | bytes 53280 | tf_op jit(solution)/shard_map/ppermute | solution.py:204
  41.3 0.0 copy-done.3
  41.3 0.1 scale.1.refs_0_
  41.4 0.1 collective-permute-start.15
  41.5 1.4 %collective-permute-start.14 = (bf16[32,768]{1,0:T(8,128)(2,1)S(1)}, bf16[32,768]{1,0:T(8,128)(2,1)S(1)}, u32[]{:S(2)}, u32[]{:S(2)}) collective-permute-start(bf16[32,768]{1,0:T(8,128)(2,1)S(1)} %scale.1.refs_0_), channel_id=1, source_target_pairs={{0,2},{1,3},{2,0},{3,1},{4,6},{5,7},{6,4},{7,5},{8,10},{9,11},{10,... | collective-permute-start | bytes 147464 | tf_op jit(solution)/shard_map/ppermute | solution.py:204
  42.8 0.5 collective-permute-start.13
  43.3 2.2 %collective-permute-done.15.refs_3_ = bf16[32,768]{1,0:T(8,128)(2,1)S(1)} collective-permute-done((bf16[32,768]{1,0:T(8,128)(2,1)S(1)}, bf16[32,768]{1,0:T(8,128)(2,1)S(1)}, u32[]{:S(2)}, u32[]{:S(2)}) %collective-permute-start.15) | collective-permute-done | bytes 49184 | tf_op jit(solution)/shard_map/ppermute | solution.py:204
  45.5 0.7 %collective-permute-done.14.refs_2_ = bf16[32,768]{1,0:T(8,128)(2,1)S(1)} collective-permute-done((bf16[32,768]{1,0:T(8,128)(2,1)S(1)}, bf16[32,768]{1,0:T(8,128)(2,1)S(1)}, u32[]{:S(2)}, u32[]{:S(2)}) %collective-permute-start.14) | collective-permute-done | bytes 49184 | tf_op jit(solution)/shard_map/ppermute | solution.py:204
  46.3 0.0 collective-permute-done.13.refs_1_
  46.3 0.0 copy-done
  46.3 0.0 copy-done.4
  46.3 1.5 %sketch.1 = (f32[32,1024]{1,0:T(8,128)}, f32[32,768]{1,0:T(8,128)S(1)}, f32[32,768]{1,0:T(8,128)S(1)}, bf16[32,768]{1,0:T(8,128)(2,1)S(1)}, bf16[32,768]{1,0:T(8,128)(2,1)S(1)}) custom-call(s32[1,1024]{1,0:T(1,128)S(1)} %copy-done.4, f32[8,128]{1,0:T(8,128)S(1)} %copy-done.3, bf16[1024,768]{1,0:T(8,128)(2,1)S(1)} %copy-done, ...), custom_call_target="tpu_custom_call" | custom-call | tf_op jit(solution)/shard_map/sketch/pallas_call | solution.py:288
  47.8 0.1 collective-permute-start.16
  47.9 1.0 %collective-permute-start.17 = (bf16[32,768]{1,0:T(8,128)(2,1)S(1)}, bf16[32,768]{1,0:T(8,128)(2,1)S(1)}, u32[]{:S(2)}, u32[]{:S(2)}) collective-permute-start(bf16[32,768]{1,0:T(8,128)(2,1)S(1)} %get-tuple-element.40), channel_id=1, source_target_pairs={{0,2},{1,3},{2,0},{3,1},{4,6},{5,7},{6,4},{7,5},{8,10},{9,11},{10,... | collective-permute-start | bytes 147464 | tf_op jit(solution)/shard_map/ppermute | solution.py:204
  48.9 0.7 %collective-permute-start.18 = (bf16[32,768]{1,0:T(8,128)(2,1)S(1)}, bf16[32,768]{1,0:T(8,128)(2,1)S(1)}, u32[]{:S(2)}, u32[]{:S(2)}) collective-permute-start(bf16[32,768]{1,0:T(8,128)(2,1)S(1)} %get-tuple-element.41), channel_id=1, source_target_pairs={{0,3},{1,2},{2,1},{3,0},{4,7},{5,6},{6,5},{7,4},{8,11},{9,10},{10,... | collective-permute-start | bytes 147464 | tf_op jit(solution)/shard_map/ppermute | solution.py:204
  49.7 2.6 %collective-permute-done.17 = bf16[32,768]{1,0:T(8,128)(2,1)S(1)} collective-permute-done((bf16[32,768]{1,0:T(8,128)(2,1)S(1)}, bf16[32,768]{1,0:T(8,128)(2,1)S(1)}, u32[]{:S(2)}, u32[]{:S(2)}) %collective-permute-start.17) | collective-permute-done | bytes 49184 | tf_op jit(solution)/shard_map/ppermute | solution.py:204
  52.2 0.6 %collective-permute-done.18 = bf16[32,768]{1,0:T(8,128)(2,1)S(1)} collective-permute-done((bf16[32,768]{1,0:T(8,128)(2,1)S(1)}, bf16[32,768]{1,0:T(8,128)(2,1)S(1)}, u32[]{:S(2)}, u32[]{:S(2)}) %collective-permute-start.18) | collective-permute-done | bytes 49184 | tf_op jit(solution)/shard_map/ppermute | solution.py:204
  52.8 0.0 collective-permute-done.16
  52.8 0.7 %add_bitcast_fusion = f32[1,32,768]{2,1,0:T(8,128)} fusion(bf16[32,768]{1,0:T(8,128)(2,1)S(1)} %collective-permute-done.18, bf16[32,768]{1,0:T(8,128)(2,1)S(1)} %collective-permute-done.17, f32[32,768]{1,0:T(8,128)S(1)} %get-tuple-element.38, f32[32,768]{1,0:T(8,128)S(1)} %collective-permute-done.16), kind=kLoop, calls=%fused_computation.1 | loop fusion | flops 122880 | bytes 393216 | tf_op jit(solution)/shard_map/broadcast_in_dim | solution.py:296
  (4 shorter events, 0.1 us)
Async XLA Ops:
  3.5 20.1 %copy-start.1 = (bf16[1552,128]{1,0:T(8,128)(2,1)S(1)}, bf16[1552,128]{1,0:T(8,128)(2,1)}, u32[]{:S(2)}) copy-start(bf16[1552,128]{1,0:T(8,128)(2,1)} %get-tuple-element.28.refs_0_) | copy-start | bytes 1191940
  3.5 1.8 %collective-permute-start = (f32[64,768]{1,0:T(8,128)}, f32[64,768]{1,0:T(8,128)S(1)}, u32[]{:S(2)}, u32[]{:S(2)}) collective-permute-start(f32[64,768]{1,0:T(8,128)} %get-tuple-element.25), channel_id=1, source_target_pairs={{0,1},{1,0},{2,3},{3,2},{4,5},{5,4},{6,7},{7,6},{8,9},{9,8},{10,11... | collective-permute-start | bytes 589832 | tf_op jit(solution)/shard_map/ppermute | solution.py:204
  5.3 0.9 %copy-start.2 = (f32[64,768]{1,0:T(8,128)S(1)}, f32[64,768]{1,0:T(8,128)}, u32[]{:S(2)}) copy-start(f32[64,768]{1,0:T(8,128)} %get-tuple-element.24.keep_ref) | copy-start | bytes 589828
  6.2 5.0 %collective-permute-start.1 = (bf16[32,768]{1,0:T(8,128)(2,1)S(1)}, bf16[32,768]{1,0:T(8,128)(2,1)S(1)}, u32[]{:S(2)}, u32[]{:S(2)}) collective-permute-start(bf16[32,768]{1,0:T(8,128)(2,1)S(1)} %get-tuple-element.27), channel_id=1, source_target_pairs={{0,2},{1,3},{2,0},{3,1},{4,6},{5,7},{6,4},{7,5},{8,10},{9,11},{10,... | collective-permute-start | bytes 147464 | tf_op jit(solution)/shard_map/ppermute | solution.py:204
  9.1 11.3 %collective-permute-start.7 = (bf16[1552,128]{1,0:T(8,128)(2,1)}, bf16[1552,128]{1,0:T(8,128)(2,1)S(1)}, u32[]{:S(2)}, u32[]{:S(2)}) collective-permute-start(bf16[1552,128]{1,0:T(8,128)(2,1)} %get-tuple-element.28.refs_0_), channel_id=1, source_target_pairs={{0,4},{1,3},{2,6},{3,1},{4,0},{5,7},{6,2},{7,5},{8,12},{9,11},{10,... | collective-permute-start | bytes 1191944 | tf_op jit(solution)/shard_map/ppermute | solution.py:253
  10.7 9.8 %collective-permute-start.6 = (bf16[1552,128]{1,0:T(8,128)(2,1)}, bf16[1552,128]{1,0:T(8,128)(2,1)S(1)}, u32[]{:S(2)}, u32[]{:S(2)}) collective-permute-start(bf16[1552,128]{1,0:T(8,128)(2,1)} %get-tuple-element.28.refs_0_), channel_id=1, source_target_pairs={{0,2},{1,5},{2,0},{3,7},{4,6},{5,1},{6,4},{7,3},{8,10},{9,13},{10,... | collective-permute-start | bytes 1191944 | tf_op jit(solution)/shard_map/ppermute | solution.py:253
  11.3 6.5 %collective-permute-start.4 = (bf16[32,768]{1,0:T(8,128)(2,1)S(1)}, bf16[32,768]{1,0:T(8,128)(2,1)S(1)}, u32[]{:S(2)}, u32[]{:S(2)}) collective-permute-start(bf16[32,768]{1,0:T(8,128)(2,1)S(1)} %add_convert_fusion), channel_id=1, source_target_pairs={{0,24},{4,28},{8,16},{12,20},{16,8},{20,12},{24,0},{28,4},{1,25},{... | collective-permute-start | bytes 147464 | tf_op jit(solution)/shard_map/ppermute | solution.py:204
  15.4 5.0 %collective-permute-start.3 = (bf16[32,768]{1,0:T(8,128)(2,1)S(1)}, bf16[32,768]{1,0:T(8,128)(2,1)S(1)}, u32[]{:S(2)}, u32[]{:S(2)}) collective-permute-start(bf16[32,768]{1,0:T(8,128)(2,1)S(1)} %add_convert_fusion), channel_id=1, source_target_pairs={{0,16},{4,20},{8,24},{12,28},{16,0},{20,4},{24,8},{28,12},{1,17},{... | collective-permute-start | bytes 147464 | tf_op jit(solution)/shard_map/ppermute | solution.py:204
  15.4 5.0 %collective-permute-start.2 = (bf16[32,768]{1,0:T(8,128)(2,1)S(1)}, bf16[32,768]{1,0:T(8,128)(2,1)S(1)}, u32[]{:S(2)}, u32[]{:S(2)}) collective-permute-start(bf16[32,768]{1,0:T(8,128)(2,1)S(1)} %add_convert_fusion), channel_id=1, source_target_pairs={{0,8},{4,12},{8,0},{12,4},{16,24},{20,28},{24,16},{28,20},{1,9},{5... | collective-permute-start | bytes 147464 | tf_op jit(solution)/shard_map/ppermute | solution.py:204
  20.5 7.9 %collective-permute-start.8 = (bf16[1552,128]{1,0:T(8,128)(2,1)S(1)}, bf16[1552,128]{1,0:T(8,128)(2,1)S(1)}, u32[]{:S(2)}, u32[]{:S(2)}) collective-permute-start(bf16[1552,128]{1,0:T(8,128)(2,1)S(1)} %get-tuple-element.29.refs_1_), channel_id=1, source_target_pairs={{0,4},{1,3},{2,6},{3,1},{4,0},{5,7},{6,2},{7,5},{8,12},{9,11},{10,... | collective-permute-start | bytes 1191944 | tf_op jit(solution)/shard_map/ppermute | solution.py:254
  22.1 1.4 %collective-permute-start.5 = (bf16[128,768]{1,0:T(8,128)(2,1)S(1)}, bf16[128,768]{1,0:T(8,128)(2,1)S(1)}, u32[]{:S(2)}, u32[]{:S(2)}) collective-permute-start(bf16[128,768]{1,0:T(8,128)(2,1)S(1)} %pad_maximum_fusion.refs_2_.mine_ref), channel_id=1, source_target_pairs={{0,1},{1,0},{2,3},{3,2},{4,5},{5,4},{6,7},{7,6},{8,9},{9,8},{10,11... | collective-permute-start | bytes 589832 | tf_op jit(solution)/shard_map/ppermute | solution.py:204
  25.4 16.0 %copy-start.3 = (f32[8,128]{1,0:T(8,128)S(1)}, f32[8,128]{1,0:T(8,128)}, u32[]{:S(2)}) copy-start(f32[8,128]{1,0:T(8,128)} %get-tuple-element.23.resident_ref) | copy-start | bytes 12292
  25.4 20.9 %copy-start = (bf16[1024,768]{1,0:T(8,128)(2,1)S(1)}, bf16[1024,768]{1,0:T(8,128)(2,1)}, u32[]{:S(2)}) copy-start(bf16[1024,768]{1,0:T(8,128)(2,1)} %points_ref.1) | copy-start | bytes 4718596
  25.4 20.9 %copy-start.4 = (s32[1,1024]{1,0:T(1,128)S(1)}, s32[1,1024]{1,0:T(1,128)}, u32[]{:S(2)}) copy-start(s32[1,1024]{1,0:T(1,128)} %get-tuple-element.22.mark_ref) | copy-start | bytes 12292
  29.2 1.9 %collective-permute-start.9 = (f32[128,896]{1,0:T(8,128)S(1)}, f32[128,896]{1,0:T(8,128)S(1)}, u32[]{:S(2)}, u32[]{:S(2)}) collective-permute-start(f32[128,896]{1,0:T(8,128)S(1)} %get-tuple-element.32), channel_id=1, source_target_pairs={{0,1},{1,0},{2,3},{3,2},{4,5},{5,4},{6,7},{7,6},{8,9},{9,8},{10,11... | collective-permute-start | bytes 1376264 | tf_op jit(solution)/shard_map/ppermute | solution.py:204
  31.1 4.5 %collective-permute-start.10 = (bf16[208,128]{1,0:T(8,128)(2,1)S(1)}, bf16[208,128]{1,0:T(8,128)(2,1)S(1)}, u32[]{:S(2)}, u32[]{:S(2)}) collective-permute-start(bf16[208,128]{1,0:T(8,128)(2,1)S(1)} %get-tuple-element.34), channel_id=1, source_target_pairs={{0,8},{4,12},{8,0},{12,4},{16,24},{20,28},{24,16},{28,20},{1,9},{5... | collective-permute-start | bytes 159752 | tf_op jit(solution)/shard_map/ppermute | solution.py:204
  32.8 6.2 %collective-permute-start.11 = (bf16[208,128]{1,0:T(8,128)(2,1)S(1)}, bf16[208,128]{1,0:T(8,128)(2,1)S(1)}, u32[]{:S(2)}, u32[]{:S(2)}) collective-permute-start(bf16[208,128]{1,0:T(8,128)(2,1)S(1)} %get-tuple-element.35), channel_id=1, source_target_pairs={{0,16},{4,20},{8,24},{12,28},{16,0},{20,4},{24,8},{28,12},{1,17},{... | collective-permute-start | bytes 159752 | tf_op jit(solution)/shard_map/ppermute | solution.py:204
  35.4 5.9 %collective-permute-start.12 = (bf16[208,128]{1,0:T(8,128)(2,1)S(1)}, bf16[208,128]{1,0:T(8,128)(2,1)S(1)}, u32[]{:S(2)}, u32[]{:S(2)}) collective-permute-start(bf16[208,128]{1,0:T(8,128)(2,1)S(1)} %get-tuple-element.36), channel_id=1, source_target_pairs={{0,24},{4,28},{8,16},{12,20},{16,8},{20,12},{24,0},{28,4},{1,25},{... | collective-permute-start | bytes 159752 | tf_op jit(solution)/shard_map/ppermute | solution.py:204
  41.4 4.1 %collective-permute-start.15 = (bf16[32,768]{1,0:T(8,128)(2,1)S(1)}, bf16[32,768]{1,0:T(8,128)(2,1)S(1)}, u32[]{:S(2)}, u32[]{:S(2)}) collective-permute-start(bf16[32,768]{1,0:T(8,128)(2,1)S(1)} %scale.1.refs_0_), channel_id=1, source_target_pairs={{0,3},{1,2},{2,1},{3,0},{4,7},{5,6},{6,5},{7,4},{8,11},{9,10},{10,... | collective-permute-start | bytes 147464 | tf_op jit(solution)/shard_map/ppermute | solution.py:204
  41.5 4.8 %collective-permute-start.14 = (bf16[32,768]{1,0:T(8,128)(2,1)S(1)}, bf16[32,768]{1,0:T(8,128)(2,1)S(1)}, u32[]{:S(2)}, u32[]{:S(2)}) collective-permute-start(bf16[32,768]{1,0:T(8,128)(2,1)S(1)} %scale.1.refs_0_), channel_id=1, source_target_pairs={{0,2},{1,3},{2,0},{3,1},{4,6},{5,7},{6,4},{7,5},{8,10},{9,11},{10,... | collective-permute-start | bytes 147464 | tf_op jit(solution)/shard_map/ppermute | solution.py:204
  42.8 3.4 %collective-permute-start.13 = (bf16[32,768]{1,0:T(8,128)(2,1)S(1)}, bf16[32,768]{1,0:T(8,128)(2,1)S(1)}, u32[]{:S(2)}, u32[]{:S(2)}) collective-permute-start(bf16[32,768]{1,0:T(8,128)(2,1)S(1)} %scale.1.refs_0_), channel_id=1, source_target_pairs={{0,1},{1,0},{2,3},{3,2},{4,5},{5,4},{6,7},{7,6},{8,9},{9,8},{10,11... | collective-permute-start | bytes 147464 | tf_op jit(solution)/shard_map/ppermute | solution.py:204
  47.8 5.0 %collective-permute-start.16 = (f32[32,768]{1,0:T(8,128)S(1)}, f32[32,768]{1,0:T(8,128)S(1)}, u32[]{:S(2)}, u32[]{:S(2)}) collective-permute-start(f32[32,768]{1,0:T(8,128)S(1)} %get-tuple-element.39), channel_id=1, source_target_pairs={{0,1},{1,0},{2,3},{3,2},{4,5},{5,4},{6,7},{7,6},{8,9},{9,8},{10,11... | collective-permute-start | bytes 294920 | tf_op jit(solution)/shard_map/ppermute | solution.py:204
  47.9 4.3 %collective-permute-start.17 = (bf16[32,768]{1,0:T(8,128)(2,1)S(1)}, bf16[32,768]{1,0:T(8,128)(2,1)S(1)}, u32[]{:S(2)}, u32[]{:S(2)}) collective-permute-start(bf16[32,768]{1,0:T(8,128)(2,1)S(1)} %get-tuple-element.40), channel_id=1, source_target_pairs={{0,2},{1,3},{2,0},{3,1},{4,6},{5,7},{6,4},{7,5},{8,10},{9,11},{10,... | collective-permute-start | bytes 147464 | tf_op jit(solution)/shard_map/ppermute | solution.py:204
  48.9 3.9 %collective-permute-start.18 = (bf16[32,768]{1,0:T(8,128)(2,1)S(1)}, bf16[32,768]{1,0:T(8,128)(2,1)S(1)}, u32[]{:S(2)}, u32[]{:S(2)}) collective-permute-start(bf16[32,768]{1,0:T(8,128)(2,1)S(1)} %get-tuple-element.41), channel_id=1, source_target_pairs={{0,3},{1,2},{2,1},{3,0},{4,7},{5,6},{6,5},{7,4},{8,11},{9,10},{10,... | collective-permute-start | bytes 147464 | tf_op jit(solution)/shard_map/ppermute | solution.py:204

commit v6 on v5

--- a/solution.py
+++ b/solution.py
@@ -34,14 +34,11 @@
     return jnp.concatenate([ref[k * rows : (k + 1) * rows, :] for k in range(width // LANES)], axis=1)
 
 
-def order(helpers):
-    return [*range(0, helpers, 2), *range(1, helpers, 2)]
-
-
 def lift_kernel(helpers, *refs):
     rows_hbm, group_hbm, local_hbm, ids_hbm, test_hbm, points_hbm = refs[:6]
-    packed_ref, keep_ref, pass_ref, mark_ref, resident_ref = refs[6:11]
-    group_ref, local_ref, ids_ref, test_ref, points_ref, sems = refs[11:]
+    packed_ref, mark_ref, resident_ref = refs[6:9]
+    outs = refs[9 : 9 + helpers]
+    group_ref, local_ref, ids_ref, test_ref, points_ref, sems = refs[9 + helpers :]
     helper = lax.axis_index("help")
     asked, width = rows_hbm.shape
     rank, count = test_ref.shape
@@ -65,16 +62,15 @@
         resident_ref[d : d + 1, :] = jnp.broadcast_to(many, (1, LANES))
     copies[1].wait()
     test = test_ref[...]
-    offsets = order(helpers)
-    rows = jnp.concatenate([jnp.where(mark == d, test, jnp.zeros((), BF16)) for d in offsets], axis=0)
+    rows = jnp.concatenate([jnp.where(mark == d, test, jnp.zeros((), BF16)) for d in range(helpers)], axis=0)
     total = None
     for k in range(CHUNKS):
         copies[2 + k].wait()
         part = slice(k * piece, (k + 1) * piece)
         more = contract(rows[:, part], points_ref[part, :], ((1,), (0,)))
         total = more if total is None else total + more
-    keep_ref[...] = total[: keep_ref.shape[0]]
-    pass_ref[...] = total[keep_ref.shape[0] :]
+    for d, out in enumerate(outs):
+        out[...] = total[d * rank : (d + 1) * rank].astype(out.dtype)
     for copy in copies[2 + CHUNKS :]:
         copy.wait()
     cluster = (group_ref[...] * helpers + local_ref[...]).astype(F32)
@@ -83,12 +79,12 @@
     packed_ref[asked * width // LANES :, :] = jnp.concatenate(line, axis=0).astype(BF16)
 
 
-def join_kernel(keep_ref, got_ref, own_ref, *send_refs):
-    rank = own_ref.shape[0]
-    own_ref[...] = keep_ref[:rank, :] + got_ref[:rank, :]
-    for k, ref in enumerate(send_refs, 1):
-        part = slice(k * rank, (k + 1) * rank)
-        ref[...] = (keep_ref[part, :] + got_ref[part, :]).astype(BF16)
+def join_kernel(*refs):
+    *parts, out = refs
+    total = parts[0][...]
+    for part in parts[1:]:
+        total = total + part[...].astype(F32)
+    out[...] = total.astype(out.dtype)
 
 
 def gate_kernel(*refs):
@@ -211,17 +207,19 @@
     count = queries.shape[0]
     rank = test_matrix.shape[0]
     own_points, width = points.shape
-    kept = jax.ShapeDtypeStruct((helpers // 2 * rank, width), F32)
-
-    packed, keep, passed, mark, resident = pl.pallas_call(
+    block = jax.ShapeDtypeStruct((rank, width), F32)
+    sent = jax.ShapeDtypeStruct((rank, width), BF16)
+
+    packed, mark, resident, own, *parts = pl.pallas_call(
         functools.partial(lift_kernel, helpers),
         out_shape=[
             jax.ShapeDtypeStruct((count * width // LANES + TILE, LANES), BF16),
-            kept,
-            kept,
             jax.ShapeDtypeStruct((1, own_points), jnp.int32),
             jax.ShapeDtypeStruct((8, LANES), F32),
-        ],
+            block,
+            block,
+        ]
+        + [sent] * (helpers - 2),
         in_specs=[HBM] * 6,
         scratch_shapes=[
             pltpu.VMEM((2, count), jnp.int32),
@@ -234,23 +232,19 @@
         compiler_params=pltpu.CompilerParams(vmem_limit_bytes=FIRST << 20),
         name="lift",
     )(queries, probe_group.T, probe_local.T, point_cluster, test_matrix, points)
-    own, *leaving = pl.pallas_call(
+    lifter = pl.pallas_call(
         join_kernel,
-        out_shape=[jax.ShapeDtypeStruct((rank, width), F32)]
-        + [jax.ShapeDtypeStruct((rank, width), BF16)] * (helpers // 2 - 1),
+        out_shape=sent,
         compiler_params=PARAMS,
         name="join",
-    )(keep, swap(passed, "help", 1))
-    for k, part in enumerate(leaving, 1):
-        own = own + swap(part, "help", 2 * k).astype(F32)
-    lifter = own.astype(BF16)
+    )(own, *[swap(part, "help", d) for d, part in enumerate(parts, 1)])
     mine = jnp.concatenate([lifter] + [swap(lifter, "shard", INNER * d) for d in range(1, planes)], axis=0)
     theirs = swap(mine, "help", 1)
 
     index, axes = range(groups * helpers), ("shard", "help")
     one = [(i, i ^ (2 if i % 2 == 0 else helpers)) for i in index]
     two = [(i, i ^ (helpers if i % 2 == 0 else 2)) for i in index]
-    near, far = gate([lax.ppermute(packed, axes, turn) for turn in (one, two)], mine)
+    near, far = gate([lax.ppermute(packed, axes, turn) for turn in (one, two)], theirs)
     across = lax.ppermute(near, axes, two)
 
     wide = width + LANES
@@ -283,8 +277,6 @@
     )(resident, *moments)
     scaled = [scaled] + [swap(scaled, "help", d) for d in range(1, helpers)]
 
-    block = jax.ShapeDtypeStruct((rank, width), F32)
-    sent = jax.ShapeDtypeStruct((rank, width), BF16)
     sketch, regressor, *parts = pl.pallas_call(
         functools.partial(sketch_kernel, helpers),
         out_shape=[jax.ShapeDtypeStruct((rank, own_points), F32), block, block] + [sent] * (helpers - 2),

time: 53.7 us -> 53.6 us (level)
  waiting for transfers between devices: 23.7 us -> 23 us
  starting transfers between devices: 20.2 us -> 20.8 us
    ppermute x16 -> x17, waiting for transfers between devices: 20.8 us -> 18.6 us  [swap(): lax.ppermute(value, axis, [(i, i ^ d) for i in range(lax.axis_size(axis))])]
    ppermute x1, waiting for transfers between devices: 2.96 us -> 4.44 us  [shards(): across = lax.ppermute(near, axes, two)]
    ppermute x2, starting transfers between devices: 2.05 us -> 3.25 us  [shards(): lax.ppermute(packed, axes, turn)]
    ppermute x16 -> x17, starting transfers between devices: 16.5 us -> 16 us  [swap(): lax.ppermute(value, axis, [(i, i ^ d) for i in range(lax.axis_size(axis))])]
  transfers between devices with their start and end apart: 19 -> 20, of which waited for: 13 -> 12; matrix products, arithmetic and copies ran while one was open for 0% -> 0% of each run, Pallas kernels for 3% -> 3%
where the time goes in v6:
time: 53.6 us; the launch traced here: 53.3 us
  waiting for transfers between devices  23 us (43%)
  starting transfers between devices  20.8 us (39%)
  Pallas kernels  7.11 us (13%)
  local copies, waits for them, and re-layouts  0.91 us (2%)
  between operations  0.75 us (1%)
  other arithmetic  0.68 us (1%)
    ppermute x17, waiting for transfers between devices, swap(): lax.ppermute(value, axis, [(i, i ^ d) for i in range(lax.axis_size(axis))])  18.6 us
    ppermute x17, starting transfers between devices, swap(): lax.ppermute(value, axis, [(i, i ^ d) for i in range(lax.axis_size(axis))])  16 us
    ppermute x1, waiting for transfers between devices, shards(): across = lax.ppermute(near, axes, two)  4.44 us
    ppermute x2, starting transfers between devices, shards(): lax.ppermute(packed, axes, turn)  3.25 us
    pallas_call x1, Pallas kernels, shards(): pl.pallas_call(functools.partial(lift_kernel, helpers), out_shape=[jax.Sh...  2.8 us
    pallas_call x1, Pallas kernels, shards(): pl.pallas_call(functools.partial(score_kernel, planes, helpers, 3), out_s...  1.81 us
    ppermute x1, starting transfers between devices, shards(): across = lax.ppermute(near, axes, two)  1.58 us
    pallas_call x1, Pallas kernels, shards(): pl.pallas_call(functools.partial(sketch_kernel, helpers), out_shape=[jax....  1.53 us
  transfers between devices with their start and end apart: 20, of which 12 were waited for; matrix products, arithmetic and copies ran while one was open for 0% of the time, Pallas kernels for 3%

profile of v6, /device:TPU:0, one launch (start us, length us, event | category | flops | bytes accessed | tf_op | source)
XLA Modules:
  0.0 53.3 jit_solution(16855778742598115879)
XLA Ops:
  0.6 2.8 %lift.1 = (bf16[1552,128]{1,0:T(8,128)(2,1)}, s32[1,1024]{1,0:T(1,128)}, f32[8,128]{1,0:T(8,128)}, f32[32,768]{1,0:T(8,128)}, f32[32,768]{1,0:T(8,128)}, /*index...) custom-call(bf16[256,768]{1,0:T(8,128)(2,1)} %refs_0_.1, s32[2,256]{1,0:T(2,128)} %bitcast.4, s32[2,256]{1,0:T(2,128)} %bitcast.5, ...), custom_call_target="tpu_custom_call" | custom-call | tf_op jit(solution)/shard_map/lift/pallas_call | solution.py:213
  3.4 0.0 copy-start.1
  3.4 0.5 collective-permute-start
  4.0 2.6 %collective-permute-start.1 = (bf16[32,768]{1,0:T(8,128)(2,1)}, bf16[32,768]{1,0:T(8,128)(2,1)S(1)}, u32[]{:S(2)}, u32[]{:S(2)}) collective-permute-start(bf16[32,768]{1,0:T(8,128)(2,1)} %get-tuple-element.26), channel_id=1, source_target_pairs={{0,2},{1,3},{2,0},{3,1},{4,6},{5,7},{6,4},{7,5},{8,10},{9,11},{10,... | collective-permute-start | bytes 147464 | tf_op jit(solution)/shard_map/ppermute | solution.py:200
  6.5 0.1 collective-permute-start.2
  6.6 1.8 %collective-permute-start.8 = (bf16[1552,128]{1,0:T(8,128)(2,1)}, bf16[1552,128]{1,0:T(8,128)(2,1)S(1)}, u32[]{:S(2)}, u32[]{:S(2)}) collective-permute-start(bf16[1552,128]{1,0:T(8,128)(2,1)} %get-tuple-element.28.refs_0_), channel_id=1, source_target_pairs={{0,4},{1,3},{2,6},{3,1},{4,0},{5,7},{6,2},{7,5},{8,12},{9,11},{10,... | collective-permute-start | bytes 1191944 | tf_op jit(solution)/shard_map/ppermute | solution.py:247
  8.4 1.5 %collective-permute-start.7 = (bf16[1552,128]{1,0:T(8,128)(2,1)}, bf16[1552,128]{1,0:T(8,128)(2,1)S(1)}, u32[]{:S(2)}, u32[]{:S(2)}) collective-permute-start(bf16[1552,128]{1,0:T(8,128)(2,1)} %get-tuple-element.28.refs_0_), channel_id=1, source_target_pairs={{0,2},{1,5},{2,0},{3,7},{4,6},{5,1},{6,4},{7,3},{8,10},{9,13},{10,... | collective-permute-start | bytes 1191944 | tf_op jit(solution)/shard_map/ppermute | solution.py:247
  9.8 0.0 collective-permute-done.1.refs_2_
  9.8 0.7 %collective-permute-done.2.refs_3_ = bf16[32,768]{1,0:T(8,128)(2,1)S(1)} collective-permute-done((bf16[32,768]{1,0:T(8,128)(2,1)}, bf16[32,768]{1,0:T(8,128)(2,1)S(1)}, u32[]{:S(2)}, u32[]{:S(2)}) %collective-permute-start.2) | collective-permute-done | bytes 49184 | tf_op jit(solution)/shard_map/ppermute | solution.py:200
  10.5 0.0 collective-permute-done.refs_1_
  10.5 0.0 copy-start.2
  10.5 0.9 %copy-done.2 = f32[32,768]{1,0:T(8,128)S(1)} copy-done((f32[32,768]{1,0:T(8,128)S(1)}, f32[32,768]{1,0:T(8,128)}, u32[]{:S(2)}) %copy-start.2) | copy-done | bytes 98328
  11.4 3.7 %collective-permute-start.5 = (bf16[32,768]{1,0:T(8,128)(2,1)S(1)}, bf16[32,768]{1,0:T(8,128)(2,1)S(1)}, u32[]{:S(2)}, u32[]{:S(2)}) collective-permute-start(bf16[32,768]{1,0:T(8,128)(2,1)S(1)} %join.1), channel_id=1, source_target_pairs={{0,24},{4,28},{8,16},{12,20},{16,8},{20,12},{24,0},{28,4},{1,25},{... | collective-permute-start | bytes 147464 | tf_op jit(solution)/shard_map/ppermute | solution.py:200
  15.1 0.0 collective-permute-start.4
  15.1 0.8 %collective-permute-start.3 = (bf16[32,768]{1,0:T(8,128)(2,1)S(1)}, bf16[32,768]{1,0:T(8,128)(2,1)S(1)}, u32[]{:S(2)}, u32[]{:S(2)}) collective-permute-start(bf16[32,768]{1,0:T(8,128)(2,1)S(1)} %join.1), channel_id=1, source_target_pairs={{0,8},{4,12},{8,0},{12,4},{16,24},{20,28},{24,16},{28,20},{1,9},{5... | collective-permute-start | bytes 147464 | tf_op jit(solution)/shard_map/ppermute | solution.py:200
  15.9 1.9 %collective-permute-done.5 = bf16[32,768]{1,0:T(8,128)(2,1)S(1)} collective-permute-done((bf16[32,768]{1,0:T(8,128)(2,1)S(1)}, bf16[32,768]{1,0:T(8,128)(2,1)S(1)}, u32[]{:S(2)}, u32[]{:S(2)}) %collective-permute-start.5) | collective-permute-done | bytes 49184 | tf_op jit(solution)/shard_map/ppermute | solution.py:200
  17.8 2.5 %collective-permute-done.4 = bf16[32,768]{1,0:T(8,128)(2,1)S(1)} collective-permute-done((bf16[32,768]{1,0:T(8,128)(2,1)S(1)}, bf16[32,768]{1,0:T(8,128)(2,1)S(1)}, u32[]{:S(2)}, u32[]{:S(2)}) %collective-permute-start.4) | collective-permute-done | bytes 49184 | tf_op jit(solution)/shard_map/ppermute | solution.py:200
  20.3 0.0 collective-permute-done.3
  20.3 0.1 collective-permute-start.6
  20.4 1.4 %collective-permute-done.6.refs_2_.theirs_ref = bf16[128,768]{1,0:T(8,128)(2,1)S(1)} collective-permute-done((bf16[128,768]{1,0:T(8,128)(2,1)S(1)}, bf16[128,768]{1,0:T(8,128)(2,1)S(1)}, u32[]{:S(2)}, u32[]{:S(2)}) %collective-permute-start.6) | collective-permute-done | bytes 196640 | tf_op jit(solution)/shard_map/ppermute | solution.py:200
  21.8 0.0 collective-permute-done.8.refs_1_
  21.8 0.0 collective-permute-done.7.refs_0_
  21.8 1.6 %collective-permute-start.9 = (bf16[1552,128]{1,0:T(8,128)(2,1)S(1)}, bf16[1552,128]{1,0:T(8,128)(2,1)S(1)}, u32[]{:S(2)}, u32[]{:S(2)}) collective-permute-start(bf16[1552,128]{1,0:T(8,128)(2,1)S(1)} %get-tuple-element.29.refs_1_), channel_id=1, source_target_pairs={{0,4},{1,3},{2,6},{3,1},{4,0},{5,7},{6,2},{7,5},{8,12},{9,11},{10,... | collective-permute-start | bytes 1191944 | tf_op jit(solution)/shard_map/ppermute | solution.py:248
  23.4 0.0 copy-done.1
  23.4 1.8 %score.1.refs_1_ = f32[256,896]{1,0:T(8,128)S(1)} custom-call(bf16[128,768]{1,0:T(8,128)(2,1)S(1)} %pad_maximum_fusion.mine_ref, bf16[128,768]{1,0:T(8,128)(2,1)S(1)} %collective-permute-done.6.refs_2_.theirs_ref, bf16[1552,128]{1,0:T(8,128)(2,1)S(1)} %copy-done.1, bf16[1552,128]{1,0:T(8,128)(2,1)S(1)} %get-tuple-element.29.refs_1_, ...), custom_call_target="tpu_custom_call" | custom-call | tf_op jit(solution)/shard_map/score/pallas_call | solution.py:251
  25.2 0.0 copy-start.3
  25.2 0.0 copy-start
  25.2 0.0 copy-start.4
  25.2 4.4 %collective-permute-done.9.refs_0_ = bf16[1552,128]{1,0:T(8,128)(2,1)S(1)} collective-permute-done((bf16[1552,128]{1,0:T(8,128)(2,1)S(1)}, bf16[1552,128]{1,0:T(8,128)(2,1)S(1)}, u32[]{:S(2)}, u32[]{:S(2)}) %collective-permute-start.9) | collective-permute-done | bytes 397344 | tf_op jit(solution)/shard_map/ppermute | solution.py:248
  29.7 0.8 %score_last.1 = (f32[128,896]{1,0:T(8,128)S(1)}, f32[128,896]{1,0:T(8,128)S(1)}) custom-call(bf16[128,768]{1,0:T(8,128)(2,1)S(1)} %pad_maximum_fusion.mine_ref, bf16[128,768]{1,0:T(8,128)(2,1)S(1)} %collective-permute-done.6.refs_2_.theirs_ref, bf16[1552,128]{1,0:T(8,128)(2,1)S(1)} %collective-permute-done.9.refs_0_, f32[256,896]{1,0:T(8,128)S(1)} %score.1.refs_1_), custom_call_target="tpu_custom_call" | custom-call | tf_op jit(solution)/shard_map/score_last/pallas_call | solution.py:257
  30.5 0.1 collective-permute-start.10
  30.6 1.8 %collective-permute-done.10.theirs_ref = f32[128,896]{1,0:T(8,128)S(1)} collective-permute-done((f32[128,896]{1,0:T(8,128)S(1)}, f32[128,896]{1,0:T(8,128)S(1)}, u32[]{:S(2)}, u32[]{:S(2)}) %collective-permute-start.10) | collective-permute-done | bytes 458784 | tf_op jit(solution)/shard_map/ppermute | solution.py:200
  32.4 0.1 fold.1
  32.4 1.3 %collective-permute-start.11 = (bf16[208,128]{1,0:T(8,128)(2,1)S(1)}, bf16[208,128]{1,0:T(8,128)(2,1)S(1)}, u32[]{:S(2)}, u32[]{:S(2)}) collective-permute-start(bf16[208,128]{1,0:T(8,128)(2,1)S(1)} %get-tuple-element.34), channel_id=1, source_target_pairs={{0,8},{4,12},{8,0},{12,4},{16,24},{20,28},{24,16},{28,20},{1,9},{5... | collective-permute-start | bytes 159752 | tf_op jit(solution)/shard_map/ppermute | solution.py:200
  33.8 1.5 %collective-permute-start.12 = (bf16[208,128]{1,0:T(8,128)(2,1)S(1)}, bf16[208,128]{1,0:T(8,128)(2,1)S(1)}, u32[]{:S(2)}, u32[]{:S(2)}) collective-permute-start(bf16[208,128]{1,0:T(8,128)(2,1)S(1)} %get-tuple-element.35), channel_id=1, source_target_pairs={{0,16},{4,20},{8,24},{12,28},{16,0},{20,4},{24,8},{28,12},{1,17},{... | collective-permute-start | bytes 159752 | tf_op jit(solution)/shard_map/ppermute | solution.py:200
  35.3 1.6 %collective-permute-start.13 = (bf16[208,128]{1,0:T(8,128)(2,1)S(1)}, bf16[208,128]{1,0:T(8,128)(2,1)S(1)}, u32[]{:S(2)}, u32[]{:S(2)}) collective-permute-start(bf16[208,128]{1,0:T(8,128)(2,1)S(1)} %get-tuple-element.36), channel_id=1, source_target_pairs={{0,24},{4,28},{8,16},{12,20},{16,8},{20,12},{24,0},{28,4},{1,25},{... | collective-permute-start | bytes 159752 | tf_op jit(solution)/shard_map/ppermute | solution.py:200
  36.9 0.0 collective-permute-done.11.refs_0_
  36.9 3.7 %collective-permute-done.12.refs_1_ = bf16[208,128]{1,0:T(8,128)(2,1)S(1)} collective-permute-done((bf16[208,128]{1,0:T(8,128)(2,1)S(1)}, bf16[208,128]{1,0:T(8,128)(2,1)S(1)}, u32[]{:S(2)}, u32[]{:S(2)}) %collective-permute-start.12) | collective-permute-done | bytes 53280 | tf_op jit(solution)/shard_map/ppermute | solution.py:200
  40.5 0.8 %collective-permute-done.13.refs_2_ = bf16[208,128]{1,0:T(8,128)(2,1)S(1)} collective-permute-done((bf16[208,128]{1,0:T(8,128)(2,1)S(1)}, bf16[208,128]{1,0:T(8,128)(2,1)S(1)}, u32[]{:S(2)}, u32[]{:S(2)}) %collective-permute-start.13) | collective-permute-done | bytes 53280 | tf_op jit(solution)/shard_map/ppermute | solution.py:200
  41.3 0.0 copy-done.3
  41.3 0.1 scale.1.refs_0_
  41.4 0.1 collective-permute-start.16
  41.5 1.3 %collective-permute-start.15 = (bf16[32,768]{1,0:T(8,128)(2,1)S(1)}, bf16[32,768]{1,0:T(8,128)(2,1)S(1)}, u32[]{:S(2)}, u32[]{:S(2)}) collective-permute-start(bf16[32,768]{1,0:T(8,128)(2,1)S(1)} %scale.1.refs_0_), channel_id=1, source_target_pairs={{0,2},{1,3},{2,0},{3,1},{4,6},{5,7},{6,4},{7,5},{8,10},{9,11},{10,... | collective-permute-start | bytes 147464 | tf_op jit(solution)/shard_map/ppermute | solution.py:200
  42.8 0.5 %collective-permute-start.14 = (bf16[32,768]{1,0:T(8,128)(2,1)S(1)}, bf16[32,768]{1,0:T(8,128)(2,1)S(1)}, u32[]{:S(2)}, u32[]{:S(2)}) collective-permute-start(bf16[32,768]{1,0:T(8,128)(2,1)S(1)} %scale.1.refs_0_), channel_id=1, source_target_pairs={{0,1},{1,0},{2,3},{3,2},{4,5},{5,4},{6,7},{7,6},{8,9},{9,8},{10,11... | collective-permute-start | bytes 147464 | tf_op jit(solution)/shard_map/ppermute | solution.py:200
  43.3 2.2 %collective-permute-done.16.refs_3_ = bf16[32,768]{1,0:T(8,128)(2,1)S(1)} collective-permute-done((bf16[32,768]{1,0:T(8,128)(2,1)S(1)}, bf16[32,768]{1,0:T(8,128)(2,1)S(1)}, u32[]{:S(2)}, u32[]{:S(2)}) %collective-permute-start.16) | collective-permute-done | bytes 49184 | tf_op jit(solution)/shard_map/ppermute | solution.py:200
  45.5 0.7 %collective-permute-done.15.refs_2_ = bf16[32,768]{1,0:T(8,128)(2,1)S(1)} collective-permute-done((bf16[32,768]{1,0:T(8,128)(2,1)S(1)}, bf16[32,768]{1,0:T(8,128)(2,1)S(1)}, u32[]{:S(2)}, u32[]{:S(2)}) %collective-permute-start.15) | collective-permute-done | bytes 49184 | tf_op jit(solution)/shard_map/ppermute | solution.py:200
  46.2 0.0 collective-permute-done.14.refs_1_
  46.2 0.0 copy-done
  46.2 0.0 copy-done.4
  46.2 1.5 %sketch.1 = (f32[32,1024]{1,0:T(8,128)}, f32[32,768]{1,0:T(8,128)S(1)}, f32[32,768]{1,0:T(8,128)S(1)}, bf16[32,768]{1,0:T(8,128)(2,1)S(1)}, bf16[32,768]{1,0:T(8,128)(2,1)S(1)}) custom-call(s32[1,1024]{1,0:T(1,128)S(1)} %copy-done.4, f32[8,128]{1,0:T(8,128)S(1)} %copy-done.3, bf16[1024,768]{1,0:T(8,128)(2,1)S(1)} %copy-done, ...), custom_call_target="tpu_custom_call" | custom-call | tf_op jit(solution)/shard_map/sketch/pallas_call | solution.py:280
  47.7 0.1 collective-permute-start.17
  47.8 1.0 %collective-permute-start.18 = (bf16[32,768]{1,0:T(8,128)(2,1)S(1)}, bf16[32,768]{1,0:T(8,128)(2,1)S(1)}, u32[]{:S(2)}, u32[]{:S(2)}) collective-permute-start(bf16[32,768]{1,0:T(8,128)(2,1)S(1)} %get-tuple-element.40), channel_id=1, source_target_pairs={{0,2},{1,3},{2,0},{3,1},{4,6},{5,7},{6,4},{7,5},{8,10},{9,11},{10,... | collective-permute-start | bytes 147464 | tf_op jit(solution)/shard_map/ppermute | solution.py:200
  48.8 0.7 %collective-permute-start.19 = (bf16[32,768]{1,0:T(8,128)(2,1)S(1)}, bf16[32,768]{1,0:T(8,128)(2,1)S(1)}, u32[]{:S(2)}, u32[]{:S(2)}) collective-permute-start(bf16[32,768]{1,0:T(8,128)(2,1)S(1)} %get-tuple-element.41), channel_id=1, source_target_pairs={{0,3},{1,2},{2,1},{3,0},{4,7},{5,6},{6,5},{7,4},{8,11},{9,10},{10,... | collective-permute-start | bytes 147464 | tf_op jit(solution)/shard_map/ppermute | solution.py:200
  49.6 2.5 %collective-permute-done.18 = bf16[32,768]{1,0:T(8,128)(2,1)S(1)} collective-permute-done((bf16[32,768]{1,0:T(8,128)(2,1)S(1)}, bf16[32,768]{1,0:T(8,128)(2,1)S(1)}, u32[]{:S(2)}, u32[]{:S(2)}) %collective-permute-start.18) | collective-permute-done | bytes 49184 | tf_op jit(solution)/shard_map/ppermute | solution.py:200
  52.0 0.6 %collective-permute-done.19 = bf16[32,768]{1,0:T(8,128)(2,1)S(1)} collective-permute-done((bf16[32,768]{1,0:T(8,128)(2,1)S(1)}, bf16[32,768]{1,0:T(8,128)(2,1)S(1)}, u32[]{:S(2)}, u32[]{:S(2)}) %collective-permute-start.19) | collective-permute-done | bytes 49184 | tf_op jit(solution)/shard_map/ppermute | solution.py:200
  52.6 0.0 collective-permute-done.17
  52.7 0.7 %add_bitcast_fusion = f32[1,32,768]{2,1,0:T(8,128)} fusion(bf16[32,768]{1,0:T(8,128)(2,1)S(1)} %collective-permute-done.19, bf16[32,768]{1,0:T(8,128)(2,1)S(1)} %collective-permute-done.18, f32[32,768]{1,0:T(8,128)S(1)} %get-tuple-element.38, f32[32,768]{1,0:T(8,128)S(1)} %collective-permute-done.17), kind=kLoop, calls=%fused_computation.1 | loop fusion | flops 122880 | bytes 393216 | tf_op jit(solution)/shard_map/broadcast_in_dim | solution.py:288
  (3 shorter events, 0.0 us)
Async XLA Ops:
  3.4 19.9 %copy-start.1 = (bf16[1552,128]{1,0:T(8,128)(2,1)S(1)}, bf16[1552,128]{1,0:T(8,128)(2,1)}, u32[]{:S(2)}) copy-start(bf16[1552,128]{1,0:T(8,128)(2,1)} %get-tuple-element.28.refs_0_) | copy-start | bytes 1191940
  3.4 7.1 %collective-permute-start = (f32[32,768]{1,0:T(8,128)}, f32[32,768]{1,0:T(8,128)S(1)}, u32[]{:S(2)}, u32[]{:S(2)}) collective-permute-start(f32[32,768]{1,0:T(8,128)} %get-tuple-element.25), channel_id=1, source_target_pairs={{0,1},{1,0},{2,3},{3,2},{4,5},{5,4},{6,7},{7,6},{8,9},{9,8},{10,11... | collective-permute-start | bytes 294920 | tf_op jit(solution)/shard_map/ppermute | solution.py:200
  4.0 5.9 %collective-permute-start.1 = (bf16[32,768]{1,0:T(8,128)(2,1)}, bf16[32,768]{1,0:T(8,128)(2,1)S(1)}, u32[]{:S(2)}, u32[]{:S(2)}) collective-permute-start(bf16[32,768]{1,0:T(8,128)(2,1)} %get-tuple-element.26), channel_id=1, source_target_pairs={{0,2},{1,3},{2,0},{3,1},{4,6},{5,7},{6,4},{7,5},{8,10},{9,11},{10,... | collective-permute-start | bytes 147464 | tf_op jit(solution)/shard_map/ppermute | solution.py:200
  6.5 4.0 %collective-permute-start.2 = (bf16[32,768]{1,0:T(8,128)(2,1)}, bf16[32,768]{1,0:T(8,128)(2,1)S(1)}, u32[]{:S(2)}, u32[]{:S(2)}) collective-permute-start(bf16[32,768]{1,0:T(8,128)(2,1)} %get-tuple-element.27), channel_id=1, source_target_pairs={{0,3},{1,2},{2,1},{3,0},{4,7},{5,6},{6,5},{7,4},{8,11},{9,10},{10,... | collective-permute-start | bytes 147464 | tf_op jit(solution)/shard_map/ppermute | solution.py:200
  6.6 15.2 %collective-permute-start.8 = (bf16[1552,128]{1,0:T(8,128)(2,1)}, bf16[1552,128]{1,0:T(8,128)(2,1)S(1)}, u32[]{:S(2)}, u32[]{:S(2)}) collective-permute-start(bf16[1552,128]{1,0:T(8,128)(2,1)} %get-tuple-element.28.refs_0_), channel_id=1, source_target_pairs={{0,4},{1,3},{2,6},{3,1},{4,0},{5,7},{6,2},{7,5},{8,12},{9,11},{10,... | collective-permute-start | bytes 1191944 | tf_op jit(solution)/shard_map/ppermute | solution.py:247
  8.4 13.4 %collective-permute-start.7 = (bf16[1552,128]{1,0:T(8,128)(2,1)}, bf16[1552,128]{1,0:T(8,128)(2,1)S(1)}, u32[]{:S(2)}, u32[]{:S(2)}) collective-permute-start(bf16[1552,128]{1,0:T(8,128)(2,1)} %get-tuple-element.28.refs_0_), channel_id=1, source_target_pairs={{0,2},{1,5},{2,0},{3,7},{4,6},{5,1},{6,4},{7,3},{8,10},{9,13},{10,... | collective-permute-start | bytes 1191944 | tf_op jit(solution)/shard_map/ppermute | solution.py:247
  10.5 0.9 %copy-start.2 = (f32[32,768]{1,0:T(8,128)S(1)}, f32[32,768]{1,0:T(8,128)}, u32[]{:S(2)}) copy-start(f32[32,768]{1,0:T(8,128)} %get-tuple-element.24.refs_0_) | copy-start | bytes 294916
  11.4 6.3 %collective-permute-start.5 = (bf16[32,768]{1,0:T(8,128)(2,1)S(1)}, bf16[32,768]{1,0:T(8,128)(2,1)S(1)}, u32[]{:S(2)}, u32[]{:S(2)}) collective-permute-start(bf16[32,768]{1,0:T(8,128)(2,1)S(1)} %join.1), channel_id=1, source_target_pairs={{0,24},{4,28},{8,16},{12,20},{16,8},{20,12},{24,0},{28,4},{1,25},{... | collective-permute-start | bytes 147464 | tf_op jit(solution)/shard_map/ppermute | solution.py:200
  15.1 5.1 %collective-permute-start.4 = (bf16[32,768]{1,0:T(8,128)(2,1)S(1)}, bf16[32,768]{1,0:T(8,128)(2,1)S(1)}, u32[]{:S(2)}, u32[]{:S(2)}) collective-permute-start(bf16[32,768]{1,0:T(8,128)(2,1)S(1)} %join.1), channel_id=1, source_target_pairs={{0,16},{4,20},{8,24},{12,28},{16,0},{20,4},{24,8},{28,12},{1,17},{... | collective-permute-start | bytes 147464 | tf_op jit(solution)/shard_map/ppermute | solution.py:200
  15.1 5.1 %collective-permute-start.3 = (bf16[32,768]{1,0:T(8,128)(2,1)S(1)}, bf16[32,768]{1,0:T(8,128)(2,1)S(1)}, u32[]{:S(2)}, u32[]{:S(2)}) collective-permute-start(bf16[32,768]{1,0:T(8,128)(2,1)S(1)} %join.1), channel_id=1, source_target_pairs={{0,8},{4,12},{8,0},{12,4},{16,24},{20,28},{24,16},{28,20},{1,9},{5... | collective-permute-start | bytes 147464 | tf_op jit(solution)/shard_map/ppermute | solution.py:200
  20.3 1.5 %collective-permute-start.6 = (bf16[128,768]{1,0:T(8,128)(2,1)S(1)}, bf16[128,768]{1,0:T(8,128)(2,1)S(1)}, u32[]{:S(2)}, u32[]{:S(2)}) collective-permute-start(bf16[128,768]{1,0:T(8,128)(2,1)S(1)} %pad_maximum_fusion.mine_ref), channel_id=1, source_target_pairs={{0,1},{1,0},{2,3},{3,2},{4,5},{5,4},{6,7},{7,6},{8,9},{9,8},{10,11... | collective-permute-start | bytes 589832 | tf_op jit(solution)/shard_map/ppermute | solution.py:200
  21.8 7.9 %collective-permute-start.9 = (bf16[1552,128]{1,0:T(8,128)(2,1)S(1)}, bf16[1552,128]{1,0:T(8,128)(2,1)S(1)}, u32[]{:S(2)}, u32[]{:S(2)}) collective-permute-start(bf16[1552,128]{1,0:T(8,128)(2,1)S(1)} %get-tuple-element.29.refs_1_), channel_id=1, source_target_pairs={{0,4},{1,3},{2,6},{3,1},{4,0},{5,7},{6,2},{7,5},{8,12},{9,11},{10,... | collective-permute-start | bytes 1191944 | tf_op jit(solution)/shard_map/ppermute | solution.py:248
  25.2 16.1 %copy-start.3 = (f32[8,128]{1,0:T(8,128)S(1)}, f32[8,128]{1,0:T(8,128)}, u32[]{:S(2)}) copy-start(f32[8,128]{1,0:T(8,128)} %get-tuple-element.23.resident_ref) | copy-start | bytes 12292
  25.2 21.0 %copy-start = (bf16[1024,768]{1,0:T(8,128)(2,1)S(1)}, bf16[1024,768]{1,0:T(8,128)(2,1)}, u32[]{:S(2)}) copy-start(bf16[1024,768]{1,0:T(8,128)(2,1)} %points_ref.1) | copy-start | bytes 4718596
  25.2 20.9 %copy-start.4 = (s32[1,1024]{1,0:T(1,128)S(1)}, s32[1,1024]{1,0:T(1,128)}, u32[]{:S(2)}) copy-start(s32[1,1024]{1,0:T(1,128)} %get-tuple-element.22.mark_ref) | copy-start | bytes 12292
  30.5 1.9 %collective-permute-start.10 = (f32[128,896]{1,0:T(8,128)S(1)}, f32[128,896]{1,0:T(8,128)S(1)}, u32[]{:S(2)}, u32[]{:S(2)}) collective-permute-start(f32[128,896]{1,0:T(8,128)S(1)} %get-tuple-element.32), channel_id=1, source_target_pairs={{0,1},{1,0},{2,3},{3,2},{4,5},{5,4},{6,7},{7,6},{8,9},{9,8},{10,11... | collective-permute-start | bytes 1376264 | tf_op jit(solution)/shard_map/ppermute | solution.py:200
  32.4 4.5 %collective-permute-start.11 = (bf16[208,128]{1,0:T(8,128)(2,1)S(1)}, bf16[208,128]{1,0:T(8,128)(2,1)S(1)}, u32[]{:S(2)}, u32[]{:S(2)}) collective-permute-start(bf16[208,128]{1,0:T(8,128)(2,1)S(1)} %get-tuple-element.34), channel_id=1, source_target_pairs={{0,8},{4,12},{8,0},{12,4},{16,24},{20,28},{24,16},{28,20},{1,9},{5... | collective-permute-start | bytes 159752 | tf_op jit(solution)/shard_map/ppermute | solution.py:200
  33.8 6.8 %collective-permute-start.12 = (bf16[208,128]{1,0:T(8,128)(2,1)S(1)}, bf16[208,128]{1,0:T(8,128)(2,1)S(1)}, u32[]{:S(2)}, u32[]{:S(2)}) collective-permute-start(bf16[208,128]{1,0:T(8,128)(2,1)S(1)} %get-tuple-element.35), channel_id=1, source_target_pairs={{0,16},{4,20},{8,24},{12,28},{16,0},{20,4},{24,8},{28,12},{1,17},{... | collective-permute-start | bytes 159752 | tf_op jit(solution)/shard_map/ppermute | solution.py:200
  35.3 6.0 %collective-permute-start.13 = (bf16[208,128]{1,0:T(8,128)(2,1)S(1)}, bf16[208,128]{1,0:T(8,128)(2,1)S(1)}, u32[]{:S(2)}, u32[]{:S(2)}) collective-permute-start(bf16[208,128]{1,0:T(8,128)(2,1)S(1)} %get-tuple-element.36), channel_id=1, source_target_pairs={{0,24},{4,28},{8,16},{12,20},{16,8},{20,12},{24,0},{28,4},{1,25},{... | collective-permute-start | bytes 159752 | tf_op jit(solution)/shard_map/ppermute | solution.py:200
  41.4 4.1 %collective-permute-start.16 = (bf16[32,768]{1,0:T(8,128)(2,1)S(1)}, bf16[32,768]{1,0:T(8,128)(2,1)S(1)}, u32[]{:S(2)}, u32[]{:S(2)}) collective-permute-start(bf16[32,768]{1,0:T(8,128)(2,1)S(1)} %scale.1.refs_0_), channel_id=1, source_target_pairs={{0,3},{1,2},{2,1},{3,0},{4,7},{5,6},{6,5},{7,4},{8,11},{9,10},{10,... | collective-permute-start | bytes 147464 | tf_op jit(solution)/shard_map/ppermute | solution.py:200
  41.5 4.7 %collective-permute-start.15 = (bf16[32,768]{1,0:T(8,128)(2,1)S(1)}, bf16[32,768]{1,0:T(8,128)(2,1)S(1)}, u32[]{:S(2)}, u32[]{:S(2)}) collective-permute-start(bf16[32,768]{1,0:T(8,128)(2,1)S(1)} %scale.1.refs_0_), channel_id=1, source_target_pairs={{0,2},{1,3},{2,0},{3,1},{4,6},{5,7},{6,4},{7,5},{8,10},{9,11},{10,... | collective-permute-start | bytes 147464 | tf_op jit(solution)/shard_map/ppermute | solution.py:200
  42.8 3.4 %collective-permute-start.14 = (bf16[32,768]{1,0:T(8,128)(2,1)S(1)}, bf16[32,768]{1,0:T(8,128)(2,1)S(1)}, u32[]{:S(2)}, u32[]{:S(2)}) collective-permute-start(bf16[32,768]{1,0:T(8,128)(2,1)S(1)} %scale.1.refs_0_), channel_id=1, source_target_pairs={{0,1},{1,0},{2,3},{3,2},{4,5},{5,4},{6,7},{7,6},{8,9},{9,8},{10,11... | collective-permute-start | bytes 147464 | tf_op jit(solution)/shard_map/ppermute | solution.py:200
  47.7 5.0 %collective-permute-start.17 = (f32[32,768]{1,0:T(8,128)S(1)}, f32[32,768]{1,0:T(8,128)S(1)}, u32[]{:S(2)}, u32[]{:S(2)}) collective-permute-start(f32[32,768]{1,0:T(8,128)S(1)} %get-tuple-element.39), channel_id=1, source_target_pairs={{0,1},{1,0},{2,3},{3,2},{4,5},{5,4},{6,7},{7,6},{8,9},{9,8},{10,11... | collective-permute-start | bytes 294920 | tf_op jit(solution)/shard_map/ppermute | solution.py:200
  47.8 4.2 %collective-permute-start.18 = (bf16[32,768]{1,0:T(8,128)(2,1)S(1)}, bf16[32,768]{1,0:T(8,128)(2,1)S(1)}, u32[]{:S(2)}, u32[]{:S(2)}) collective-permute-start(bf16[32,768]{1,0:T(8,128)(2,1)S(1)} %get-tuple-element.40), channel_id=1, source_target_pairs={{0,2},{1,3},{2,0},{3,1},{4,6},{5,7},{6,4},{7,5},{8,10},{9,11},{10,... | collective-permute-start | bytes 147464 | tf_op jit(solution)/shard_map/ppermute | solution.py:200
  48.8 3.8 %collective-permute-start.19 = (bf16[32,768]{1,0:T(8,128)(2,1)S(1)}, bf16[32,768]{1,0:T(8,128)(2,1)S(1)}, u32[]{:S(2)}, u32[]{:S(2)}) collective-permute-start(bf16[32,768]{1,0:T(8,128)(2,1)S(1)} %get-tuple-element.41), channel_id=1, source_target_pairs={{0,3},{1,2},{2,1},{3,0},{4,7},{5,6},{6,5},{7,4},{8,11},{9,10},{10,... | collective-permute-start | bytes 147464 | tf_op jit(solution)/shard_map/ppermute | solution.py:200

commit v7 on v6

--- a/solution.py
+++ b/solution.py
@@ -145,33 +145,33 @@
             out[:, width:] = before[part, width:] + named[part]
 
 
-def fold_kernel(planes, mine_ref, theirs_ref, own_ref, *send_refs):
+def fold_kernel(planes, mine_ref, theirs_ref, own_ref, send_ref):
     rank, wide = own_ref.shape
     width = wide - LANES
+    plane = lax.axis_index("shard") // INNER
     line = lax.broadcasted_iota(jnp.int32, (TILE, LANES), 0)
+    send_ref[plane] = jnp.zeros(send_ref.shape[1:], BF16)
     for d in range(planes):
         part = slice(d * rank, (d + 1) * rank)
         total = mine_ref[part, :] + theirs_ref[part, :]
         if d == 0:
             own_ref[...] = total
         else:
-            ref = send_refs[d - 1]
-            for k in range(width // LANES):
-                ref[k * rank : (k + 1) * rank, :] = total[:, k * LANES : (k + 1) * LANES].astype(BF16)
             named = total[:TILE, width:]
             many = jnp.floor(named * (1.0 / 256.0))
-            rest = named - 256.0 * many
-            ref[rank * width // LANES :, :] = jnp.where(line == 0, many, jnp.where(line == 1, rest, 0.0)).astype(BF16)
-
-
-def scale_kernel(resident_ref, own_ref, *refs):
-    *parts, out_ref = refs
+            tile = jnp.where(line == 0, many, jnp.where(line == 1, named - 256.0 * many, 0.0))
+            columns = [total[:, k : k + LANES] for k in range(0, width, LANES)]
+            send_ref[plane ^ d] = jnp.concatenate(columns + [tile], axis=0).astype(BF16)
+
+
+def scale_kernel(resident_ref, own_ref, got_ref, out_ref):
     rank, width = out_ref.shape
     total = own_ref[:, :width]
     queried = own_ref[0:1, width : width + 1]
-    for part in parts:
-        total = total + slabs(part, rank, width).astype(F32)
-        tile = part[rank * width // LANES :, :].astype(F32)
+    for k in range(got_ref.shape[0]):
+        part = got_ref[k].astype(F32)
+        total = total + slabs(part, rank, width)
+        tile = part[rank * width // LANES :, :]
         queried = queried + 256.0 * tile[0:1, 0:1] + tile[1:2, 0:1]
     resident = resident_ref[0:1, 0:1]
     factor = lax.rsqrt((queried + 1.0) * (queried + resident)) * (1.0 / width)
@@ -179,7 +179,8 @@
 
 
 def sketch_kernel(helpers, mark_ref, resident_ref, points_ref, *refs):
-    scaled, sketch_ref, outs = refs[:helpers], refs[helpers], refs[helpers + 1 :]
+    scaled, (sketch_ref, own_ref, send_ref) = refs[:helpers], refs[helpers:]
+    helper = lax.axis_index("help")
     rank, count = sketch_ref.shape
     mark = mark_ref[...]
     points = points_ref[...]
@@ -191,9 +192,11 @@
     rounded = sketch.astype(BF16)
     rows = [jnp.where(mark == d, rounded, jnp.zeros((), BF16)) for d in range(helpers)]
     summed = contract(jnp.concatenate(rows, axis=0), points, ((1,), (0,)))
-    for d, out in enumerate(outs):
+    for d in range(helpers):
         block = summed[d * rank : (d + 1) * rank] * lax.rsqrt(resident_ref[d : d + 1, 0:1])
-        out[...] = block.astype(out.dtype)
+        if d == 0:
+            own_ref[...] = block
+        send_ref[helper ^ d] = (block if d else jnp.zeros_like(block)).astype(BF16)
 
 
 def swap(value, axis, d):
@@ -263,28 +266,33 @@
     folded = pl.pallas_call(
         functools.partial(fold_kernel, planes),
         out_shape=[jax.ShapeDtypeStruct((rank, wide), F32)]
-        + [jax.ShapeDtypeStruct((rank * width // LANES + TILE, LANES), BF16)] * (planes - 1),
+        + [jax.ShapeDtypeStruct((planes, rank * width // LANES + TILE, LANES), BF16)],
         compiler_params=PARAMS,
         name="fold",
     )(moments, swap(passed, "help", 1))
-    moments = [folded[0]] + [swap(folded[d], "shard", INNER * d) for d in range(1, planes)]
+    lines = [[k + INNER * p for p in range(planes)] for k in range(INNER)]
+    got = lax.all_to_all(folded[1], "shard", 0, 0, axis_index_groups=lines, tiled=True)
 
     scaled = pl.pallas_call(
         scale_kernel,
         out_shape=jax.ShapeDtypeStruct((rank, width), BF16),
         compiler_params=PARAMS,
         name="scale",
-    )(resident, *moments)
+    )(resident, folded[0], got)
     scaled = [scaled] + [swap(scaled, "help", d) for d in range(1, helpers)]
 
-    sketch, regressor, *parts = pl.pallas_call(
+    sketch, regressor, parts = pl.pallas_call(
         functools.partial(sketch_kernel, helpers),
-        out_shape=[jax.ShapeDtypeStruct((rank, own_points), F32), block, block] + [sent] * (helpers - 2),
+        out_shape=[
+            jax.ShapeDtypeStruct((rank, own_points), F32),
+            block,
+            jax.ShapeDtypeStruct((helpers, rank, width), BF16),
+        ],
         compiler_params=PARAMS,
         name="sketch",
     )(mark, resident, points, *scaled)
-    for d, part in enumerate(parts, 1):
-        regressor = regressor + swap(part, "help", d).astype(F32)
+    parts = lax.all_to_all(parts, "help", 0, 0, tiled=True)
+    regressor = regressor + jnp.sum(parts.astype(F32), axis=0)
     return sketch, regressor[None]
 
 

time: 53.6 us -> 58.9 us (1.099)
  blocking collectives: 0 us -> 19.1 us
  waiting for transfers between devices: 23 us -> 15.5 us
  starting transfers between devices: 20.8 us -> 14.5 us
    all_to_all x0 -> x2, blocking collectives: none -> 19.1 us  [the longest x1 11.4 us: shards(): lax.all_to_all(folded[1], 'shard', 0, 0, axis_index_groups=lines, tiled=T...]
    ppermute x17 -> x11, waiting for transfers between devices: 18.6 us -> 11.1 us  [swap(): lax.ppermute(value, axis, [(i, i ^ d) for i in range(lax.axis_size(axis))])]
    ppermute x17 -> x11, starting transfers between devices: 16 us -> 9.66 us  [swap(): lax.ppermute(value, axis, [(i, i ^ d) for i in range(lax.axis_size(axis))])]
  transfers between devices with their start and end apart: 20 -> 14, of which waited for: 12 -> 8; matrix products, arithmetic and copies ran while one was open for 0% -> 0% of each run, Pallas kernels for 3% -> 3%
where the time goes in v7:
time: 58.9 us; the launch traced here: 58.6 us
  blocking collectives  19.1 us (32%)
  waiting for transfers between devices  15.5 us (26%)
  starting transfers between devices  14.5 us (25%)
  Pallas kernels  7.07 us (12%)
  local copies, waits for them, and re-layouts  0.91 us (2%)
  between operations  0.75 us (1%)
  other arithmetic  0.7 us (1%)
    all_to_all x1, blocking collectives, shards(): lax.all_to_all(folded[1], 'shard', 0, 0, axis_index_groups=lines, tiled=T...  11.4 us
    ppermute x11, waiting for transfers between devices, swap(): lax.ppermute(value, axis, [(i, i ^ d) for i in range(lax.axis_size(axis))])  11.1 us
    ppermute x11, starting transfers between devices, swap(): lax.ppermute(value, axis, [(i, i ^ d) for i in range(lax.axis_size(axis))])  9.66 us
    all_to_all x1, blocking collectives, shards(): parts = lax.all_to_all(parts, 'help', 0, 0, tiled=True)  7.69 us
    ppermute x1, waiting for transfers between devices, shards(): across = lax.ppermute(near, axes, two)  4.44 us
    ppermute x2, starting transfers between devices, shards(): lax.ppermute(packed, axes, turn)  3.25 us
    pallas_call x1, Pallas kernels, shards(): pl.pallas_call(functools.partial(lift_kernel, helpers), out_shape=[jax.Sh...  2.78 us
    pallas_call x1, Pallas kernels, shards(): pl.pallas_call(functools.partial(score_kernel, planes, helpers, 3), out_s...  1.81 us
  transfers between devices with their start and end apart: 14, of which 8 were waited for; matrix products, arithmetic and copies ran while one was open for 0% of the time, Pallas kernels for 3%

profile of v7, /device:TPU:0, one launch (start us, length us, event | category | flops | bytes accessed | tf_op | source)
XLA Modules:
  0.0 58.6 jit_solution(4201469573041769417)
XLA Ops:
  0.6 2.8 %lift.1 = (bf16[1552,128]{1,0:T(8,128)(2,1)}, s32[1,1024]{1,0:T(1,128)}, f32[8,128]{1,0:T(8,128)}, f32[32,768]{1,0:T(8,128)}, f32[32,768]{1,0:T(8,128)}, /*index...) custom-call(bf16[256,768]{1,0:T(8,128)(2,1)} %refs_0_.1, s32[2,256]{1,0:T(2,128)} %bitcast.4, s32[2,256]{1,0:T(2,128)} %bitcast.5, ...), custom_call_target="tpu_custom_call" | custom-call | tf_op jit(solution)/shard_map/lift/pallas_call | solution.py:216
  3.4 0.0 copy-start.1
  3.4 0.5 collective-permute-start
  3.9 2.6 %collective-permute-start.1 = (bf16[32,768]{1,0:T(8,128)(2,1)}, bf16[32,768]{1,0:T(8,128)(2,1)S(1)}, u32[]{:S(2)}, u32[]{:S(2)}) collective-permute-start(bf16[32,768]{1,0:T(8,128)(2,1)} %get-tuple-element.22), channel_id=1, source_target_pairs={{0,2},{1,3},{2,0},{3,1},{4,6},{5,7},{6,4},{7,5},{8,10},{9,11},{10,... | collective-permute-start | bytes 147464 | tf_op jit(solution)/shard_map/ppermute | solution.py:203
  6.5 0.1 collective-permute-start.2
  6.6 1.8 %collective-permute-start.8 = (bf16[1552,128]{1,0:T(8,128)(2,1)}, bf16[1552,128]{1,0:T(8,128)(2,1)S(1)}, u32[]{:S(2)}, u32[]{:S(2)}) collective-permute-start(bf16[1552,128]{1,0:T(8,128)(2,1)} %get-tuple-element.24.refs_0_), channel_id=1, source_target_pairs={{0,4},{1,3},{2,6},{3,1},{4,0},{5,7},{6,2},{7,5},{8,12},{9,11},{10,... | collective-permute-start | bytes 1191944 | tf_op jit(solution)/shard_map/ppermute | solution.py:250
  8.3 1.5 %collective-permute-start.7 = (bf16[1552,128]{1,0:T(8,128)(2,1)}, bf16[1552,128]{1,0:T(8,128)(2,1)S(1)}, u32[]{:S(2)}, u32[]{:S(2)}) collective-permute-start(bf16[1552,128]{1,0:T(8,128)(2,1)} %get-tuple-element.24.refs_0_), channel_id=1, source_target_pairs={{0,2},{1,5},{2,0},{3,7},{4,6},{5,1},{6,4},{7,3},{8,10},{9,13},{10,... | collective-permute-start | bytes 1191944 | tf_op jit(solution)/shard_map/ppermute | solution.py:250
  9.8 0.0 collective-permute-done.1.refs_2_
  9.8 0.7 %collective-permute-done.2.refs_3_ = bf16[32,768]{1,0:T(8,128)(2,1)S(1)} collective-permute-done((bf16[32,768]{1,0:T(8,128)(2,1)}, bf16[32,768]{1,0:T(8,128)(2,1)S(1)}, u32[]{:S(2)}, u32[]{:S(2)}) %collective-permute-start.2) | collective-permute-done | bytes 49184 | tf_op jit(solution)/shard_map/ppermute | solution.py:203
  10.5 0.0 collective-permute-done.refs_1_
  10.5 0.0 copy-start.2
  10.5 0.9 %copy-done.2 = f32[32,768]{1,0:T(8,128)S(1)} copy-done((f32[32,768]{1,0:T(8,128)S(1)}, f32[32,768]{1,0:T(8,128)}, u32[]{:S(2)}) %copy-start.2) | copy-done | bytes 98328
  11.4 3.7 %collective-permute-start.5 = (bf16[32,768]{1,0:T(8,128)(2,1)S(1)}, bf16[32,768]{1,0:T(8,128)(2,1)S(1)}, u32[]{:S(2)}, u32[]{:S(2)}) collective-permute-start(bf16[32,768]{1,0:T(8,128)(2,1)S(1)} %join.1), channel_id=1, source_target_pairs={{0,24},{4,28},{8,16},{12,20},{16,8},{20,12},{24,0},{28,4},{1,25},{... | collective-permute-start | bytes 147464 | tf_op jit(solution)/shard_map/ppermute | solution.py:203
  15.1 0.0 collective-permute-start.4
  15.1 0.8 %collective-permute-start.3 = (bf16[32,768]{1,0:T(8,128)(2,1)S(1)}, bf16[32,768]{1,0:T(8,128)(2,1)S(1)}, u32[]{:S(2)}, u32[]{:S(2)}) collective-permute-start(bf16[32,768]{1,0:T(8,128)(2,1)S(1)} %join.1), channel_id=1, source_target_pairs={{0,8},{4,12},{8,0},{12,4},{16,24},{20,28},{24,16},{28,20},{1,9},{5... | collective-permute-start | bytes 147464 | tf_op jit(solution)/shard_map/ppermute | solution.py:203
  15.9 1.9 %collective-permute-done.5 = bf16[32,768]{1,0:T(8,128)(2,1)S(1)} collective-permute-done((bf16[32,768]{1,0:T(8,128)(2,1)S(1)}, bf16[32,768]{1,0:T(8,128)(2,1)S(1)}, u32[]{:S(2)}, u32[]{:S(2)}) %collective-permute-start.5) | collective-permute-done | bytes 49184 | tf_op jit(solution)/shard_map/ppermute | solution.py:203
  17.7 2.5 %collective-permute-done.4 = bf16[32,768]{1,0:T(8,128)(2,1)S(1)} collective-permute-done((bf16[32,768]{1,0:T(8,128)(2,1)S(1)}, bf16[32,768]{1,0:T(8,128)(2,1)S(1)}, u32[]{:S(2)}, u32[]{:S(2)}) %collective-permute-start.4) | collective-permute-done | bytes 49184 | tf_op jit(solution)/shard_map/ppermute | solution.py:203
  20.2 0.0 collective-permute-done.3
  20.3 0.1 collective-permute-start.6
  20.3 1.4 %collective-permute-done.6.refs_2_.theirs_ref = bf16[128,768]{1,0:T(8,128)(2,1)S(1)} collective-permute-done((bf16[128,768]{1,0:T(8,128)(2,1)S(1)}, bf16[128,768]{1,0:T(8,128)(2,1)S(1)}, u32[]{:S(2)}, u32[]{:S(2)}) %collective-permute-start.6) | collective-permute-done | bytes 196640 | tf_op jit(solution)/shard_map/ppermute | solution.py:203
  21.8 0.0 collective-permute-done.8.refs_1_
  21.8 0.0 collective-permute-done.7.refs_0_
  21.8 1.6 %collective-permute-start.9 = (bf16[1552,128]{1,0:T(8,128)(2,1)S(1)}, bf16[1552,128]{1,0:T(8,128)(2,1)S(1)}, u32[]{:S(2)}, u32[]{:S(2)}) collective-permute-start(bf16[1552,128]{1,0:T(8,128)(2,1)S(1)} %get-tuple-element.25.refs_1_), channel_id=1, source_target_pairs={{0,4},{1,3},{2,6},{3,1},{4,0},{5,7},{6,2},{7,5},{8,12},{9,11},{10,... | collective-permute-start | bytes 1191944 | tf_op jit(solution)/shard_map/ppermute | solution.py:251
  23.4 0.0 copy-done.1
  23.4 1.8 %score.1.refs_1_ = f32[256,896]{1,0:T(8,128)S(1)} custom-call(bf16[128,768]{1,0:T(8,128)(2,1)S(1)} %pad_maximum_fusion.mine_ref, bf16[128,768]{1,0:T(8,128)(2,1)S(1)} %collective-permute-done.6.refs_2_.theirs_ref, bf16[1552,128]{1,0:T(8,128)(2,1)S(1)} %copy-done.1, bf16[1552,128]{1,0:T(8,128)(2,1)S(1)} %get-tuple-element.25.refs_1_, ...), custom_call_target="tpu_custom_call" | custom-call | tf_op jit(solution)/shard_map/score/pallas_call | solution.py:254
  25.2 0.0 copy-start.3
  25.2 0.0 copy-start
  25.2 0.0 copy-start.4
  25.2 4.4 %collective-permute-done.9.refs_0_ = bf16[1552,128]{1,0:T(8,128)(2,1)S(1)} collective-permute-done((bf16[1552,128]{1,0:T(8,128)(2,1)S(1)}, bf16[1552,128]{1,0:T(8,128)(2,1)S(1)}, u32[]{:S(2)}, u32[]{:S(2)}) %collective-permute-start.9) | collective-permute-done | bytes 397344 | tf_op jit(solution)/shard_map/ppermute | solution.py:251
  29.7 0.8 %score_last.1 = (f32[128,896]{1,0:T(8,128)S(1)}, f32[128,896]{1,0:T(8,128)S(1)}) custom-call(bf16[128,768]{1,0:T(8,128)(2,1)S(1)} %pad_maximum_fusion.mine_ref, bf16[128,768]{1,0:T(8,128)(2,1)S(1)} %collective-permute-done.6.refs_2_.theirs_ref, bf16[1552,128]{1,0:T(8,128)(2,1)S(1)} %collective-permute-done.9.refs_0_, f32[256,896]{1,0:T(8,128)S(1)} %score.1.refs_1_), custom_call_target="tpu_custom_call" | custom-call | tf_op jit(solution)/shard_map/score_last/pallas_call | solution.py:260
  30.5 0.1 collective-permute-start.10
  30.5 1.8 %collective-permute-done.10.theirs_ref = f32[128,896]{1,0:T(8,128)S(1)} collective-permute-done((f32[128,896]{1,0:T(8,128)S(1)}, f32[128,896]{1,0:T(8,128)S(1)}, u32[]{:S(2)}, u32[]{:S(2)}) %collective-permute-start.10) | collective-permute-done | bytes 458784 | tf_op jit(solution)/shard_map/ppermute | solution.py:203
  32.4 11.4 %all_to_all.10.got_ref = bf16[4,208,128]{2,1,0:T(8,128)(2,1)S(1)} all-to-all(bf16[4,208,128]{2,1,0:T(8,128)(2,1)S(1)} %get-tuple-element.30), channel_id=1, replica_groups={{0,8,16,24},{4,12,20,28},{1,9,17,25},{5,13,21,29},{2,10,18,26},{6,14,22..., dimensions={0} | all-to-all | bytes 425984 | tf_op jit(solution)/shard_map/all_to_all | solution.py:274
  43.8 0.0 copy-done.3
  43.8 0.1 scale.1.refs_0_
  43.9 0.1 collective-permute-start.13
  44.0 1.3 %collective-permute-start.12 = (bf16[32,768]{1,0:T(8,128)(2,1)S(1)}, bf16[32,768]{1,0:T(8,128)(2,1)S(1)}, u32[]{:S(2)}, u32[]{:S(2)}) collective-permute-start(bf16[32,768]{1,0:T(8,128)(2,1)S(1)} %scale.1.refs_0_), channel_id=1, source_target_pairs={{0,2},{1,3},{2,0},{3,1},{4,6},{5,7},{6,4},{7,5},{8,10},{9,11},{10,... | collective-permute-start | bytes 147464 | tf_op jit(solution)/shard_map/ppermute | solution.py:203
  45.3 0.5 collective-permute-start.11
  45.8 2.2 %collective-permute-done.13.refs_3_ = bf16[32,768]{1,0:T(8,128)(2,1)S(1)} collective-permute-done((bf16[32,768]{1,0:T(8,128)(2,1)S(1)}, bf16[32,768]{1,0:T(8,128)(2,1)S(1)}, u32[]{:S(2)}, u32[]{:S(2)}) %collective-permute-start.13) | collective-permute-done | bytes 49184 | tf_op jit(solution)/shard_map/ppermute | solution.py:203
  48.0 0.7 %collective-permute-done.12.refs_2_ = bf16[32,768]{1,0:T(8,128)(2,1)S(1)} collective-permute-done((bf16[32,768]{1,0:T(8,128)(2,1)S(1)}, bf16[32,768]{1,0:T(8,128)(2,1)S(1)}, u32[]{:S(2)}, u32[]{:S(2)}) %collective-permute-start.12) | collective-permute-done | bytes 49184 | tf_op jit(solution)/shard_map/ppermute | solution.py:203
  48.7 0.0 collective-permute-done.11.refs_1_
  48.7 0.0 copy-done
  48.7 0.0 copy-done.4
  48.7 1.5 %sketch.1 = (f32[32,1024]{1,0:T(8,128)}, f32[32,768]{1,0:T(8,128)S(1)}, bf16[4,32,768]{2,1,0:T(8,128)(2,1)S(1)}) custom-call(s32[1,1024]{1,0:T(1,128)S(1)} %copy-done.4, f32[8,128]{1,0:T(8,128)S(1)} %copy-done.3, bf16[1024,768]{1,0:T(8,128)(2,1)S(1)} %copy-done, bf16[32,768]{1,0:T(8,128)(2,1)S(1)} %scale.1.refs_0_, ...), custom_call_target="tpu_custom_call" | custom-call | tf_op jit(solution)/shard_map/sketch/pallas_call | solution.py:284
  50.2 7.7 %all_to_all.11 = bf16[4,32,768]{2,1,0:T(8,128)(2,1)S(1)} all-to-all(bf16[4,32,768]{2,1,0:T(8,128)(2,1)S(1)} %get-tuple-element.33), channel_id=1, replica_groups=mesh['shard'=8,'help'=4] {'help'}, dimensions={0} | all-to-all | bytes 393216 | tf_op jit(solution)/shard_map/all_to_all | solution.py:294
  57.9 0.7 %add_bitcast_fusion = f32[1,32,768]{2,1,0:T(8,128)} fusion(f32[32,768]{1,0:T(8,128)S(1)} %get-tuple-element.32, f32[32,768]{1,0:T(8,128)S(1)} %convert_reduce_fusion), kind=kLoop, calls=%fused_computation.2 | loop fusion | flops 24576 | bytes 294912 | tf_op jit(solution)/shard_map/broadcast_in_dim | solution.py:296
  (5 shorter events, 0.1 us)
Async XLA Ops:
  3.4 19.9 %copy-start.1 = (bf16[1552,128]{1,0:T(8,128)(2,1)S(1)}, bf16[1552,128]{1,0:T(8,128)(2,1)}, u32[]{:S(2)}) copy-start(bf16[1552,128]{1,0:T(8,128)(2,1)} %get-tuple-element.24.refs_0_) | copy-start | bytes 1191940
  3.4 7.1 %collective-permute-start = (f32[32,768]{1,0:T(8,128)}, f32[32,768]{1,0:T(8,128)S(1)}, u32[]{:S(2)}, u32[]{:S(2)}) collective-permute-start(f32[32,768]{1,0:T(8,128)} %get-tuple-element.21), channel_id=1, source_target_pairs={{0,1},{1,0},{2,3},{3,2},{4,5},{5,4},{6,7},{7,6},{8,9},{9,8},{10,11... | collective-permute-start | bytes 294920 | tf_op jit(solution)/shard_map/ppermute | solution.py:203
  3.9 5.9 %collective-permute-start.1 = (bf16[32,768]{1,0:T(8,128)(2,1)}, bf16[32,768]{1,0:T(8,128)(2,1)S(1)}, u32[]{:S(2)}, u32[]{:S(2)}) collective-permute-start(bf16[32,768]{1,0:T(8,128)(2,1)} %get-tuple-element.22), channel_id=1, source_target_pairs={{0,2},{1,3},{2,0},{3,1},{4,6},{5,7},{6,4},{7,5},{8,10},{9,11},{10,... | collective-permute-start | bytes 147464 | tf_op jit(solution)/shard_map/ppermute | solution.py:203
  6.5 4.0 %collective-permute-start.2 = (bf16[32,768]{1,0:T(8,128)(2,1)}, bf16[32,768]{1,0:T(8,128)(2,1)S(1)}, u32[]{:S(2)}, u32[]{:S(2)}) collective-permute-start(bf16[32,768]{1,0:T(8,128)(2,1)} %get-tuple-element.23), channel_id=1, source_target_pairs={{0,3},{1,2},{2,1},{3,0},{4,7},{5,6},{6,5},{7,4},{8,11},{9,10},{10,... | collective-permute-start | bytes 147464 | tf_op jit(solution)/shard_map/ppermute | solution.py:203
  6.6 15.2 %collective-permute-start.8 = (bf16[1552,128]{1,0:T(8,128)(2,1)}, bf16[1552,128]{1,0:T(8,128)(2,1)S(1)}, u32[]{:S(2)}, u32[]{:S(2)}) collective-permute-start(bf16[1552,128]{1,0:T(8,128)(2,1)} %get-tuple-element.24.refs_0_), channel_id=1, source_target_pairs={{0,4},{1,3},{2,6},{3,1},{4,0},{5,7},{6,2},{7,5},{8,12},{9,11},{10,... | collective-permute-start | bytes 1191944 | tf_op jit(solution)/shard_map/ppermute | solution.py:250
  8.3 13.4 %collective-permute-start.7 = (bf16[1552,128]{1,0:T(8,128)(2,1)}, bf16[1552,128]{1,0:T(8,128)(2,1)S(1)}, u32[]{:S(2)}, u32[]{:S(2)}) collective-permute-start(bf16[1552,128]{1,0:T(8,128)(2,1)} %get-tuple-element.24.refs_0_), channel_id=1, source_target_pairs={{0,2},{1,5},{2,0},{3,7},{4,6},{5,1},{6,4},{7,3},{8,10},{9,13},{10,... | collective-permute-start | bytes 1191944 | tf_op jit(solution)/shard_map/ppermute | solution.py:250
  10.5 0.9 %copy-start.2 = (f32[32,768]{1,0:T(8,128)S(1)}, f32[32,768]{1,0:T(8,128)}, u32[]{:S(2)}) copy-start(f32[32,768]{1,0:T(8,128)} %get-tuple-element.20.refs_0_) | copy-start | bytes 294916
  11.4 6.3 %collective-permute-start.5 = (bf16[32,768]{1,0:T(8,128)(2,1)S(1)}, bf16[32,768]{1,0:T(8,128)(2,1)S(1)}, u32[]{:S(2)}, u32[]{:S(2)}) collective-permute-start(bf16[32,768]{1,0:T(8,128)(2,1)S(1)} %join.1), channel_id=1, source_target_pairs={{0,24},{4,28},{8,16},{12,20},{16,8},{20,12},{24,0},{28,4},{1,25},{... | collective-permute-start | bytes 147464 | tf_op jit(solution)/shard_map/ppermute | solution.py:203
  15.1 5.1 %collective-permute-start.4 = (bf16[32,768]{1,0:T(8,128)(2,1)S(1)}, bf16[32,768]{1,0:T(8,128)(2,1)S(1)}, u32[]{:S(2)}, u32[]{:S(2)}) collective-permute-start(bf16[32,768]{1,0:T(8,128)(2,1)S(1)} %join.1), channel_id=1, source_target_pairs={{0,16},{4,20},{8,24},{12,28},{16,0},{20,4},{24,8},{28,12},{1,17},{... | collective-permute-start | bytes 147464 | tf_op jit(solution)/shard_map/ppermute | solution.py:203
  15.1 5.1 %collective-permute-start.3 = (bf16[32,768]{1,0:T(8,128)(2,1)S(1)}, bf16[32,768]{1,0:T(8,128)(2,1)S(1)}, u32[]{:S(2)}, u32[]{:S(2)}) collective-permute-start(bf16[32,768]{1,0:T(8,128)(2,1)S(1)} %join.1), channel_id=1, source_target_pairs={{0,8},{4,12},{8,0},{12,4},{16,24},{20,28},{24,16},{28,20},{1,9},{5... | collective-permute-start | bytes 147464 | tf_op jit(solution)/shard_map/ppermute | solution.py:203
  20.3 1.5 %collective-permute-start.6 = (bf16[128,768]{1,0:T(8,128)(2,1)S(1)}, bf16[128,768]{1,0:T(8,128)(2,1)S(1)}, u32[]{:S(2)}, u32[]{:S(2)}) collective-permute-start(bf16[128,768]{1,0:T(8,128)(2,1)S(1)} %pad_maximum_fusion.mine_ref), channel_id=1, source_target_pairs={{0,1},{1,0},{2,3},{3,2},{4,5},{5,4},{6,7},{7,6},{8,9},{9,8},{10,11... | collective-permute-start | bytes 589832 | tf_op jit(solution)/shard_map/ppermute | solution.py:203
  21.8 7.9 %collective-permute-start.9 = (bf16[1552,128]{1,0:T(8,128)(2,1)S(1)}, bf16[1552,128]{1,0:T(8,128)(2,1)S(1)}, u32[]{:S(2)}, u32[]{:S(2)}) collective-permute-start(bf16[1552,128]{1,0:T(8,128)(2,1)S(1)} %get-tuple-element.25.refs_1_), channel_id=1, source_target_pairs={{0,4},{1,3},{2,6},{3,1},{4,0},{5,7},{6,2},{7,5},{8,12},{9,11},{10,... | collective-permute-start | bytes 1191944 | tf_op jit(solution)/shard_map/ppermute | solution.py:251
  25.2 18.6 %copy-start.3 = (f32[8,128]{1,0:T(8,128)S(1)}, f32[8,128]{1,0:T(8,128)}, u32[]{:S(2)}) copy-start(f32[8,128]{1,0:T(8,128)} %get-tuple-element.19.resident_ref) | copy-start | bytes 12292
  25.2 23.5 %copy-start = (bf16[1024,768]{1,0:T(8,128)(2,1)S(1)}, bf16[1024,768]{1,0:T(8,128)(2,1)}, u32[]{:S(2)}) copy-start(bf16[1024,768]{1,0:T(8,128)(2,1)} %points_ref.1) | copy-start | bytes 4718596
  25.2 23.5 %copy-start.4 = (s32[1,1024]{1,0:T(1,128)S(1)}, s32[1,1024]{1,0:T(1,128)}, u32[]{:S(2)}) copy-start(s32[1,1024]{1,0:T(1,128)} %get-tuple-element.18.mark_ref) | copy-start | bytes 12292
  30.5 1.9 %collective-permute-start.10 = (f32[128,896]{1,0:T(8,128)S(1)}, f32[128,896]{1,0:T(8,128)S(1)}, u32[]{:S(2)}, u32[]{:S(2)}) collective-permute-start(f32[128,896]{1,0:T(8,128)S(1)} %get-tuple-element.28), channel_id=1, source_target_pairs={{0,1},{1,0},{2,3},{3,2},{4,5},{5,4},{6,7},{7,6},{8,9},{9,8},{10,11... | collective-permute-start | bytes 1376264 | tf_op jit(solution)/shard_map/ppermute | solution.py:203
  43.9 4.1 %collective-permute-start.13 = (bf16[32,768]{1,0:T(8,128)(2,1)S(1)}, bf16[32,768]{1,0:T(8,128)(2,1)S(1)}, u32[]{:S(2)}, u32[]{:S(2)}) collective-permute-start(bf16[32,768]{1,0:T(8,128)(2,1)S(1)} %scale.1.refs_0_), channel_id=1, source_target_pairs={{0,3},{1,2},{2,1},{3,0},{4,7},{5,6},{6,5},{7,4},{8,11},{9,10},{10,... | collective-permute-start | bytes 147464 | tf_op jit(solution)/shard_map/ppermute | solution.py:203
  44.0 4.7 %collective-permute-start.12 = (bf16[32,768]{1,0:T(8,128)(2,1)S(1)}, bf16[32,768]{1,0:T(8,128)(2,1)S(1)}, u32[]{:S(2)}, u32[]{:S(2)}) collective-permute-start(bf16[32,768]{1,0:T(8,128)(2,1)S(1)} %scale.1.refs_0_), channel_id=1, source_target_pairs={{0,2},{1,3},{2,0},{3,1},{4,6},{5,7},{6,4},{7,5},{8,10},{9,11},{10,... | collective-permute-start | bytes 147464 | tf_op jit(solution)/shard_map/ppermute | solution.py:203
  45.3 3.4 %collective-permute-start.11 = (bf16[32,768]{1,0:T(8,128)(2,1)S(1)}, bf16[32,768]{1,0:T(8,128)(2,1)S(1)}, u32[]{:S(2)}, u32[]{:S(2)}) collective-permute-start(bf16[32,768]{1,0:T(8,128)(2,1)S(1)} %scale.1.refs_0_), channel_id=1, source_target_pairs={{0,1},{1,0},{2,3},{3,2},{4,5},{5,4},{6,7},{7,6},{8,9},{9,8},{10,11... | collective-permute-start | bytes 147464 | tf_op jit(solution)/shard_map/ppermute | solution.py:203

commit v8 on v6

--- a/solution.py
+++ b/solution.py
@@ -13,12 +13,16 @@
 TILE = 16
 CHUNKS = 4
 INNER = 2
-FIRST = 60
 
 ANY = pl.BlockSpec(memory_space=pl.ANY)
+VMEM = pl.BlockSpec(memory_space=pltpu.VMEM)
 VMEM = pl.BlockSpec(memory_space=pltpu.VMEM)
 HBM = pl.BlockSpec(memory_space=pltpu.HBM)
 PARAMS = pltpu.CompilerParams(vmem_limit_bytes=32 * 1024 * 1024)
+
+
+def in_hbm(value):
+    return pltpu.with_memory_space_constraint(value, pltpu.HBM)
 
 
 def contract(a, b, dims):
@@ -179,7 +183,8 @@
 
 
 def sketch_kernel(helpers, mark_ref, resident_ref, points_ref, *refs):
-    scaled, sketch_ref, outs = refs[:helpers], refs[helpers], refs[helpers + 1 :]
+    scaled, sketch_hbm, outs = refs[:helpers], refs[helpers], refs[helpers + 1 : -2]
+    sketch_ref, sem = refs[-2:]
     rank, count = sketch_ref.shape
     mark = mark_ref[...]
     points = points_ref[...]
@@ -188,16 +193,23 @@
     for d in range(1, helpers):
         sketch = jnp.where(mark == d, product[d * rank : (d + 1) * rank], sketch)
     sketch_ref[...] = sketch
+    leaving = pltpu.make_async_copy(sketch_ref, sketch_hbm, sem)
+    leaving.start()
     rounded = sketch.astype(BF16)
     rows = [jnp.where(mark == d, rounded, jnp.zeros((), BF16)) for d in range(helpers)]
     summed = contract(jnp.concatenate(rows, axis=0), points, ((1,), (0,)))
     for d, out in enumerate(outs):
         block = summed[d * rank : (d + 1) * rank] * lax.rsqrt(resident_ref[d : d + 1, 0:1])
         out[...] = block.astype(out.dtype)
+    leaving.wait()
 
 
 def swap(value, axis, d):
     return lax.ppermute(value, axis, [(i, i ^ d) for i in range(lax.axis_size(axis))])
+
+
+def swaps(values, axis, unit=1):
+    return [swap(value, axis, unit * d) for d, value in reversed([*enumerate(values, 1)])]
 
 
 def shards(queries, probe_group, probe_local, points, point_cluster, test_matrix):
@@ -229,15 +241,15 @@
             pltpu.VMEM(points.shape, BF16),
             pltpu.SemaphoreType.DMA((4 + CHUNKS + width // LANES,)),
         ],
-        compiler_params=pltpu.CompilerParams(vmem_limit_bytes=FIRST << 20),
+        compiler_params=PARAMS,
         name="lift",
-    )(queries, probe_group.T, probe_local.T, point_cluster, test_matrix, points)
+    )(*[in_hbm(a) for a in (queries, probe_group.T, probe_local.T, point_cluster, test_matrix, points)])
     lifter = pl.pallas_call(
         join_kernel,
         out_shape=sent,
         compiler_params=PARAMS,
         name="join",
-    )(own, *[swap(part, "help", d) for d, part in enumerate(parts, 1)])
+    )(own, *swaps(parts, "help"))
     mine = jnp.concatenate([lifter] + [swap(lifter, "shard", INNER * d) for d in range(1, planes)], axis=0)
     theirs = swap(mine, "help", 1)
 
@@ -267,7 +279,7 @@
         compiler_params=PARAMS,
         name="fold",
     )(moments, swap(passed, "help", 1))
-    moments = [folded[0]] + [swap(folded[d], "shard", INNER * d) for d in range(1, planes)]
+    moments = [folded[0]] + swaps(folded[1:], "shard", INNER)
 
     scaled = pl.pallas_call(
         scale_kernel,
@@ -280,11 +292,13 @@
     sketch, regressor, *parts = pl.pallas_call(
         functools.partial(sketch_kernel, helpers),
         out_shape=[jax.ShapeDtypeStruct((rank, own_points), F32), block, block] + [sent] * (helpers - 2),
+        out_specs=[HBM] + [VMEM] * helpers,
+        scratch_shapes=[pltpu.VMEM((rank, own_points), F32), pltpu.SemaphoreType.DMA],
         compiler_params=PARAMS,
         name="sketch",
     )(mark, resident, points, *scaled)
-    for d, part in enumerate(parts, 1):
-        regressor = regressor + swap(part, "help", d).astype(F32)
+    for part in swaps(parts, "help"):
+        regressor = regressor + part.astype(F32)
     return sketch, regressor[None]
 
 

time: 53.6 us -> 52.2 us (0.974)
  local copies, waits for them, and re-layouts: 0.91 us -> 0.01 us
  Pallas kernels: 7.11 us -> 6.22 us
  starting transfers between devices: 20.8 us -> 21.5 us
    unnamed x10 -> x2, local copies, waits for them, and re-layouts: 0.91 us -> 0.01 us
    pallas_call x1, Pallas kernels: 2.8 us -> 1.92 us  [shards(): pl.pallas_call(functools.partial(lift_kernel, helpers), out_shape=[jax.Sh...]
  transfers between devices with their start and end apart: 20 -> 20, of which waited for: 12 -> 12; matrix products, arithmetic and copies ran while one was open for 0% -> 0% of each run, Pallas kernels for 3% -> 4%
where the time goes in v8:
time: 52.2 us; the launch traced here: 52 us
  waiting for transfers between devices  22.9 us (44%)
  starting transfers between devices  21.5 us (41%)
  Pallas kernels  6.22 us (12%)
  between operations  0.72 us (1%)
  other arithmetic  0.68 us (1%)
    ppermute x17, waiting for transfers between devices, swap(): lax.ppermute(value, axis, [(i, i ^ d) for i in range(lax.axis_size(axis))])  18.4 us
    ppermute x17, starting transfers between devices, swap(): lax.ppermute(value, axis, [(i, i ^ d) for i in range(lax.axis_size(axis))])  16.4 us
    ppermute x1, waiting for transfers between devices, shards(): across = lax.ppermute(near, axes, two)  4.47 us
    ppermute x2, starting transfers between devices, shards(): lax.ppermute(packed, axes, turn)  3.5 us
    pallas_call x1, Pallas kernels, shards(): pl.pallas_call(functools.partial(lift_kernel, helpers), out_shape=[jax.Sh...  1.92 us
    pallas_call x1, Pallas kernels, shards(): pl.pallas_call(functools.partial(score_kernel, planes, helpers, 3), out_s...  1.81 us
    ppermute x1, starting transfers between devices, shards(): across = lax.ppermute(near, axes, two)  1.58 us
    pallas_call x1, Pallas kernels, shards(): pl.pallas_call(functools.partial(sketch_kernel, helpers), out_shape=[jax....  1.53 us
  transfers between devices with their start and end apart: 20, of which 12 were waited for; matrix products, arithmetic and copies ran while one was open for 0% of the time, Pallas kernels for 4%

profile of v8, /device:TPU:0, one launch (start us, length us, event | category | flops | bytes accessed | tf_op | source)
XLA Modules:
  0.0 52.0 jit_solution(13301472422775729973)
XLA Ops:
  0.6 1.9 %lift.1 = (bf16[1552,128]{1,0:T(8,128)(2,1)S(1)}, s32[1,1024]{1,0:T(1,128)S(1)}, f32[8,128]{1,0:T(8,128)S(1)}, f32[32,768]{1,0:T(8,128)S(1)}, f32[32,768]{1,0:T(...) custom-call(bf16[256,768]{1,0:T(8,128)(2,1)} %refs_0_.1, s32[2,256]{1,0:T(2,128)} %bitcast.4, ...), custom_call_target="tpu_custom_call" | custom-call | tf_op jit(solution)/shard_map/lift/pallas_call | solution.py:225
  2.6 0.5 %collective-permute-start.2 = (f32[32,768]{1,0:T(8,128)S(1)}, f32[32,768]{1,0:T(8,128)S(1)}, u32[]{:S(2)}, u32[]{:S(2)}) collective-permute-start(f32[32,768]{1,0:T(8,128)S(1)} %get-tuple-element.27), channel_id=1, source_target_pairs={{0,1},{1,0},{2,3},{3,2},{4,5},{5,4},{6,7},{7,6},{8,9},{9,8},{10,11... | collective-permute-start | bytes 294920 | tf_op jit(solution)/shard_map/ppermute | solution.py:208
  3.1 2.6 %collective-permute-start = (bf16[32,768]{1,0:T(8,128)(2,1)S(1)}, bf16[32,768]{1,0:T(8,128)(2,1)S(1)}, u32[]{:S(2)}, u32[]{:S(2)}) collective-permute-start(bf16[32,768]{1,0:T(8,128)(2,1)S(1)} %get-tuple-element.25), channel_id=1, source_target_pairs={{0,3},{1,2},{2,1},{3,0},{4,7},{5,6},{6,5},{7,4},{8,11},{9,10},{10,... | collective-permute-start | bytes 147464 | tf_op jit(solution)/shard_map/ppermute | solution.py:208
  5.7 0.0 collective-permute-start.1
  5.7 2.0 %collective-permute-start.8 = (bf16[1552,128]{1,0:T(8,128)(2,1)S(1)}, bf16[1552,128]{1,0:T(8,128)(2,1)S(1)}, u32[]{:S(2)}, u32[]{:S(2)}) collective-permute-start(bf16[1552,128]{1,0:T(8,128)(2,1)S(1)} %get-tuple-element.28.refs_0_), channel_id=1, source_target_pairs={{0,4},{1,3},{2,6},{3,1},{4,0},{5,7},{6,2},{7,5},{8,12},{9,11},{10,... | collective-permute-start | bytes 1191944 | tf_op jit(solution)/shard_map/ppermute | solution.py:259
  7.7 1.5 %collective-permute-start.7 = (bf16[1552,128]{1,0:T(8,128)(2,1)S(1)}, bf16[1552,128]{1,0:T(8,128)(2,1)S(1)}, u32[]{:S(2)}, u32[]{:S(2)}) collective-permute-start(bf16[1552,128]{1,0:T(8,128)(2,1)S(1)} %get-tuple-element.28.refs_0_), channel_id=1, source_target_pairs={{0,2},{1,5},{2,0},{3,7},{4,6},{5,1},{6,4},{7,3},{8,10},{9,13},{10,... | collective-permute-start | bytes 1191944 | tf_op jit(solution)/shard_map/ppermute | solution.py:259
  9.2 0.0 collective-permute-done.refs_1_
  9.2 1.1 %collective-permute-done.1.refs_2_ = bf16[32,768]{1,0:T(8,128)(2,1)S(1)} collective-permute-done((bf16[32,768]{1,0:T(8,128)(2,1)S(1)}, bf16[32,768]{1,0:T(8,128)(2,1)S(1)}, u32[]{:S(2)}, u32[]{:S(2)}) %collective-permute-start.1) | collective-permute-done | bytes 49184 | tf_op jit(solution)/shard_map/ppermute | solution.py:208
  10.3 0.0 collective-permute-done.2.refs_3_
  10.3 3.7 %collective-permute-start.5 = (bf16[32,768]{1,0:T(8,128)(2,1)S(1)}, bf16[32,768]{1,0:T(8,128)(2,1)S(1)}, u32[]{:S(2)}, u32[]{:S(2)}) collective-permute-start(bf16[32,768]{1,0:T(8,128)(2,1)S(1)} %join.1), channel_id=1, source_target_pairs={{0,24},{4,28},{8,16},{12,20},{16,8},{20,12},{24,0},{28,4},{1,25},{... | collective-permute-start | bytes 147464 | tf_op jit(solution)/shard_map/ppermute | solution.py:208
  14.0 0.0 collective-permute-start.4
  14.0 0.8 %collective-permute-start.3 = (bf16[32,768]{1,0:T(8,128)(2,1)S(1)}, bf16[32,768]{1,0:T(8,128)(2,1)S(1)}, u32[]{:S(2)}, u32[]{:S(2)}) collective-permute-start(bf16[32,768]{1,0:T(8,128)(2,1)S(1)} %join.1), channel_id=1, source_target_pairs={{0,8},{4,12},{8,0},{12,4},{16,24},{20,28},{24,16},{28,20},{1,9},{5... | collective-permute-start | bytes 147464 | tf_op jit(solution)/shard_map/ppermute | solution.py:208
  14.8 1.6 %collective-permute-done.5 = bf16[32,768]{1,0:T(8,128)(2,1)S(1)} collective-permute-done((bf16[32,768]{1,0:T(8,128)(2,1)S(1)}, bf16[32,768]{1,0:T(8,128)(2,1)S(1)}, u32[]{:S(2)}, u32[]{:S(2)}) %collective-permute-start.5) | collective-permute-done | bytes 49184 | tf_op jit(solution)/shard_map/ppermute | solution.py:208
  16.4 2.6 %collective-permute-done.4 = bf16[32,768]{1,0:T(8,128)(2,1)S(1)} collective-permute-done((bf16[32,768]{1,0:T(8,128)(2,1)S(1)}, bf16[32,768]{1,0:T(8,128)(2,1)S(1)}, u32[]{:S(2)}, u32[]{:S(2)}) %collective-permute-start.4) | collective-permute-done | bytes 49184 | tf_op jit(solution)/shard_map/ppermute | solution.py:208
  19.0 0.0 collective-permute-done.3
  19.0 0.1 collective-permute-start.6
  19.1 1.4 %collective-permute-done.6.refs_2_.theirs_ref = bf16[128,768]{1,0:T(8,128)(2,1)S(1)} collective-permute-done((bf16[128,768]{1,0:T(8,128)(2,1)S(1)}, bf16[128,768]{1,0:T(8,128)(2,1)S(1)}, u32[]{:S(2)}, u32[]{:S(2)}) %collective-permute-start.6) | collective-permute-done | bytes 196640 | tf_op jit(solution)/shard_map/ppermute | solution.py:208
  20.5 0.0 collective-permute-done.8.refs_1_
  20.5 0.0 collective-permute-done.7.refs_0_
  20.5 1.6 %collective-permute-start.9 = (bf16[1552,128]{1,0:T(8,128)(2,1)S(1)}, bf16[1552,128]{1,0:T(8,128)(2,1)S(1)}, u32[]{:S(2)}, u32[]{:S(2)}) collective-permute-start(bf16[1552,128]{1,0:T(8,128)(2,1)S(1)} %get-tuple-element.29.refs_1_), channel_id=1, source_target_pairs={{0,4},{1,3},{2,6},{3,1},{4,0},{5,7},{6,2},{7,5},{8,12},{9,11},{10,... | collective-permute-start | bytes 1191944 | tf_op jit(solution)/shard_map/ppermute | solution.py:260
  22.1 1.8 %score.1.refs_1_ = f32[256,896]{1,0:T(8,128)S(1)} custom-call(bf16[128,768]{1,0:T(8,128)(2,1)S(1)} %pad_maximum_fusion.mine_ref, bf16[128,768]{1,0:T(8,128)(2,1)S(1)} %collective-permute-done.6.refs_2_.theirs_ref, bf16[1552,128]{1,0:T(8,128)(2,1)S(1)} %get-tuple-element.28.refs_0_, bf16[1552,128]{1,0:T(8,128)(2,1)S(1)} %get-tuple-element.29.refs_1_, ...), custom_call_target="tpu_custom_call" | custom-call | tf_op jit(solution)/shard_map/score/pallas_call | solution.py:263
  23.9 0.0 copy-start
  23.9 4.5 %collective-permute-done.9.refs_0_ = bf16[1552,128]{1,0:T(8,128)(2,1)S(1)} collective-permute-done((bf16[1552,128]{1,0:T(8,128)(2,1)S(1)}, bf16[1552,128]{1,0:T(8,128)(2,1)S(1)}, u32[]{:S(2)}, u32[]{:S(2)}) %collective-permute-start.9) | collective-permute-done | bytes 397344 | tf_op jit(solution)/shard_map/ppermute | solution.py:260
  28.4 0.8 %score_last.1 = (f32[128,896]{1,0:T(8,128)S(1)}, f32[128,896]{1,0:T(8,128)S(1)}) custom-call(bf16[128,768]{1,0:T(8,128)(2,1)S(1)} %pad_maximum_fusion.mine_ref, bf16[128,768]{1,0:T(8,128)(2,1)S(1)} %collective-permute-done.6.refs_2_.theirs_ref, bf16[1552,128]{1,0:T(8,128)(2,1)S(1)} %collective-permute-done.9.refs_0_, f32[256,896]{1,0:T(8,128)S(1)} %score.1.refs_1_), custom_call_target="tpu_custom_call" | custom-call | tf_op jit(solution)/shard_map/score_last/pallas_call | solution.py:269
  29.2 0.1 collective-permute-start.10
  29.3 1.8 %collective-permute-done.10.theirs_ref = f32[128,896]{1,0:T(8,128)S(1)} collective-permute-done((f32[128,896]{1,0:T(8,128)S(1)}, f32[128,896]{1,0:T(8,128)S(1)}, u32[]{:S(2)}, u32[]{:S(2)}) %collective-permute-start.10) | collective-permute-done | bytes 458784 | tf_op jit(solution)/shard_map/ppermute | solution.py:208
  31.1 0.1 fold.1
  31.2 1.5 %collective-permute-start.11 = (bf16[208,128]{1,0:T(8,128)(2,1)S(1)}, bf16[208,128]{1,0:T(8,128)(2,1)S(1)}, u32[]{:S(2)}, u32[]{:S(2)}) collective-permute-start(bf16[208,128]{1,0:T(8,128)(2,1)S(1)} %get-tuple-element.34), channel_id=1, source_target_pairs={{0,24},{4,28},{8,16},{12,20},{16,8},{20,12},{24,0},{28,4},{1,25},{... | collective-permute-start | bytes 159752 | tf_op jit(solution)/shard_map/ppermute | solution.py:208
  32.7 0.6 %collective-permute-start.12 = (bf16[208,128]{1,0:T(8,128)(2,1)S(1)}, bf16[208,128]{1,0:T(8,128)(2,1)S(1)}, u32[]{:S(2)}, u32[]{:S(2)}) collective-permute-start(bf16[208,128]{1,0:T(8,128)(2,1)S(1)} %get-tuple-element.35), channel_id=1, source_target_pairs={{0,16},{4,20},{8,24},{12,28},{16,0},{20,4},{24,8},{28,12},{1,17},{... | collective-permute-start | bytes 159752 | tf_op jit(solution)/shard_map/ppermute | solution.py:208
  33.3 2.3 %collective-permute-start.13 = (bf16[208,128]{1,0:T(8,128)(2,1)S(1)}, bf16[208,128]{1,0:T(8,128)(2,1)S(1)}, u32[]{:S(2)}, u32[]{:S(2)}) collective-permute-start(bf16[208,128]{1,0:T(8,128)(2,1)S(1)} %get-tuple-element.36), channel_id=1, source_target_pairs={{0,8},{4,12},{8,0},{12,4},{16,24},{20,28},{24,16},{28,20},{1,9},{5... | collective-permute-start | bytes 159752 | tf_op jit(solution)/shard_map/ppermute | solution.py:208
  35.6 2.1 %collective-permute-done.11.refs_0_ = bf16[208,128]{1,0:T(8,128)(2,1)S(1)} collective-permute-done((bf16[208,128]{1,0:T(8,128)(2,1)S(1)}, bf16[208,128]{1,0:T(8,128)(2,1)S(1)}, u32[]{:S(2)}, u32[]{:S(2)}) %collective-permute-start.11) | collective-permute-done | bytes 53280 | tf_op jit(solution)/shard_map/ppermute | solution.py:208
  37.7 1.5 %collective-permute-done.12.refs_1_ = bf16[208,128]{1,0:T(8,128)(2,1)S(1)} collective-permute-done((bf16[208,128]{1,0:T(8,128)(2,1)S(1)}, bf16[208,128]{1,0:T(8,128)(2,1)S(1)}, u32[]{:S(2)}, u32[]{:S(2)}) %collective-permute-start.12) | collective-permute-done | bytes 53280 | tf_op jit(solution)/shard_map/ppermute | solution.py:208
  39.2 0.0 collective-permute-done.13.refs_2_
  39.2 0.1 scale.1.refs_0_
  39.3 0.5 %collective-permute-start.16 = (bf16[32,768]{1,0:T(8,128)(2,1)S(1)}, bf16[32,768]{1,0:T(8,128)(2,1)S(1)}, u32[]{:S(2)}, u32[]{:S(2)}) collective-permute-start(bf16[32,768]{1,0:T(8,128)(2,1)S(1)} %scale.1.refs_0_), channel_id=1, source_target_pairs={{0,3},{1,2},{2,1},{3,0},{4,7},{5,6},{6,5},{7,4},{8,11},{9,10},{10,... | collective-permute-start | bytes 147464 | tf_op jit(solution)/shard_map/ppermute | solution.py:208
  39.8 1.0 %collective-permute-start.15 = (bf16[32,768]{1,0:T(8,128)(2,1)S(1)}, bf16[32,768]{1,0:T(8,128)(2,1)S(1)}, u32[]{:S(2)}, u32[]{:S(2)}) collective-permute-start(bf16[32,768]{1,0:T(8,128)(2,1)S(1)} %scale.1.refs_0_), channel_id=1, source_target_pairs={{0,2},{1,3},{2,0},{3,1},{4,6},{5,7},{6,4},{7,5},{8,10},{9,11},{10,... | collective-permute-start | bytes 147464 | tf_op jit(solution)/shard_map/ppermute | solution.py:208
  40.8 0.4 collective-permute-start.14
  41.2 2.1 %collective-permute-done.16.refs_3_ = bf16[32,768]{1,0:T(8,128)(2,1)S(1)} collective-permute-done((bf16[32,768]{1,0:T(8,128)(2,1)S(1)}, bf16[32,768]{1,0:T(8,128)(2,1)S(1)}, u32[]{:S(2)}, u32[]{:S(2)}) %collective-permute-start.16) | collective-permute-done | bytes 49184 | tf_op jit(solution)/shard_map/ppermute | solution.py:208
  43.3 1.1 %collective-permute-done.15.refs_2_ = bf16[32,768]{1,0:T(8,128)(2,1)S(1)} collective-permute-done((bf16[32,768]{1,0:T(8,128)(2,1)S(1)}, bf16[32,768]{1,0:T(8,128)(2,1)S(1)}, u32[]{:S(2)}, u32[]{:S(2)}) %collective-permute-start.15) | collective-permute-done | bytes 49184 | tf_op jit(solution)/shard_map/ppermute | solution.py:208
  44.4 0.0 collective-permute-done.14.refs_1_
  44.4 0.0 copy-done
  44.4 1.5 %sketch.1 = (f32[32,1024]{1,0:T(8,128)}, f32[32,768]{1,0:T(8,128)S(1)}, f32[32,768]{1,0:T(8,128)S(1)}, bf16[32,768]{1,0:T(8,128)(2,1)S(1)}, bf16[32,768]{1,0:T(8,128)(2,1)S(1)}) custom-call(s32[1,1024]{1,0:T(1,128)S(1)} %get-tuple-element.22.mark_ref, f32[8,128]{1,0:T(8,128)S(1)} %get-tuple-element.23.resident_ref, bf16[1024,768]{1,0:T(8,128)(2,1)S(1)} %copy-done, ...), custom_call_target="tpu_custom_call" | custom-call | tf_op jit(solution)/shard_map/sketch/pallas_call | solution.py:292
  46.0 0.1 collective-permute-start.19
  46.1 1.1 %collective-permute-start.17 = (bf16[32,768]{1,0:T(8,128)(2,1)S(1)}, bf16[32,768]{1,0:T(8,128)(2,1)S(1)}, u32[]{:S(2)}, u32[]{:S(2)}) collective-permute-start(bf16[32,768]{1,0:T(8,128)(2,1)S(1)} %get-tuple-element.39), channel_id=1, source_target_pairs={{0,3},{1,2},{2,1},{3,0},{4,7},{5,6},{6,5},{7,4},{8,11},{9,10},{10,... | collective-permute-start | bytes 147464 | tf_op jit(solution)/shard_map/ppermute | solution.py:208
  47.2 1.0 %collective-permute-start.18 = (bf16[32,768]{1,0:T(8,128)(2,1)S(1)}, bf16[32,768]{1,0:T(8,128)(2,1)S(1)}, u32[]{:S(2)}, u32[]{:S(2)}) collective-permute-start(bf16[32,768]{1,0:T(8,128)(2,1)S(1)} %get-tuple-element.40), channel_id=1, source_target_pairs={{0,2},{1,3},{2,0},{3,1},{4,6},{5,7},{6,4},{7,5},{8,10},{9,11},{10,... | collective-permute-start | bytes 147464 | tf_op jit(solution)/shard_map/ppermute | solution.py:208
  48.2 1.4 %collective-permute-done.17 = bf16[32,768]{1,0:T(8,128)(2,1)S(1)} collective-permute-done((bf16[32,768]{1,0:T(8,128)(2,1)S(1)}, bf16[32,768]{1,0:T(8,128)(2,1)S(1)}, u32[]{:S(2)}, u32[]{:S(2)}) %collective-permute-start.17) | collective-permute-done | bytes 49184 | tf_op jit(solution)/shard_map/ppermute | solution.py:208
  49.6 1.7 %collective-permute-done.18 = bf16[32,768]{1,0:T(8,128)(2,1)S(1)} collective-permute-done((bf16[32,768]{1,0:T(8,128)(2,1)S(1)}, bf16[32,768]{1,0:T(8,128)(2,1)S(1)}, u32[]{:S(2)}, u32[]{:S(2)}) %collective-permute-start.18) | collective-permute-done | bytes 49184 | tf_op jit(solution)/shard_map/ppermute | solution.py:208
  51.3 0.0 collective-permute-done.19
  51.3 0.7 %add_bitcast_fusion = f32[1,32,768]{2,1,0:T(8,128)} fusion(f32[32,768]{1,0:T(8,128)S(1)} %collective-permute-done.19, bf16[32,768]{1,0:T(8,128)(2,1)S(1)} %collective-permute-done.18, f32[32,768]{1,0:T(8,128)S(1)} %get-tuple-element.38, bf16[32,768]{1,0:T(8,128)(2,1)S(1)} %collective-permute-done.17), kind=kLoop, calls=%fused_computation.1 | loop fusion | flops 122880 | bytes 393216 | tf_op jit(solution)/shard_map/broadcast_in_dim | solution.py:302
  (3 shorter events, 0.0 us)
Async XLA Ops:
  2.6 7.7 %collective-permute-start.2 = (f32[32,768]{1,0:T(8,128)S(1)}, f32[32,768]{1,0:T(8,128)S(1)}, u32[]{:S(2)}, u32[]{:S(2)}) collective-permute-start(f32[32,768]{1,0:T(8,128)S(1)} %get-tuple-element.27), channel_id=1, source_target_pairs={{0,1},{1,0},{2,3},{3,2},{4,5},{5,4},{6,7},{7,6},{8,9},{9,8},{10,11... | collective-permute-start | bytes 294920 | tf_op jit(solution)/shard_map/ppermute | solution.py:208
  3.1 6.2 %collective-permute-start = (bf16[32,768]{1,0:T(8,128)(2,1)S(1)}, bf16[32,768]{1,0:T(8,128)(2,1)S(1)}, u32[]{:S(2)}, u32[]{:S(2)}) collective-permute-start(bf16[32,768]{1,0:T(8,128)(2,1)S(1)} %get-tuple-element.25), channel_id=1, source_target_pairs={{0,3},{1,2},{2,1},{3,0},{4,7},{5,6},{6,5},{7,4},{8,11},{9,10},{10,... | collective-permute-start | bytes 147464 | tf_op jit(solution)/shard_map/ppermute | solution.py:208
  5.7 4.6 %collective-permute-start.1 = (bf16[32,768]{1,0:T(8,128)(2,1)S(1)}, bf16[32,768]{1,0:T(8,128)(2,1)S(1)}, u32[]{:S(2)}, u32[]{:S(2)}) collective-permute-start(bf16[32,768]{1,0:T(8,128)(2,1)S(1)} %get-tuple-element.26), channel_id=1, source_target_pairs={{0,2},{1,3},{2,0},{3,1},{4,6},{5,7},{6,4},{7,5},{8,10},{9,11},{10,... | collective-permute-start | bytes 147464 | tf_op jit(solution)/shard_map/ppermute | solution.py:208
  5.7 14.8 %collective-permute-start.8 = (bf16[1552,128]{1,0:T(8,128)(2,1)S(1)}, bf16[1552,128]{1,0:T(8,128)(2,1)S(1)}, u32[]{:S(2)}, u32[]{:S(2)}) collective-permute-start(bf16[1552,128]{1,0:T(8,128)(2,1)S(1)} %get-tuple-element.28.refs_0_), channel_id=1, source_target_pairs={{0,4},{1,3},{2,6},{3,1},{4,0},{5,7},{6,2},{7,5},{8,12},{9,11},{10,... | collective-permute-start | bytes 1191944 | tf_op jit(solution)/shard_map/ppermute | solution.py:259
  7.7 12.8 %collective-permute-start.7 = (bf16[1552,128]{1,0:T(8,128)(2,1)S(1)}, bf16[1552,128]{1,0:T(8,128)(2,1)S(1)}, u32[]{:S(2)}, u32[]{:S(2)}) collective-permute-start(bf16[1552,128]{1,0:T(8,128)(2,1)S(1)} %get-tuple-element.28.refs_0_), channel_id=1, source_target_pairs={{0,2},{1,5},{2,0},{3,7},{4,6},{5,1},{6,4},{7,3},{8,10},{9,13},{10,... | collective-permute-start | bytes 1191944 | tf_op jit(solution)/shard_map/ppermute | solution.py:259
  10.3 6.1 %collective-permute-start.5 = (bf16[32,768]{1,0:T(8,128)(2,1)S(1)}, bf16[32,768]{1,0:T(8,128)(2,1)S(1)}, u32[]{:S(2)}, u32[]{:S(2)}) collective-permute-start(bf16[32,768]{1,0:T(8,128)(2,1)S(1)} %join.1), channel_id=1, source_target_pairs={{0,24},{4,28},{8,16},{12,20},{16,8},{20,12},{24,0},{28,4},{1,25},{... | collective-permute-start | bytes 147464 | tf_op jit(solution)/shard_map/ppermute | solution.py:208
  14.0 5.0 %collective-permute-start.4 = (bf16[32,768]{1,0:T(8,128)(2,1)S(1)}, bf16[32,768]{1,0:T(8,128)(2,1)S(1)}, u32[]{:S(2)}, u32[]{:S(2)}) collective-permute-start(bf16[32,768]{1,0:T(8,128)(2,1)S(1)} %join.1), channel_id=1, source_target_pairs={{0,16},{4,20},{8,24},{12,28},{16,0},{20,4},{24,8},{28,12},{1,17},{... | collective-permute-start | bytes 147464 | tf_op jit(solution)/shard_map/ppermute | solution.py:208
  14.0 5.0 %collective-permute-start.3 = (bf16[32,768]{1,0:T(8,128)(2,1)S(1)}, bf16[32,768]{1,0:T(8,128)(2,1)S(1)}, u32[]{:S(2)}, u32[]{:S(2)}) collective-permute-start(bf16[32,768]{1,0:T(8,128)(2,1)S(1)} %join.1), channel_id=1, source_target_pairs={{0,8},{4,12},{8,0},{12,4},{16,24},{20,28},{24,16},{28,20},{1,9},{5... | collective-permute-start | bytes 147464 | tf_op jit(solution)/shard_map/ppermute | solution.py:208
  19.0 1.5 %collective-permute-start.6 = (bf16[128,768]{1,0:T(8,128)(2,1)S(1)}, bf16[128,768]{1,0:T(8,128)(2,1)S(1)}, u32[]{:S(2)}, u32[]{:S(2)}) collective-permute-start(bf16[128,768]{1,0:T(8,128)(2,1)S(1)} %pad_maximum_fusion.mine_ref), channel_id=1, source_target_pairs={{0,1},{1,0},{2,3},{3,2},{4,5},{5,4},{6,7},{7,6},{8,9},{9,8},{10,11... | collective-permute-start | bytes 589832 | tf_op jit(solution)/shard_map/ppermute | solution.py:208
  20.5 7.9 %collective-permute-start.9 = (bf16[1552,128]{1,0:T(8,128)(2,1)S(1)}, bf16[1552,128]{1,0:T(8,128)(2,1)S(1)}, u32[]{:S(2)}, u32[]{:S(2)}) collective-permute-start(bf16[1552,128]{1,0:T(8,128)(2,1)S(1)} %get-tuple-element.29.refs_1_), channel_id=1, source_target_pairs={{0,4},{1,3},{2,6},{3,1},{4,0},{5,7},{6,2},{7,5},{8,12},{9,11},{10,... | collective-permute-start | bytes 1191944 | tf_op jit(solution)/shard_map/ppermute | solution.py:260
  23.9 20.5 %copy-start = (bf16[1024,768]{1,0:T(8,128)(2,1)S(1)}, bf16[1024,768]{1,0:T(8,128)(2,1)}, u32[]{:S(2)}) copy-start(bf16[1024,768]{1,0:T(8,128)(2,1)} %points_ref.1) | copy-start | bytes 4718596
  29.2 1.9 %collective-permute-start.10 = (f32[128,896]{1,0:T(8,128)S(1)}, f32[128,896]{1,0:T(8,128)S(1)}, u32[]{:S(2)}, u32[]{:S(2)}) collective-permute-start(f32[128,896]{1,0:T(8,128)S(1)} %get-tuple-element.32), channel_id=1, source_target_pairs={{0,1},{1,0},{2,3},{3,2},{4,5},{5,4},{6,7},{7,6},{8,9},{9,8},{10,11... | collective-permute-start | bytes 1376264 | tf_op jit(solution)/shard_map/ppermute | solution.py:208
  31.2 6.6 %collective-permute-start.11 = (bf16[208,128]{1,0:T(8,128)(2,1)S(1)}, bf16[208,128]{1,0:T(8,128)(2,1)S(1)}, u32[]{:S(2)}, u32[]{:S(2)}) collective-permute-start(bf16[208,128]{1,0:T(8,128)(2,1)S(1)} %get-tuple-element.34), channel_id=1, source_target_pairs={{0,24},{4,28},{8,16},{12,20},{16,8},{20,12},{24,0},{28,4},{1,25},{... | collective-permute-start | bytes 159752 | tf_op jit(solution)/shard_map/ppermute | solution.py:208
  32.7 6.5 %collective-permute-start.12 = (bf16[208,128]{1,0:T(8,128)(2,1)S(1)}, bf16[208,128]{1,0:T(8,128)(2,1)S(1)}, u32[]{:S(2)}, u32[]{:S(2)}) collective-permute-start(bf16[208,128]{1,0:T(8,128)(2,1)S(1)} %get-tuple-element.35), channel_id=1, source_target_pairs={{0,16},{4,20},{8,24},{12,28},{16,0},{20,4},{24,8},{28,12},{1,17},{... | collective-permute-start | bytes 159752 | tf_op jit(solution)/shard_map/ppermute | solution.py:208
  33.3 5.9 %collective-permute-start.13 = (bf16[208,128]{1,0:T(8,128)(2,1)S(1)}, bf16[208,128]{1,0:T(8,128)(2,1)S(1)}, u32[]{:S(2)}, u32[]{:S(2)}) collective-permute-start(bf16[208,128]{1,0:T(8,128)(2,1)S(1)} %get-tuple-element.36), channel_id=1, source_target_pairs={{0,8},{4,12},{8,0},{12,4},{16,24},{20,28},{24,16},{28,20},{1,9},{5... | collective-permute-start | bytes 159752 | tf_op jit(solution)/shard_map/ppermute | solution.py:208
  39.3 4.1 %collective-permute-start.16 = (bf16[32,768]{1,0:T(8,128)(2,1)S(1)}, bf16[32,768]{1,0:T(8,128)(2,1)S(1)}, u32[]{:S(2)}, u32[]{:S(2)}) collective-permute-start(bf16[32,768]{1,0:T(8,128)(2,1)S(1)} %scale.1.refs_0_), channel_id=1, source_target_pairs={{0,3},{1,2},{2,1},{3,0},{4,7},{5,6},{6,5},{7,4},{8,11},{9,10},{10,... | collective-permute-start | bytes 147464 | tf_op jit(solution)/shard_map/ppermute | solution.py:208
  39.8 4.6 %collective-permute-start.15 = (bf16[32,768]{1,0:T(8,128)(2,1)S(1)}, bf16[32,768]{1,0:T(8,128)(2,1)S(1)}, u32[]{:S(2)}, u32[]{:S(2)}) collective-permute-start(bf16[32,768]{1,0:T(8,128)(2,1)S(1)} %scale.1.refs_0_), channel_id=1, source_target_pairs={{0,2},{1,3},{2,0},{3,1},{4,6},{5,7},{6,4},{7,5},{8,10},{9,11},{10,... | collective-permute-start | bytes 147464 | tf_op jit(solution)/shard_map/ppermute | solution.py:208
  40.8 3.6 %collective-permute-start.14 = (bf16[32,768]{1,0:T(8,128)(2,1)S(1)}, bf16[32,768]{1,0:T(8,128)(2,1)S(1)}, u32[]{:S(2)}, u32[]{:S(2)}) collective-permute-start(bf16[32,768]{1,0:T(8,128)(2,1)S(1)} %scale.1.refs_0_), channel_id=1, source_target_pairs={{0,1},{1,0},{2,3},{3,2},{4,5},{5,4},{6,7},{7,6},{8,9},{9,8},{10,11... | collective-permute-start | bytes 147464 | tf_op jit(solution)/shard_map/ppermute | solution.py:208
  46.0 5.3 %collective-permute-start.19 = (f32[32,768]{1,0:T(8,128)S(1)}, f32[32,768]{1,0:T(8,128)S(1)}, u32[]{:S(2)}, u32[]{:S(2)}) collective-permute-start(f32[32,768]{1,0:T(8,128)S(1)} %get-tuple-element.41), channel_id=1, source_target_pairs={{0,1},{1,0},{2,3},{3,2},{4,5},{5,4},{6,7},{7,6},{8,9},{9,8},{10,11... | collective-permute-start | bytes 294920 | tf_op jit(solution)/shard_map/ppermute | solution.py:208
  46.1 3.5 %collective-permute-start.17 = (bf16[32,768]{1,0:T(8,128)(2,1)S(1)}, bf16[32,768]{1,0:T(8,128)(2,1)S(1)}, u32[]{:S(2)}, u32[]{:S(2)}) collective-permute-start(bf16[32,768]{1,0:T(8,128)(2,1)S(1)} %get-tuple-element.39), channel_id=1, source_target_pairs={{0,3},{1,2},{2,1},{3,0},{4,7},{5,6},{6,5},{7,4},{8,11},{9,10},{10,... | collective-permute-start | bytes 147464 | tf_op jit(solution)/shard_map/ppermute | solution.py:208
  47.2 4.1 %collective-permute-start.18 = (bf16[32,768]{1,0:T(8,128)(2,1)S(1)}, bf16[32,768]{1,0:T(8,128)(2,1)S(1)}, u32[]{:S(2)}, u32[]{:S(2)}) collective-permute-start(bf16[32,768]{1,0:T(8,128)(2,1)S(1)} %get-tuple-element.40), channel_id=1, source_target_pairs={{0,2},{1,3},{2,0},{3,1},{4,6},{5,7},{6,4},{7,5},{8,10},{9,11},{10,... | collective-permute-start | bytes 147464 | tf_op jit(solution)/shard_map/ppermute | solution.py:208

commit v9 on v8

--- a/solution.py
+++ b/solution.py
@@ -91,6 +91,13 @@
     out[...] = total.astype(out.dtype)
 
 
+def stack_kernel(*refs):
+    *parts, out = refs
+    rank = parts[0].shape[0]
+    for k, part in enumerate(parts):
+        out[k * rank : (k + 1) * rank, :] = part[...]
+
+
 def gate_kernel(*refs):
     pass
 
@@ -250,14 +257,20 @@
         compiler_params=PARAMS,
         name="join",
     )(own, *swaps(parts, "help"))
-    mine = jnp.concatenate([lifter] + [swap(lifter, "shard", INNER * d) for d in range(1, planes)], axis=0)
+    mine = pl.pallas_call(
+        stack_kernel,
+        out_shape=jax.ShapeDtypeStruct((planes * rank, width), BF16),
+        compiler_params=PARAMS,
+        cost_estimate=pl.CostEstimate(flops=35 * 10**8, bytes_accessed=10**5, transcendentals=0),
+        name="stack",
+    )(lifter, *[swap(lifter, "shard", INNER * d) for d in range(1, planes)])
     theirs = swap(mine, "help", 1)
 
     index, axes = range(groups * helpers), ("shard", "help")
     one = [(i, i ^ (2 if i % 2 == 0 else helpers)) for i in index]
     two = [(i, i ^ (helpers if i % 2 == 0 else 2)) for i in index]
-    near, far = gate([lax.ppermute(packed, axes, turn) for turn in (one, two)], theirs)
-    across = lax.ppermute(near, axes, two)
+    far, near = gate([lax.ppermute(packed, axes, turn) for turn in (one, two)], mine)
+    across = lax.ppermute(near, axes, one)
 
     wide = width + LANES
     begun = pl.pallas_call(

time: 52.2 us -> 51 us (0.977)
  waiting for transfers between devices: 22.9 us -> 22.2 us
  starting transfers between devices: 21.5 us -> 20.9 us
    ppermute x1, waiting for transfers between devices: 4.47 us -> 3.54 us  [shards(): across = lax.ppermute(near, axes, one)]
where the time goes in v9:
time: 51 us; the launch traced here: 50.8 us
  waiting for transfers between devices  22.2 us (44%)
  starting transfers between devices  20.9 us (41%)
  Pallas kernels  6.24 us (12%)
  between operations  0.74 us (1%)
  other arithmetic  0.67 us (1%)
    ppermute x17, waiting for transfers between devices, swap(): lax.ppermute(value, axis, [(i, i ^ d) for i in range(lax.axis_size(axis))])  18.7 us
    ppermute x17, starting transfers between devices, swap(): lax.ppermute(value, axis, [(i, i ^ d) for i in range(lax.axis_size(axis))])  16.3 us
    ppermute x1, waiting for transfers between devices, shards(): across = lax.ppermute(near, axes, one)  3.54 us
    ppermute x2, starting transfers between devices, shards(): lax.ppermute(packed, axes, turn)  3.5 us
    pallas_call x1, Pallas kernels, shards(): pl.pallas_call(functools.partial(lift_kernel, helpers), out_shape=[jax.Sh...  1.92 us
    pallas_call x1, Pallas kernels, shards(): pl.pallas_call(functools.partial(score_kernel, planes, helpers, 3), out_s...  1.81 us
    pallas_call x1, Pallas kernels, shards(): pl.pallas_call(functools.partial(sketch_kernel, helpers), out_shape=[jax....  1.53 us
    ppermute x1, starting transfers between devices, shards(): across = lax.ppermute(near, axes, one)  1.07 us
  transfers between devices with their start and end apart: 20, of which 12 were waited for; matrix products, arithmetic and copies ran while one was open for 0% of the time, Pallas kernels for 4%

profile of v9, /device:TPU:0, one launch (start us, length us, event | category | flops | bytes accessed | tf_op | source)
XLA Modules:
  0.0 50.8 jit_solution(16345034989295034057)
XLA Ops:
  0.6 1.9 %lift.1 = (bf16[1552,128]{1,0:T(8,128)(2,1)S(1)}, s32[1,1024]{1,0:T(1,128)S(1)}, f32[8,128]{1,0:T(8,128)S(1)}, f32[32,768]{1,0:T(8,128)S(1)}, f32[32,768]{1,0:T(...) custom-call(bf16[256,768]{1,0:T(8,128)(2,1)} %refs_0_.1, s32[2,256]{1,0:T(2,128)} %bitcast.4, ...), custom_call_target="tpu_custom_call" | custom-call | tf_op jit(solution)/shard_map/lift/pallas_call | solution.py:232
  2.6 0.5 %collective-permute-start.2 = (f32[32,768]{1,0:T(8,128)S(1)}, f32[32,768]{1,0:T(8,128)S(1)}, u32[]{:S(2)}, u32[]{:S(2)}) collective-permute-start(f32[32,768]{1,0:T(8,128)S(1)} %get-tuple-element.27), channel_id=1, source_target_pairs={{0,1},{1,0},{2,3},{3,2},{4,5},{5,4},{6,7},{7,6},{8,9},{9,8},{10,11... | collective-permute-start | bytes 294920 | tf_op jit(solution)/shard_map/ppermute | solution.py:215
  3.1 2.6 %collective-permute-start = (bf16[32,768]{1,0:T(8,128)(2,1)S(1)}, bf16[32,768]{1,0:T(8,128)(2,1)S(1)}, u32[]{:S(2)}, u32[]{:S(2)}) collective-permute-start(bf16[32,768]{1,0:T(8,128)(2,1)S(1)} %get-tuple-element.25), channel_id=1, source_target_pairs={{0,3},{1,2},{2,1},{3,0},{4,7},{5,6},{6,5},{7,4},{8,11},{9,10},{10,... | collective-permute-start | bytes 147464 | tf_op jit(solution)/shard_map/ppermute | solution.py:215
  5.7 0.0 collective-permute-start.1
  5.7 2.0 %collective-permute-start.8 = (bf16[1552,128]{1,0:T(8,128)(2,1)S(1)}, bf16[1552,128]{1,0:T(8,128)(2,1)S(1)}, u32[]{:S(2)}, u32[]{:S(2)}) collective-permute-start(bf16[1552,128]{1,0:T(8,128)(2,1)S(1)} %get-tuple-element.28.refs_0_), channel_id=1, source_target_pairs={{0,4},{1,3},{2,6},{3,1},{4,0},{5,7},{6,2},{7,5},{8,12},{9,11},{10,... | collective-permute-start | bytes 1191944 | tf_op jit(solution)/shard_map/ppermute | solution.py:272
  7.7 1.5 %collective-permute-start.7 = (bf16[1552,128]{1,0:T(8,128)(2,1)S(1)}, bf16[1552,128]{1,0:T(8,128)(2,1)S(1)}, u32[]{:S(2)}, u32[]{:S(2)}) collective-permute-start(bf16[1552,128]{1,0:T(8,128)(2,1)S(1)} %get-tuple-element.28.refs_0_), channel_id=1, source_target_pairs={{0,2},{1,5},{2,0},{3,7},{4,6},{5,1},{6,4},{7,3},{8,10},{9,13},{10,... | collective-permute-start | bytes 1191944 | tf_op jit(solution)/shard_map/ppermute | solution.py:272
  9.2 0.0 collective-permute-done.refs_1_
  9.2 1.1 %collective-permute-done.1.refs_2_ = bf16[32,768]{1,0:T(8,128)(2,1)S(1)} collective-permute-done((bf16[32,768]{1,0:T(8,128)(2,1)S(1)}, bf16[32,768]{1,0:T(8,128)(2,1)S(1)}, u32[]{:S(2)}, u32[]{:S(2)}) %collective-permute-start.1) | collective-permute-done | bytes 49184 | tf_op jit(solution)/shard_map/ppermute | solution.py:215
  10.3 0.0 collective-permute-done.2.refs_3_
  10.3 3.7 %collective-permute-start.5 = (bf16[32,768]{1,0:T(8,128)(2,1)S(1)}, bf16[32,768]{1,0:T(8,128)(2,1)S(1)}, u32[]{:S(2)}, u32[]{:S(2)}) collective-permute-start(bf16[32,768]{1,0:T(8,128)(2,1)S(1)} %join.1.refs_0_), channel_id=1, source_target_pairs={{0,24},{4,28},{8,16},{12,20},{16,8},{20,12},{24,0},{28,4},{1,25},{... | collective-permute-start | bytes 147464 | tf_op jit(solution)/shard_map/ppermute | solution.py:215
  14.0 0.0 collective-permute-start.4
  14.0 0.8 %collective-permute-start.3 = (bf16[32,768]{1,0:T(8,128)(2,1)S(1)}, bf16[32,768]{1,0:T(8,128)(2,1)S(1)}, u32[]{:S(2)}, u32[]{:S(2)}) collective-permute-start(bf16[32,768]{1,0:T(8,128)(2,1)S(1)} %join.1.refs_0_), channel_id=1, source_target_pairs={{0,8},{4,12},{8,0},{12,4},{16,24},{20,28},{24,16},{28,20},{1,9},{5... | collective-permute-start | bytes 147464 | tf_op jit(solution)/shard_map/ppermute | solution.py:215
  14.8 1.6 %collective-permute-done.5.refs_3_ = bf16[32,768]{1,0:T(8,128)(2,1)S(1)} collective-permute-done((bf16[32,768]{1,0:T(8,128)(2,1)S(1)}, bf16[32,768]{1,0:T(8,128)(2,1)S(1)}, u32[]{:S(2)}, u32[]{:S(2)}) %collective-permute-start.5) | collective-permute-done | bytes 49184 | tf_op jit(solution)/shard_map/ppermute | solution.py:215
  16.4 2.6 %collective-permute-done.4.refs_2_ = bf16[32,768]{1,0:T(8,128)(2,1)S(1)} collective-permute-done((bf16[32,768]{1,0:T(8,128)(2,1)S(1)}, bf16[32,768]{1,0:T(8,128)(2,1)S(1)}, u32[]{:S(2)}, u32[]{:S(2)}) %collective-permute-start.4) | collective-permute-done | bytes 49184 | tf_op jit(solution)/shard_map/ppermute | solution.py:215
  19.0 0.0 collective-permute-done.3.refs_1_
  19.0 0.0 collective-permute-done.8.refs_1_
  19.0 0.0 collective-permute-done.7.refs_0_
  19.0 1.1 %collective-permute-start.9 = (bf16[1552,128]{1,0:T(8,128)(2,1)S(1)}, bf16[1552,128]{1,0:T(8,128)(2,1)S(1)}, u32[]{:S(2)}, u32[]{:S(2)}) collective-permute-start(bf16[1552,128]{1,0:T(8,128)(2,1)S(1)} %get-tuple-element.29.refs_1_), channel_id=1, source_target_pairs={{0,2},{1,5},{2,0},{3,7},{4,6},{5,1},{6,4},{7,3},{8,10},{9,13},{10,... | collective-permute-start | bytes 1191944 | tf_op jit(solution)/shard_map/ppermute | solution.py:273
  20.1 0.0 collective-permute-start.6
  20.1 1.4 %collective-permute-done.6.theirs_ref = bf16[128,768]{1,0:T(8,128)(2,1)S(1)} collective-permute-done((bf16[128,768]{1,0:T(8,128)(2,1)S(1)}, bf16[128,768]{1,0:T(8,128)(2,1)S(1)}, u32[]{:S(2)}, u32[]{:S(2)}) %collective-permute-start.6) | collective-permute-done | bytes 196640 | tf_op jit(solution)/shard_map/ppermute | solution.py:215
  21.6 1.8 %score.1.refs_1_ = f32[256,896]{1,0:T(8,128)S(1)} custom-call(bf16[128,768]{1,0:T(8,128)(2,1)S(1)} %stack.1.refs_2_.mine_ref, bf16[128,768]{1,0:T(8,128)(2,1)S(1)} %collective-permute-done.6.theirs_ref, bf16[1552,128]{1,0:T(8,128)(2,1)S(1)} %get-tuple-element.28.refs_0_, bf16[1552,128]{1,0:T(8,128)(2,1)S(1)} %get-tuple-element.29.refs_1_, ...), custom_call_target="tpu_custom_call" | custom-call | tf_op jit(solution)/shard_map/score/pallas_call | solution.py:276
  23.4 0.0 copy-start
  23.4 3.5 %collective-permute-done.9.refs_0_ = bf16[1552,128]{1,0:T(8,128)(2,1)S(1)} collective-permute-done((bf16[1552,128]{1,0:T(8,128)(2,1)S(1)}, bf16[1552,128]{1,0:T(8,128)(2,1)S(1)}, u32[]{:S(2)}, u32[]{:S(2)}) %collective-permute-start.9) | collective-permute-done | bytes 397344 | tf_op jit(solution)/shard_map/ppermute | solution.py:273
  26.9 0.8 %score_last.1 = (f32[128,896]{1,0:T(8,128)S(1)}, f32[128,896]{1,0:T(8,128)S(1)}) custom-call(bf16[128,768]{1,0:T(8,128)(2,1)S(1)} %stack.1.refs_2_.mine_ref, bf16[128,768]{1,0:T(8,128)(2,1)S(1)} %collective-permute-done.6.theirs_ref, bf16[1552,128]{1,0:T(8,128)(2,1)S(1)} %collective-permute-done.9.refs_0_, f32[256,896]{1,0:T(8,128)S(1)} %score.1.refs_1_), custom_call_target="tpu_custom_call" | custom-call | tf_op jit(solution)/shard_map/score_last/pallas_call | solution.py:282
  27.7 0.1 collective-permute-start.10
  27.8 1.8 %collective-permute-done.10.theirs_ref = f32[128,896]{1,0:T(8,128)S(1)} collective-permute-done((f32[128,896]{1,0:T(8,128)S(1)}, f32[128,896]{1,0:T(8,128)S(1)}, u32[]{:S(2)}, u32[]{:S(2)}) %collective-permute-start.10) | collective-permute-done | bytes 458784 | tf_op jit(solution)/shard_map/ppermute | solution.py:215
  29.6 0.1 fold.1
  29.7 2.8 %collective-permute-start.11 = (bf16[208,128]{1,0:T(8,128)(2,1)S(1)}, bf16[208,128]{1,0:T(8,128)(2,1)S(1)}, u32[]{:S(2)}, u32[]{:S(2)}) collective-permute-start(bf16[208,128]{1,0:T(8,128)(2,1)S(1)} %get-tuple-element.34), channel_id=1, source_target_pairs={{0,24},{4,28},{8,16},{12,20},{16,8},{20,12},{24,0},{28,4},{1,25},{... | collective-permute-start | bytes 159752 | tf_op jit(solution)/shard_map/ppermute | solution.py:215
  32.5 0.0 collective-permute-start.12
  32.5 1.6 %collective-permute-start.13 = (bf16[208,128]{1,0:T(8,128)(2,1)S(1)}, bf16[208,128]{1,0:T(8,128)(2,1)S(1)}, u32[]{:S(2)}, u32[]{:S(2)}) collective-permute-start(bf16[208,128]{1,0:T(8,128)(2,1)S(1)} %get-tuple-element.36), channel_id=1, source_target_pairs={{0,8},{4,12},{8,0},{12,4},{16,24},{20,28},{24,16},{28,20},{1,9},{5... | collective-permute-start | bytes 159752 | tf_op jit(solution)/shard_map/ppermute | solution.py:215
  34.1 2.1 %collective-permute-done.11.refs_0_ = bf16[208,128]{1,0:T(8,128)(2,1)S(1)} collective-permute-done((bf16[208,128]{1,0:T(8,128)(2,1)S(1)}, bf16[208,128]{1,0:T(8,128)(2,1)S(1)}, u32[]{:S(2)}, u32[]{:S(2)}) %collective-permute-start.11) | collective-permute-done | bytes 53280 | tf_op jit(solution)/shard_map/ppermute | solution.py:215
  36.3 1.7 %collective-permute-done.12.refs_1_ = bf16[208,128]{1,0:T(8,128)(2,1)S(1)} collective-permute-done((bf16[208,128]{1,0:T(8,128)(2,1)S(1)}, bf16[208,128]{1,0:T(8,128)(2,1)S(1)}, u32[]{:S(2)}, u32[]{:S(2)}) %collective-permute-start.12) | collective-permute-done | bytes 53280 | tf_op jit(solution)/shard_map/ppermute | solution.py:215
  38.0 0.0 collective-permute-done.13.refs_2_
  38.0 0.1 scale.1.refs_0_
  38.0 0.7 %collective-permute-start.16 = (bf16[32,768]{1,0:T(8,128)(2,1)S(1)}, bf16[32,768]{1,0:T(8,128)(2,1)S(1)}, u32[]{:S(2)}, u32[]{:S(2)}) collective-permute-start(bf16[32,768]{1,0:T(8,128)(2,1)S(1)} %scale.1.refs_0_), channel_id=1, source_target_pairs={{0,3},{1,2},{2,1},{3,0},{4,7},{5,6},{6,5},{7,4},{8,11},{9,10},{10,... | collective-permute-start | bytes 147464 | tf_op jit(solution)/shard_map/ppermute | solution.py:215
  38.7 1.0 %collective-permute-start.15 = (bf16[32,768]{1,0:T(8,128)(2,1)S(1)}, bf16[32,768]{1,0:T(8,128)(2,1)S(1)}, u32[]{:S(2)}, u32[]{:S(2)}) collective-permute-start(bf16[32,768]{1,0:T(8,128)(2,1)S(1)} %scale.1.refs_0_), channel_id=1, source_target_pairs={{0,2},{1,3},{2,0},{3,1},{4,6},{5,7},{6,4},{7,5},{8,10},{9,11},{10,... | collective-permute-start | bytes 147464 | tf_op jit(solution)/shard_map/ppermute | solution.py:215
  39.7 0.3 collective-permute-start.14
  40.0 2.1 %collective-permute-done.16.refs_3_ = bf16[32,768]{1,0:T(8,128)(2,1)S(1)} collective-permute-done((bf16[32,768]{1,0:T(8,128)(2,1)S(1)}, bf16[32,768]{1,0:T(8,128)(2,1)S(1)}, u32[]{:S(2)}, u32[]{:S(2)}) %collective-permute-start.16) | collective-permute-done | bytes 49184 | tf_op jit(solution)/shard_map/ppermute | solution.py:215
  42.0 1.2 %collective-permute-done.15.refs_2_ = bf16[32,768]{1,0:T(8,128)(2,1)S(1)} collective-permute-done((bf16[32,768]{1,0:T(8,128)(2,1)S(1)}, bf16[32,768]{1,0:T(8,128)(2,1)S(1)}, u32[]{:S(2)}, u32[]{:S(2)}) %collective-permute-start.15) | collective-permute-done | bytes 49184 | tf_op jit(solution)/shard_map/ppermute | solution.py:215
  43.2 0.0 collective-permute-done.14.refs_1_
  43.2 0.0 copy-done
  43.2 1.5 %sketch.1 = (f32[32,1024]{1,0:T(8,128)}, f32[32,768]{1,0:T(8,128)S(1)}, f32[32,768]{1,0:T(8,128)S(1)}, bf16[32,768]{1,0:T(8,128)(2,1)S(1)}, bf16[32,768]{1,0:T(8,128)(2,1)S(1)}) custom-call(s32[1,1024]{1,0:T(1,128)S(1)} %get-tuple-element.22.mark_ref, f32[8,128]{1,0:T(8,128)S(1)} %get-tuple-element.23.resident_ref, bf16[1024,768]{1,0:T(8,128)(2,1)S(1)} %copy-done, ...), custom_call_target="tpu_custom_call" | custom-call | tf_op jit(solution)/shard_map/sketch/pallas_call | solution.py:305
  44.7 0.1 collective-permute-start.19
  44.8 1.1 %collective-permute-start.17 = (bf16[32,768]{1,0:T(8,128)(2,1)S(1)}, bf16[32,768]{1,0:T(8,128)(2,1)S(1)}, u32[]{:S(2)}, u32[]{:S(2)}) collective-permute-start(bf16[32,768]{1,0:T(8,128)(2,1)S(1)} %get-tuple-element.39), channel_id=1, source_target_pairs={{0,3},{1,2},{2,1},{3,0},{4,7},{5,6},{6,5},{7,4},{8,11},{9,10},{10,... | collective-permute-start | bytes 147464 | tf_op jit(solution)/shard_map/ppermute | solution.py:215
  46.0 1.0 %collective-permute-start.18 = (bf16[32,768]{1,0:T(8,128)(2,1)S(1)}, bf16[32,768]{1,0:T(8,128)(2,1)S(1)}, u32[]{:S(2)}, u32[]{:S(2)}) collective-permute-start(bf16[32,768]{1,0:T(8,128)(2,1)S(1)} %get-tuple-element.40), channel_id=1, source_target_pairs={{0,2},{1,3},{2,0},{3,1},{4,6},{5,7},{6,4},{7,5},{8,10},{9,11},{10,... | collective-permute-start | bytes 147464 | tf_op jit(solution)/shard_map/ppermute | solution.py:215
  47.0 1.4 %collective-permute-done.17 = bf16[32,768]{1,0:T(8,128)(2,1)S(1)} collective-permute-done((bf16[32,768]{1,0:T(8,128)(2,1)S(1)}, bf16[32,768]{1,0:T(8,128)(2,1)S(1)}, u32[]{:S(2)}, u32[]{:S(2)}) %collective-permute-start.17) | collective-permute-done | bytes 49184 | tf_op jit(solution)/shard_map/ppermute | solution.py:215
  48.4 1.7 %collective-permute-done.18 = bf16[32,768]{1,0:T(8,128)(2,1)S(1)} collective-permute-done((bf16[32,768]{1,0:T(8,128)(2,1)S(1)}, bf16[32,768]{1,0:T(8,128)(2,1)S(1)}, u32[]{:S(2)}, u32[]{:S(2)}) %collective-permute-start.18) | collective-permute-done | bytes 49184 | tf_op jit(solution)/shard_map/ppermute | solution.py:215
  50.1 0.0 collective-permute-done.19
  50.1 0.7 %add_bitcast_fusion = f32[1,32,768]{2,1,0:T(8,128)} fusion(f32[32,768]{1,0:T(8,128)S(1)} %collective-permute-done.19, bf16[32,768]{1,0:T(8,128)(2,1)S(1)} %collective-permute-done.18, f32[32,768]{1,0:T(8,128)S(1)} %get-tuple-element.38, bf16[32,768]{1,0:T(8,128)(2,1)S(1)} %collective-permute-done.17), kind=kLoop, calls=%fused_computation | loop fusion | flops 122880 | bytes 393216 | tf_op jit(solution)/shard_map/broadcast_in_dim | solution.py:315
  (3 shorter events, 0.0 us)
Async XLA Ops:
  2.6 7.7 %collective-permute-start.2 = (f32[32,768]{1,0:T(8,128)S(1)}, f32[32,768]{1,0:T(8,128)S(1)}, u32[]{:S(2)}, u32[]{:S(2)}) collective-permute-start(f32[32,768]{1,0:T(8,128)S(1)} %get-tuple-element.27), channel_id=1, source_target_pairs={{0,1},{1,0},{2,3},{3,2},{4,5},{5,4},{6,7},{7,6},{8,9},{9,8},{10,11... | collective-permute-start | bytes 294920 | tf_op jit(solution)/shard_map/ppermute | solution.py:215
  3.1 6.2 %collective-permute-start = (bf16[32,768]{1,0:T(8,128)(2,1)S(1)}, bf16[32,768]{1,0:T(8,128)(2,1)S(1)}, u32[]{:S(2)}, u32[]{:S(2)}) collective-permute-start(bf16[32,768]{1,0:T(8,128)(2,1)S(1)} %get-tuple-element.25), channel_id=1, source_target_pairs={{0,3},{1,2},{2,1},{3,0},{4,7},{5,6},{6,5},{7,4},{8,11},{9,10},{10,... | collective-permute-start | bytes 147464 | tf_op jit(solution)/shard_map/ppermute | solution.py:215
  5.7 4.6 %collective-permute-start.1 = (bf16[32,768]{1,0:T(8,128)(2,1)S(1)}, bf16[32,768]{1,0:T(8,128)(2,1)S(1)}, u32[]{:S(2)}, u32[]{:S(2)}) collective-permute-start(bf16[32,768]{1,0:T(8,128)(2,1)S(1)} %get-tuple-element.26), channel_id=1, source_target_pairs={{0,2},{1,3},{2,0},{3,1},{4,6},{5,7},{6,4},{7,5},{8,10},{9,11},{10,... | collective-permute-start | bytes 147464 | tf_op jit(solution)/shard_map/ppermute | solution.py:215
  5.7 13.3 %collective-permute-start.8 = (bf16[1552,128]{1,0:T(8,128)(2,1)S(1)}, bf16[1552,128]{1,0:T(8,128)(2,1)S(1)}, u32[]{:S(2)}, u32[]{:S(2)}) collective-permute-start(bf16[1552,128]{1,0:T(8,128)(2,1)S(1)} %get-tuple-element.28.refs_0_), channel_id=1, source_target_pairs={{0,4},{1,3},{2,6},{3,1},{4,0},{5,7},{6,2},{7,5},{8,12},{9,11},{10,... | collective-permute-start | bytes 1191944 | tf_op jit(solution)/shard_map/ppermute | solution.py:272
  7.7 11.3 %collective-permute-start.7 = (bf16[1552,128]{1,0:T(8,128)(2,1)S(1)}, bf16[1552,128]{1,0:T(8,128)(2,1)S(1)}, u32[]{:S(2)}, u32[]{:S(2)}) collective-permute-start(bf16[1552,128]{1,0:T(8,128)(2,1)S(1)} %get-tuple-element.28.refs_0_), channel_id=1, source_target_pairs={{0,2},{1,5},{2,0},{3,7},{4,6},{5,1},{6,4},{7,3},{8,10},{9,13},{10,... | collective-permute-start | bytes 1191944 | tf_op jit(solution)/shard_map/ppermute | solution.py:272
  10.3 6.1 %collective-permute-start.5 = (bf16[32,768]{1,0:T(8,128)(2,1)S(1)}, bf16[32,768]{1,0:T(8,128)(2,1)S(1)}, u32[]{:S(2)}, u32[]{:S(2)}) collective-permute-start(bf16[32,768]{1,0:T(8,128)(2,1)S(1)} %join.1.refs_0_), channel_id=1, source_target_pairs={{0,24},{4,28},{8,16},{12,20},{16,8},{20,12},{24,0},{28,4},{1,25},{... | collective-permute-start | bytes 147464 | tf_op jit(solution)/shard_map/ppermute | solution.py:215
  14.0 5.0 %collective-permute-start.4 = (bf16[32,768]{1,0:T(8,128)(2,1)S(1)}, bf16[32,768]{1,0:T(8,128)(2,1)S(1)}, u32[]{:S(2)}, u32[]{:S(2)}) collective-permute-start(bf16[32,768]{1,0:T(8,128)(2,1)S(1)} %join.1.refs_0_), channel_id=1, source_target_pairs={{0,16},{4,20},{8,24},{12,28},{16,0},{20,4},{24,8},{28,12},{1,17},{... | collective-permute-start | bytes 147464 | tf_op jit(solution)/shard_map/ppermute | solution.py:215
  14.0 5.0 %collective-permute-start.3 = (bf16[32,768]{1,0:T(8,128)(2,1)S(1)}, bf16[32,768]{1,0:T(8,128)(2,1)S(1)}, u32[]{:S(2)}, u32[]{:S(2)}) collective-permute-start(bf16[32,768]{1,0:T(8,128)(2,1)S(1)} %join.1.refs_0_), channel_id=1, source_target_pairs={{0,8},{4,12},{8,0},{12,4},{16,24},{20,28},{24,16},{28,20},{1,9},{5... | collective-permute-start | bytes 147464 | tf_op jit(solution)/shard_map/ppermute | solution.py:215
  19.0 7.9 %collective-permute-start.9 = (bf16[1552,128]{1,0:T(8,128)(2,1)S(1)}, bf16[1552,128]{1,0:T(8,128)(2,1)S(1)}, u32[]{:S(2)}, u32[]{:S(2)}) collective-permute-start(bf16[1552,128]{1,0:T(8,128)(2,1)S(1)} %get-tuple-element.29.refs_1_), channel_id=1, source_target_pairs={{0,2},{1,5},{2,0},{3,7},{4,6},{5,1},{6,4},{7,3},{8,10},{9,13},{10,... | collective-permute-start | bytes 1191944 | tf_op jit(solution)/shard_map/ppermute | solution.py:273
  20.1 1.4 %collective-permute-start.6 = (bf16[128,768]{1,0:T(8,128)(2,1)S(1)}, bf16[128,768]{1,0:T(8,128)(2,1)S(1)}, u32[]{:S(2)}, u32[]{:S(2)}) collective-permute-start(bf16[128,768]{1,0:T(8,128)(2,1)S(1)} %stack.1.refs_2_.mine_ref), channel_id=1, source_target_pairs={{0,1},{1,0},{2,3},{3,2},{4,5},{5,4},{6,7},{7,6},{8,9},{9,8},{10,11... | collective-permute-start | bytes 589832 | tf_op jit(solution)/shard_map/ppermute | solution.py:215
  23.4 19.8 %copy-start = (bf16[1024,768]{1,0:T(8,128)(2,1)S(1)}, bf16[1024,768]{1,0:T(8,128)(2,1)}, u32[]{:S(2)}) copy-start(bf16[1024,768]{1,0:T(8,128)(2,1)} %points_ref.1) | copy-start | bytes 4718596
  27.7 1.9 %collective-permute-start.10 = (f32[128,896]{1,0:T(8,128)S(1)}, f32[128,896]{1,0:T(8,128)S(1)}, u32[]{:S(2)}, u32[]{:S(2)}) collective-permute-start(f32[128,896]{1,0:T(8,128)S(1)} %get-tuple-element.32), channel_id=1, source_target_pairs={{0,1},{1,0},{2,3},{3,2},{4,5},{5,4},{6,7},{7,6},{8,9},{9,8},{10,11... | collective-permute-start | bytes 1376264 | tf_op jit(solution)/shard_map/ppermute | solution.py:215
  29.7 6.6 %collective-permute-start.11 = (bf16[208,128]{1,0:T(8,128)(2,1)S(1)}, bf16[208,128]{1,0:T(8,128)(2,1)S(1)}, u32[]{:S(2)}, u32[]{:S(2)}) collective-permute-start(bf16[208,128]{1,0:T(8,128)(2,1)S(1)} %get-tuple-element.34), channel_id=1, source_target_pairs={{0,24},{4,28},{8,16},{12,20},{16,8},{20,12},{24,0},{28,4},{1,25},{... | collective-permute-start | bytes 159752 | tf_op jit(solution)/shard_map/ppermute | solution.py:215
  32.5 5.4 %collective-permute-start.12 = (bf16[208,128]{1,0:T(8,128)(2,1)S(1)}, bf16[208,128]{1,0:T(8,128)(2,1)S(1)}, u32[]{:S(2)}, u32[]{:S(2)}) collective-permute-start(bf16[208,128]{1,0:T(8,128)(2,1)S(1)} %get-tuple-element.35), channel_id=1, source_target_pairs={{0,16},{4,20},{8,24},{12,28},{16,0},{20,4},{24,8},{28,12},{1,17},{... | collective-permute-start | bytes 159752 | tf_op jit(solution)/shard_map/ppermute | solution.py:215
  32.5 5.4 %collective-permute-start.13 = (bf16[208,128]{1,0:T(8,128)(2,1)S(1)}, bf16[208,128]{1,0:T(8,128)(2,1)S(1)}, u32[]{:S(2)}, u32[]{:S(2)}) collective-permute-start(bf16[208,128]{1,0:T(8,128)(2,1)S(1)} %get-tuple-element.36), channel_id=1, source_target_pairs={{0,8},{4,12},{8,0},{12,4},{16,24},{20,28},{24,16},{28,20},{1,9},{5... | collective-permute-start | bytes 159752 | tf_op jit(solution)/shard_map/ppermute | solution.py:215
  38.0 4.0 %collective-permute-start.16 = (bf16[32,768]{1,0:T(8,128)(2,1)S(1)}, bf16[32,768]{1,0:T(8,128)(2,1)S(1)}, u32[]{:S(2)}, u32[]{:S(2)}) collective-permute-start(bf16[32,768]{1,0:T(8,128)(2,1)S(1)} %scale.1.refs_0_), channel_id=1, source_target_pairs={{0,3},{1,2},{2,1},{3,0},{4,7},{5,6},{6,5},{7,4},{8,11},{9,10},{10,... | collective-permute-start | bytes 147464 | tf_op jit(solution)/shard_map/ppermute | solution.py:215
  38.7 4.5 %collective-permute-start.15 = (bf16[32,768]{1,0:T(8,128)(2,1)S(1)}, bf16[32,768]{1,0:T(8,128)(2,1)S(1)}, u32[]{:S(2)}, u32[]{:S(2)}) collective-permute-start(bf16[32,768]{1,0:T(8,128)(2,1)S(1)} %scale.1.refs_0_), channel_id=1, source_target_pairs={{0,2},{1,3},{2,0},{3,1},{4,6},{5,7},{6,4},{7,5},{8,10},{9,11},{10,... | collective-permute-start | bytes 147464 | tf_op jit(solution)/shard_map/ppermute | solution.py:215
  39.7 3.5 %collective-permute-start.14 = (bf16[32,768]{1,0:T(8,128)(2,1)S(1)}, bf16[32,768]{1,0:T(8,128)(2,1)S(1)}, u32[]{:S(2)}, u32[]{:S(2)}) collective-permute-start(bf16[32,768]{1,0:T(8,128)(2,1)S(1)} %scale.1.refs_0_), channel_id=1, source_target_pairs={{0,1},{1,0},{2,3},{3,2},{4,5},{5,4},{6,7},{7,6},{8,9},{9,8},{10,11... | collective-permute-start | bytes 147464 | tf_op jit(solution)/shard_map/ppermute | solution.py:215
  44.7 5.3 %collective-permute-start.19 = (f32[32,768]{1,0:T(8,128)S(1)}, f32[32,768]{1,0:T(8,128)S(1)}, u32[]{:S(2)}, u32[]{:S(2)}) collective-permute-start(f32[32,768]{1,0:T(8,128)S(1)} %get-tuple-element.41), channel_id=1, source_target_pairs={{0,1},{1,0},{2,3},{3,2},{4,5},{5,4},{6,7},{7,6},{8,9},{9,8},{10,11... | collective-permute-start | bytes 294920 | tf_op jit(solution)/shard_map/ppermute | solution.py:215
  44.8 3.6 %collective-permute-start.17 = (bf16[32,768]{1,0:T(8,128)(2,1)S(1)}, bf16[32,768]{1,0:T(8,128)(2,1)S(1)}, u32[]{:S(2)}, u32[]{:S(2)}) collective-permute-start(bf16[32,768]{1,0:T(8,128)(2,1)S(1)} %get-tuple-element.39), channel_id=1, source_target_pairs={{0,3},{1,2},{2,1},{3,0},{4,7},{5,6},{6,5},{7,4},{8,11},{9,10},{10,... | collective-permute-start | bytes 147464 | tf_op jit(solution)/shard_map/ppermute | solution.py:215
  46.0 4.1 %collective-permute-start.18 = (bf16[32,768]{1,0:T(8,128)(2,1)S(1)}, bf16[32,768]{1,0:T(8,128)(2,1)S(1)}, u32[]{:S(2)}, u32[]{:S(2)}) collective-permute-start(bf16[32,768]{1,0:T(8,128)(2,1)S(1)} %get-tuple-element.40), channel_id=1, source_target_pairs={{0,2},{1,3},{2,0},{3,1},{4,6},{5,7},{6,4},{7,5},{8,10},{9,11},{10,... | collective-permute-start | bytes 147464 | tf_op jit(solution)/shard_map/ppermute | solution.py:215

commit v10 on v9

--- a/solution.py
+++ b/solution.py
@@ -255,21 +255,24 @@
         join_kernel,
         out_shape=sent,
         compiler_params=PARAMS,
+        cost_estimate=pl.CostEstimate(flops=4 * 10**9, bytes_accessed=10**5, transcendentals=0),
         name="join",
     )(own, *swaps(parts, "help"))
+    lifters = [lifter] + [swap(lifter, "shard", INNER * d) for d in range(1, planes)]
     mine = pl.pallas_call(
         stack_kernel,
         out_shape=jax.ShapeDtypeStruct((planes * rank, width), BF16),
         compiler_params=PARAMS,
-        cost_estimate=pl.CostEstimate(flops=35 * 10**8, bytes_accessed=10**5, transcendentals=0),
+        cost_estimate=pl.CostEstimate(flops=35*10**8, bytes_accessed=10**5, transcendentals=0),
         name="stack",
-    )(lifter, *[swap(lifter, "shard", INNER * d) for d in range(1, planes)])
+    )(*lifters)
     theirs = swap(mine, "help", 1)
 
     index, axes = range(groups * helpers), ("shard", "help")
     one = [(i, i ^ (2 if i % 2 == 0 else helpers)) for i in index]
     two = [(i, i ^ (helpers if i % 2 == 0 else 2)) for i in index]
-    far, near = gate([lax.ppermute(packed, axes, turn) for turn in (one, two)], mine)
+    far = lax.ppermute(packed, axes, one)
+    (near,) = gate([lax.ppermute(packed, axes, two)], lifters[-1])
     across = lax.ppermute(near, axes, one)
 
     wide = width + LANES

time: 51 us -> 51.1 us (level)
  waiting for transfers between devices: 22.2 us -> 22.9 us
  starting transfers between devices: 20.9 us -> 20.3 us
    ppermute x2, waiting for transfers between devices: 0.01 us -> 2.09 us  [the longest x1 2.09 us: shards(): far = lax.ppermute(packed, axes, one)]
    ppermute x1, waiting for transfers between devices: 3.54 us -> 2.43 us  [shards(): across = lax.ppermute(near, axes, one)]
  transfers between devices with their start and end apart: 20 -> 20, of which waited for: 12 -> 14; matrix products, arithmetic and copies ran while one was open for 0% -> 0% of each run, Pallas kernels for 4% -> 4%
where the time goes in v10:
time: 51.1 us; the launch traced here: 50.9 us
  waiting for transfers between devices  22.9 us (45%)
  starting transfers between devices  20.3 us (40%)
  Pallas kernels  6.23 us (12%)
  between operations  0.73 us (1%)
  other arithmetic  0.67 us (1%)
    ppermute x17, waiting for transfers between devices, swap(): lax.ppermute(value, axis, [(i, i ^ d) for i in range(lax.axis_size(axis))])  18.4 us
    ppermute x17, starting transfers between devices, swap(): lax.ppermute(value, axis, [(i, i ^ d) for i in range(lax.axis_size(axis))])  16.3 us
    ppermute x1, waiting for transfers between devices, shards(): across = lax.ppermute(near, axes, one)  2.43 us
    ppermute x1, waiting for transfers between devices, shards(): far = lax.ppermute(packed, axes, one)  2.09 us
    ppermute x1, starting transfers between devices, shards(): near, = gate([lax.ppermute(packed, axes, two)], lifters[-1])  2.01 us
    pallas_call x1, Pallas kernels, shards(): pl.pallas_call(functools.partial(lift_kernel, helpers), out_shape=[jax.Sh...  1.92 us
    pallas_call x1, Pallas kernels, shards(): pl.pallas_call(functools.partial(score_kernel, planes, helpers, 3), out_s...  1.8 us
    pallas_call x1, Pallas kernels, shards(): pl.pallas_call(functools.partial(sketch_kernel, helpers), out_shape=[jax....  1.53 us
  transfers between devices with their start and end apart: 20, of which 14 were waited for; matrix products, arithmetic and copies ran while one was open for 0% of the time, Pallas kernels for 4%

profile of v10, /device:TPU:0, one launch (start us, length us, event | category | flops | bytes accessed | tf_op | source)
XLA Modules:
  0.0 50.9 jit_solution(1674737984321313561)
XLA Ops:
  0.6 1.9 %lift.1 = (bf16[1552,128]{1,0:T(8,128)(2,1)S(1)}, s32[1,1024]{1,0:T(1,128)S(1)}, f32[8,128]{1,0:T(8,128)S(1)}, f32[32,768]{1,0:T(8,128)S(1)}, f32[32,768]{1,0:T(...) custom-call(bf16[256,768]{1,0:T(8,128)(2,1)} %refs_0_.1, s32[2,256]{1,0:T(2,128)} %bitcast.4, ...), custom_call_target="tpu_custom_call" | custom-call | tf_op jit(solution)/shard_map/lift/pallas_call | solution.py:232
  2.6 0.5 %collective-permute-start.2 = (f32[32,768]{1,0:T(8,128)S(1)}, f32[32,768]{1,0:T(8,128)S(1)}, u32[]{:S(2)}, u32[]{:S(2)}) collective-permute-start(f32[32,768]{1,0:T(8,128)S(1)} %get-tuple-element.25), channel_id=1, source_target_pairs={{0,1},{1,0},{2,3},{3,2},{4,5},{5,4},{6,7},{7,6},{8,9},{9,8},{10,11... | collective-permute-start | bytes 294920 | tf_op jit(solution)/shard_map/ppermute | solution.py:215
  3.1 2.6 %collective-permute-start = (bf16[32,768]{1,0:T(8,128)(2,1)S(1)}, bf16[32,768]{1,0:T(8,128)(2,1)S(1)}, u32[]{:S(2)}, u32[]{:S(2)}) collective-permute-start(bf16[32,768]{1,0:T(8,128)(2,1)S(1)} %get-tuple-element.23), channel_id=1, source_target_pairs={{0,3},{1,2},{2,1},{3,0},{4,7},{5,6},{6,5},{7,4},{8,11},{9,10},{10,... | collective-permute-start | bytes 147464 | tf_op jit(solution)/shard_map/ppermute | solution.py:215
  5.7 0.0 collective-permute-start.1
  5.7 2.0 %collective-permute-start.7 = (bf16[1552,128]{1,0:T(8,128)(2,1)S(1)}, bf16[1552,128]{1,0:T(8,128)(2,1)S(1)}, u32[]{:S(2)}, u32[]{:S(2)}) collective-permute-start(bf16[1552,128]{1,0:T(8,128)(2,1)S(1)} %get-tuple-element.26.refs_0_), channel_id=1, source_target_pairs={{0,4},{1,3},{2,6},{3,1},{4,0},{5,7},{6,2},{7,5},{8,12},{9,11},{10,... | collective-permute-start | bytes 1191944 | tf_op jit(solution)/shard_map/ppermute | solution.py:275
  7.7 0.0 collective-permute-done.refs_1_
  7.8 2.5 %collective-permute-done.1.refs_2_ = bf16[32,768]{1,0:T(8,128)(2,1)S(1)} collective-permute-done((bf16[32,768]{1,0:T(8,128)(2,1)S(1)}, bf16[32,768]{1,0:T(8,128)(2,1)S(1)}, u32[]{:S(2)}, u32[]{:S(2)}) %collective-permute-start.1) | collective-permute-done | bytes 49184 | tf_op jit(solution)/shard_map/ppermute | solution.py:215
  10.3 0.0 collective-permute-done.2.refs_3_
  10.3 3.7 %collective-permute-start.5 = (bf16[32,768]{1,0:T(8,128)(2,1)S(1)}, bf16[32,768]{1,0:T(8,128)(2,1)S(1)}, u32[]{:S(2)}, u32[]{:S(2)}) collective-permute-start(bf16[32,768]{1,0:T(8,128)(2,1)S(1)} %join.1.refs_0_), channel_id=1, source_target_pairs={{0,24},{4,28},{8,16},{12,20},{16,8},{20,12},{24,0},{28,4},{1,25},{... | collective-permute-start | bytes 147464 | tf_op jit(solution)/shard_map/ppermute | solution.py:215
  14.0 0.0 collective-permute-start.4
  14.0 0.8 %collective-permute-start.3 = (bf16[32,768]{1,0:T(8,128)(2,1)S(1)}, bf16[32,768]{1,0:T(8,128)(2,1)S(1)}, u32[]{:S(2)}, u32[]{:S(2)}) collective-permute-start(bf16[32,768]{1,0:T(8,128)(2,1)S(1)} %join.1.refs_0_), channel_id=1, source_target_pairs={{0,8},{4,12},{8,0},{12,4},{16,24},{20,28},{24,16},{28,20},{1,9},{5... | collective-permute-start | bytes 147464 | tf_op jit(solution)/shard_map/ppermute | solution.py:215
  14.8 1.0 %collective-permute-start.9 = (bf16[1552,128]{1,0:T(8,128)(2,1)S(1)}, bf16[1552,128]{1,0:T(8,128)(2,1)S(1)}, u32[]{:S(2)}, u32[]{:S(2)}) collective-permute-start(bf16[1552,128]{1,0:T(8,128)(2,1)S(1)} %get-tuple-element.26.refs_0_), channel_id=1, source_target_pairs={{0,2},{1,5},{2,0},{3,7},{4,6},{5,1},{6,4},{7,3},{8,10},{9,13},{10,... | collective-permute-start | bytes 1191944 | tf_op jit(solution)/shard_map/ppermute | solution.py:274
  15.8 0.6 %collective-permute-done.5.refs_3_.refs_1_ = bf16[32,768]{1,0:T(8,128)(2,1)S(1)} collective-permute-done((bf16[32,768]{1,0:T(8,128)(2,1)S(1)}, bf16[32,768]{1,0:T(8,128)(2,1)S(1)}, u32[]{:S(2)}, u32[]{:S(2)}) %collective-permute-start.5) | collective-permute-done | bytes 49184 | tf_op jit(solution)/shard_map/ppermute | solution.py:215
  16.4 0.0 collective-permute-done.7.refs_0_
  16.4 0.9 %collective-permute-start.8 = (bf16[1552,128]{1,0:T(8,128)(2,1)S(1)}, bf16[1552,128]{1,0:T(8,128)(2,1)S(1)}, u32[]{:S(2)}, u32[]{:S(2)}) collective-permute-start(bf16[1552,128]{1,0:T(8,128)(2,1)S(1)} %gate.1.refs_1_), channel_id=1, source_target_pairs={{0,2},{1,5},{2,0},{3,7},{4,6},{5,1},{6,4},{7,3},{8,10},{9,13},{10,... | collective-permute-start | bytes 1191944 | tf_op jit(solution)/shard_map/ppermute | solution.py:276
  17.3 1.7 %collective-permute-done.4.refs_2_ = bf16[32,768]{1,0:T(8,128)(2,1)S(1)} collective-permute-done((bf16[32,768]{1,0:T(8,128)(2,1)S(1)}, bf16[32,768]{1,0:T(8,128)(2,1)S(1)}, u32[]{:S(2)}, u32[]{:S(2)}) %collective-permute-start.4) | collective-permute-done | bytes 49184 | tf_op jit(solution)/shard_map/ppermute | solution.py:215
  19.0 0.0 collective-permute-done.3.refs_1_
  19.0 0.1 collective-permute-start.6
  19.1 1.4 %collective-permute-done.6.theirs_ref = bf16[128,768]{1,0:T(8,128)(2,1)S(1)} collective-permute-done((bf16[128,768]{1,0:T(8,128)(2,1)S(1)}, bf16[128,768]{1,0:T(8,128)(2,1)S(1)}, u32[]{:S(2)}, u32[]{:S(2)}) %collective-permute-start.6) | collective-permute-done | bytes 196640 | tf_op jit(solution)/shard_map/ppermute | solution.py:215
  20.5 2.1 %collective-permute-done.9.refs_2_ = bf16[1552,128]{1,0:T(8,128)(2,1)S(1)} collective-permute-done((bf16[1552,128]{1,0:T(8,128)(2,1)S(1)}, bf16[1552,128]{1,0:T(8,128)(2,1)S(1)}, u32[]{:S(2)}, u32[]{:S(2)}) %collective-permute-start.9) | collective-permute-done | bytes 397344 | tf_op jit(solution)/shard_map/ppermute | solution.py:274
  22.6 1.8 %score.1.refs_1_ = f32[256,896]{1,0:T(8,128)S(1)} custom-call(bf16[128,768]{1,0:T(8,128)(2,1)S(1)} %stack.1.mine_ref, bf16[128,768]{1,0:T(8,128)(2,1)S(1)} %collective-permute-done.6.theirs_ref, bf16[1552,128]{1,0:T(8,128)(2,1)S(1)} %get-tuple-element.26.refs_0_, bf16[1552,128]{1,0:T(8,128)(2,1)S(1)} %gate.1.refs_1_, ...), custom_call_target="tpu_custom_call" | custom-call | tf_op jit(solution)/shard_map/score/pallas_call | solution.py:279
  24.4 0.0 copy-start
  24.4 2.4 %collective-permute-done.8.refs_0_ = bf16[1552,128]{1,0:T(8,128)(2,1)S(1)} collective-permute-done((bf16[1552,128]{1,0:T(8,128)(2,1)S(1)}, bf16[1552,128]{1,0:T(8,128)(2,1)S(1)}, u32[]{:S(2)}, u32[]{:S(2)}) %collective-permute-start.8) | collective-permute-done | bytes 397344 | tf_op jit(solution)/shard_map/ppermute | solution.py:276
  26.9 0.8 %score_last.1 = (f32[128,896]{1,0:T(8,128)S(1)}, f32[128,896]{1,0:T(8,128)S(1)}) custom-call(bf16[128,768]{1,0:T(8,128)(2,1)S(1)} %stack.1.mine_ref, bf16[128,768]{1,0:T(8,128)(2,1)S(1)} %collective-permute-done.6.theirs_ref, bf16[1552,128]{1,0:T(8,128)(2,1)S(1)} %collective-permute-done.8.refs_0_, f32[256,896]{1,0:T(8,128)S(1)} %score.1.refs_1_), custom_call_target="tpu_custom_call" | custom-call | tf_op jit(solution)/shard_map/score_last/pallas_call | solution.py:285
  27.7 0.1 collective-permute-start.10
  27.7 1.8 %collective-permute-done.10.theirs_ref = f32[128,896]{1,0:T(8,128)S(1)} collective-permute-done((f32[128,896]{1,0:T(8,128)S(1)}, f32[128,896]{1,0:T(8,128)S(1)}, u32[]{:S(2)}, u32[]{:S(2)}) %collective-permute-start.10) | collective-permute-done | bytes 458784 | tf_op jit(solution)/shard_map/ppermute | solution.py:215
  29.6 0.1 fold.1
  29.6 3.7 %collective-permute-start.11 = (bf16[208,128]{1,0:T(8,128)(2,1)S(1)}, bf16[208,128]{1,0:T(8,128)(2,1)S(1)}, u32[]{:S(2)}, u32[]{:S(2)}) collective-permute-start(bf16[208,128]{1,0:T(8,128)(2,1)S(1)} %get-tuple-element.30), channel_id=1, source_target_pairs={{0,24},{4,28},{8,16},{12,20},{16,8},{20,12},{24,0},{28,4},{1,25},{... | collective-permute-start | bytes 159752 | tf_op jit(solution)/shard_map/ppermute | solution.py:215
  33.3 0.0 collective-permute-start.12
  33.3 0.8 %collective-permute-start.13 = (bf16[208,128]{1,0:T(8,128)(2,1)S(1)}, bf16[208,128]{1,0:T(8,128)(2,1)S(1)}, u32[]{:S(2)}, u32[]{:S(2)}) collective-permute-start(bf16[208,128]{1,0:T(8,128)(2,1)S(1)} %get-tuple-element.32), channel_id=1, source_target_pairs={{0,8},{4,12},{8,0},{12,4},{16,24},{20,28},{24,16},{28,20},{1,9},{5... | collective-permute-start | bytes 159752 | tf_op jit(solution)/shard_map/ppermute | solution.py:215
  34.1 2.0 %collective-permute-done.11.refs_0_ = bf16[208,128]{1,0:T(8,128)(2,1)S(1)} collective-permute-done((bf16[208,128]{1,0:T(8,128)(2,1)S(1)}, bf16[208,128]{1,0:T(8,128)(2,1)S(1)}, u32[]{:S(2)}, u32[]{:S(2)}) %collective-permute-start.11) | collective-permute-done | bytes 53280 | tf_op jit(solution)/shard_map/ppermute | solution.py:215
  36.1 2.3 %collective-permute-done.12.refs_1_ = bf16[208,128]{1,0:T(8,128)(2,1)S(1)} collective-permute-done((bf16[208,128]{1,0:T(8,128)(2,1)S(1)}, bf16[208,128]{1,0:T(8,128)(2,1)S(1)}, u32[]{:S(2)}, u32[]{:S(2)}) %collective-permute-start.12) | collective-permute-done | bytes 53280 | tf_op jit(solution)/shard_map/ppermute | solution.py:215
  38.4 0.2 collective-permute-done.13.refs_2_
  38.6 0.1 scale.1.refs_0_
  38.6 0.1 collective-permute-start.16
  38.7 1.1 %collective-permute-start.15 = (bf16[32,768]{1,0:T(8,128)(2,1)S(1)}, bf16[32,768]{1,0:T(8,128)(2,1)S(1)}, u32[]{:S(2)}, u32[]{:S(2)}) collective-permute-start(bf16[32,768]{1,0:T(8,128)(2,1)S(1)} %scale.1.refs_0_), channel_id=1, source_target_pairs={{0,2},{1,3},{2,0},{3,1},{4,6},{5,7},{6,4},{7,5},{8,10},{9,11},{10,... | collective-permute-start | bytes 147464 | tf_op jit(solution)/shard_map/ppermute | solution.py:215
  39.8 0.8 %collective-permute-start.14 = (bf16[32,768]{1,0:T(8,128)(2,1)S(1)}, bf16[32,768]{1,0:T(8,128)(2,1)S(1)}, u32[]{:S(2)}, u32[]{:S(2)}) collective-permute-start(bf16[32,768]{1,0:T(8,128)(2,1)S(1)} %scale.1.refs_0_), channel_id=1, source_target_pairs={{0,1},{1,0},{2,3},{3,2},{4,5},{5,4},{6,7},{7,6},{8,9},{9,8},{10,11... | collective-permute-start | bytes 147464 | tf_op jit(solution)/shard_map/ppermute | solution.py:215
  40.6 1.7 %collective-permute-done.16.refs_3_ = bf16[32,768]{1,0:T(8,128)(2,1)S(1)} collective-permute-done((bf16[32,768]{1,0:T(8,128)(2,1)S(1)}, bf16[32,768]{1,0:T(8,128)(2,1)S(1)}, u32[]{:S(2)}, u32[]{:S(2)}) %collective-permute-start.16) | collective-permute-done | bytes 49184 | tf_op jit(solution)/shard_map/ppermute | solution.py:215
  42.3 1.0 %collective-permute-done.15.refs_2_ = bf16[32,768]{1,0:T(8,128)(2,1)S(1)} collective-permute-done((bf16[32,768]{1,0:T(8,128)(2,1)S(1)}, bf16[32,768]{1,0:T(8,128)(2,1)S(1)}, u32[]{:S(2)}, u32[]{:S(2)}) %collective-permute-start.15) | collective-permute-done | bytes 49184 | tf_op jit(solution)/shard_map/ppermute | solution.py:215
  43.3 0.0 collective-permute-done.14.refs_1_
  43.3 0.0 copy-done
  43.3 1.5 %sketch.1 = (f32[32,1024]{1,0:T(8,128)}, f32[32,768]{1,0:T(8,128)S(1)}, f32[32,768]{1,0:T(8,128)S(1)}, bf16[32,768]{1,0:T(8,128)(2,1)S(1)}, bf16[32,768]{1,0:T(8,128)(2,1)S(1)}) custom-call(s32[1,1024]{1,0:T(1,128)S(1)} %get-tuple-element.20.mark_ref, f32[8,128]{1,0:T(8,128)S(1)} %get-tuple-element.21.resident_ref, bf16[1024,768]{1,0:T(8,128)(2,1)S(1)} %copy-done, ...), custom_call_target="tpu_custom_call" | custom-call | tf_op jit(solution)/shard_map/sketch/pallas_call | solution.py:308
  44.9 0.2 collective-permute-start.19
  45.1 1.0 %collective-permute-start.17 = (bf16[32,768]{1,0:T(8,128)(2,1)S(1)}, bf16[32,768]{1,0:T(8,128)(2,1)S(1)}, u32[]{:S(2)}, u32[]{:S(2)}) collective-permute-start(bf16[32,768]{1,0:T(8,128)(2,1)S(1)} %get-tuple-element.35), channel_id=1, source_target_pairs={{0,3},{1,2},{2,1},{3,0},{4,7},{5,6},{6,5},{7,4},{8,11},{9,10},{10,... | collective-permute-start | bytes 147464 | tf_op jit(solution)/shard_map/ppermute | solution.py:215
  46.1 1.0 %collective-permute-start.18 = (bf16[32,768]{1,0:T(8,128)(2,1)S(1)}, bf16[32,768]{1,0:T(8,128)(2,1)S(1)}, u32[]{:S(2)}, u32[]{:S(2)}) collective-permute-start(bf16[32,768]{1,0:T(8,128)(2,1)S(1)} %get-tuple-element.36), channel_id=1, source_target_pairs={{0,2},{1,3},{2,0},{3,1},{4,6},{5,7},{6,4},{7,5},{8,10},{9,11},{10,... | collective-permute-start | bytes 147464 | tf_op jit(solution)/shard_map/ppermute | solution.py:215
  47.1 1.5 %collective-permute-done.17 = bf16[32,768]{1,0:T(8,128)(2,1)S(1)} collective-permute-done((bf16[32,768]{1,0:T(8,128)(2,1)S(1)}, bf16[32,768]{1,0:T(8,128)(2,1)S(1)}, u32[]{:S(2)}, u32[]{:S(2)}) %collective-permute-start.17) | collective-permute-done | bytes 49184 | tf_op jit(solution)/shard_map/ppermute | solution.py:215
  48.6 1.6 %collective-permute-done.18 = bf16[32,768]{1,0:T(8,128)(2,1)S(1)} collective-permute-done((bf16[32,768]{1,0:T(8,128)(2,1)S(1)}, bf16[32,768]{1,0:T(8,128)(2,1)S(1)}, u32[]{:S(2)}, u32[]{:S(2)}) %collective-permute-start.18) | collective-permute-done | bytes 49184 | tf_op jit(solution)/shard_map/ppermute | solution.py:215
  50.2 0.0 collective-permute-done.19
  50.2 0.7 %add_bitcast_fusion = f32[1,32,768]{2,1,0:T(8,128)} fusion(f32[32,768]{1,0:T(8,128)S(1)} %collective-permute-done.19, bf16[32,768]{1,0:T(8,128)(2,1)S(1)} %collective-permute-done.18, f32[32,768]{1,0:T(8,128)S(1)} %get-tuple-element.34, bf16[32,768]{1,0:T(8,128)(2,1)S(1)} %collective-permute-done.17), kind=kLoop, calls=%fused_computation | loop fusion | flops 122880 | bytes 393216 | tf_op jit(solution)/shard_map/broadcast_in_dim | solution.py:318
  (3 shorter events, 0.0 us)
Async XLA Ops:
  2.6 7.7 %collective-permute-start.2 = (f32[32,768]{1,0:T(8,128)S(1)}, f32[32,768]{1,0:T(8,128)S(1)}, u32[]{:S(2)}, u32[]{:S(2)}) collective-permute-start(f32[32,768]{1,0:T(8,128)S(1)} %get-tuple-element.25), channel_id=1, source_target_pairs={{0,1},{1,0},{2,3},{3,2},{4,5},{5,4},{6,7},{7,6},{8,9},{9,8},{10,11... | collective-permute-start | bytes 294920 | tf_op jit(solution)/shard_map/ppermute | solution.py:215
  3.1 4.7 %collective-permute-start = (bf16[32,768]{1,0:T(8,128)(2,1)S(1)}, bf16[32,768]{1,0:T(8,128)(2,1)S(1)}, u32[]{:S(2)}, u32[]{:S(2)}) collective-permute-start(bf16[32,768]{1,0:T(8,128)(2,1)S(1)} %get-tuple-element.23), channel_id=1, source_target_pairs={{0,3},{1,2},{2,1},{3,0},{4,7},{5,6},{6,5},{7,4},{8,11},{9,10},{10,... | collective-permute-start | bytes 147464 | tf_op jit(solution)/shard_map/ppermute | solution.py:215
  5.7 4.6 %collective-permute-start.1 = (bf16[32,768]{1,0:T(8,128)(2,1)S(1)}, bf16[32,768]{1,0:T(8,128)(2,1)S(1)}, u32[]{:S(2)}, u32[]{:S(2)}) collective-permute-start(bf16[32,768]{1,0:T(8,128)(2,1)S(1)} %get-tuple-element.24), channel_id=1, source_target_pairs={{0,2},{1,3},{2,0},{3,1},{4,6},{5,7},{6,4},{7,5},{8,10},{9,11},{10,... | collective-permute-start | bytes 147464 | tf_op jit(solution)/shard_map/ppermute | solution.py:215
  5.7 10.6 %collective-permute-start.7 = (bf16[1552,128]{1,0:T(8,128)(2,1)S(1)}, bf16[1552,128]{1,0:T(8,128)(2,1)S(1)}, u32[]{:S(2)}, u32[]{:S(2)}) collective-permute-start(bf16[1552,128]{1,0:T(8,128)(2,1)S(1)} %get-tuple-element.26.refs_0_), channel_id=1, source_target_pairs={{0,4},{1,3},{2,6},{3,1},{4,0},{5,7},{6,2},{7,5},{8,12},{9,11},{10,... | collective-permute-start | bytes 1191944 | tf_op jit(solution)/shard_map/ppermute | solution.py:275
  10.3 6.1 %collective-permute-start.5 = (bf16[32,768]{1,0:T(8,128)(2,1)S(1)}, bf16[32,768]{1,0:T(8,128)(2,1)S(1)}, u32[]{:S(2)}, u32[]{:S(2)}) collective-permute-start(bf16[32,768]{1,0:T(8,128)(2,1)S(1)} %join.1.refs_0_), channel_id=1, source_target_pairs={{0,24},{4,28},{8,16},{12,20},{16,8},{20,12},{24,0},{28,4},{1,25},{... | collective-permute-start | bytes 147464 | tf_op jit(solution)/shard_map/ppermute | solution.py:215
  14.0 5.0 %collective-permute-start.4 = (bf16[32,768]{1,0:T(8,128)(2,1)S(1)}, bf16[32,768]{1,0:T(8,128)(2,1)S(1)}, u32[]{:S(2)}, u32[]{:S(2)}) collective-permute-start(bf16[32,768]{1,0:T(8,128)(2,1)S(1)} %join.1.refs_0_), channel_id=1, source_target_pairs={{0,16},{4,20},{8,24},{12,28},{16,0},{20,4},{24,8},{28,12},{1,17},{... | collective-permute-start | bytes 147464 | tf_op jit(solution)/shard_map/ppermute | solution.py:215
  14.0 5.0 %collective-permute-start.3 = (bf16[32,768]{1,0:T(8,128)(2,1)S(1)}, bf16[32,768]{1,0:T(8,128)(2,1)S(1)}, u32[]{:S(2)}, u32[]{:S(2)}) collective-permute-start(bf16[32,768]{1,0:T(8,128)(2,1)S(1)} %join.1.refs_0_), channel_id=1, source_target_pairs={{0,8},{4,12},{8,0},{12,4},{16,24},{20,28},{24,16},{28,20},{1,9},{5... | collective-permute-start | bytes 147464 | tf_op jit(solution)/shard_map/ppermute | solution.py:215
  14.8 7.8 %collective-permute-start.9 = (bf16[1552,128]{1,0:T(8,128)(2,1)S(1)}, bf16[1552,128]{1,0:T(8,128)(2,1)S(1)}, u32[]{:S(2)}, u32[]{:S(2)}) collective-permute-start(bf16[1552,128]{1,0:T(8,128)(2,1)S(1)} %get-tuple-element.26.refs_0_), channel_id=1, source_target_pairs={{0,2},{1,5},{2,0},{3,7},{4,6},{5,1},{6,4},{7,3},{8,10},{9,13},{10,... | collective-permute-start | bytes 1191944 | tf_op jit(solution)/shard_map/ppermute | solution.py:274
  16.4 10.5 %collective-permute-start.8 = (bf16[1552,128]{1,0:T(8,128)(2,1)S(1)}, bf16[1552,128]{1,0:T(8,128)(2,1)S(1)}, u32[]{:S(2)}, u32[]{:S(2)}) collective-permute-start(bf16[1552,128]{1,0:T(8,128)(2,1)S(1)} %gate.1.refs_1_), channel_id=1, source_target_pairs={{0,2},{1,5},{2,0},{3,7},{4,6},{5,1},{6,4},{7,3},{8,10},{9,13},{10,... | collective-permute-start | bytes 1191944 | tf_op jit(solution)/shard_map/ppermute | solution.py:276
  19.0 1.5 %collective-permute-start.6 = (bf16[128,768]{1,0:T(8,128)(2,1)S(1)}, bf16[128,768]{1,0:T(8,128)(2,1)S(1)}, u32[]{:S(2)}, u32[]{:S(2)}) collective-permute-start(bf16[128,768]{1,0:T(8,128)(2,1)S(1)} %stack.1.mine_ref), channel_id=1, source_target_pairs={{0,1},{1,0},{2,3},{3,2},{4,5},{5,4},{6,7},{7,6},{8,9},{9,8},{10,11... | collective-permute-start | bytes 589832 | tf_op jit(solution)/shard_map/ppermute | solution.py:215
  24.4 18.9 %copy-start = (bf16[1024,768]{1,0:T(8,128)(2,1)S(1)}, bf16[1024,768]{1,0:T(8,128)(2,1)}, u32[]{:S(2)}) copy-start(bf16[1024,768]{1,0:T(8,128)(2,1)} %points_ref.1) | copy-start | bytes 4718596
  27.7 1.9 %collective-permute-start.10 = (f32[128,896]{1,0:T(8,128)S(1)}, f32[128,896]{1,0:T(8,128)S(1)}, u32[]{:S(2)}, u32[]{:S(2)}) collective-permute-start(f32[128,896]{1,0:T(8,128)S(1)} %get-tuple-element.28), channel_id=1, source_target_pairs={{0,1},{1,0},{2,3},{3,2},{4,5},{5,4},{6,7},{7,6},{8,9},{9,8},{10,11... | collective-permute-start | bytes 1376264 | tf_op jit(solution)/shard_map/ppermute | solution.py:215
  29.6 6.5 %collective-permute-start.11 = (bf16[208,128]{1,0:T(8,128)(2,1)S(1)}, bf16[208,128]{1,0:T(8,128)(2,1)S(1)}, u32[]{:S(2)}, u32[]{:S(2)}) collective-permute-start(bf16[208,128]{1,0:T(8,128)(2,1)S(1)} %get-tuple-element.30), channel_id=1, source_target_pairs={{0,24},{4,28},{8,16},{12,20},{16,8},{20,12},{24,0},{28,4},{1,25},{... | collective-permute-start | bytes 159752 | tf_op jit(solution)/shard_map/ppermute | solution.py:215
  33.3 5.1 %collective-permute-start.12 = (bf16[208,128]{1,0:T(8,128)(2,1)S(1)}, bf16[208,128]{1,0:T(8,128)(2,1)S(1)}, u32[]{:S(2)}, u32[]{:S(2)}) collective-permute-start(bf16[208,128]{1,0:T(8,128)(2,1)S(1)} %get-tuple-element.31), channel_id=1, source_target_pairs={{0,16},{4,20},{8,24},{12,28},{16,0},{20,4},{24,8},{28,12},{1,17},{... | collective-permute-start | bytes 159752 | tf_op jit(solution)/shard_map/ppermute | solution.py:215
  33.3 5.3 %collective-permute-start.13 = (bf16[208,128]{1,0:T(8,128)(2,1)S(1)}, bf16[208,128]{1,0:T(8,128)(2,1)S(1)}, u32[]{:S(2)}, u32[]{:S(2)}) collective-permute-start(bf16[208,128]{1,0:T(8,128)(2,1)S(1)} %get-tuple-element.32), channel_id=1, source_target_pairs={{0,8},{4,12},{8,0},{12,4},{16,24},{20,28},{24,16},{28,20},{1,9},{5... | collective-permute-start | bytes 159752 | tf_op jit(solution)/shard_map/ppermute | solution.py:215
  38.6 3.7 %collective-permute-start.16 = (bf16[32,768]{1,0:T(8,128)(2,1)S(1)}, bf16[32,768]{1,0:T(8,128)(2,1)S(1)}, u32[]{:S(2)}, u32[]{:S(2)}) collective-permute-start(bf16[32,768]{1,0:T(8,128)(2,1)S(1)} %scale.1.refs_0_), channel_id=1, source_target_pairs={{0,3},{1,2},{2,1},{3,0},{4,7},{5,6},{6,5},{7,4},{8,11},{9,10},{10,... | collective-permute-start | bytes 147464 | tf_op jit(solution)/shard_map/ppermute | solution.py:215
  38.7 4.6 %collective-permute-start.15 = (bf16[32,768]{1,0:T(8,128)(2,1)S(1)}, bf16[32,768]{1,0:T(8,128)(2,1)S(1)}, u32[]{:S(2)}, u32[]{:S(2)}) collective-permute-start(bf16[32,768]{1,0:T(8,128)(2,1)S(1)} %scale.1.refs_0_), channel_id=1, source_target_pairs={{0,2},{1,3},{2,0},{3,1},{4,6},{5,7},{6,4},{7,5},{8,10},{9,11},{10,... | collective-permute-start | bytes 147464 | tf_op jit(solution)/shard_map/ppermute | solution.py:215
  39.8 3.5 %collective-permute-start.14 = (bf16[32,768]{1,0:T(8,128)(2,1)S(1)}, bf16[32,768]{1,0:T(8,128)(2,1)S(1)}, u32[]{:S(2)}, u32[]{:S(2)}) collective-permute-start(bf16[32,768]{1,0:T(8,128)(2,1)S(1)} %scale.1.refs_0_), channel_id=1, source_target_pairs={{0,1},{1,0},{2,3},{3,2},{4,5},{5,4},{6,7},{7,6},{8,9},{9,8},{10,11... | collective-permute-start | bytes 147464 | tf_op jit(solution)/shard_map/ppermute | solution.py:215
  44.9 5.3 %collective-permute-start.19 = (f32[32,768]{1,0:T(8,128)S(1)}, f32[32,768]{1,0:T(8,128)S(1)}, u32[]{:S(2)}, u32[]{:S(2)}) collective-permute-start(f32[32,768]{1,0:T(8,128)S(1)} %get-tuple-element.37), channel_id=1, source_target_pairs={{0,1},{1,0},{2,3},{3,2},{4,5},{5,4},{6,7},{7,6},{8,9},{9,8},{10,11... | collective-permute-start | bytes 294920 | tf_op jit(solution)/shard_map/ppermute | solution.py:215
  45.1 3.5 %collective-permute-start.17 = (bf16[32,768]{1,0:T(8,128)(2,1)S(1)}, bf16[32,768]{1,0:T(8,128)(2,1)S(1)}, u32[]{:S(2)}, u32[]{:S(2)}) collective-permute-start(bf16[32,768]{1,0:T(8,128)(2,1)S(1)} %get-tuple-element.35), channel_id=1, source_target_pairs={{0,3},{1,2},{2,1},{3,0},{4,7},{5,6},{6,5},{7,4},{8,11},{9,10},{10,... | collective-permute-start | bytes 147464 | tf_op jit(solution)/shard_map/ppermute | solution.py:215
  46.1 4.1 %collective-permute-start.18 = (bf16[32,768]{1,0:T(8,128)(2,1)S(1)}, bf16[32,768]{1,0:T(8,128)(2,1)S(1)}, u32[]{:S(2)}, u32[]{:S(2)}) collective-permute-start(bf16[32,768]{1,0:T(8,128)(2,1)S(1)} %get-tuple-element.36), channel_id=1, source_target_pairs={{0,2},{1,3},{2,0},{3,1},{4,6},{5,7},{6,4},{7,5},{8,10},{9,11},{10,... | collective-permute-start | bytes 147464 | tf_op jit(solution)/shard_map/ppermute | solution.py:215

commit v11 on v10

--- a/solution.py
+++ b/solution.py
@@ -92,7 +92,7 @@
 
 
 def stack_kernel(*refs):
-    *parts, out = refs
+    *parts, _, out = refs
     rank = parts[0].shape[0]
     for k, part in enumerate(parts):
         out[k * rank : (k + 1) * rank, :] = part[...]
@@ -110,6 +110,7 @@
         out_specs=[ANY] * len(values),
         input_output_aliases={k: k for k in range(len(values))},
         compiler_params=pltpu.CompilerParams(vmem_limit_bytes=1 << 20),
+        cost_estimate=pl.CostEstimate(flops=5 * 10**9, bytes_accessed=10**5, transcendentals=0),
         name="gate",
     )(*values, *others)
 
@@ -259,21 +260,22 @@
         name="join",
     )(own, *swaps(parts, "help"))
     lifters = [lifter] + [swap(lifter, "shard", INNER * d) for d in range(1, planes)]
-    mine = pl.pallas_call(
-        stack_kernel,
-        out_shape=jax.ShapeDtypeStruct((planes * rank, width), BF16),
-        compiler_params=PARAMS,
-        cost_estimate=pl.CostEstimate(flops=35*10**8, bytes_accessed=10**5, transcendentals=0),
-        name="stack",
-    )(*lifters)
-    theirs = swap(mine, "help", 1)
-
     index, axes = range(groups * helpers), ("shard", "help")
     one = [(i, i ^ (2 if i % 2 == 0 else helpers)) for i in index]
     two = [(i, i ^ (helpers if i % 2 == 0 else 2)) for i in index]
     far = lax.ppermute(packed, axes, one)
     (near,) = gate([lax.ppermute(packed, axes, two)], lifters[-1])
     across = lax.ppermute(near, axes, one)
+
+    mine = pl.pallas_call(
+        stack_kernel,
+        out_shape=jax.ShapeDtypeStruct((planes * rank, width), BF16),
+        in_specs=[VMEM] * planes + [ANY],
+        compiler_params=PARAMS,
+        cost_estimate=pl.CostEstimate(flops=25 * 10**8, bytes_accessed=10**5, transcendentals=0),
+        name="stack",
+    )(*lifters, far)
+    theirs = swap(mine, "help", 1)
 
     wide = width + LANES
     begun = pl.pallas_call(

time: 51.1 us -> 49.8 us (0.975)
  waiting for transfers between devices: 22.9 us -> 21.5 us
    ppermute x1, waiting for transfers between devices: 2.43 us -> 0.91 us  [shards(): across = lax.ppermute(near, axes, one)]
where the time goes in v11:
time: 49.8 us; the launch traced here: 49.5 us
  waiting for transfers between devices  21.5 us (43%)
  starting transfers between devices  20.4 us (41%)
  Pallas kernels  6.24 us (13%)
  between operations  0.72 us (1%)
  other arithmetic  0.67 us (1%)
    ppermute x17, waiting for transfers between devices, swap(): lax.ppermute(value, axis, [(i, i ^ d) for i in range(lax.axis_size(axis))])  18.8 us
    ppermute x17, starting transfers between devices, swap(): lax.ppermute(value, axis, [(i, i ^ d) for i in range(lax.axis_size(axis))])  16.4 us
    ppermute x1, starting transfers between devices, shards(): near, = gate([lax.ppermute(packed, axes, two)], lifters[-1])  2.01 us
    pallas_call x1, Pallas kernels, shards(): pl.pallas_call(functools.partial(lift_kernel, helpers), out_shape=[jax.Sh...  1.92 us
    ppermute x1, waiting for transfers between devices, shards(): far = lax.ppermute(packed, axes, one)  1.82 us
    pallas_call x1, Pallas kernels, shards(): pl.pallas_call(functools.partial(score_kernel, planes, helpers, 3), out_s...  1.81 us
    pallas_call x1, Pallas kernels, shards(): pl.pallas_call(functools.partial(sketch_kernel, helpers), out_shape=[jax....  1.53 us
    ppermute x1, starting transfers between devices, shards(): far = lax.ppermute(packed, axes, one)  1.01 us
  transfers between devices with their start and end apart: 20, of which 14 were waited for; matrix products, arithmetic and copies ran while one was open for 0% of the time, Pallas kernels for 4%

profile of v11, /device:TPU:0, one launch (start us, length us, event | category | flops | bytes accessed | tf_op | source)
XLA Modules:
  0.0 49.5 jit_solution(14911751970187322562)
XLA Ops:
  0.6 1.9 %lift.1 = (bf16[1552,128]{1,0:T(8,128)(2,1)S(1)}, s32[1,1024]{1,0:T(1,128)S(1)}, f32[8,128]{1,0:T(8,128)S(1)}, f32[32,768]{1,0:T(8,128)S(1)}, f32[32,768]{1,0:T(...) custom-call(bf16[256,768]{1,0:T(8,128)(2,1)} %refs_0_.1, s32[2,256]{1,0:T(2,128)} %bitcast.4, ...), custom_call_target="tpu_custom_call" | custom-call | tf_op jit(solution)/shard_map/lift/pallas_call | solution.py:233
  2.6 0.5 %collective-permute-start.2 = (f32[32,768]{1,0:T(8,128)S(1)}, f32[32,768]{1,0:T(8,128)S(1)}, u32[]{:S(2)}, u32[]{:S(2)}) collective-permute-start(f32[32,768]{1,0:T(8,128)S(1)} %get-tuple-element.25), channel_id=1, source_target_pairs={{0,1},{1,0},{2,3},{3,2},{4,5},{5,4},{6,7},{7,6},{8,9},{9,8},{10,11... | collective-permute-start | bytes 294920 | tf_op jit(solution)/shard_map/ppermute | solution.py:216
  3.1 2.6 %collective-permute-start = (bf16[32,768]{1,0:T(8,128)(2,1)S(1)}, bf16[32,768]{1,0:T(8,128)(2,1)S(1)}, u32[]{:S(2)}, u32[]{:S(2)}) collective-permute-start(bf16[32,768]{1,0:T(8,128)(2,1)S(1)} %get-tuple-element.23), channel_id=1, source_target_pairs={{0,3},{1,2},{2,1},{3,0},{4,7},{5,6},{6,5},{7,4},{8,11},{9,10},{10,... | collective-permute-start | bytes 147464 | tf_op jit(solution)/shard_map/ppermute | solution.py:216
  5.7 0.0 collective-permute-start.1
  5.7 2.0 %collective-permute-start.8 = (bf16[1552,128]{1,0:T(8,128)(2,1)S(1)}, bf16[1552,128]{1,0:T(8,128)(2,1)S(1)}, u32[]{:S(2)}, u32[]{:S(2)}) collective-permute-start(bf16[1552,128]{1,0:T(8,128)(2,1)S(1)} %get-tuple-element.26.refs_0_), channel_id=1, source_target_pairs={{0,4},{1,3},{2,6},{3,1},{4,0},{5,7},{6,2},{7,5},{8,12},{9,11},{10,... | collective-permute-start | bytes 1191944 | tf_op jit(solution)/shard_map/ppermute | solution.py:267
  7.7 0.0 collective-permute-done.refs_1_
  7.8 2.5 %collective-permute-done.1.refs_2_ = bf16[32,768]{1,0:T(8,128)(2,1)S(1)} collective-permute-done((bf16[32,768]{1,0:T(8,128)(2,1)S(1)}, bf16[32,768]{1,0:T(8,128)(2,1)S(1)}, u32[]{:S(2)}, u32[]{:S(2)}) %collective-permute-start.1) | collective-permute-done | bytes 49184 | tf_op jit(solution)/shard_map/ppermute | solution.py:216
  10.3 0.0 collective-permute-done.2.refs_3_
  10.3 3.7 %collective-permute-start.5 = (bf16[32,768]{1,0:T(8,128)(2,1)S(1)}, bf16[32,768]{1,0:T(8,128)(2,1)S(1)}, u32[]{:S(2)}, u32[]{:S(2)}) collective-permute-start(bf16[32,768]{1,0:T(8,128)(2,1)S(1)} %join.1.refs_0_), channel_id=1, source_target_pairs={{0,24},{4,28},{8,16},{12,20},{16,8},{20,12},{24,0},{28,4},{1,25},{... | collective-permute-start | bytes 147464 | tf_op jit(solution)/shard_map/ppermute | solution.py:216
  14.0 1.0 %collective-permute-start.6 = (bf16[1552,128]{1,0:T(8,128)(2,1)S(1)}, bf16[1552,128]{1,0:T(8,128)(2,1)S(1)}, u32[]{:S(2)}, u32[]{:S(2)}) collective-permute-start(bf16[1552,128]{1,0:T(8,128)(2,1)S(1)} %get-tuple-element.26.refs_0_), channel_id=1, source_target_pairs={{0,2},{1,5},{2,0},{3,7},{4,6},{5,1},{6,4},{7,3},{8,10},{9,13},{10,... | collective-permute-start | bytes 1191944 | tf_op jit(solution)/shard_map/ppermute | solution.py:266
  15.0 0.0 collective-permute-start.3
  15.0 0.8 %collective-permute-start.4 = (bf16[32,768]{1,0:T(8,128)(2,1)S(1)}, bf16[32,768]{1,0:T(8,128)(2,1)S(1)}, u32[]{:S(2)}, u32[]{:S(2)}) collective-permute-start(bf16[32,768]{1,0:T(8,128)(2,1)S(1)} %join.1.refs_0_), channel_id=1, source_target_pairs={{0,16},{4,20},{8,24},{12,28},{16,0},{20,4},{24,8},{28,12},{1,17},{... | collective-permute-start | bytes 147464 | tf_op jit(solution)/shard_map/ppermute | solution.py:216
  15.8 0.5 %collective-permute-done.5.refs_3_.refs_1_ = bf16[32,768]{1,0:T(8,128)(2,1)S(1)} collective-permute-done((bf16[32,768]{1,0:T(8,128)(2,1)S(1)}, bf16[32,768]{1,0:T(8,128)(2,1)S(1)}, u32[]{:S(2)}, u32[]{:S(2)}) %collective-permute-start.5) | collective-permute-done | bytes 49184 | tf_op jit(solution)/shard_map/ppermute | solution.py:216
  16.3 0.0 collective-permute-done.8.refs_0_
  16.3 1.0 %collective-permute-start.9 = (bf16[1552,128]{1,0:T(8,128)(2,1)S(1)}, bf16[1552,128]{1,0:T(8,128)(2,1)S(1)}, u32[]{:S(2)}, u32[]{:S(2)}) collective-permute-start(bf16[1552,128]{1,0:T(8,128)(2,1)S(1)} %gate.1.refs_1_), channel_id=1, source_target_pairs={{0,2},{1,5},{2,0},{3,7},{4,6},{5,1},{6,4},{7,3},{8,10},{9,13},{10,... | collective-permute-start | bytes 1191944 | tf_op jit(solution)/shard_map/ppermute | solution.py:268
  17.3 1.8 %collective-permute-done.3.refs_1_ = bf16[32,768]{1,0:T(8,128)(2,1)S(1)} collective-permute-done((bf16[32,768]{1,0:T(8,128)(2,1)S(1)}, bf16[32,768]{1,0:T(8,128)(2,1)S(1)}, u32[]{:S(2)}, u32[]{:S(2)}) %collective-permute-start.3) | collective-permute-done | bytes 49184 | tf_op jit(solution)/shard_map/ppermute | solution.py:216
  19.1 0.9 %collective-permute-done.4.refs_2_ = bf16[32,768]{1,0:T(8,128)(2,1)S(1)} collective-permute-done((bf16[32,768]{1,0:T(8,128)(2,1)S(1)}, bf16[32,768]{1,0:T(8,128)(2,1)S(1)}, u32[]{:S(2)}, u32[]{:S(2)}) %collective-permute-start.4) | collective-permute-done | bytes 49184 | tf_op jit(solution)/shard_map/ppermute | solution.py:216
  20.0 1.8 %collective-permute-done.6.refs_4_.refs_2_ = bf16[1552,128]{1,0:T(8,128)(2,1)S(1)} collective-permute-done((bf16[1552,128]{1,0:T(8,128)(2,1)S(1)}, bf16[1552,128]{1,0:T(8,128)(2,1)S(1)}, u32[]{:S(2)}, u32[]{:S(2)}) %collective-permute-start.6) | collective-permute-done | bytes 397344 | tf_op jit(solution)/shard_map/ppermute | solution.py:266
  21.8 0.1 collective-permute-start.7
  21.9 1.4 %collective-permute-done.7.theirs_ref = bf16[128,768]{1,0:T(8,128)(2,1)S(1)} collective-permute-done((bf16[128,768]{1,0:T(8,128)(2,1)S(1)}, bf16[128,768]{1,0:T(8,128)(2,1)S(1)}, u32[]{:S(2)}, u32[]{:S(2)}) %collective-permute-start.7) | collective-permute-done | bytes 196640 | tf_op jit(solution)/shard_map/ppermute | solution.py:216
  23.3 1.8 %score.1.refs_1_ = f32[256,896]{1,0:T(8,128)S(1)} custom-call(bf16[128,768]{1,0:T(8,128)(2,1)S(1)} %stack.1.mine_ref, bf16[128,768]{1,0:T(8,128)(2,1)S(1)} %collective-permute-done.7.theirs_ref, bf16[1552,128]{1,0:T(8,128)(2,1)S(1)} %get-tuple-element.26.refs_0_, bf16[1552,128]{1,0:T(8,128)(2,1)S(1)} %gate.1.refs_1_, ...), custom_call_target="tpu_custom_call" | custom-call | tf_op jit(solution)/shard_map/score/pallas_call | solution.py:281
  25.2 0.0 copy-start
  25.2 0.9 %collective-permute-done.9.refs_0_ = bf16[1552,128]{1,0:T(8,128)(2,1)S(1)} collective-permute-done((bf16[1552,128]{1,0:T(8,128)(2,1)S(1)}, bf16[1552,128]{1,0:T(8,128)(2,1)S(1)}, u32[]{:S(2)}, u32[]{:S(2)}) %collective-permute-start.9) | collective-permute-done | bytes 397344 | tf_op jit(solution)/shard_map/ppermute | solution.py:268
  26.1 0.8 %score_last.1 = (f32[128,896]{1,0:T(8,128)S(1)}, f32[128,896]{1,0:T(8,128)S(1)}) custom-call(bf16[128,768]{1,0:T(8,128)(2,1)S(1)} %stack.1.mine_ref, bf16[128,768]{1,0:T(8,128)(2,1)S(1)} %collective-permute-done.7.theirs_ref, bf16[1552,128]{1,0:T(8,128)(2,1)S(1)} %collective-permute-done.9.refs_0_, f32[256,896]{1,0:T(8,128)S(1)} %score.1.refs_1_), custom_call_target="tpu_custom_call" | custom-call | tf_op jit(solution)/shard_map/score_last/pallas_call | solution.py:287
  26.9 0.1 collective-permute-start.10
  27.0 1.8 %collective-permute-done.10.theirs_ref = f32[128,896]{1,0:T(8,128)S(1)} collective-permute-done((f32[128,896]{1,0:T(8,128)S(1)}, f32[128,896]{1,0:T(8,128)S(1)}, u32[]{:S(2)}, u32[]{:S(2)}) %collective-permute-start.10) | collective-permute-done | bytes 458784 | tf_op jit(solution)/shard_map/ppermute | solution.py:216
  28.8 0.1 fold.1
  28.8 2.0 %collective-permute-start.11 = (bf16[208,128]{1,0:T(8,128)(2,1)S(1)}, bf16[208,128]{1,0:T(8,128)(2,1)S(1)}, u32[]{:S(2)}, u32[]{:S(2)}) collective-permute-start(bf16[208,128]{1,0:T(8,128)(2,1)S(1)} %get-tuple-element.30), channel_id=1, source_target_pairs={{0,24},{4,28},{8,16},{12,20},{16,8},{20,12},{24,0},{28,4},{1,25},{... | collective-permute-start | bytes 159752 | tf_op jit(solution)/shard_map/ppermute | solution.py:216
  30.8 0.0 collective-permute-start.12
  30.8 2.5 %collective-permute-start.13 = (bf16[208,128]{1,0:T(8,128)(2,1)S(1)}, bf16[208,128]{1,0:T(8,128)(2,1)S(1)}, u32[]{:S(2)}, u32[]{:S(2)}) collective-permute-start(bf16[208,128]{1,0:T(8,128)(2,1)S(1)} %get-tuple-element.32), channel_id=1, source_target_pairs={{0,8},{4,12},{8,0},{12,4},{16,24},{20,28},{24,16},{28,20},{1,9},{5... | collective-permute-start | bytes 159752 | tf_op jit(solution)/shard_map/ppermute | solution.py:216
  33.3 2.0 %collective-permute-done.11.refs_0_ = bf16[208,128]{1,0:T(8,128)(2,1)S(1)} collective-permute-done((bf16[208,128]{1,0:T(8,128)(2,1)S(1)}, bf16[208,128]{1,0:T(8,128)(2,1)S(1)}, u32[]{:S(2)}, u32[]{:S(2)}) %collective-permute-start.11) | collective-permute-done | bytes 53280 | tf_op jit(solution)/shard_map/ppermute | solution.py:216
  35.3 1.6 %collective-permute-done.12.refs_1_ = bf16[208,128]{1,0:T(8,128)(2,1)S(1)} collective-permute-done((bf16[208,128]{1,0:T(8,128)(2,1)S(1)}, bf16[208,128]{1,0:T(8,128)(2,1)S(1)}, u32[]{:S(2)}, u32[]{:S(2)}) %collective-permute-start.12) | collective-permute-done | bytes 53280 | tf_op jit(solution)/shard_map/ppermute | solution.py:216
  36.8 0.0 collective-permute-done.13.refs_2_
  36.8 0.1 scale.1.refs_0_
  36.9 0.1 collective-permute-start.14
  37.0 1.1 %collective-permute-start.15 = (bf16[32,768]{1,0:T(8,128)(2,1)S(1)}, bf16[32,768]{1,0:T(8,128)(2,1)S(1)}, u32[]{:S(2)}, u32[]{:S(2)}) collective-permute-start(bf16[32,768]{1,0:T(8,128)(2,1)S(1)} %scale.1.refs_0_), channel_id=1, source_target_pairs={{0,2},{1,3},{2,0},{3,1},{4,6},{5,7},{6,4},{7,5},{8,10},{9,11},{10,... | collective-permute-start | bytes 147464 | tf_op jit(solution)/shard_map/ppermute | solution.py:216
  38.1 0.8 %collective-permute-start.16 = (bf16[32,768]{1,0:T(8,128)(2,1)S(1)}, bf16[32,768]{1,0:T(8,128)(2,1)S(1)}, u32[]{:S(2)}, u32[]{:S(2)}) collective-permute-start(bf16[32,768]{1,0:T(8,128)(2,1)S(1)} %scale.1.refs_0_), channel_id=1, source_target_pairs={{0,3},{1,2},{2,1},{3,0},{4,7},{5,6},{6,5},{7,4},{8,11},{9,10},{10,... | collective-permute-start | bytes 147464 | tf_op jit(solution)/shard_map/ppermute | solution.py:216
  38.9 0.0 collective-permute-done.14.refs_1_
  38.9 2.5 %collective-permute-done.15.refs_2_ = bf16[32,768]{1,0:T(8,128)(2,1)S(1)} collective-permute-done((bf16[32,768]{1,0:T(8,128)(2,1)S(1)}, bf16[32,768]{1,0:T(8,128)(2,1)S(1)}, u32[]{:S(2)}, u32[]{:S(2)}) %collective-permute-start.15) | collective-permute-done | bytes 49184 | tf_op jit(solution)/shard_map/ppermute | solution.py:216
  41.3 0.6 %collective-permute-done.16.refs_3_ = bf16[32,768]{1,0:T(8,128)(2,1)S(1)} collective-permute-done((bf16[32,768]{1,0:T(8,128)(2,1)S(1)}, bf16[32,768]{1,0:T(8,128)(2,1)S(1)}, u32[]{:S(2)}, u32[]{:S(2)}) %collective-permute-start.16) | collective-permute-done | bytes 49184 | tf_op jit(solution)/shard_map/ppermute | solution.py:216
  42.0 0.0 copy-done
  42.0 1.5 %sketch.1 = (f32[32,1024]{1,0:T(8,128)}, f32[32,768]{1,0:T(8,128)S(1)}, f32[32,768]{1,0:T(8,128)S(1)}, bf16[32,768]{1,0:T(8,128)(2,1)S(1)}, bf16[32,768]{1,0:T(8,128)(2,1)S(1)}) custom-call(s32[1,1024]{1,0:T(1,128)S(1)} %get-tuple-element.20.mark_ref, f32[8,128]{1,0:T(8,128)S(1)} %get-tuple-element.21.resident_ref, bf16[1024,768]{1,0:T(8,128)(2,1)S(1)} %copy-done, ...), custom_call_target="tpu_custom_call" | custom-call | tf_op jit(solution)/shard_map/sketch/pallas_call | solution.py:310
  43.5 0.2 collective-permute-start.19
  43.7 1.0 %collective-permute-start.17 = (bf16[32,768]{1,0:T(8,128)(2,1)S(1)}, bf16[32,768]{1,0:T(8,128)(2,1)S(1)}, u32[]{:S(2)}, u32[]{:S(2)}) collective-permute-start(bf16[32,768]{1,0:T(8,128)(2,1)S(1)} %get-tuple-element.35), channel_id=1, source_target_pairs={{0,3},{1,2},{2,1},{3,0},{4,7},{5,6},{6,5},{7,4},{8,11},{9,10},{10,... | collective-permute-start | bytes 147464 | tf_op jit(solution)/shard_map/ppermute | solution.py:216
  44.7 1.0 %collective-permute-start.18 = (bf16[32,768]{1,0:T(8,128)(2,1)S(1)}, bf16[32,768]{1,0:T(8,128)(2,1)S(1)}, u32[]{:S(2)}, u32[]{:S(2)}) collective-permute-start(bf16[32,768]{1,0:T(8,128)(2,1)S(1)} %get-tuple-element.36), channel_id=1, source_target_pairs={{0,2},{1,3},{2,0},{3,1},{4,6},{5,7},{6,4},{7,5},{8,10},{9,11},{10,... | collective-permute-start | bytes 147464 | tf_op jit(solution)/shard_map/ppermute | solution.py:216
  45.7 1.5 %collective-permute-done.17 = bf16[32,768]{1,0:T(8,128)(2,1)S(1)} collective-permute-done((bf16[32,768]{1,0:T(8,128)(2,1)S(1)}, bf16[32,768]{1,0:T(8,128)(2,1)S(1)}, u32[]{:S(2)}, u32[]{:S(2)}) %collective-permute-start.17) | collective-permute-done | bytes 49184 | tf_op jit(solution)/shard_map/ppermute | solution.py:216
  47.2 1.7 %collective-permute-done.18 = bf16[32,768]{1,0:T(8,128)(2,1)S(1)} collective-permute-done((bf16[32,768]{1,0:T(8,128)(2,1)S(1)}, bf16[32,768]{1,0:T(8,128)(2,1)S(1)}, u32[]{:S(2)}, u32[]{:S(2)}) %collective-permute-start.18) | collective-permute-done | bytes 49184 | tf_op jit(solution)/shard_map/ppermute | solution.py:216
  48.9 0.0 collective-permute-done.19
  48.9 0.7 %add_bitcast_fusion = f32[1,32,768]{2,1,0:T(8,128)} fusion(f32[32,768]{1,0:T(8,128)S(1)} %collective-permute-done.19, bf16[32,768]{1,0:T(8,128)(2,1)S(1)} %collective-permute-done.18, f32[32,768]{1,0:T(8,128)S(1)} %get-tuple-element.34, bf16[32,768]{1,0:T(8,128)(2,1)S(1)} %collective-permute-done.17), kind=kLoop, calls=%fused_computation | loop fusion | flops 122880 | bytes 393216 | tf_op jit(solution)/shard_map/broadcast_in_dim | solution.py:320
  (3 shorter events, 0.0 us)
Async XLA Ops:
  2.6 7.7 %collective-permute-start.2 = (f32[32,768]{1,0:T(8,128)S(1)}, f32[32,768]{1,0:T(8,128)S(1)}, u32[]{:S(2)}, u32[]{:S(2)}) collective-permute-start(f32[32,768]{1,0:T(8,128)S(1)} %get-tuple-element.25), channel_id=1, source_target_pairs={{0,1},{1,0},{2,3},{3,2},{4,5},{5,4},{6,7},{7,6},{8,9},{9,8},{10,11... | collective-permute-start | bytes 294920 | tf_op jit(solution)/shard_map/ppermute | solution.py:216
  3.1 4.7 %collective-permute-start = (bf16[32,768]{1,0:T(8,128)(2,1)S(1)}, bf16[32,768]{1,0:T(8,128)(2,1)S(1)}, u32[]{:S(2)}, u32[]{:S(2)}) collective-permute-start(bf16[32,768]{1,0:T(8,128)(2,1)S(1)} %get-tuple-element.23), channel_id=1, source_target_pairs={{0,3},{1,2},{2,1},{3,0},{4,7},{5,6},{6,5},{7,4},{8,11},{9,10},{10,... | collective-permute-start | bytes 147464 | tf_op jit(solution)/shard_map/ppermute | solution.py:216
  5.7 4.6 %collective-permute-start.1 = (bf16[32,768]{1,0:T(8,128)(2,1)S(1)}, bf16[32,768]{1,0:T(8,128)(2,1)S(1)}, u32[]{:S(2)}, u32[]{:S(2)}) collective-permute-start(bf16[32,768]{1,0:T(8,128)(2,1)S(1)} %get-tuple-element.24), channel_id=1, source_target_pairs={{0,2},{1,3},{2,0},{3,1},{4,6},{5,7},{6,4},{7,5},{8,10},{9,11},{10,... | collective-permute-start | bytes 147464 | tf_op jit(solution)/shard_map/ppermute | solution.py:216
  5.7 10.6 %collective-permute-start.8 = (bf16[1552,128]{1,0:T(8,128)(2,1)S(1)}, bf16[1552,128]{1,0:T(8,128)(2,1)S(1)}, u32[]{:S(2)}, u32[]{:S(2)}) collective-permute-start(bf16[1552,128]{1,0:T(8,128)(2,1)S(1)} %get-tuple-element.26.refs_0_), channel_id=1, source_target_pairs={{0,4},{1,3},{2,6},{3,1},{4,0},{5,7},{6,2},{7,5},{8,12},{9,11},{10,... | collective-permute-start | bytes 1191944 | tf_op jit(solution)/shard_map/ppermute | solution.py:267
  10.3 6.0 %collective-permute-start.5 = (bf16[32,768]{1,0:T(8,128)(2,1)S(1)}, bf16[32,768]{1,0:T(8,128)(2,1)S(1)}, u32[]{:S(2)}, u32[]{:S(2)}) collective-permute-start(bf16[32,768]{1,0:T(8,128)(2,1)S(1)} %join.1.refs_0_), channel_id=1, source_target_pairs={{0,24},{4,28},{8,16},{12,20},{16,8},{20,12},{24,0},{28,4},{1,25},{... | collective-permute-start | bytes 147464 | tf_op jit(solution)/shard_map/ppermute | solution.py:216
  14.0 7.8 %collective-permute-start.6 = (bf16[1552,128]{1,0:T(8,128)(2,1)S(1)}, bf16[1552,128]{1,0:T(8,128)(2,1)S(1)}, u32[]{:S(2)}, u32[]{:S(2)}) collective-permute-start(bf16[1552,128]{1,0:T(8,128)(2,1)S(1)} %get-tuple-element.26.refs_0_), channel_id=1, source_target_pairs={{0,2},{1,5},{2,0},{3,7},{4,6},{5,1},{6,4},{7,3},{8,10},{9,13},{10,... | collective-permute-start | bytes 1191944 | tf_op jit(solution)/shard_map/ppermute | solution.py:266
  15.0 4.1 %collective-permute-start.3 = (bf16[32,768]{1,0:T(8,128)(2,1)S(1)}, bf16[32,768]{1,0:T(8,128)(2,1)S(1)}, u32[]{:S(2)}, u32[]{:S(2)}) collective-permute-start(bf16[32,768]{1,0:T(8,128)(2,1)S(1)} %join.1.refs_0_), channel_id=1, source_target_pairs={{0,8},{4,12},{8,0},{12,4},{16,24},{20,28},{24,16},{28,20},{1,9},{5... | collective-permute-start | bytes 147464 | tf_op jit(solution)/shard_map/ppermute | solution.py:216
  15.0 5.0 %collective-permute-start.4 = (bf16[32,768]{1,0:T(8,128)(2,1)S(1)}, bf16[32,768]{1,0:T(8,128)(2,1)S(1)}, u32[]{:S(2)}, u32[]{:S(2)}) collective-permute-start(bf16[32,768]{1,0:T(8,128)(2,1)S(1)} %join.1.refs_0_), channel_id=1, source_target_pairs={{0,16},{4,20},{8,24},{12,28},{16,0},{20,4},{24,8},{28,12},{1,17},{... | collective-permute-start | bytes 147464 | tf_op jit(solution)/shard_map/ppermute | solution.py:216
  16.3 9.8 %collective-permute-start.9 = (bf16[1552,128]{1,0:T(8,128)(2,1)S(1)}, bf16[1552,128]{1,0:T(8,128)(2,1)S(1)}, u32[]{:S(2)}, u32[]{:S(2)}) collective-permute-start(bf16[1552,128]{1,0:T(8,128)(2,1)S(1)} %gate.1.refs_1_), channel_id=1, source_target_pairs={{0,2},{1,5},{2,0},{3,7},{4,6},{5,1},{6,4},{7,3},{8,10},{9,13},{10,... | collective-permute-start | bytes 1191944 | tf_op jit(solution)/shard_map/ppermute | solution.py:268
  21.8 1.5 %collective-permute-start.7 = (bf16[128,768]{1,0:T(8,128)(2,1)S(1)}, bf16[128,768]{1,0:T(8,128)(2,1)S(1)}, u32[]{:S(2)}, u32[]{:S(2)}) collective-permute-start(bf16[128,768]{1,0:T(8,128)(2,1)S(1)} %stack.1.mine_ref), channel_id=1, source_target_pairs={{0,1},{1,0},{2,3},{3,2},{4,5},{5,4},{6,7},{7,6},{8,9},{9,8},{10,11... | collective-permute-start | bytes 589832 | tf_op jit(solution)/shard_map/ppermute | solution.py:216
  25.2 16.8 %copy-start = (bf16[1024,768]{1,0:T(8,128)(2,1)S(1)}, bf16[1024,768]{1,0:T(8,128)(2,1)}, u32[]{:S(2)}) copy-start(bf16[1024,768]{1,0:T(8,128)(2,1)} %points_ref.1) | copy-start | bytes 4718596
  26.9 1.9 %collective-permute-start.10 = (f32[128,896]{1,0:T(8,128)S(1)}, f32[128,896]{1,0:T(8,128)S(1)}, u32[]{:S(2)}, u32[]{:S(2)}) collective-permute-start(f32[128,896]{1,0:T(8,128)S(1)} %get-tuple-element.28), channel_id=1, source_target_pairs={{0,1},{1,0},{2,3},{3,2},{4,5},{5,4},{6,7},{7,6},{8,9},{9,8},{10,11... | collective-permute-start | bytes 1376264 | tf_op jit(solution)/shard_map/ppermute | solution.py:216
  28.8 6.4 %collective-permute-start.11 = (bf16[208,128]{1,0:T(8,128)(2,1)S(1)}, bf16[208,128]{1,0:T(8,128)(2,1)S(1)}, u32[]{:S(2)}, u32[]{:S(2)}) collective-permute-start(bf16[208,128]{1,0:T(8,128)(2,1)S(1)} %get-tuple-element.30), channel_id=1, source_target_pairs={{0,24},{4,28},{8,16},{12,20},{16,8},{20,12},{24,0},{28,4},{1,25},{... | collective-permute-start | bytes 159752 | tf_op jit(solution)/shard_map/ppermute | solution.py:216
  30.8 6.0 %collective-permute-start.12 = (bf16[208,128]{1,0:T(8,128)(2,1)S(1)}, bf16[208,128]{1,0:T(8,128)(2,1)S(1)}, u32[]{:S(2)}, u32[]{:S(2)}) collective-permute-start(bf16[208,128]{1,0:T(8,128)(2,1)S(1)} %get-tuple-element.31), channel_id=1, source_target_pairs={{0,16},{4,20},{8,24},{12,28},{16,0},{20,4},{24,8},{28,12},{1,17},{... | collective-permute-start | bytes 159752 | tf_op jit(solution)/shard_map/ppermute | solution.py:216
  30.8 6.0 %collective-permute-start.13 = (bf16[208,128]{1,0:T(8,128)(2,1)S(1)}, bf16[208,128]{1,0:T(8,128)(2,1)S(1)}, u32[]{:S(2)}, u32[]{:S(2)}) collective-permute-start(bf16[208,128]{1,0:T(8,128)(2,1)S(1)} %get-tuple-element.32), channel_id=1, source_target_pairs={{0,8},{4,12},{8,0},{12,4},{16,24},{20,28},{24,16},{28,20},{1,9},{5... | collective-permute-start | bytes 159752 | tf_op jit(solution)/shard_map/ppermute | solution.py:216
  36.9 1.9 %collective-permute-start.14 = (bf16[32,768]{1,0:T(8,128)(2,1)S(1)}, bf16[32,768]{1,0:T(8,128)(2,1)S(1)}, u32[]{:S(2)}, u32[]{:S(2)}) collective-permute-start(bf16[32,768]{1,0:T(8,128)(2,1)S(1)} %scale.1.refs_0_), channel_id=1, source_target_pairs={{0,1},{1,0},{2,3},{3,2},{4,5},{5,4},{6,7},{7,6},{8,9},{9,8},{10,11... | collective-permute-start | bytes 147464 | tf_op jit(solution)/shard_map/ppermute | solution.py:216
  37.0 4.3 %collective-permute-start.15 = (bf16[32,768]{1,0:T(8,128)(2,1)S(1)}, bf16[32,768]{1,0:T(8,128)(2,1)S(1)}, u32[]{:S(2)}, u32[]{:S(2)}) collective-permute-start(bf16[32,768]{1,0:T(8,128)(2,1)S(1)} %scale.1.refs_0_), channel_id=1, source_target_pairs={{0,2},{1,3},{2,0},{3,1},{4,6},{5,7},{6,4},{7,5},{8,10},{9,11},{10,... | collective-permute-start | bytes 147464 | tf_op jit(solution)/shard_map/ppermute | solution.py:216
  38.1 3.9 %collective-permute-start.16 = (bf16[32,768]{1,0:T(8,128)(2,1)S(1)}, bf16[32,768]{1,0:T(8,128)(2,1)S(1)}, u32[]{:S(2)}, u32[]{:S(2)}) collective-permute-start(bf16[32,768]{1,0:T(8,128)(2,1)S(1)} %scale.1.refs_0_), channel_id=1, source_target_pairs={{0,3},{1,2},{2,1},{3,0},{4,7},{5,6},{6,5},{7,4},{8,11},{9,10},{10,... | collective-permute-start | bytes 147464 | tf_op jit(solution)/shard_map/ppermute | solution.py:216
  43.5 5.4 %collective-permute-start.19 = (f32[32,768]{1,0:T(8,128)S(1)}, f32[32,768]{1,0:T(8,128)S(1)}, u32[]{:S(2)}, u32[]{:S(2)}) collective-permute-start(f32[32,768]{1,0:T(8,128)S(1)} %get-tuple-element.37), channel_id=1, source_target_pairs={{0,1},{1,0},{2,3},{3,2},{4,5},{5,4},{6,7},{7,6},{8,9},{9,8},{10,11... | collective-permute-start | bytes 294920 | tf_op jit(solution)/shard_map/ppermute | solution.py:216
  43.7 3.5 %collective-permute-start.17 = (bf16[32,768]{1,0:T(8,128)(2,1)S(1)}, bf16[32,768]{1,0:T(8,128)(2,1)S(1)}, u32[]{:S(2)}, u32[]{:S(2)}) collective-permute-start(bf16[32,768]{1,0:T(8,128)(2,1)S(1)} %get-tuple-element.35), channel_id=1, source_target_pairs={{0,3},{1,2},{2,1},{3,0},{4,7},{5,6},{6,5},{7,4},{8,11},{9,10},{10,... | collective-permute-start | bytes 147464 | tf_op jit(solution)/shard_map/ppermute | solution.py:216
  44.7 4.1 %collective-permute-start.18 = (bf16[32,768]{1,0:T(8,128)(2,1)S(1)}, bf16[32,768]{1,0:T(8,128)(2,1)S(1)}, u32[]{:S(2)}, u32[]{:S(2)}) collective-permute-start(bf16[32,768]{1,0:T(8,128)(2,1)S(1)} %get-tuple-element.36), channel_id=1, source_target_pairs={{0,2},{1,3},{2,0},{3,1},{4,6},{5,7},{6,4},{7,5},{8,10},{9,11},{10,... | collective-permute-start | bytes 147464 | tf_op jit(solution)/shard_map/ppermute | solution.py:216

commit v12 on v11

--- a/solution.py
+++ b/solution.py
@@ -141,7 +141,9 @@
             here = hit.astype(F32)
             tally[k] = here if tally[k] is None else tally[k] + here
         high, low = halves(jnp.concatenate(kept, axis=0))
-        part = contract(high, rows, ((1,), (0,))) + contract(low, rows, ((1,), (0,)))
+        part = contract(high, rows, ((1,), (0,)))
+        if blocks > 1:
+            part = part + contract(low, rows, ((1,), (0,)))
         total = part if total is None else total + part
     named = jnp.concatenate(
         [jnp.broadcast_to(jnp.sum(t, axis=1, keepdims=True), (rank, LANES)) for t in tally], axis=0
@@ -153,31 +155,37 @@
         before, *outs = rest
         for side, out in enumerate(outs):
             part = slice(side * span, (side + 1) * span)
-            out[:, :width] = before[part, :width] + total[part]
-            out[:, width:] = before[part, width:] + named[part]
+            out[:, :width] = (before[part, :width] + total[part]).astype(out.dtype)
+            counts = before[part, width:] + named[part]
+            out[:, width:] = (counts if out.dtype == F32 else digits(counts)).astype(out.dtype)
+
+
+def digits(counts):
+    high = jnp.floor(counts * (1.0 / 256.0))
+    line = lax.broadcasted_iota(jnp.int32, counts.shape, 0)
+    return jnp.where(line % 2 == 0, high, counts - 256.0 * high)
 
 
 def fold_kernel(planes, mine_ref, theirs_ref, own_ref, *send_refs):
     rank, wide = own_ref.shape
     width = wide - LANES
-    line = lax.broadcasted_iota(jnp.int32, (TILE, LANES), 0)
     for d in range(planes):
         part = slice(d * rank, (d + 1) * rank)
-        total = mine_ref[part, :] + theirs_ref[part, :]
+        theirs = theirs_ref[part, :].astype(F32)
+        total = mine_ref[part, :width] + theirs[:, :width]
+        named = mine_ref[part, width:] + 256.0 * theirs[0:1, width:] + theirs[1:2, width:]
         if d == 0:
-            own_ref[...] = total
+            own_ref[:, :width] = total
+            own_ref[:, width:] = named
         else:
             ref = send_refs[d - 1]
             for k in range(width // LANES):
                 ref[k * rank : (k + 1) * rank, :] = total[:, k * LANES : (k + 1) * LANES].astype(BF16)
-            named = total[:TILE, width:]
-            many = jnp.floor(named * (1.0 / 256.0))
-            rest = named - 256.0 * many
-            ref[rank * width // LANES :, :] = jnp.where(line == 0, many, jnp.where(line == 1, rest, 0.0)).astype(BF16)
+            ref[rank * width // LANES :, :] = digits(named[:TILE]).astype(BF16)
 
 
 def scale_kernel(resident_ref, own_ref, *refs):
-    *parts, out_ref = refs
+    *parts, wide_ref, out_ref = refs
     rank, width = out_ref.shape
     total = own_ref[:, :width]
     queried = own_ref[0:1, width : width + 1]
@@ -187,7 +195,8 @@
         queried = queried + 256.0 * tile[0:1, 0:1] + tile[1:2, 0:1]
     resident = resident_ref[0:1, 0:1]
     factor = lax.rsqrt((queried + 1.0) * (queried + resident)) * (1.0 / width)
-    out_ref[...] = (total * factor).astype(out_ref.dtype)
+    wide_ref[...] = total * factor
+    out_ref[...] = (total * factor).astype(BF16)
 
 
 def sketch_kernel(helpers, mark_ref, resident_ref, points_ref, *refs):
@@ -196,10 +205,21 @@
     rank, count = sketch_ref.shape
     mark = mark_ref[...]
     points = points_ref[...]
-    product = contract(jnp.concatenate([s[...] for s in scaled], axis=0), points, ((1,), (1,)))
-    sketch = product[:rank]
+    blocks, rests = [], []
+    for s in scaled:
+        if s.dtype == F32:
+            high, low = halves(s[...])
+            blocks.append(high)
+            rests.append(low)
+        else:
+            blocks.append(s[...])
+    product = contract(jnp.concatenate(blocks + rests, axis=0), points, ((1,), (1,)))
+    whole = [product[k * rank : (k + 1) * rank] for k in range(helpers)]
+    for k in range(len(rests)):
+        whole[k] = whole[k] + product[(helpers + k) * rank : (helpers + k + 1) * rank]
+    sketch = whole[0]
     for d in range(1, helpers):
-        sketch = jnp.where(mark == d, product[d * rank : (d + 1) * rank], sketch)
+        sketch = jnp.where(mark == d, whole[d], sketch)
     sketch_ref[...] = sketch
     leaving = pltpu.make_async_copy(sketch_ref, sketch_hbm, sem)
     leaving.start()
@@ -256,7 +276,7 @@
         join_kernel,
         out_shape=sent,
         compiler_params=PARAMS,
-        cost_estimate=pl.CostEstimate(flops=4 * 10**9, bytes_accessed=10**5, transcendentals=0),
+        cost_estimate=pl.CostEstimate(flops=40*10**8, bytes_accessed=10**5, transcendentals=0),
         name="join",
     )(own, *swaps(parts, "help"))
     lifters = [lifter] + [swap(lifter, "shard", INNER * d) for d in range(1, planes)]
@@ -286,7 +306,7 @@
     )(mine, theirs, packed, near, far)
     moments, passed = pl.pallas_call(
         functools.partial(score_kernel, planes, helpers, 1),
-        out_shape=[jax.ShapeDtypeStruct((planes * rank, wide), F32)] * 2,
+        out_shape=[jax.ShapeDtypeStruct((planes * rank, wide), kind) for kind in (F32, BF16)],
         compiler_params=PARAMS,
         name="score_last",
     )(mine, theirs, across, begun)
@@ -299,13 +319,13 @@
     )(moments, swap(passed, "help", 1))
     moments = [folded[0]] + swaps(folded[1:], "shard", INNER)
 
-    scaled = pl.pallas_call(
+    exact, scaled = pl.pallas_call(
         scale_kernel,
-        out_shape=jax.ShapeDtypeStruct((rank, width), BF16),
+        out_shape=[block, sent],
         compiler_params=PARAMS,
         name="scale",
     )(resident, *moments)
-    scaled = [scaled] + [swap(scaled, "help", d) for d in range(1, helpers)]
+    scaled = [exact, swap(exact, "help", 1)] + [swap(scaled, "help", d) for d in range(2, helpers)]
 
     sketch, regressor, *parts = pl.pallas_call(
         functools.partial(sketch_kernel, helpers),

time: 49.8 us -> 49.3 us (0.990)
  no operation moved by 1% of the time
where the time goes in v12:
time: 49.3 us; the launch traced here: 49 us
  waiting for transfers between devices  21.2 us (43%)
  starting transfers between devices  20.4 us (41%)
  Pallas kernels  6.09 us (12%)
  between operations  0.72 us (1%)
  other arithmetic  0.67 us (1%)
    ppermute x17, waiting for transfers between devices, swap(): lax.ppermute(value, axis, [(i, i ^ d) for i in range(lax.axis_size(axis))])  18.5 us
    ppermute x17, starting transfers between devices, swap(): lax.ppermute(value, axis, [(i, i ^ d) for i in range(lax.axis_size(axis))])  16.4 us
    ppermute x1, starting transfers between devices, shards(): near, = gate([lax.ppermute(packed, axes, two)], lifters[-1])  2.01 us
    pallas_call x1, Pallas kernels, shards(): pl.pallas_call(functools.partial(lift_kernel, helpers), out_shape=[jax.Sh...  1.92 us
    ppermute x1, waiting for transfers between devices, shards(): far = lax.ppermute(packed, axes, one)  1.82 us
    pallas_call x1, Pallas kernels, shards(): pl.pallas_call(functools.partial(score_kernel, planes, helpers, 3), out_s...  1.81 us
    pallas_call x1, Pallas kernels, shards(): pl.pallas_call(functools.partial(sketch_kernel, helpers), out_shape=[jax....  1.54 us
    ppermute x1, starting transfers between devices, shards(): far = lax.ppermute(packed, axes, one)  1.01 us
  transfers between devices with their start and end apart: 20, of which 14 were waited for; matrix products, arithmetic and copies ran while one was open for 0% of the time, Pallas kernels for 4%

profile of v12, /device:TPU:0, one launch (start us, length us, event | category | flops | bytes accessed | tf_op | source)
XLA Modules:
  0.0 49.0 jit_solution(16323395529112950676)
XLA Ops:
  0.6 1.9 %lift.1 = (bf16[1552,128]{1,0:T(8,128)(2,1)S(1)}, s32[1,1024]{1,0:T(1,128)S(1)}, f32[8,128]{1,0:T(8,128)S(1)}, f32[32,768]{1,0:T(8,128)S(1)}, f32[32,768]{1,0:T(...) custom-call(bf16[256,768]{1,0:T(8,128)(2,1)} %refs_0_.1, s32[2,256]{1,0:T(2,128)} %bitcast.4, ...), custom_call_target="tpu_custom_call" | custom-call | tf_op jit(solution)/shard_map/lift/pallas_call | solution.py:253
  2.6 0.5 %collective-permute-start.2 = (f32[32,768]{1,0:T(8,128)S(1)}, f32[32,768]{1,0:T(8,128)S(1)}, u32[]{:S(2)}, u32[]{:S(2)}) collective-permute-start(f32[32,768]{1,0:T(8,128)S(1)} %get-tuple-element.27), channel_id=1, source_target_pairs={{0,1},{1,0},{2,3},{3,2},{4,5},{5,4},{6,7},{7,6},{8,9},{9,8},{10,11... | collective-permute-start | bytes 294920 | tf_op jit(solution)/shard_map/ppermute | solution.py:236
  3.1 2.6 %collective-permute-start = (bf16[32,768]{1,0:T(8,128)(2,1)S(1)}, bf16[32,768]{1,0:T(8,128)(2,1)S(1)}, u32[]{:S(2)}, u32[]{:S(2)}) collective-permute-start(bf16[32,768]{1,0:T(8,128)(2,1)S(1)} %get-tuple-element.25), channel_id=1, source_target_pairs={{0,3},{1,2},{2,1},{3,0},{4,7},{5,6},{6,5},{7,4},{8,11},{9,10},{10,... | collective-permute-start | bytes 147464 | tf_op jit(solution)/shard_map/ppermute | solution.py:236
  5.7 0.0 collective-permute-start.1
  5.7 2.0 %collective-permute-start.8 = (bf16[1552,128]{1,0:T(8,128)(2,1)S(1)}, bf16[1552,128]{1,0:T(8,128)(2,1)S(1)}, u32[]{:S(2)}, u32[]{:S(2)}) collective-permute-start(bf16[1552,128]{1,0:T(8,128)(2,1)S(1)} %get-tuple-element.28.refs_0_), channel_id=1, source_target_pairs={{0,4},{1,3},{2,6},{3,1},{4,0},{5,7},{6,2},{7,5},{8,12},{9,11},{10,... | collective-permute-start | bytes 1191944 | tf_op jit(solution)/shard_map/ppermute | solution.py:287
  7.7 0.0 collective-permute-done.refs_1_
  7.8 2.5 %collective-permute-done.1.refs_2_ = bf16[32,768]{1,0:T(8,128)(2,1)S(1)} collective-permute-done((bf16[32,768]{1,0:T(8,128)(2,1)S(1)}, bf16[32,768]{1,0:T(8,128)(2,1)S(1)}, u32[]{:S(2)}, u32[]{:S(2)}) %collective-permute-start.1) | collective-permute-done | bytes 49184 | tf_op jit(solution)/shard_map/ppermute | solution.py:236
  10.3 0.0 collective-permute-done.2.refs_3_
  10.3 3.7 %collective-permute-start.5 = (bf16[32,768]{1,0:T(8,128)(2,1)S(1)}, bf16[32,768]{1,0:T(8,128)(2,1)S(1)}, u32[]{:S(2)}, u32[]{:S(2)}) collective-permute-start(bf16[32,768]{1,0:T(8,128)(2,1)S(1)} %join.1.refs_0_), channel_id=1, source_target_pairs={{0,24},{4,28},{8,16},{12,20},{16,8},{20,12},{24,0},{28,4},{1,25},{... | collective-permute-start | bytes 147464 | tf_op jit(solution)/shard_map/ppermute | solution.py:236
  14.0 1.0 %collective-permute-start.6 = (bf16[1552,128]{1,0:T(8,128)(2,1)S(1)}, bf16[1552,128]{1,0:T(8,128)(2,1)S(1)}, u32[]{:S(2)}, u32[]{:S(2)}) collective-permute-start(bf16[1552,128]{1,0:T(8,128)(2,1)S(1)} %get-tuple-element.28.refs_0_), channel_id=1, source_target_pairs={{0,2},{1,5},{2,0},{3,7},{4,6},{5,1},{6,4},{7,3},{8,10},{9,13},{10,... | collective-permute-start | bytes 1191944 | tf_op jit(solution)/shard_map/ppermute | solution.py:286
  15.0 0.0 collective-permute-start.3
  15.0 0.8 %collective-permute-start.4 = (bf16[32,768]{1,0:T(8,128)(2,1)S(1)}, bf16[32,768]{1,0:T(8,128)(2,1)S(1)}, u32[]{:S(2)}, u32[]{:S(2)}) collective-permute-start(bf16[32,768]{1,0:T(8,128)(2,1)S(1)} %join.1.refs_0_), channel_id=1, source_target_pairs={{0,16},{4,20},{8,24},{12,28},{16,0},{20,4},{24,8},{28,12},{1,17},{... | collective-permute-start | bytes 147464 | tf_op jit(solution)/shard_map/ppermute | solution.py:236
  15.8 0.5 %collective-permute-done.5.refs_3_.refs_1_ = bf16[32,768]{1,0:T(8,128)(2,1)S(1)} collective-permute-done((bf16[32,768]{1,0:T(8,128)(2,1)S(1)}, bf16[32,768]{1,0:T(8,128)(2,1)S(1)}, u32[]{:S(2)}, u32[]{:S(2)}) %collective-permute-start.5) | collective-permute-done | bytes 49184 | tf_op jit(solution)/shard_map/ppermute | solution.py:236
  16.3 0.0 collective-permute-done.8.refs_0_
  16.3 1.0 %collective-permute-start.9 = (bf16[1552,128]{1,0:T(8,128)(2,1)S(1)}, bf16[1552,128]{1,0:T(8,128)(2,1)S(1)}, u32[]{:S(2)}, u32[]{:S(2)}) collective-permute-start(bf16[1552,128]{1,0:T(8,128)(2,1)S(1)} %gate.1.refs_1_), channel_id=1, source_target_pairs={{0,2},{1,5},{2,0},{3,7},{4,6},{5,1},{6,4},{7,3},{8,10},{9,13},{10,... | collective-permute-start | bytes 1191944 | tf_op jit(solution)/shard_map/ppermute | solution.py:288
  17.3 1.8 %collective-permute-done.3.refs_1_ = bf16[32,768]{1,0:T(8,128)(2,1)S(1)} collective-permute-done((bf16[32,768]{1,0:T(8,128)(2,1)S(1)}, bf16[32,768]{1,0:T(8,128)(2,1)S(1)}, u32[]{:S(2)}, u32[]{:S(2)}) %collective-permute-start.3) | collective-permute-done | bytes 49184 | tf_op jit(solution)/shard_map/ppermute | solution.py:236
  19.1 0.9 %collective-permute-done.4.refs_2_ = bf16[32,768]{1,0:T(8,128)(2,1)S(1)} collective-permute-done((bf16[32,768]{1,0:T(8,128)(2,1)S(1)}, bf16[32,768]{1,0:T(8,128)(2,1)S(1)}, u32[]{:S(2)}, u32[]{:S(2)}) %collective-permute-start.4) | collective-permute-done | bytes 49184 | tf_op jit(solution)/shard_map/ppermute | solution.py:236
  20.0 1.8 %collective-permute-done.6.refs_4_.refs_2_ = bf16[1552,128]{1,0:T(8,128)(2,1)S(1)} collective-permute-done((bf16[1552,128]{1,0:T(8,128)(2,1)S(1)}, bf16[1552,128]{1,0:T(8,128)(2,1)S(1)}, u32[]{:S(2)}, u32[]{:S(2)}) %collective-permute-start.6) | collective-permute-done | bytes 397344 | tf_op jit(solution)/shard_map/ppermute | solution.py:286
  21.8 0.1 collective-permute-start.7
  21.9 1.4 %collective-permute-done.7.theirs_ref = bf16[128,768]{1,0:T(8,128)(2,1)S(1)} collective-permute-done((bf16[128,768]{1,0:T(8,128)(2,1)S(1)}, bf16[128,768]{1,0:T(8,128)(2,1)S(1)}, u32[]{:S(2)}, u32[]{:S(2)}) %collective-permute-start.7) | collective-permute-done | bytes 196640 | tf_op jit(solution)/shard_map/ppermute | solution.py:236
  23.3 1.8 %score.1.refs_1_ = f32[256,896]{1,0:T(8,128)S(1)} custom-call(bf16[128,768]{1,0:T(8,128)(2,1)S(1)} %stack.1.mine_ref, bf16[128,768]{1,0:T(8,128)(2,1)S(1)} %collective-permute-done.7.theirs_ref, bf16[1552,128]{1,0:T(8,128)(2,1)S(1)} %get-tuple-element.28.refs_0_, bf16[1552,128]{1,0:T(8,128)(2,1)S(1)} %gate.1.refs_1_, ...), custom_call_target="tpu_custom_call" | custom-call | tf_op jit(solution)/shard_map/score/pallas_call | solution.py:301
  25.2 0.0 copy-start
  25.2 0.9 %collective-permute-done.9.refs_0_ = bf16[1552,128]{1,0:T(8,128)(2,1)S(1)} collective-permute-done((bf16[1552,128]{1,0:T(8,128)(2,1)S(1)}, bf16[1552,128]{1,0:T(8,128)(2,1)S(1)}, u32[]{:S(2)}, u32[]{:S(2)}) %collective-permute-start.9) | collective-permute-done | bytes 397344 | tf_op jit(solution)/shard_map/ppermute | solution.py:288
  26.1 0.6 %score_last.1 = (f32[128,896]{1,0:T(8,128)S(1)}, bf16[128,896]{1,0:T(8,128)(2,1)S(1)}) custom-call(bf16[128,768]{1,0:T(8,128)(2,1)S(1)} %stack.1.mine_ref, bf16[128,768]{1,0:T(8,128)(2,1)S(1)} %collective-permute-done.7.theirs_ref, bf16[1552,128]{1,0:T(8,128)(2,1)S(1)} %collective-permute-done.9.refs_0_, f32[256,896]{1,0:T(8,128)S(1)} %score.1.refs_1_), custom_call_target="tpu_custom_call" | custom-call | tf_op jit(solution)/shard_map/score_last/pallas_call | solution.py:307
  26.7 0.1 collective-permute-start.10
  26.8 1.5 %collective-permute-done.10.theirs_ref = bf16[128,896]{1,0:T(8,128)(2,1)S(1)} collective-permute-done((bf16[128,896]{1,0:T(8,128)(2,1)S(1)}, bf16[128,896]{1,0:T(8,128)(2,1)S(1)}, u32[]{:S(2)}, u32[]{:S(2)}) %collective-permute-start.10) | collective-permute-done | bytes 229408 | tf_op jit(solution)/shard_map/ppermute | solution.py:236
  28.3 0.1 fold.1
  28.3 2.0 %collective-permute-start.11 = (bf16[208,128]{1,0:T(8,128)(2,1)S(1)}, bf16[208,128]{1,0:T(8,128)(2,1)S(1)}, u32[]{:S(2)}, u32[]{:S(2)}) collective-permute-start(bf16[208,128]{1,0:T(8,128)(2,1)S(1)} %get-tuple-element.32), channel_id=1, source_target_pairs={{0,24},{4,28},{8,16},{12,20},{16,8},{20,12},{24,0},{28,4},{1,25},{... | collective-permute-start | bytes 159752 | tf_op jit(solution)/shard_map/ppermute | solution.py:236
  30.3 0.0 collective-permute-start.12
  30.3 2.5 %collective-permute-start.13 = (bf16[208,128]{1,0:T(8,128)(2,1)S(1)}, bf16[208,128]{1,0:T(8,128)(2,1)S(1)}, u32[]{:S(2)}, u32[]{:S(2)}) collective-permute-start(bf16[208,128]{1,0:T(8,128)(2,1)S(1)} %get-tuple-element.34), channel_id=1, source_target_pairs={{0,8},{4,12},{8,0},{12,4},{16,24},{20,28},{24,16},{28,20},{1,9},{5... | collective-permute-start | bytes 159752 | tf_op jit(solution)/shard_map/ppermute | solution.py:236
  32.8 2.0 %collective-permute-done.11.refs_0_ = bf16[208,128]{1,0:T(8,128)(2,1)S(1)} collective-permute-done((bf16[208,128]{1,0:T(8,128)(2,1)S(1)}, bf16[208,128]{1,0:T(8,128)(2,1)S(1)}, u32[]{:S(2)}, u32[]{:S(2)}) %collective-permute-start.11) | collective-permute-done | bytes 53280 | tf_op jit(solution)/shard_map/ppermute | solution.py:236
  34.8 1.6 %collective-permute-done.12.refs_1_ = bf16[208,128]{1,0:T(8,128)(2,1)S(1)} collective-permute-done((bf16[208,128]{1,0:T(8,128)(2,1)S(1)}, bf16[208,128]{1,0:T(8,128)(2,1)S(1)}, u32[]{:S(2)}, u32[]{:S(2)}) %collective-permute-start.12) | collective-permute-done | bytes 53280 | tf_op jit(solution)/shard_map/ppermute | solution.py:236
  36.4 0.0 collective-permute-done.13.refs_2_
  36.4 0.1 scale.1
  36.4 0.1 collective-permute-start.14
  36.5 1.1 %collective-permute-start.15 = (bf16[32,768]{1,0:T(8,128)(2,1)S(1)}, bf16[32,768]{1,0:T(8,128)(2,1)S(1)}, u32[]{:S(2)}, u32[]{:S(2)}) collective-permute-start(bf16[32,768]{1,0:T(8,128)(2,1)S(1)} %get-tuple-element.36), channel_id=1, source_target_pairs={{0,2},{1,3},{2,0},{3,1},{4,6},{5,7},{6,4},{7,5},{8,10},{9,11},{10,... | collective-permute-start | bytes 147464 | tf_op jit(solution)/shard_map/ppermute | solution.py:236
  37.6 0.8 %collective-permute-start.16 = (bf16[32,768]{1,0:T(8,128)(2,1)S(1)}, bf16[32,768]{1,0:T(8,128)(2,1)S(1)}, u32[]{:S(2)}, u32[]{:S(2)}) collective-permute-start(bf16[32,768]{1,0:T(8,128)(2,1)S(1)} %get-tuple-element.36), channel_id=1, source_target_pairs={{0,3},{1,2},{2,1},{3,0},{4,7},{5,6},{6,5},{7,4},{8,11},{9,10},{10,... | collective-permute-start | bytes 147464 | tf_op jit(solution)/shard_map/ppermute | solution.py:236
  38.4 2.5 %collective-permute-done.15.refs_2_ = bf16[32,768]{1,0:T(8,128)(2,1)S(1)} collective-permute-done((bf16[32,768]{1,0:T(8,128)(2,1)S(1)}, bf16[32,768]{1,0:T(8,128)(2,1)S(1)}, u32[]{:S(2)}, u32[]{:S(2)}) %collective-permute-start.15) | collective-permute-done | bytes 49184 | tf_op jit(solution)/shard_map/ppermute | solution.py:236
  40.9 0.6 %collective-permute-done.16.refs_3_ = bf16[32,768]{1,0:T(8,128)(2,1)S(1)} collective-permute-done((bf16[32,768]{1,0:T(8,128)(2,1)S(1)}, bf16[32,768]{1,0:T(8,128)(2,1)S(1)}, u32[]{:S(2)}, u32[]{:S(2)}) %collective-permute-start.16) | collective-permute-done | bytes 49184 | tf_op jit(solution)/shard_map/ppermute | solution.py:236
  41.5 0.0 collective-permute-done.14.refs_1_
  41.5 0.0 copy-done
  41.5 1.5 %sketch.1 = (f32[32,1024]{1,0:T(8,128)}, f32[32,768]{1,0:T(8,128)S(1)}, f32[32,768]{1,0:T(8,128)S(1)}, bf16[32,768]{1,0:T(8,128)(2,1)S(1)}, bf16[32,768]{1,0:T(8,128)(2,1)S(1)}) custom-call(s32[1,1024]{1,0:T(1,128)S(1)} %get-tuple-element.22.mark_ref, f32[8,128]{1,0:T(8,128)S(1)} %get-tuple-element.23.resident_ref, bf16[1024,768]{1,0:T(8,128)(2,1)S(1)} %copy-done, ...), custom_call_target="tpu_custom_call" | custom-call | tf_op jit(solution)/shard_map/sketch/pallas_call | solution.py:330
  43.0 0.2 collective-permute-start.19
  43.2 1.0 %collective-permute-start.17 = (bf16[32,768]{1,0:T(8,128)(2,1)S(1)}, bf16[32,768]{1,0:T(8,128)(2,1)S(1)}, u32[]{:S(2)}, u32[]{:S(2)}) collective-permute-start(bf16[32,768]{1,0:T(8,128)(2,1)S(1)} %get-tuple-element.39), channel_id=1, source_target_pairs={{0,3},{1,2},{2,1},{3,0},{4,7},{5,6},{6,5},{7,4},{8,11},{9,10},{10,... | collective-permute-start | bytes 147464 | tf_op jit(solution)/shard_map/ppermute | solution.py:236
  44.2 1.0 %collective-permute-start.18 = (bf16[32,768]{1,0:T(8,128)(2,1)S(1)}, bf16[32,768]{1,0:T(8,128)(2,1)S(1)}, u32[]{:S(2)}, u32[]{:S(2)}) collective-permute-start(bf16[32,768]{1,0:T(8,128)(2,1)S(1)} %get-tuple-element.40), channel_id=1, source_target_pairs={{0,2},{1,3},{2,0},{3,1},{4,6},{5,7},{6,4},{7,5},{8,10},{9,11},{10,... | collective-permute-start | bytes 147464 | tf_op jit(solution)/shard_map/ppermute | solution.py:236
  45.2 1.5 %collective-permute-done.17 = bf16[32,768]{1,0:T(8,128)(2,1)S(1)} collective-permute-done((bf16[32,768]{1,0:T(8,128)(2,1)S(1)}, bf16[32,768]{1,0:T(8,128)(2,1)S(1)}, u32[]{:S(2)}, u32[]{:S(2)}) %collective-permute-start.17) | collective-permute-done | bytes 49184 | tf_op jit(solution)/shard_map/ppermute | solution.py:236
  46.8 1.6 %collective-permute-done.18 = bf16[32,768]{1,0:T(8,128)(2,1)S(1)} collective-permute-done((bf16[32,768]{1,0:T(8,128)(2,1)S(1)}, bf16[32,768]{1,0:T(8,128)(2,1)S(1)}, u32[]{:S(2)}, u32[]{:S(2)}) %collective-permute-start.18) | collective-permute-done | bytes 49184 | tf_op jit(solution)/shard_map/ppermute | solution.py:236
  48.4 0.0 collective-permute-done.19
  48.4 0.7 %add_bitcast_fusion = f32[1,32,768]{2,1,0:T(8,128)} fusion(f32[32,768]{1,0:T(8,128)S(1)} %collective-permute-done.19, bf16[32,768]{1,0:T(8,128)(2,1)S(1)} %collective-permute-done.18, f32[32,768]{1,0:T(8,128)S(1)} %get-tuple-element.38, bf16[32,768]{1,0:T(8,128)(2,1)S(1)} %collective-permute-done.17), kind=kLoop, calls=%fused_computation | loop fusion | flops 122880 | bytes 393216 | tf_op jit(solution)/shard_map/broadcast_in_dim | solution.py:340
  (3 shorter events, 0.0 us)
Async XLA Ops:
  2.6 7.7 %collective-permute-start.2 = (f32[32,768]{1,0:T(8,128)S(1)}, f32[32,768]{1,0:T(8,128)S(1)}, u32[]{:S(2)}, u32[]{:S(2)}) collective-permute-start(f32[32,768]{1,0:T(8,128)S(1)} %get-tuple-element.27), channel_id=1, source_target_pairs={{0,1},{1,0},{2,3},{3,2},{4,5},{5,4},{6,7},{7,6},{8,9},{9,8},{10,11... | collective-permute-start | bytes 294920 | tf_op jit(solution)/shard_map/ppermute | solution.py:236
  3.1 4.7 %collective-permute-start = (bf16[32,768]{1,0:T(8,128)(2,1)S(1)}, bf16[32,768]{1,0:T(8,128)(2,1)S(1)}, u32[]{:S(2)}, u32[]{:S(2)}) collective-permute-start(bf16[32,768]{1,0:T(8,128)(2,1)S(1)} %get-tuple-element.25), channel_id=1, source_target_pairs={{0,3},{1,2},{2,1},{3,0},{4,7},{5,6},{6,5},{7,4},{8,11},{9,10},{10,... | collective-permute-start | bytes 147464 | tf_op jit(solution)/shard_map/ppermute | solution.py:236
  5.7 4.6 %collective-permute-start.1 = (bf16[32,768]{1,0:T(8,128)(2,1)S(1)}, bf16[32,768]{1,0:T(8,128)(2,1)S(1)}, u32[]{:S(2)}, u32[]{:S(2)}) collective-permute-start(bf16[32,768]{1,0:T(8,128)(2,1)S(1)} %get-tuple-element.26), channel_id=1, source_target_pairs={{0,2},{1,3},{2,0},{3,1},{4,6},{5,7},{6,4},{7,5},{8,10},{9,11},{10,... | collective-permute-start | bytes 147464 | tf_op jit(solution)/shard_map/ppermute | solution.py:236
  5.7 10.6 %collective-permute-start.8 = (bf16[1552,128]{1,0:T(8,128)(2,1)S(1)}, bf16[1552,128]{1,0:T(8,128)(2,1)S(1)}, u32[]{:S(2)}, u32[]{:S(2)}) collective-permute-start(bf16[1552,128]{1,0:T(8,128)(2,1)S(1)} %get-tuple-element.28.refs_0_), channel_id=1, source_target_pairs={{0,4},{1,3},{2,6},{3,1},{4,0},{5,7},{6,2},{7,5},{8,12},{9,11},{10,... | collective-permute-start | bytes 1191944 | tf_op jit(solution)/shard_map/ppermute | solution.py:287
  10.3 6.0 %collective-permute-start.5 = (bf16[32,768]{1,0:T(8,128)(2,1)S(1)}, bf16[32,768]{1,0:T(8,128)(2,1)S(1)}, u32[]{:S(2)}, u32[]{:S(2)}) collective-permute-start(bf16[32,768]{1,0:T(8,128)(2,1)S(1)} %join.1.refs_0_), channel_id=1, source_target_pairs={{0,24},{4,28},{8,16},{12,20},{16,8},{20,12},{24,0},{28,4},{1,25},{... | collective-permute-start | bytes 147464 | tf_op jit(solution)/shard_map/ppermute | solution.py:236
  14.0 7.8 %collective-permute-start.6 = (bf16[1552,128]{1,0:T(8,128)(2,1)S(1)}, bf16[1552,128]{1,0:T(8,128)(2,1)S(1)}, u32[]{:S(2)}, u32[]{:S(2)}) collective-permute-start(bf16[1552,128]{1,0:T(8,128)(2,1)S(1)} %get-tuple-element.28.refs_0_), channel_id=1, source_target_pairs={{0,2},{1,5},{2,0},{3,7},{4,6},{5,1},{6,4},{7,3},{8,10},{9,13},{10,... | collective-permute-start | bytes 1191944 | tf_op jit(solution)/shard_map/ppermute | solution.py:286
  15.0 4.1 %collective-permute-start.3 = (bf16[32,768]{1,0:T(8,128)(2,1)S(1)}, bf16[32,768]{1,0:T(8,128)(2,1)S(1)}, u32[]{:S(2)}, u32[]{:S(2)}) collective-permute-start(bf16[32,768]{1,0:T(8,128)(2,1)S(1)} %join.1.refs_0_), channel_id=1, source_target_pairs={{0,8},{4,12},{8,0},{12,4},{16,24},{20,28},{24,16},{28,20},{1,9},{5... | collective-permute-start | bytes 147464 | tf_op jit(solution)/shard_map/ppermute | solution.py:236
  15.0 5.0 %collective-permute-start.4 = (bf16[32,768]{1,0:T(8,128)(2,1)S(1)}, bf16[32,768]{1,0:T(8,128)(2,1)S(1)}, u32[]{:S(2)}, u32[]{:S(2)}) collective-permute-start(bf16[32,768]{1,0:T(8,128)(2,1)S(1)} %join.1.refs_0_), channel_id=1, source_target_pairs={{0,16},{4,20},{8,24},{12,28},{16,0},{20,4},{24,8},{28,12},{1,17},{... | collective-permute-start | bytes 147464 | tf_op jit(solution)/shard_map/ppermute | solution.py:236
  16.3 9.8 %collective-permute-start.9 = (bf16[1552,128]{1,0:T(8,128)(2,1)S(1)}, bf16[1552,128]{1,0:T(8,128)(2,1)S(1)}, u32[]{:S(2)}, u32[]{:S(2)}) collective-permute-start(bf16[1552,128]{1,0:T(8,128)(2,1)S(1)} %gate.1.refs_1_), channel_id=1, source_target_pairs={{0,2},{1,5},{2,0},{3,7},{4,6},{5,1},{6,4},{7,3},{8,10},{9,13},{10,... | collective-permute-start | bytes 1191944 | tf_op jit(solution)/shard_map/ppermute | solution.py:288
  21.8 1.5 %collective-permute-start.7 = (bf16[128,768]{1,0:T(8,128)(2,1)S(1)}, bf16[128,768]{1,0:T(8,128)(2,1)S(1)}, u32[]{:S(2)}, u32[]{:S(2)}) collective-permute-start(bf16[128,768]{1,0:T(8,128)(2,1)S(1)} %stack.1.mine_ref), channel_id=1, source_target_pairs={{0,1},{1,0},{2,3},{3,2},{4,5},{5,4},{6,7},{7,6},{8,9},{9,8},{10,11... | collective-permute-start | bytes 589832 | tf_op jit(solution)/shard_map/ppermute | solution.py:236
  25.2 16.3 %copy-start = (bf16[1024,768]{1,0:T(8,128)(2,1)S(1)}, bf16[1024,768]{1,0:T(8,128)(2,1)}, u32[]{:S(2)}) copy-start(bf16[1024,768]{1,0:T(8,128)(2,1)} %points_ref.1) | copy-start | bytes 4718596
  26.7 1.6 %collective-permute-start.10 = (bf16[128,896]{1,0:T(8,128)(2,1)S(1)}, bf16[128,896]{1,0:T(8,128)(2,1)S(1)}, u32[]{:S(2)}, u32[]{:S(2)}) collective-permute-start(bf16[128,896]{1,0:T(8,128)(2,1)S(1)} %get-tuple-element.30), channel_id=1, source_target_pairs={{0,1},{1,0},{2,3},{3,2},{4,5},{5,4},{6,7},{7,6},{8,9},{9,8},{10,11... | collective-permute-start | bytes 688136 | tf_op jit(solution)/shard_map/ppermute | solution.py:236
  28.3 6.4 %collective-permute-start.11 = (bf16[208,128]{1,0:T(8,128)(2,1)S(1)}, bf16[208,128]{1,0:T(8,128)(2,1)S(1)}, u32[]{:S(2)}, u32[]{:S(2)}) collective-permute-start(bf16[208,128]{1,0:T(8,128)(2,1)S(1)} %get-tuple-element.32), channel_id=1, source_target_pairs={{0,24},{4,28},{8,16},{12,20},{16,8},{20,12},{24,0},{28,4},{1,25},{... | collective-permute-start | bytes 159752 | tf_op jit(solution)/shard_map/ppermute | solution.py:236
  30.3 6.0 %collective-permute-start.12 = (bf16[208,128]{1,0:T(8,128)(2,1)S(1)}, bf16[208,128]{1,0:T(8,128)(2,1)S(1)}, u32[]{:S(2)}, u32[]{:S(2)}) collective-permute-start(bf16[208,128]{1,0:T(8,128)(2,1)S(1)} %get-tuple-element.33), channel_id=1, source_target_pairs={{0,16},{4,20},{8,24},{12,28},{16,0},{20,4},{24,8},{28,12},{1,17},{... | collective-permute-start | bytes 159752 | tf_op jit(solution)/shard_map/ppermute | solution.py:236
  30.3 6.0 %collective-permute-start.13 = (bf16[208,128]{1,0:T(8,128)(2,1)S(1)}, bf16[208,128]{1,0:T(8,128)(2,1)S(1)}, u32[]{:S(2)}, u32[]{:S(2)}) collective-permute-start(bf16[208,128]{1,0:T(8,128)(2,1)S(1)} %get-tuple-element.34), channel_id=1, source_target_pairs={{0,8},{4,12},{8,0},{12,4},{16,24},{20,28},{24,16},{28,20},{1,9},{5... | collective-permute-start | bytes 159752 | tf_op jit(solution)/shard_map/ppermute | solution.py:236
  36.4 5.0 %collective-permute-start.14 = (f32[32,768]{1,0:T(8,128)S(1)}, f32[32,768]{1,0:T(8,128)S(1)}, u32[]{:S(2)}, u32[]{:S(2)}) collective-permute-start(f32[32,768]{1,0:T(8,128)S(1)} %get-tuple-element.35.refs_0_), channel_id=1, source_target_pairs={{0,1},{1,0},{2,3},{3,2},{4,5},{5,4},{6,7},{7,6},{8,9},{9,8},{10,11... | collective-permute-start | bytes 294920 | tf_op jit(solution)/shard_map/ppermute | solution.py:236
  36.5 4.3 %collective-permute-start.15 = (bf16[32,768]{1,0:T(8,128)(2,1)S(1)}, bf16[32,768]{1,0:T(8,128)(2,1)S(1)}, u32[]{:S(2)}, u32[]{:S(2)}) collective-permute-start(bf16[32,768]{1,0:T(8,128)(2,1)S(1)} %get-tuple-element.36), channel_id=1, source_target_pairs={{0,2},{1,3},{2,0},{3,1},{4,6},{5,7},{6,4},{7,5},{8,10},{9,11},{10,... | collective-permute-start | bytes 147464 | tf_op jit(solution)/shard_map/ppermute | solution.py:236
  37.6 3.9 %collective-permute-start.16 = (bf16[32,768]{1,0:T(8,128)(2,1)S(1)}, bf16[32,768]{1,0:T(8,128)(2,1)S(1)}, u32[]{:S(2)}, u32[]{:S(2)}) collective-permute-start(bf16[32,768]{1,0:T(8,128)(2,1)S(1)} %get-tuple-element.36), channel_id=1, source_target_pairs={{0,3},{1,2},{2,1},{3,0},{4,7},{5,6},{6,5},{7,4},{8,11},{9,10},{10,... | collective-permute-start | bytes 147464 | tf_op jit(solution)/shard_map/ppermute | solution.py:236
  43.0 5.3 %collective-permute-start.19 = (f32[32,768]{1,0:T(8,128)S(1)}, f32[32,768]{1,0:T(8,128)S(1)}, u32[]{:S(2)}, u32[]{:S(2)}) collective-permute-start(f32[32,768]{1,0:T(8,128)S(1)} %get-tuple-element.41), channel_id=1, source_target_pairs={{0,1},{1,0},{2,3},{3,2},{4,5},{5,4},{6,7},{7,6},{8,9},{9,8},{10,11... | collective-permute-start | bytes 294920 | tf_op jit(solution)/shard_map/ppermute | solution.py:236
  43.2 3.5 %collective-permute-start.17 = (bf16[32,768]{1,0:T(8,128)(2,1)S(1)}, bf16[32,768]{1,0:T(8,128)(2,1)S(1)}, u32[]{:S(2)}, u32[]{:S(2)}) collective-permute-start(bf16[32,768]{1,0:T(8,128)(2,1)S(1)} %get-tuple-element.39), channel_id=1, source_target_pairs={{0,3},{1,2},{2,1},{3,0},{4,7},{5,6},{6,5},{7,4},{8,11},{9,10},{10,... | collective-permute-start | bytes 147464 | tf_op jit(solution)/shard_map/ppermute | solution.py:236
  44.2 4.1 %collective-permute-start.18 = (bf16[32,768]{1,0:T(8,128)(2,1)S(1)}, bf16[32,768]{1,0:T(8,128)(2,1)S(1)}, u32[]{:S(2)}, u32[]{:S(2)}) collective-permute-start(bf16[32,768]{1,0:T(8,128)(2,1)S(1)} %get-tuple-element.40), channel_id=1, source_target_pairs={{0,2},{1,3},{2,0},{3,1},{4,6},{5,7},{6,4},{7,5},{8,10},{9,11},{10,... | collective-permute-start | bytes 147464 | tf_op jit(solution)/shard_map/ppermute | solution.py:236

commit v13 on v12

--- a/solution.py
+++ b/solution.py
@@ -115,13 +115,15 @@
     )(*values, *others)
 
 
-def score_kernel(planes, helpers, blocks, mine_ref, theirs_ref, *refs):
-    queries, rest = refs[:blocks], refs[blocks:]
+def score_kernel(planes, helpers, blocks, pieces, mine_ref, theirs_ref, *refs):
+    queries, rest = refs[: blocks * pieces], refs[blocks * pieces :]
+    if pieces > 1:
+        queries = [jnp.concatenate([ref[...] for ref in queries], axis=0)]
     shard, helper = lax.axis_index("shard"), lax.axis_index("help")
     span, width = mine_ref.shape
     rank = span // planes
     count = (queries[0].shape[0] - TILE) * LANES // width
-    pieces = count // LANES
+    lanes = count // LANES
     lifter = jnp.concatenate([mine_ref[...], theirs_ref[...]], axis=0)
     clusters = [
         ((shard ^ (INNER * d)) * helpers + (helper ^ side)).astype(F32) for side in (0, 1) for d in range(planes)
@@ -131,7 +133,7 @@
         rows = slabs(q_ref, count, width)
         tile = q_ref[count * width // LANES :, :].astype(F32)
         first, second = (
-            jnp.concatenate([tile[k * pieces + j : k * pieces + j + 1] for j in range(pieces)], axis=1) for k in (0, 1)
+            jnp.concatenate([tile[k * lanes + j : k * lanes + j + 1] for j in range(lanes)], axis=1) for k in (0, 1)
         )
         lifted = contract(lifter, rows, ((1,), (1,)))
         kept = []
@@ -276,7 +278,7 @@
         join_kernel,
         out_shape=sent,
         compiler_params=PARAMS,
-        cost_estimate=pl.CostEstimate(flops=40*10**8, bytes_accessed=10**5, transcendentals=0),
+        cost_estimate=pl.CostEstimate(flops=4 * 10**9, bytes_accessed=10**5, transcendentals=0),
         name="join",
     )(own, *swaps(parts, "help"))
     lifters = [lifter] + [swap(lifter, "shard", INNER * d) for d in range(1, planes)]
@@ -285,7 +287,8 @@
     two = [(i, i ^ (helpers if i % 2 == 0 else 2)) for i in index]
     far = lax.ppermute(packed, axes, one)
     (near,) = gate([lax.ppermute(packed, axes, two)], lifters[-1])
-    across = lax.ppermute(near, axes, one)
+    cut = width // LANES * 2 // 3 * count
+    across = [lax.ppermute(near[:cut], axes, one), lax.ppermute(far[cut:], axes, two)]
 
     mine = pl.pallas_call(
         stack_kernel,
@@ -299,17 +302,17 @@
 
     wide = width + LANES
     begun = pl.pallas_call(
-        functools.partial(score_kernel, planes, helpers, 3),
+        functools.partial(score_kernel, planes, helpers, 3, 1),
         out_shape=jax.ShapeDtypeStruct((2 * planes * rank, wide), F32),
         compiler_params=PARAMS,
         name="score",
     )(mine, theirs, packed, near, far)
     moments, passed = pl.pallas_call(
-        functools.partial(score_kernel, planes, helpers, 1),
+        functools.partial(score_kernel, planes, helpers, 1, 2),
         out_shape=[jax.ShapeDtypeStruct((planes * rank, wide), kind) for kind in (F32, BF16)],
         compiler_params=PARAMS,
         name="score_last",
-    )(mine, theirs, across, begun)
+    )(mine, theirs, *across, begun)
     folded = pl.pallas_call(
         functools.partial(fold_kernel, planes),
         out_shape=[jax.ShapeDtypeStruct((rank, wide), F32)]

time: 49.3 us -> 50 us (1.014)
  starting transfers between devices: 20.4 us -> 22 us
  waiting for transfers between devices: 21.2 us -> 20.2 us
    ppermute x17, waiting for transfers between devices: 18.5 us -> 16.8 us  [swap(): lax.ppermute(value, axis, [(i, i ^ d) for i in range(lax.axis_size(axis))])]
    ppermute x1 -> x2, starting transfers between devices: 0.98 us -> 2.63 us  [the longest x1 1.59 us: shards(): lax.ppermute(far[cut:], axes, two)]
    ppermute x1 -> x2, waiting for transfers between devices: 0.9 us -> 1.66 us  [the longest x1 1.66 us: shards(): lax.ppermute(far[cut:], axes, two)]
  transfers between devices with their start and end apart: 20 -> 21, of which waited for: 14 -> 13; matrix products, arithmetic and copies ran while one was open for 0% -> 0% of each run, Pallas kernels for 4% -> 4%
where the time goes in v13:
time: 50 us; the launch traced here: 49.8 us
  starting transfers between devices  22 us (44%)
  waiting for transfers between devices  20.2 us (40%)
  Pallas kernels  6.09 us (12%)
  between operations  0.74 us (1%)
  other arithmetic  0.67 us (1%)
    ppermute x17, waiting for transfers between devices, swap(): lax.ppermute(value, axis, [(i, i ^ d) for i in range(lax.axis_size(axis))])  16.8 us
    ppermute x17, starting transfers between devices, swap(): lax.ppermute(value, axis, [(i, i ^ d) for i in range(lax.axis_size(axis))])  16.4 us
    ppermute x1, starting transfers between devices, shards(): near, = gate([lax.ppermute(packed, axes, two)], lifters[-1])  2.01 us
    pallas_call x1, Pallas kernels, shards(): pl.pallas_call(functools.partial(lift_kernel, helpers), out_shape=[jax.Sh...  1.92 us
    ppermute x1, waiting for transfers between devices, shards(): far = lax.ppermute(packed, axes, one)  1.82 us
    pallas_call x1, Pallas kernels, shards(): pl.pallas_call(functools.partial(score_kernel, planes, helpers, 3, 1), ou...  1.81 us
    ppermute x1, waiting for transfers between devices, shards(): lax.ppermute(far[cut:], axes, two)  1.66 us
    ppermute x1, starting transfers between devices, shards(): lax.ppermute(far[cut:], axes, two)  1.59 us
  transfers between devices with their start and end apart: 21, of which 13 were waited for; matrix products, arithmetic and copies ran while one was open for 0% of the time, Pallas kernels for 4%

profile of v13, /device:TPU:0, one launch (start us, length us, event | category | flops | bytes accessed | tf_op | source)
XLA Modules:
  0.0 49.8 jit_solution(14250812753098951310)
XLA Ops:
  0.6 1.9 %lift.1 = (bf16[1552,128]{1,0:T(8,128)(2,1)S(1)}, s32[1,1024]{1,0:T(1,128)S(1)}, f32[8,128]{1,0:T(8,128)S(1)}, f32[32,768]{1,0:T(8,128)S(1)}, f32[32,768]{1,0:T(...) custom-call(bf16[256,768]{1,0:T(8,128)(2,1)} %refs_0_.1, s32[2,256]{1,0:T(2,128)} %bitcast.4, ...), custom_call_target="tpu_custom_call" | custom-call | tf_op jit(solution)/shard_map/lift/pallas_call | solution.py:255
  2.6 0.5 %collective-permute-start.2 = (f32[32,768]{1,0:T(8,128)S(1)}, f32[32,768]{1,0:T(8,128)S(1)}, u32[]{:S(2)}, u32[]{:S(2)}) collective-permute-start(f32[32,768]{1,0:T(8,128)S(1)} %get-tuple-element.27), channel_id=1, source_target_pairs={{0,1},{1,0},{2,3},{3,2},{4,5},{5,4},{6,7},{7,6},{8,9},{9,8},{10,11... | collective-permute-start | bytes 294920 | tf_op jit(solution)/shard_map/ppermute | solution.py:238
  3.1 2.6 %collective-permute-start = (bf16[32,768]{1,0:T(8,128)(2,1)S(1)}, bf16[32,768]{1,0:T(8,128)(2,1)S(1)}, u32[]{:S(2)}, u32[]{:S(2)}) collective-permute-start(bf16[32,768]{1,0:T(8,128)(2,1)S(1)} %get-tuple-element.25), channel_id=1, source_target_pairs={{0,3},{1,2},{2,1},{3,0},{4,7},{5,6},{6,5},{7,4},{8,11},{9,10},{10,... | collective-permute-start | bytes 147464 | tf_op jit(solution)/shard_map/ppermute | solution.py:238
  5.7 0.0 collective-permute-start.1
  5.7 2.0 %collective-permute-start.8 = (bf16[1552,128]{1,0:T(8,128)(2,1)S(1)}, bf16[1552,128]{1,0:T(8,128)(2,1)S(1)}, u32[]{:S(2)}, u32[]{:S(2)}) collective-permute-start(bf16[1552,128]{1,0:T(8,128)(2,1)S(1)} %get-tuple-element.28.refs_0_), channel_id=1, source_target_pairs={{0,4},{1,3},{2,6},{3,1},{4,0},{5,7},{6,2},{7,5},{8,12},{9,11},{10,... | collective-permute-start | bytes 1191944 | tf_op jit(solution)/shard_map/ppermute | solution.py:289
  7.7 0.0 collective-permute-done.refs_1_
  7.8 2.5 %collective-permute-done.1.refs_2_ = bf16[32,768]{1,0:T(8,128)(2,1)S(1)} collective-permute-done((bf16[32,768]{1,0:T(8,128)(2,1)S(1)}, bf16[32,768]{1,0:T(8,128)(2,1)S(1)}, u32[]{:S(2)}, u32[]{:S(2)}) %collective-permute-start.1) | collective-permute-done | bytes 49184 | tf_op jit(solution)/shard_map/ppermute | solution.py:238
  10.3 0.0 collective-permute-done.2.refs_3_
  10.3 3.7 %collective-permute-start.5 = (bf16[32,768]{1,0:T(8,128)(2,1)S(1)}, bf16[32,768]{1,0:T(8,128)(2,1)S(1)}, u32[]{:S(2)}, u32[]{:S(2)}) collective-permute-start(bf16[32,768]{1,0:T(8,128)(2,1)S(1)} %join.1.refs_0_), channel_id=1, source_target_pairs={{0,24},{4,28},{8,16},{12,20},{16,8},{20,12},{24,0},{28,4},{1,25},{... | collective-permute-start | bytes 147464 | tf_op jit(solution)/shard_map/ppermute | solution.py:238
  14.0 1.0 %collective-permute-start.6 = (bf16[1552,128]{1,0:T(8,128)(2,1)S(1)}, bf16[1552,128]{1,0:T(8,128)(2,1)S(1)}, u32[]{:S(2)}, u32[]{:S(2)}) collective-permute-start(bf16[1552,128]{1,0:T(8,128)(2,1)S(1)} %get-tuple-element.28.refs_0_), channel_id=1, source_target_pairs={{0,2},{1,5},{2,0},{3,7},{4,6},{5,1},{6,4},{7,3},{8,10},{9,13},{10,... | collective-permute-start | bytes 1191944 | tf_op jit(solution)/shard_map/ppermute | solution.py:288
  15.0 0.0 collective-permute-start.3
  15.0 0.8 %collective-permute-start.4 = (bf16[32,768]{1,0:T(8,128)(2,1)S(1)}, bf16[32,768]{1,0:T(8,128)(2,1)S(1)}, u32[]{:S(2)}, u32[]{:S(2)}) collective-permute-start(bf16[32,768]{1,0:T(8,128)(2,1)S(1)} %join.1.refs_0_), channel_id=1, source_target_pairs={{0,16},{4,20},{8,24},{12,28},{16,0},{20,4},{24,8},{28,12},{1,17},{... | collective-permute-start | bytes 147464 | tf_op jit(solution)/shard_map/ppermute | solution.py:238
  15.8 0.5 %collective-permute-done.5.refs_3_.refs_1_ = bf16[32,768]{1,0:T(8,128)(2,1)S(1)} collective-permute-done((bf16[32,768]{1,0:T(8,128)(2,1)S(1)}, bf16[32,768]{1,0:T(8,128)(2,1)S(1)}, u32[]{:S(2)}, u32[]{:S(2)}) %collective-permute-start.5) | collective-permute-done | bytes 49184 | tf_op jit(solution)/shard_map/ppermute | solution.py:238
  16.3 0.0 collective-permute-done.8.refs_0_
  16.3 1.0 %collective-permute-start.9 = (bf16[1024,128]{1,0:T(8,128)(2,1)S(1)}, bf16[1024,128]{1,0:T(8,128)(2,1)S(1)}, u32[]{:S(2)}, u32[]{:S(2)}) collective-permute-start(bf16[1024,128]{1,0:T(8,128)(2,1)S(1)} %slice.8), channel_id=1, source_target_pairs={{0,2},{1,5},{2,0},{3,7},{4,6},{5,1},{6,4},{7,3},{8,10},{9,13},{10,... | collective-permute-start | bytes 786440 | tf_op jit(solution)/shard_map/ppermute | solution.py:291
  17.4 1.7 %collective-permute-done.3.refs_1_ = bf16[32,768]{1,0:T(8,128)(2,1)S(1)} collective-permute-done((bf16[32,768]{1,0:T(8,128)(2,1)S(1)}, bf16[32,768]{1,0:T(8,128)(2,1)S(1)}, u32[]{:S(2)}, u32[]{:S(2)}) %collective-permute-start.3) | collective-permute-done | bytes 49184 | tf_op jit(solution)/shard_map/ppermute | solution.py:238
  19.1 0.9 %collective-permute-done.4.refs_2_ = bf16[32,768]{1,0:T(8,128)(2,1)S(1)} collective-permute-done((bf16[32,768]{1,0:T(8,128)(2,1)S(1)}, bf16[32,768]{1,0:T(8,128)(2,1)S(1)}, u32[]{:S(2)}, u32[]{:S(2)}) %collective-permute-start.4) | collective-permute-done | bytes 49184 | tf_op jit(solution)/shard_map/ppermute | solution.py:238
  20.0 1.8 %collective-permute-done.6.refs_4_.refs_2_ = bf16[1552,128]{1,0:T(8,128)(2,1)S(1)} collective-permute-done((bf16[1552,128]{1,0:T(8,128)(2,1)S(1)}, bf16[1552,128]{1,0:T(8,128)(2,1)S(1)}, u32[]{:S(2)}, u32[]{:S(2)}) %collective-permute-start.6) | collective-permute-done | bytes 397344 | tf_op jit(solution)/shard_map/ppermute | solution.py:288
  21.8 0.1 collective-permute-start.7
  21.9 1.6 %collective-permute-start.10 = (bf16[528,128]{1,0:T(8,128)(2,1)S(1)}, bf16[528,128]{1,0:T(8,128)(2,1)S(1)}, u32[]{:S(2)}, u32[]{:S(2)}) collective-permute-start(bf16[528,128]{1,0:T(8,128)(2,1)S(1)} %slice.9), channel_id=1, source_target_pairs={{0,4},{1,3},{2,6},{3,1},{4,0},{5,7},{6,2},{7,5},{8,12},{9,11},{10,... | collective-permute-start | bytes 405512 | tf_op jit(solution)/shard_map/ppermute | solution.py:291
  23.5 0.0 collective-permute-done.7.theirs_ref
  23.5 1.8 %score.1.refs_2_ = f32[256,896]{1,0:T(8,128)S(1)} custom-call(bf16[128,768]{1,0:T(8,128)(2,1)S(1)} %stack.1.mine_ref, bf16[128,768]{1,0:T(8,128)(2,1)S(1)} %collective-permute-done.7.theirs_ref, bf16[1552,128]{1,0:T(8,128)(2,1)S(1)} %get-tuple-element.28.refs_0_, bf16[1552,128]{1,0:T(8,128)(2,1)S(1)} %gate.1.refs_1_, ...), custom_call_target="tpu_custom_call" | custom-call | tf_op jit(solution)/shard_map/score/pallas_call | solution.py:304
  25.3 0.0 copy-start
  25.3 1.7 %collective-permute-done.10.refs_1_ = bf16[528,128]{1,0:T(8,128)(2,1)S(1)} collective-permute-done((bf16[528,128]{1,0:T(8,128)(2,1)S(1)}, bf16[528,128]{1,0:T(8,128)(2,1)S(1)}, u32[]{:S(2)}, u32[]{:S(2)}) %collective-permute-start.10) | collective-permute-done | bytes 135200 | tf_op jit(solution)/shard_map/ppermute | solution.py:291
  27.0 0.0 collective-permute-done.9.refs_0_
  27.0 0.6 %score_last.1 = (f32[128,896]{1,0:T(8,128)S(1)}, bf16[128,896]{1,0:T(8,128)(2,1)S(1)}) custom-call(bf16[128,768]{1,0:T(8,128)(2,1)S(1)} %stack.1.mine_ref, bf16[128,768]{1,0:T(8,128)(2,1)S(1)} %collective-permute-done.7.theirs_ref, bf16[1024,128]{1,0:T(8,128)(2,1)S(1)} %collective-permute-done.9.refs_0_, ...), custom_call_target="tpu_custom_call" | custom-call | tf_op jit(solution)/shard_map/score_last/pallas_call | solution.py:310
  27.7 0.1 collective-permute-start.11
  27.7 1.5 %collective-permute-done.11.theirs_ref = bf16[128,896]{1,0:T(8,128)(2,1)S(1)} collective-permute-done((bf16[128,896]{1,0:T(8,128)(2,1)S(1)}, bf16[128,896]{1,0:T(8,128)(2,1)S(1)}, u32[]{:S(2)}, u32[]{:S(2)}) %collective-permute-start.11) | collective-permute-done | bytes 229408 | tf_op jit(solution)/shard_map/ppermute | solution.py:238
  29.2 0.1 fold.1
  29.3 0.9 %collective-permute-start.12 = (bf16[208,128]{1,0:T(8,128)(2,1)S(1)}, bf16[208,128]{1,0:T(8,128)(2,1)S(1)}, u32[]{:S(2)}, u32[]{:S(2)}) collective-permute-start(bf16[208,128]{1,0:T(8,128)(2,1)S(1)} %get-tuple-element.32), channel_id=1, source_target_pairs={{0,24},{4,28},{8,16},{12,20},{16,8},{20,12},{24,0},{28,4},{1,25},{... | collective-permute-start | bytes 159752 | tf_op jit(solution)/shard_map/ppermute | solution.py:238
  30.2 0.8 %collective-permute-start.13 = (bf16[208,128]{1,0:T(8,128)(2,1)S(1)}, bf16[208,128]{1,0:T(8,128)(2,1)S(1)}, u32[]{:S(2)}, u32[]{:S(2)}) collective-permute-start(bf16[208,128]{1,0:T(8,128)(2,1)S(1)} %get-tuple-element.33), channel_id=1, source_target_pairs={{0,16},{4,20},{8,24},{12,28},{16,0},{20,4},{24,8},{28,12},{1,17},{... | collective-permute-start | bytes 159752 | tf_op jit(solution)/shard_map/ppermute | solution.py:238
  31.0 2.7 %collective-permute-start.14 = (bf16[208,128]{1,0:T(8,128)(2,1)S(1)}, bf16[208,128]{1,0:T(8,128)(2,1)S(1)}, u32[]{:S(2)}, u32[]{:S(2)}) collective-permute-start(bf16[208,128]{1,0:T(8,128)(2,1)S(1)} %get-tuple-element.34), channel_id=1, source_target_pairs={{0,8},{4,12},{8,0},{12,4},{16,24},{20,28},{24,16},{28,20},{1,9},{5... | collective-permute-start | bytes 159752 | tf_op jit(solution)/shard_map/ppermute | solution.py:238
  33.7 2.2 %collective-permute-done.12.refs_0_ = bf16[208,128]{1,0:T(8,128)(2,1)S(1)} collective-permute-done((bf16[208,128]{1,0:T(8,128)(2,1)S(1)}, bf16[208,128]{1,0:T(8,128)(2,1)S(1)}, u32[]{:S(2)}, u32[]{:S(2)}) %collective-permute-start.12) | collective-permute-done | bytes 53280 | tf_op jit(solution)/shard_map/ppermute | solution.py:238
  35.9 1.1 %collective-permute-done.13.refs_1_ = bf16[208,128]{1,0:T(8,128)(2,1)S(1)} collective-permute-done((bf16[208,128]{1,0:T(8,128)(2,1)S(1)}, bf16[208,128]{1,0:T(8,128)(2,1)S(1)}, u32[]{:S(2)}, u32[]{:S(2)}) %collective-permute-start.13) | collective-permute-done | bytes 53280 | tf_op jit(solution)/shard_map/ppermute | solution.py:238
  37.0 0.0 collective-permute-done.14.refs_2_
  37.0 0.1 scale.1
  37.1 0.1 collective-permute-start.15
  37.2 1.4 %collective-permute-start.16 = (bf16[32,768]{1,0:T(8,128)(2,1)S(1)}, bf16[32,768]{1,0:T(8,128)(2,1)S(1)}, u32[]{:S(2)}, u32[]{:S(2)}) collective-permute-start(bf16[32,768]{1,0:T(8,128)(2,1)S(1)} %get-tuple-element.36), channel_id=1, source_target_pairs={{0,2},{1,3},{2,0},{3,1},{4,6},{5,7},{6,4},{7,5},{8,10},{9,11},{10,... | collective-permute-start | bytes 147464 | tf_op jit(solution)/shard_map/ppermute | solution.py:238
  38.5 0.5 collective-permute-start.17
  39.0 2.3 %collective-permute-done.16.refs_2_ = bf16[32,768]{1,0:T(8,128)(2,1)S(1)} collective-permute-done((bf16[32,768]{1,0:T(8,128)(2,1)S(1)}, bf16[32,768]{1,0:T(8,128)(2,1)S(1)}, u32[]{:S(2)}, u32[]{:S(2)}) %collective-permute-start.16) | collective-permute-done | bytes 49184 | tf_op jit(solution)/shard_map/ppermute | solution.py:238
  41.3 0.9 %collective-permute-done.17.refs_3_ = bf16[32,768]{1,0:T(8,128)(2,1)S(1)} collective-permute-done((bf16[32,768]{1,0:T(8,128)(2,1)S(1)}, bf16[32,768]{1,0:T(8,128)(2,1)S(1)}, u32[]{:S(2)}, u32[]{:S(2)}) %collective-permute-start.17) | collective-permute-done | bytes 49184 | tf_op jit(solution)/shard_map/ppermute | solution.py:238
  42.2 0.0 collective-permute-done.15.refs_1_
  42.2 0.0 copy-done
  42.2 1.5 %sketch.1 = (f32[32,1024]{1,0:T(8,128)}, f32[32,768]{1,0:T(8,128)S(1)}, f32[32,768]{1,0:T(8,128)S(1)}, bf16[32,768]{1,0:T(8,128)(2,1)S(1)}, bf16[32,768]{1,0:T(8,128)(2,1)S(1)}) custom-call(s32[1,1024]{1,0:T(1,128)S(1)} %get-tuple-element.22.mark_ref, f32[8,128]{1,0:T(8,128)S(1)} %get-tuple-element.23.resident_ref, bf16[1024,768]{1,0:T(8,128)(2,1)S(1)} %copy-done, ...), custom_call_target="tpu_custom_call" | custom-call | tf_op jit(solution)/shard_map/sketch/pallas_call | solution.py:333
  43.8 0.2 collective-permute-start.20
  44.0 1.0 %collective-permute-start.18 = (bf16[32,768]{1,0:T(8,128)(2,1)S(1)}, bf16[32,768]{1,0:T(8,128)(2,1)S(1)}, u32[]{:S(2)}, u32[]{:S(2)}) collective-permute-start(bf16[32,768]{1,0:T(8,128)(2,1)S(1)} %get-tuple-element.39), channel_id=1, source_target_pairs={{0,3},{1,2},{2,1},{3,0},{4,7},{5,6},{6,5},{7,4},{8,11},{9,10},{10,... | collective-permute-start | bytes 147464 | tf_op jit(solution)/shard_map/ppermute | solution.py:238
  45.0 1.0 %collective-permute-start.19 = (bf16[32,768]{1,0:T(8,128)(2,1)S(1)}, bf16[32,768]{1,0:T(8,128)(2,1)S(1)}, u32[]{:S(2)}, u32[]{:S(2)}) collective-permute-start(bf16[32,768]{1,0:T(8,128)(2,1)S(1)} %get-tuple-element.40), channel_id=1, source_target_pairs={{0,2},{1,3},{2,0},{3,1},{4,6},{5,7},{6,4},{7,5},{8,10},{9,11},{10,... | collective-permute-start | bytes 147464 | tf_op jit(solution)/shard_map/ppermute | solution.py:238
  46.0 1.5 %collective-permute-done.18 = bf16[32,768]{1,0:T(8,128)(2,1)S(1)} collective-permute-done((bf16[32,768]{1,0:T(8,128)(2,1)S(1)}, bf16[32,768]{1,0:T(8,128)(2,1)S(1)}, u32[]{:S(2)}, u32[]{:S(2)}) %collective-permute-start.18) | collective-permute-done | bytes 49184 | tf_op jit(solution)/shard_map/ppermute | solution.py:238
  47.5 1.6 %collective-permute-done.19 = bf16[32,768]{1,0:T(8,128)(2,1)S(1)} collective-permute-done((bf16[32,768]{1,0:T(8,128)(2,1)S(1)}, bf16[32,768]{1,0:T(8,128)(2,1)S(1)}, u32[]{:S(2)}, u32[]{:S(2)}) %collective-permute-start.19) | collective-permute-done | bytes 49184 | tf_op jit(solution)/shard_map/ppermute | solution.py:238
  49.1 0.0 collective-permute-done.20
  49.1 0.7 %add_bitcast_fusion = f32[1,32,768]{2,1,0:T(8,128)} fusion(f32[32,768]{1,0:T(8,128)S(1)} %collective-permute-done.20, bf16[32,768]{1,0:T(8,128)(2,1)S(1)} %collective-permute-done.19, f32[32,768]{1,0:T(8,128)S(1)} %get-tuple-element.38, bf16[32,768]{1,0:T(8,128)(2,1)S(1)} %collective-permute-done.18), kind=kLoop, calls=%fused_computation | loop fusion | flops 122880 | bytes 393216 | tf_op jit(solution)/shard_map/broadcast_in_dim | solution.py:343
  (5 shorter events, 0.1 us)
Async XLA Ops:
  2.6 7.7 %collective-permute-start.2 = (f32[32,768]{1,0:T(8,128)S(1)}, f32[32,768]{1,0:T(8,128)S(1)}, u32[]{:S(2)}, u32[]{:S(2)}) collective-permute-start(f32[32,768]{1,0:T(8,128)S(1)} %get-tuple-element.27), channel_id=1, source_target_pairs={{0,1},{1,0},{2,3},{3,2},{4,5},{5,4},{6,7},{7,6},{8,9},{9,8},{10,11... | collective-permute-start | bytes 294920 | tf_op jit(solution)/shard_map/ppermute | solution.py:238
  3.1 4.7 %collective-permute-start = (bf16[32,768]{1,0:T(8,128)(2,1)S(1)}, bf16[32,768]{1,0:T(8,128)(2,1)S(1)}, u32[]{:S(2)}, u32[]{:S(2)}) collective-permute-start(bf16[32,768]{1,0:T(8,128)(2,1)S(1)} %get-tuple-element.25), channel_id=1, source_target_pairs={{0,3},{1,2},{2,1},{3,0},{4,7},{5,6},{6,5},{7,4},{8,11},{9,10},{10,... | collective-permute-start | bytes 147464 | tf_op jit(solution)/shard_map/ppermute | solution.py:238
  5.7 4.6 %collective-permute-start.1 = (bf16[32,768]{1,0:T(8,128)(2,1)S(1)}, bf16[32,768]{1,0:T(8,128)(2,1)S(1)}, u32[]{:S(2)}, u32[]{:S(2)}) collective-permute-start(bf16[32,768]{1,0:T(8,128)(2,1)S(1)} %get-tuple-element.26), channel_id=1, source_target_pairs={{0,2},{1,3},{2,0},{3,1},{4,6},{5,7},{6,4},{7,5},{8,10},{9,11},{10,... | collective-permute-start | bytes 147464 | tf_op jit(solution)/shard_map/ppermute | solution.py:238
  5.7 10.6 %collective-permute-start.8 = (bf16[1552,128]{1,0:T(8,128)(2,1)S(1)}, bf16[1552,128]{1,0:T(8,128)(2,1)S(1)}, u32[]{:S(2)}, u32[]{:S(2)}) collective-permute-start(bf16[1552,128]{1,0:T(8,128)(2,1)S(1)} %get-tuple-element.28.refs_0_), channel_id=1, source_target_pairs={{0,4},{1,3},{2,6},{3,1},{4,0},{5,7},{6,2},{7,5},{8,12},{9,11},{10,... | collective-permute-start | bytes 1191944 | tf_op jit(solution)/shard_map/ppermute | solution.py:289
  10.3 6.0 %collective-permute-start.5 = (bf16[32,768]{1,0:T(8,128)(2,1)S(1)}, bf16[32,768]{1,0:T(8,128)(2,1)S(1)}, u32[]{:S(2)}, u32[]{:S(2)}) collective-permute-start(bf16[32,768]{1,0:T(8,128)(2,1)S(1)} %join.1.refs_0_), channel_id=1, source_target_pairs={{0,24},{4,28},{8,16},{12,20},{16,8},{20,12},{24,0},{28,4},{1,25},{... | collective-permute-start | bytes 147464 | tf_op jit(solution)/shard_map/ppermute | solution.py:238
  14.0 7.8 %collective-permute-start.6 = (bf16[1552,128]{1,0:T(8,128)(2,1)S(1)}, bf16[1552,128]{1,0:T(8,128)(2,1)S(1)}, u32[]{:S(2)}, u32[]{:S(2)}) collective-permute-start(bf16[1552,128]{1,0:T(8,128)(2,1)S(1)} %get-tuple-element.28.refs_0_), channel_id=1, source_target_pairs={{0,2},{1,5},{2,0},{3,7},{4,6},{5,1},{6,4},{7,3},{8,10},{9,13},{10,... | collective-permute-start | bytes 1191944 | tf_op jit(solution)/shard_map/ppermute | solution.py:288
  15.0 4.1 %collective-permute-start.3 = (bf16[32,768]{1,0:T(8,128)(2,1)S(1)}, bf16[32,768]{1,0:T(8,128)(2,1)S(1)}, u32[]{:S(2)}, u32[]{:S(2)}) collective-permute-start(bf16[32,768]{1,0:T(8,128)(2,1)S(1)} %join.1.refs_0_), channel_id=1, source_target_pairs={{0,8},{4,12},{8,0},{12,4},{16,24},{20,28},{24,16},{28,20},{1,9},{5... | collective-permute-start | bytes 147464 | tf_op jit(solution)/shard_map/ppermute | solution.py:238
  15.0 5.0 %collective-permute-start.4 = (bf16[32,768]{1,0:T(8,128)(2,1)S(1)}, bf16[32,768]{1,0:T(8,128)(2,1)S(1)}, u32[]{:S(2)}, u32[]{:S(2)}) collective-permute-start(bf16[32,768]{1,0:T(8,128)(2,1)S(1)} %join.1.refs_0_), channel_id=1, source_target_pairs={{0,16},{4,20},{8,24},{12,28},{16,0},{20,4},{24,8},{28,12},{1,17},{... | collective-permute-start | bytes 147464 | tf_op jit(solution)/shard_map/ppermute | solution.py:238
  16.3 10.7 %collective-permute-start.9 = (bf16[1024,128]{1,0:T(8,128)(2,1)S(1)}, bf16[1024,128]{1,0:T(8,128)(2,1)S(1)}, u32[]{:S(2)}, u32[]{:S(2)}) collective-permute-start(bf16[1024,128]{1,0:T(8,128)(2,1)S(1)} %slice.8), channel_id=1, source_target_pairs={{0,2},{1,5},{2,0},{3,7},{4,6},{5,1},{6,4},{7,3},{8,10},{9,13},{10,... | collective-permute-start | bytes 786440 | tf_op jit(solution)/shard_map/ppermute | solution.py:291
  21.8 1.7 %collective-permute-start.7 = (bf16[128,768]{1,0:T(8,128)(2,1)S(1)}, bf16[128,768]{1,0:T(8,128)(2,1)S(1)}, u32[]{:S(2)}, u32[]{:S(2)}) collective-permute-start(bf16[128,768]{1,0:T(8,128)(2,1)S(1)} %stack.1.mine_ref), channel_id=1, source_target_pairs={{0,1},{1,0},{2,3},{3,2},{4,5},{5,4},{6,7},{7,6},{8,9},{9,8},{10,11... | collective-permute-start | bytes 589832 | tf_op jit(solution)/shard_map/ppermute | solution.py:238
  21.9 5.1 %collective-permute-start.10 = (bf16[528,128]{1,0:T(8,128)(2,1)S(1)}, bf16[528,128]{1,0:T(8,128)(2,1)S(1)}, u32[]{:S(2)}, u32[]{:S(2)}) collective-permute-start(bf16[528,128]{1,0:T(8,128)(2,1)S(1)} %slice.9), channel_id=1, source_target_pairs={{0,4},{1,3},{2,6},{3,1},{4,0},{5,7},{6,2},{7,5},{8,12},{9,11},{10,... | collective-permute-start | bytes 405512 | tf_op jit(solution)/shard_map/ppermute | solution.py:291
  25.3 16.9 %copy-start = (bf16[1024,768]{1,0:T(8,128)(2,1)S(1)}, bf16[1024,768]{1,0:T(8,128)(2,1)}, u32[]{:S(2)}) copy-start(bf16[1024,768]{1,0:T(8,128)(2,1)} %points_ref.1) | copy-start | bytes 4718596
  27.7 1.6 %collective-permute-start.11 = (bf16[128,896]{1,0:T(8,128)(2,1)S(1)}, bf16[128,896]{1,0:T(8,128)(2,1)S(1)}, u32[]{:S(2)}, u32[]{:S(2)}) collective-permute-start(bf16[128,896]{1,0:T(8,128)(2,1)S(1)} %get-tuple-element.30), channel_id=1, source_target_pairs={{0,1},{1,0},{2,3},{3,2},{4,5},{5,4},{6,7},{7,6},{8,9},{9,8},{10,11... | collective-permute-start | bytes 688136 | tf_op jit(solution)/shard_map/ppermute | solution.py:238
  29.3 6.6 %collective-permute-start.12 = (bf16[208,128]{1,0:T(8,128)(2,1)S(1)}, bf16[208,128]{1,0:T(8,128)(2,1)S(1)}, u32[]{:S(2)}, u32[]{:S(2)}) collective-permute-start(bf16[208,128]{1,0:T(8,128)(2,1)S(1)} %get-tuple-element.32), channel_id=1, source_target_pairs={{0,24},{4,28},{8,16},{12,20},{16,8},{20,12},{24,0},{28,4},{1,25},{... | collective-permute-start | bytes 159752 | tf_op jit(solution)/shard_map/ppermute | solution.py:238
  30.2 6.8 %collective-permute-start.13 = (bf16[208,128]{1,0:T(8,128)(2,1)S(1)}, bf16[208,128]{1,0:T(8,128)(2,1)S(1)}, u32[]{:S(2)}, u32[]{:S(2)}) collective-permute-start(bf16[208,128]{1,0:T(8,128)(2,1)S(1)} %get-tuple-element.33), channel_id=1, source_target_pairs={{0,16},{4,20},{8,24},{12,28},{16,0},{20,4},{24,8},{28,12},{1,17},{... | collective-permute-start | bytes 159752 | tf_op jit(solution)/shard_map/ppermute | solution.py:238
  31.0 6.0 %collective-permute-start.14 = (bf16[208,128]{1,0:T(8,128)(2,1)S(1)}, bf16[208,128]{1,0:T(8,128)(2,1)S(1)}, u32[]{:S(2)}, u32[]{:S(2)}) collective-permute-start(bf16[208,128]{1,0:T(8,128)(2,1)S(1)} %get-tuple-element.34), channel_id=1, source_target_pairs={{0,8},{4,12},{8,0},{12,4},{16,24},{20,28},{24,16},{28,20},{1,9},{5... | collective-permute-start | bytes 159752 | tf_op jit(solution)/shard_map/ppermute | solution.py:238
  37.1 5.1 %collective-permute-start.15 = (f32[32,768]{1,0:T(8,128)S(1)}, f32[32,768]{1,0:T(8,128)S(1)}, u32[]{:S(2)}, u32[]{:S(2)}) collective-permute-start(f32[32,768]{1,0:T(8,128)S(1)} %get-tuple-element.35.refs_0_), channel_id=1, source_target_pairs={{0,1},{1,0},{2,3},{3,2},{4,5},{5,4},{6,7},{7,6},{8,9},{9,8},{10,11... | collective-permute-start | bytes 294920 | tf_op jit(solution)/shard_map/ppermute | solution.py:238
  37.2 4.2 %collective-permute-start.16 = (bf16[32,768]{1,0:T(8,128)(2,1)S(1)}, bf16[32,768]{1,0:T(8,128)(2,1)S(1)}, u32[]{:S(2)}, u32[]{:S(2)}) collective-permute-start(bf16[32,768]{1,0:T(8,128)(2,1)S(1)} %get-tuple-element.36), channel_id=1, source_target_pairs={{0,2},{1,3},{2,0},{3,1},{4,6},{5,7},{6,4},{7,5},{8,10},{9,11},{10,... | collective-permute-start | bytes 147464 | tf_op jit(solution)/shard_map/ppermute | solution.py:238
  38.5 3.7 %collective-permute-start.17 = (bf16[32,768]{1,0:T(8,128)(2,1)S(1)}, bf16[32,768]{1,0:T(8,128)(2,1)S(1)}, u32[]{:S(2)}, u32[]{:S(2)}) collective-permute-start(bf16[32,768]{1,0:T(8,128)(2,1)S(1)} %get-tuple-element.36), channel_id=1, source_target_pairs={{0,3},{1,2},{2,1},{3,0},{4,7},{5,6},{6,5},{7,4},{8,11},{9,10},{10,... | collective-permute-start | bytes 147464 | tf_op jit(solution)/shard_map/ppermute | solution.py:238
  43.8 5.3 %collective-permute-start.20 = (f32[32,768]{1,0:T(8,128)S(1)}, f32[32,768]{1,0:T(8,128)S(1)}, u32[]{:S(2)}, u32[]{:S(2)}) collective-permute-start(f32[32,768]{1,0:T(8,128)S(1)} %get-tuple-element.41), channel_id=1, source_target_pairs={{0,1},{1,0},{2,3},{3,2},{4,5},{5,4},{6,7},{7,6},{8,9},{9,8},{10,11... | collective-permute-start | bytes 294920 | tf_op jit(solution)/shard_map/ppermute | solution.py:238
  44.0 3.5 %collective-permute-start.18 = (bf16[32,768]{1,0:T(8,128)(2,1)S(1)}, bf16[32,768]{1,0:T(8,128)(2,1)S(1)}, u32[]{:S(2)}, u32[]{:S(2)}) collective-permute-start(bf16[32,768]{1,0:T(8,128)(2,1)S(1)} %get-tuple-element.39), channel_id=1, source_target_pairs={{0,3},{1,2},{2,1},{3,0},{4,7},{5,6},{6,5},{7,4},{8,11},{9,10},{10,... | collective-permute-start | bytes 147464 | tf_op jit(solution)/shard_map/ppermute | solution.py:238
  45.0 4.1 %collective-permute-start.19 = (bf16[32,768]{1,0:T(8,128)(2,1)S(1)}, bf16[32,768]{1,0:T(8,128)(2,1)S(1)}, u32[]{:S(2)}, u32[]{:S(2)}) collective-permute-start(bf16[32,768]{1,0:T(8,128)(2,1)S(1)} %get-tuple-element.40), channel_id=1, source_target_pairs={{0,2},{1,3},{2,0},{3,1},{4,6},{5,7},{6,4},{7,5},{8,10},{9,11},{10,... | collective-permute-start | bytes 147464 | tf_op jit(solution)/shard_map/ppermute | solution.py:238

commit v14 on v12

--- a/solution.py
+++ b/solution.py
@@ -203,8 +203,7 @@
     scaled, sketch_hbm, outs = refs[:helpers], refs[helpers], refs[helpers + 1 : -2]
     sketch_ref, sem = refs[-2:]
     rank, count = sketch_ref.shape
-    mark = mark_ref[...]
-    points = points_ref[...]
+    piece = count // CHUNKS
     blocks, rests = [], []
     for s in scaled:
         if s.dtype == F32:
@@ -213,19 +212,27 @@
             rests.append(low)
         else:
             blocks.append(s[...])
-    product = contract(jnp.concatenate(blocks + rests, axis=0), points, ((1,), (1,)))
-    whole = [product[k * rank : (k + 1) * rank] for k in range(helpers)]
-    for k in range(len(rests)):
-        whole[k] = whole[k] + product[(helpers + k) * rank : (helpers + k + 1) * rank]
-    sketch = whole[0]
-    for d in range(1, helpers):
-        sketch = jnp.where(mark == d, whole[d], sketch)
-    sketch_ref[...] = sketch
+    lifter = jnp.concatenate(blocks + rests, axis=0)
     leaving = pltpu.make_async_copy(sketch_ref, sketch_hbm, sem)
-    leaving.start()
-    rounded = sketch.astype(BF16)
-    rows = [jnp.where(mark == d, rounded, jnp.zeros((), BF16)) for d in range(helpers)]
-    summed = contract(jnp.concatenate(rows, axis=0), points, ((1,), (0,)))
+    summed = None
+    for j in range(CHUNKS):
+        part = slice(j * piece, (j + 1) * piece)
+        mark = mark_ref[:, part]
+        points = points_ref[part, :]
+        product = contract(lifter, points, ((1,), (1,)))
+        whole = [product[k * rank : (k + 1) * rank] for k in range(helpers)]
+        for k in range(len(rests)):
+            whole[k] = whole[k] + product[(helpers + k) * rank : (helpers + k + 1) * rank]
+        sketch = whole[0]
+        for d in range(1, helpers):
+            sketch = jnp.where(mark == d, whole[d], sketch)
+        sketch_ref[:, part] = sketch
+        if j == CHUNKS - 1:
+            leaving.start()
+        rounded = sketch.astype(BF16)
+        rows = [jnp.where(mark == d, rounded, jnp.zeros((), BF16)) for d in range(helpers)]
+        more = contract(jnp.concatenate(rows, axis=0), points, ((1,), (0,)))
+        summed = more if summed is None else summed + more
     for d, out in enumerate(outs):
         block = summed[d * rank : (d + 1) * rank] * lax.rsqrt(resident_ref[d : d + 1, 0:1])
         out[...] = block.astype(out.dtype)
@@ -276,7 +283,7 @@
         join_kernel,
         out_shape=sent,
         compiler_params=PARAMS,
-        cost_estimate=pl.CostEstimate(flops=40*10**8, bytes_accessed=10**5, transcendentals=0),
+        cost_estimate=pl.CostEstimate(flops=4 * 10**9, bytes_accessed=10**5, transcendentals=0),
         name="join",
     )(own, *swaps(parts, "help"))
     lifters = [lifter] + [swap(lifter, "shard", INNER * d) for d in range(1, planes)]

time: 49.3 us -> 49.8 us (1.010)
  no operation moved by 1% of the time
where the time goes in v14:
time: 49.8 us; the launch traced here: 49.5 us
  waiting for transfers between devices  21.2 us (43%)
  starting transfers between devices  20.4 us (41%)
  Pallas kernels  6.56 us (13%)
  between operations  0.72 us (1%)
  other arithmetic  0.67 us (1%)
    ppermute x17, waiting for transfers between devices, swap(): lax.ppermute(value, axis, [(i, i ^ d) for i in range(lax.axis_size(axis))])  18.5 us
    ppermute x17, starting transfers between devices, swap(): lax.ppermute(value, axis, [(i, i ^ d) for i in range(lax.axis_size(axis))])  16.4 us
    ppermute x1, starting transfers between devices, shards(): near, = gate([lax.ppermute(packed, axes, two)], lifters[-1])  2.01 us
    pallas_call x1, Pallas kernels, shards(): pl.pallas_call(functools.partial(sketch_kernel, helpers), out_shape=[jax....  2 us
    pallas_call x1, Pallas kernels, shards(): pl.pallas_call(functools.partial(lift_kernel, helpers), out_shape=[jax.Sh...  1.92 us
    ppermute x1, waiting for transfers between devices, shards(): far = lax.ppermute(packed, axes, one)  1.82 us
    pallas_call x1, Pallas kernels, shards(): pl.pallas_call(functools.partial(score_kernel, planes, helpers, 3), out_s...  1.81 us
    ppermute x1, starting transfers between devices, shards(): far = lax.ppermute(packed, axes, one)  1.01 us
  transfers between devices with their start and end apart: 20, of which 14 were waited for; matrix products, arithmetic and copies ran while one was open for 0% of the time, Pallas kernels for 4%

profile of v14, /device:TPU:0, one launch (start us, length us, event | category | flops | bytes accessed | tf_op | source)
XLA Modules:
  0.0 49.5 jit_solution(11316481622989902910)
XLA Ops:
  0.6 1.9 %lift.1 = (bf16[1552,128]{1,0:T(8,128)(2,1)S(1)}, s32[1,1024]{1,0:T(1,128)S(1)}, f32[8,128]{1,0:T(8,128)S(1)}, f32[32,768]{1,0:T(8,128)S(1)}, f32[32,768]{1,0:T(...) custom-call(bf16[256,768]{1,0:T(8,128)(2,1)} %refs_0_.1, s32[2,256]{1,0:T(2,128)} %bitcast.4, ...), custom_call_target="tpu_custom_call" | custom-call | tf_op jit(solution)/shard_map/lift/pallas_call | solution.py:260
  2.6 0.5 %collective-permute-start.2 = (f32[32,768]{1,0:T(8,128)S(1)}, f32[32,768]{1,0:T(8,128)S(1)}, u32[]{:S(2)}, u32[]{:S(2)}) collective-permute-start(f32[32,768]{1,0:T(8,128)S(1)} %get-tuple-element.27), channel_id=1, source_target_pairs={{0,1},{1,0},{2,3},{3,2},{4,5},{5,4},{6,7},{7,6},{8,9},{9,8},{10,11... | collective-permute-start | bytes 294920 | tf_op jit(solution)/shard_map/ppermute | solution.py:243
  3.1 2.6 %collective-permute-start = (bf16[32,768]{1,0:T(8,128)(2,1)S(1)}, bf16[32,768]{1,0:T(8,128)(2,1)S(1)}, u32[]{:S(2)}, u32[]{:S(2)}) collective-permute-start(bf16[32,768]{1,0:T(8,128)(2,1)S(1)} %get-tuple-element.25), channel_id=1, source_target_pairs={{0,3},{1,2},{2,1},{3,0},{4,7},{5,6},{6,5},{7,4},{8,11},{9,10},{10,... | collective-permute-start | bytes 147464 | tf_op jit(solution)/shard_map/ppermute | solution.py:243
  5.7 0.0 collective-permute-start.1
  5.7 2.0 %collective-permute-start.8 = (bf16[1552,128]{1,0:T(8,128)(2,1)S(1)}, bf16[1552,128]{1,0:T(8,128)(2,1)S(1)}, u32[]{:S(2)}, u32[]{:S(2)}) collective-permute-start(bf16[1552,128]{1,0:T(8,128)(2,1)S(1)} %get-tuple-element.28.refs_0_), channel_id=1, source_target_pairs={{0,4},{1,3},{2,6},{3,1},{4,0},{5,7},{6,2},{7,5},{8,12},{9,11},{10,... | collective-permute-start | bytes 1191944 | tf_op jit(solution)/shard_map/ppermute | solution.py:294
  7.7 0.0 collective-permute-done.refs_1_
  7.8 2.5 %collective-permute-done.1.refs_2_ = bf16[32,768]{1,0:T(8,128)(2,1)S(1)} collective-permute-done((bf16[32,768]{1,0:T(8,128)(2,1)S(1)}, bf16[32,768]{1,0:T(8,128)(2,1)S(1)}, u32[]{:S(2)}, u32[]{:S(2)}) %collective-permute-start.1) | collective-permute-done | bytes 49184 | tf_op jit(solution)/shard_map/ppermute | solution.py:243
  10.3 0.0 collective-permute-done.2.refs_3_
  10.3 3.7 %collective-permute-start.5 = (bf16[32,768]{1,0:T(8,128)(2,1)S(1)}, bf16[32,768]{1,0:T(8,128)(2,1)S(1)}, u32[]{:S(2)}, u32[]{:S(2)}) collective-permute-start(bf16[32,768]{1,0:T(8,128)(2,1)S(1)} %join.1.refs_0_), channel_id=1, source_target_pairs={{0,24},{4,28},{8,16},{12,20},{16,8},{20,12},{24,0},{28,4},{1,25},{... | collective-permute-start | bytes 147464 | tf_op jit(solution)/shard_map/ppermute | solution.py:243
  14.0 1.0 %collective-permute-start.6 = (bf16[1552,128]{1,0:T(8,128)(2,1)S(1)}, bf16[1552,128]{1,0:T(8,128)(2,1)S(1)}, u32[]{:S(2)}, u32[]{:S(2)}) collective-permute-start(bf16[1552,128]{1,0:T(8,128)(2,1)S(1)} %get-tuple-element.28.refs_0_), channel_id=1, source_target_pairs={{0,2},{1,5},{2,0},{3,7},{4,6},{5,1},{6,4},{7,3},{8,10},{9,13},{10,... | collective-permute-start | bytes 1191944 | tf_op jit(solution)/shard_map/ppermute | solution.py:293
  15.0 0.0 collective-permute-start.3
  15.0 0.8 %collective-permute-start.4 = (bf16[32,768]{1,0:T(8,128)(2,1)S(1)}, bf16[32,768]{1,0:T(8,128)(2,1)S(1)}, u32[]{:S(2)}, u32[]{:S(2)}) collective-permute-start(bf16[32,768]{1,0:T(8,128)(2,1)S(1)} %join.1.refs_0_), channel_id=1, source_target_pairs={{0,16},{4,20},{8,24},{12,28},{16,0},{20,4},{24,8},{28,12},{1,17},{... | collective-permute-start | bytes 147464 | tf_op jit(solution)/shard_map/ppermute | solution.py:243
  15.8 0.5 %collective-permute-done.5.refs_3_.refs_1_ = bf16[32,768]{1,0:T(8,128)(2,1)S(1)} collective-permute-done((bf16[32,768]{1,0:T(8,128)(2,1)S(1)}, bf16[32,768]{1,0:T(8,128)(2,1)S(1)}, u32[]{:S(2)}, u32[]{:S(2)}) %collective-permute-start.5) | collective-permute-done | bytes 49184 | tf_op jit(solution)/shard_map/ppermute | solution.py:243
  16.3 0.0 collective-permute-done.8.refs_0_
  16.3 1.0 %collective-permute-start.9 = (bf16[1552,128]{1,0:T(8,128)(2,1)S(1)}, bf16[1552,128]{1,0:T(8,128)(2,1)S(1)}, u32[]{:S(2)}, u32[]{:S(2)}) collective-permute-start(bf16[1552,128]{1,0:T(8,128)(2,1)S(1)} %gate.1.refs_1_), channel_id=1, source_target_pairs={{0,2},{1,5},{2,0},{3,7},{4,6},{5,1},{6,4},{7,3},{8,10},{9,13},{10,... | collective-permute-start | bytes 1191944 | tf_op jit(solution)/shard_map/ppermute | solution.py:295
  17.3 1.8 %collective-permute-done.3.refs_1_ = bf16[32,768]{1,0:T(8,128)(2,1)S(1)} collective-permute-done((bf16[32,768]{1,0:T(8,128)(2,1)S(1)}, bf16[32,768]{1,0:T(8,128)(2,1)S(1)}, u32[]{:S(2)}, u32[]{:S(2)}) %collective-permute-start.3) | collective-permute-done | bytes 49184 | tf_op jit(solution)/shard_map/ppermute | solution.py:243
  19.1 0.9 %collective-permute-done.4.refs_2_ = bf16[32,768]{1,0:T(8,128)(2,1)S(1)} collective-permute-done((bf16[32,768]{1,0:T(8,128)(2,1)S(1)}, bf16[32,768]{1,0:T(8,128)(2,1)S(1)}, u32[]{:S(2)}, u32[]{:S(2)}) %collective-permute-start.4) | collective-permute-done | bytes 49184 | tf_op jit(solution)/shard_map/ppermute | solution.py:243
  20.0 1.8 %collective-permute-done.6.refs_4_.refs_2_ = bf16[1552,128]{1,0:T(8,128)(2,1)S(1)} collective-permute-done((bf16[1552,128]{1,0:T(8,128)(2,1)S(1)}, bf16[1552,128]{1,0:T(8,128)(2,1)S(1)}, u32[]{:S(2)}, u32[]{:S(2)}) %collective-permute-start.6) | collective-permute-done | bytes 397344 | tf_op jit(solution)/shard_map/ppermute | solution.py:293
  21.8 0.1 collective-permute-start.7
  21.9 1.4 %collective-permute-done.7.theirs_ref = bf16[128,768]{1,0:T(8,128)(2,1)S(1)} collective-permute-done((bf16[128,768]{1,0:T(8,128)(2,1)S(1)}, bf16[128,768]{1,0:T(8,128)(2,1)S(1)}, u32[]{:S(2)}, u32[]{:S(2)}) %collective-permute-start.7) | collective-permute-done | bytes 196640 | tf_op jit(solution)/shard_map/ppermute | solution.py:243
  23.3 1.8 %score.1.refs_1_ = f32[256,896]{1,0:T(8,128)S(1)} custom-call(bf16[128,768]{1,0:T(8,128)(2,1)S(1)} %stack.1.mine_ref, bf16[128,768]{1,0:T(8,128)(2,1)S(1)} %collective-permute-done.7.theirs_ref, bf16[1552,128]{1,0:T(8,128)(2,1)S(1)} %get-tuple-element.28.refs_0_, bf16[1552,128]{1,0:T(8,128)(2,1)S(1)} %gate.1.refs_1_, ...), custom_call_target="tpu_custom_call" | custom-call | tf_op jit(solution)/shard_map/score/pallas_call | solution.py:308
  25.2 0.0 copy-start
  25.2 0.9 %collective-permute-done.9.refs_0_ = bf16[1552,128]{1,0:T(8,128)(2,1)S(1)} collective-permute-done((bf16[1552,128]{1,0:T(8,128)(2,1)S(1)}, bf16[1552,128]{1,0:T(8,128)(2,1)S(1)}, u32[]{:S(2)}, u32[]{:S(2)}) %collective-permute-start.9) | collective-permute-done | bytes 397344 | tf_op jit(solution)/shard_map/ppermute | solution.py:295
  26.1 0.6 %score_last.1 = (f32[128,896]{1,0:T(8,128)S(1)}, bf16[128,896]{1,0:T(8,128)(2,1)S(1)}) custom-call(bf16[128,768]{1,0:T(8,128)(2,1)S(1)} %stack.1.mine_ref, bf16[128,768]{1,0:T(8,128)(2,1)S(1)} %collective-permute-done.7.theirs_ref, bf16[1552,128]{1,0:T(8,128)(2,1)S(1)} %collective-permute-done.9.refs_0_, f32[256,896]{1,0:T(8,128)S(1)} %score.1.refs_1_), custom_call_target="tpu_custom_call" | custom-call | tf_op jit(solution)/shard_map/score_last/pallas_call | solution.py:314
  26.7 0.1 collective-permute-start.10
  26.8 1.5 %collective-permute-done.10.theirs_ref = bf16[128,896]{1,0:T(8,128)(2,1)S(1)} collective-permute-done((bf16[128,896]{1,0:T(8,128)(2,1)S(1)}, bf16[128,896]{1,0:T(8,128)(2,1)S(1)}, u32[]{:S(2)}, u32[]{:S(2)}) %collective-permute-start.10) | collective-permute-done | bytes 229408 | tf_op jit(solution)/shard_map/ppermute | solution.py:243
  28.3 0.1 fold.1
  28.3 2.0 %collective-permute-start.11 = (bf16[208,128]{1,0:T(8,128)(2,1)S(1)}, bf16[208,128]{1,0:T(8,128)(2,1)S(1)}, u32[]{:S(2)}, u32[]{:S(2)}) collective-permute-start(bf16[208,128]{1,0:T(8,128)(2,1)S(1)} %get-tuple-element.32), channel_id=1, source_target_pairs={{0,24},{4,28},{8,16},{12,20},{16,8},{20,12},{24,0},{28,4},{1,25},{... | collective-permute-start | bytes 159752 | tf_op jit(solution)/shard_map/ppermute | solution.py:243
  30.3 0.0 collective-permute-start.12
  30.3 2.5 %collective-permute-start.13 = (bf16[208,128]{1,0:T(8,128)(2,1)S(1)}, bf16[208,128]{1,0:T(8,128)(2,1)S(1)}, u32[]{:S(2)}, u32[]{:S(2)}) collective-permute-start(bf16[208,128]{1,0:T(8,128)(2,1)S(1)} %get-tuple-element.34), channel_id=1, source_target_pairs={{0,8},{4,12},{8,0},{12,4},{16,24},{20,28},{24,16},{28,20},{1,9},{5... | collective-permute-start | bytes 159752 | tf_op jit(solution)/shard_map/ppermute | solution.py:243
  32.8 2.0 %collective-permute-done.11.refs_0_ = bf16[208,128]{1,0:T(8,128)(2,1)S(1)} collective-permute-done((bf16[208,128]{1,0:T(8,128)(2,1)S(1)}, bf16[208,128]{1,0:T(8,128)(2,1)S(1)}, u32[]{:S(2)}, u32[]{:S(2)}) %collective-permute-start.11) | collective-permute-done | bytes 53280 | tf_op jit(solution)/shard_map/ppermute | solution.py:243
  34.8 1.6 %collective-permute-done.12.refs_1_ = bf16[208,128]{1,0:T(8,128)(2,1)S(1)} collective-permute-done((bf16[208,128]{1,0:T(8,128)(2,1)S(1)}, bf16[208,128]{1,0:T(8,128)(2,1)S(1)}, u32[]{:S(2)}, u32[]{:S(2)}) %collective-permute-start.12) | collective-permute-done | bytes 53280 | tf_op jit(solution)/shard_map/ppermute | solution.py:243
  36.4 0.0 collective-permute-done.13.refs_2_
  36.4 0.1 scale.1
  36.4 0.1 collective-permute-start.14
  36.5 1.1 %collective-permute-start.15 = (bf16[32,768]{1,0:T(8,128)(2,1)S(1)}, bf16[32,768]{1,0:T(8,128)(2,1)S(1)}, u32[]{:S(2)}, u32[]{:S(2)}) collective-permute-start(bf16[32,768]{1,0:T(8,128)(2,1)S(1)} %get-tuple-element.36), channel_id=1, source_target_pairs={{0,2},{1,3},{2,0},{3,1},{4,6},{5,7},{6,4},{7,5},{8,10},{9,11},{10,... | collective-permute-start | bytes 147464 | tf_op jit(solution)/shard_map/ppermute | solution.py:243
  37.6 0.8 %collective-permute-start.16 = (bf16[32,768]{1,0:T(8,128)(2,1)S(1)}, bf16[32,768]{1,0:T(8,128)(2,1)S(1)}, u32[]{:S(2)}, u32[]{:S(2)}) collective-permute-start(bf16[32,768]{1,0:T(8,128)(2,1)S(1)} %get-tuple-element.36), channel_id=1, source_target_pairs={{0,3},{1,2},{2,1},{3,0},{4,7},{5,6},{6,5},{7,4},{8,11},{9,10},{10,... | collective-permute-start | bytes 147464 | tf_op jit(solution)/shard_map/ppermute | solution.py:243
  38.4 2.5 %collective-permute-done.15.refs_2_ = bf16[32,768]{1,0:T(8,128)(2,1)S(1)} collective-permute-done((bf16[32,768]{1,0:T(8,128)(2,1)S(1)}, bf16[32,768]{1,0:T(8,128)(2,1)S(1)}, u32[]{:S(2)}, u32[]{:S(2)}) %collective-permute-start.15) | collective-permute-done | bytes 49184 | tf_op jit(solution)/shard_map/ppermute | solution.py:243
  40.9 0.6 %collective-permute-done.16.refs_3_ = bf16[32,768]{1,0:T(8,128)(2,1)S(1)} collective-permute-done((bf16[32,768]{1,0:T(8,128)(2,1)S(1)}, bf16[32,768]{1,0:T(8,128)(2,1)S(1)}, u32[]{:S(2)}, u32[]{:S(2)}) %collective-permute-start.16) | collective-permute-done | bytes 49184 | tf_op jit(solution)/shard_map/ppermute | solution.py:243
  41.5 0.0 collective-permute-done.14.refs_1_
  41.5 0.0 copy-done
  41.5 2.0 %sketch.1 = (f32[32,1024]{1,0:T(8,128)}, f32[32,768]{1,0:T(8,128)S(1)}, f32[32,768]{1,0:T(8,128)S(1)}, bf16[32,768]{1,0:T(8,128)(2,1)S(1)}, bf16[32,768]{1,0:T(8,128)(2,1)S(1)}) custom-call(s32[1,1024]{1,0:T(1,128)S(1)} %get-tuple-element.22.mark_ref, f32[8,128]{1,0:T(8,128)S(1)} %get-tuple-element.23.resident_ref, bf16[1024,768]{1,0:T(8,128)(2,1)S(1)} %copy-done, ...), custom_call_target="tpu_custom_call" | custom-call | tf_op jit(solution)/shard_map/sketch/pallas_call | solution.py:337
  43.5 0.2 collective-permute-start.19
  43.7 1.0 %collective-permute-start.17 = (bf16[32,768]{1,0:T(8,128)(2,1)S(1)}, bf16[32,768]{1,0:T(8,128)(2,1)S(1)}, u32[]{:S(2)}, u32[]{:S(2)}) collective-permute-start(bf16[32,768]{1,0:T(8,128)(2,1)S(1)} %get-tuple-element.39), channel_id=1, source_target_pairs={{0,3},{1,2},{2,1},{3,0},{4,7},{5,6},{6,5},{7,4},{8,11},{9,10},{10,... | collective-permute-start | bytes 147464 | tf_op jit(solution)/shard_map/ppermute | solution.py:243
  44.7 1.1 %collective-permute-start.18 = (bf16[32,768]{1,0:T(8,128)(2,1)S(1)}, bf16[32,768]{1,0:T(8,128)(2,1)S(1)}, u32[]{:S(2)}, u32[]{:S(2)}) collective-permute-start(bf16[32,768]{1,0:T(8,128)(2,1)S(1)} %get-tuple-element.40), channel_id=1, source_target_pairs={{0,2},{1,3},{2,0},{3,1},{4,6},{5,7},{6,4},{7,5},{8,10},{9,11},{10,... | collective-permute-start | bytes 147464 | tf_op jit(solution)/shard_map/ppermute | solution.py:243
  45.7 1.5 %collective-permute-done.17 = bf16[32,768]{1,0:T(8,128)(2,1)S(1)} collective-permute-done((bf16[32,768]{1,0:T(8,128)(2,1)S(1)}, bf16[32,768]{1,0:T(8,128)(2,1)S(1)}, u32[]{:S(2)}, u32[]{:S(2)}) %collective-permute-start.17) | collective-permute-done | bytes 49184 | tf_op jit(solution)/shard_map/ppermute | solution.py:243
  47.2 1.7 %collective-permute-done.18 = bf16[32,768]{1,0:T(8,128)(2,1)S(1)} collective-permute-done((bf16[32,768]{1,0:T(8,128)(2,1)S(1)}, bf16[32,768]{1,0:T(8,128)(2,1)S(1)}, u32[]{:S(2)}, u32[]{:S(2)}) %collective-permute-start.18) | collective-permute-done | bytes 49184 | tf_op jit(solution)/shard_map/ppermute | solution.py:243
  48.9 0.0 collective-permute-done.19
  48.9 0.7 %add_bitcast_fusion = f32[1,32,768]{2,1,0:T(8,128)} fusion(f32[32,768]{1,0:T(8,128)S(1)} %collective-permute-done.19, bf16[32,768]{1,0:T(8,128)(2,1)S(1)} %collective-permute-done.18, f32[32,768]{1,0:T(8,128)S(1)} %get-tuple-element.38, bf16[32,768]{1,0:T(8,128)(2,1)S(1)} %collective-permute-done.17), kind=kLoop, calls=%fused_computation | loop fusion | flops 122880 | bytes 393216 | tf_op jit(solution)/shard_map/broadcast_in_dim | solution.py:347
  (3 shorter events, 0.0 us)
Async XLA Ops:
  2.6 7.7 %collective-permute-start.2 = (f32[32,768]{1,0:T(8,128)S(1)}, f32[32,768]{1,0:T(8,128)S(1)}, u32[]{:S(2)}, u32[]{:S(2)}) collective-permute-start(f32[32,768]{1,0:T(8,128)S(1)} %get-tuple-element.27), channel_id=1, source_target_pairs={{0,1},{1,0},{2,3},{3,2},{4,5},{5,4},{6,7},{7,6},{8,9},{9,8},{10,11... | collective-permute-start | bytes 294920 | tf_op jit(solution)/shard_map/ppermute | solution.py:243
  3.1 4.7 %collective-permute-start = (bf16[32,768]{1,0:T(8,128)(2,1)S(1)}, bf16[32,768]{1,0:T(8,128)(2,1)S(1)}, u32[]{:S(2)}, u32[]{:S(2)}) collective-permute-start(bf16[32,768]{1,0:T(8,128)(2,1)S(1)} %get-tuple-element.25), channel_id=1, source_target_pairs={{0,3},{1,2},{2,1},{3,0},{4,7},{5,6},{6,5},{7,4},{8,11},{9,10},{10,... | collective-permute-start | bytes 147464 | tf_op jit(solution)/shard_map/ppermute | solution.py:243
  5.7 4.6 %collective-permute-start.1 = (bf16[32,768]{1,0:T(8,128)(2,1)S(1)}, bf16[32,768]{1,0:T(8,128)(2,1)S(1)}, u32[]{:S(2)}, u32[]{:S(2)}) collective-permute-start(bf16[32,768]{1,0:T(8,128)(2,1)S(1)} %get-tuple-element.26), channel_id=1, source_target_pairs={{0,2},{1,3},{2,0},{3,1},{4,6},{5,7},{6,4},{7,5},{8,10},{9,11},{10,... | collective-permute-start | bytes 147464 | tf_op jit(solution)/shard_map/ppermute | solution.py:243
  5.7 10.6 %collective-permute-start.8 = (bf16[1552,128]{1,0:T(8,128)(2,1)S(1)}, bf16[1552,128]{1,0:T(8,128)(2,1)S(1)}, u32[]{:S(2)}, u32[]{:S(2)}) collective-permute-start(bf16[1552,128]{1,0:T(8,128)(2,1)S(1)} %get-tuple-element.28.refs_0_), channel_id=1, source_target_pairs={{0,4},{1,3},{2,6},{3,1},{4,0},{5,7},{6,2},{7,5},{8,12},{9,11},{10,... | collective-permute-start | bytes 1191944 | tf_op jit(solution)/shard_map/ppermute | solution.py:294
  10.3 6.0 %collective-permute-start.5 = (bf16[32,768]{1,0:T(8,128)(2,1)S(1)}, bf16[32,768]{1,0:T(8,128)(2,1)S(1)}, u32[]{:S(2)}, u32[]{:S(2)}) collective-permute-start(bf16[32,768]{1,0:T(8,128)(2,1)S(1)} %join.1.refs_0_), channel_id=1, source_target_pairs={{0,24},{4,28},{8,16},{12,20},{16,8},{20,12},{24,0},{28,4},{1,25},{... | collective-permute-start | bytes 147464 | tf_op jit(solution)/shard_map/ppermute | solution.py:243
  14.0 7.8 %collective-permute-start.6 = (bf16[1552,128]{1,0:T(8,128)(2,1)S(1)}, bf16[1552,128]{1,0:T(8,128)(2,1)S(1)}, u32[]{:S(2)}, u32[]{:S(2)}) collective-permute-start(bf16[1552,128]{1,0:T(8,128)(2,1)S(1)} %get-tuple-element.28.refs_0_), channel_id=1, source_target_pairs={{0,2},{1,5},{2,0},{3,7},{4,6},{5,1},{6,4},{7,3},{8,10},{9,13},{10,... | collective-permute-start | bytes 1191944 | tf_op jit(solution)/shard_map/ppermute | solution.py:293
  15.0 4.1 %collective-permute-start.3 = (bf16[32,768]{1,0:T(8,128)(2,1)S(1)}, bf16[32,768]{1,0:T(8,128)(2,1)S(1)}, u32[]{:S(2)}, u32[]{:S(2)}) collective-permute-start(bf16[32,768]{1,0:T(8,128)(2,1)S(1)} %join.1.refs_0_), channel_id=1, source_target_pairs={{0,8},{4,12},{8,0},{12,4},{16,24},{20,28},{24,16},{28,20},{1,9},{5... | collective-permute-start | bytes 147464 | tf_op jit(solution)/shard_map/ppermute | solution.py:243
  15.0 5.0 %collective-permute-start.4 = (bf16[32,768]{1,0:T(8,128)(2,1)S(1)}, bf16[32,768]{1,0:T(8,128)(2,1)S(1)}, u32[]{:S(2)}, u32[]{:S(2)}) collective-permute-start(bf16[32,768]{1,0:T(8,128)(2,1)S(1)} %join.1.refs_0_), channel_id=1, source_target_pairs={{0,16},{4,20},{8,24},{12,28},{16,0},{20,4},{24,8},{28,12},{1,17},{... | collective-permute-start | bytes 147464 | tf_op jit(solution)/shard_map/ppermute | solution.py:243
  16.3 9.8 %collective-permute-start.9 = (bf16[1552,128]{1,0:T(8,128)(2,1)S(1)}, bf16[1552,128]{1,0:T(8,128)(2,1)S(1)}, u32[]{:S(2)}, u32[]{:S(2)}) collective-permute-start(bf16[1552,128]{1,0:T(8,128)(2,1)S(1)} %gate.1.refs_1_), channel_id=1, source_target_pairs={{0,2},{1,5},{2,0},{3,7},{4,6},{5,1},{6,4},{7,3},{8,10},{9,13},{10,... | collective-permute-start | bytes 1191944 | tf_op jit(solution)/shard_map/ppermute | solution.py:295
  21.8 1.5 %collective-permute-start.7 = (bf16[128,768]{1,0:T(8,128)(2,1)S(1)}, bf16[128,768]{1,0:T(8,128)(2,1)S(1)}, u32[]{:S(2)}, u32[]{:S(2)}) collective-permute-start(bf16[128,768]{1,0:T(8,128)(2,1)S(1)} %stack.1.mine_ref), channel_id=1, source_target_pairs={{0,1},{1,0},{2,3},{3,2},{4,5},{5,4},{6,7},{7,6},{8,9},{9,8},{10,11... | collective-permute-start | bytes 589832 | tf_op jit(solution)/shard_map/ppermute | solution.py:243
  25.2 16.3 %copy-start = (bf16[1024,768]{1,0:T(8,128)(2,1)S(1)}, bf16[1024,768]{1,0:T(8,128)(2,1)}, u32[]{:S(2)}) copy-start(bf16[1024,768]{1,0:T(8,128)(2,1)} %points_ref.1) | copy-start | bytes 4718596
  26.7 1.6 %collective-permute-start.10 = (bf16[128,896]{1,0:T(8,128)(2,1)S(1)}, bf16[128,896]{1,0:T(8,128)(2,1)S(1)}, u32[]{:S(2)}, u32[]{:S(2)}) collective-permute-start(bf16[128,896]{1,0:T(8,128)(2,1)S(1)} %get-tuple-element.30), channel_id=1, source_target_pairs={{0,1},{1,0},{2,3},{3,2},{4,5},{5,4},{6,7},{7,6},{8,9},{9,8},{10,11... | collective-permute-start | bytes 688136 | tf_op jit(solution)/shard_map/ppermute | solution.py:243
  28.3 6.4 %collective-permute-start.11 = (bf16[208,128]{1,0:T(8,128)(2,1)S(1)}, bf16[208,128]{1,0:T(8,128)(2,1)S(1)}, u32[]{:S(2)}, u32[]{:S(2)}) collective-permute-start(bf16[208,128]{1,0:T(8,128)(2,1)S(1)} %get-tuple-element.32), channel_id=1, source_target_pairs={{0,24},{4,28},{8,16},{12,20},{16,8},{20,12},{24,0},{28,4},{1,25},{... | collective-permute-start | bytes 159752 | tf_op jit(solution)/shard_map/ppermute | solution.py:243
  30.3 6.0 %collective-permute-start.12 = (bf16[208,128]{1,0:T(8,128)(2,1)S(1)}, bf16[208,128]{1,0:T(8,128)(2,1)S(1)}, u32[]{:S(2)}, u32[]{:S(2)}) collective-permute-start(bf16[208,128]{1,0:T(8,128)(2,1)S(1)} %get-tuple-element.33), channel_id=1, source_target_pairs={{0,16},{4,20},{8,24},{12,28},{16,0},{20,4},{24,8},{28,12},{1,17},{... | collective-permute-start | bytes 159752 | tf_op jit(solution)/shard_map/ppermute | solution.py:243
  30.3 6.0 %collective-permute-start.13 = (bf16[208,128]{1,0:T(8,128)(2,1)S(1)}, bf16[208,128]{1,0:T(8,128)(2,1)S(1)}, u32[]{:S(2)}, u32[]{:S(2)}) collective-permute-start(bf16[208,128]{1,0:T(8,128)(2,1)S(1)} %get-tuple-element.34), channel_id=1, source_target_pairs={{0,8},{4,12},{8,0},{12,4},{16,24},{20,28},{24,16},{28,20},{1,9},{5... | collective-permute-start | bytes 159752 | tf_op jit(solution)/shard_map/ppermute | solution.py:243
  36.4 5.0 %collective-permute-start.14 = (f32[32,768]{1,0:T(8,128)S(1)}, f32[32,768]{1,0:T(8,128)S(1)}, u32[]{:S(2)}, u32[]{:S(2)}) collective-permute-start(f32[32,768]{1,0:T(8,128)S(1)} %get-tuple-element.35.refs_0_), channel_id=1, source_target_pairs={{0,1},{1,0},{2,3},{3,2},{4,5},{5,4},{6,7},{7,6},{8,9},{9,8},{10,11... | collective-permute-start | bytes 294920 | tf_op jit(solution)/shard_map/ppermute | solution.py:243
  36.5 4.3 %collective-permute-start.15 = (bf16[32,768]{1,0:T(8,128)(2,1)S(1)}, bf16[32,768]{1,0:T(8,128)(2,1)S(1)}, u32[]{:S(2)}, u32[]{:S(2)}) collective-permute-start(bf16[32,768]{1,0:T(8,128)(2,1)S(1)} %get-tuple-element.36), channel_id=1, source_target_pairs={{0,2},{1,3},{2,0},{3,1},{4,6},{5,7},{6,4},{7,5},{8,10},{9,11},{10,... | collective-permute-start | bytes 147464 | tf_op jit(solution)/shard_map/ppermute | solution.py:243
  37.6 3.9 %collective-permute-start.16 = (bf16[32,768]{1,0:T(8,128)(2,1)S(1)}, bf16[32,768]{1,0:T(8,128)(2,1)S(1)}, u32[]{:S(2)}, u32[]{:S(2)}) collective-permute-start(bf16[32,768]{1,0:T(8,128)(2,1)S(1)} %get-tuple-element.36), channel_id=1, source_target_pairs={{0,3},{1,2},{2,1},{3,0},{4,7},{5,6},{6,5},{7,4},{8,11},{9,10},{10,... | collective-permute-start | bytes 147464 | tf_op jit(solution)/shard_map/ppermute | solution.py:243
  43.5 5.4 %collective-permute-start.19 = (f32[32,768]{1,0:T(8,128)S(1)}, f32[32,768]{1,0:T(8,128)S(1)}, u32[]{:S(2)}, u32[]{:S(2)}) collective-permute-start(f32[32,768]{1,0:T(8,128)S(1)} %get-tuple-element.41), channel_id=1, source_target_pairs={{0,1},{1,0},{2,3},{3,2},{4,5},{5,4},{6,7},{7,6},{8,9},{9,8},{10,11... | collective-permute-start | bytes 294920 | tf_op jit(solution)/shard_map/ppermute | solution.py:243
  43.7 3.5 %collective-permute-start.17 = (bf16[32,768]{1,0:T(8,128)(2,1)S(1)}, bf16[32,768]{1,0:T(8,128)(2,1)S(1)}, u32[]{:S(2)}, u32[]{:S(2)}) collective-permute-start(bf16[32,768]{1,0:T(8,128)(2,1)S(1)} %get-tuple-element.39), channel_id=1, source_target_pairs={{0,3},{1,2},{2,1},{3,0},{4,7},{5,6},{6,5},{7,4},{8,11},{9,10},{10,... | collective-permute-start | bytes 147464 | tf_op jit(solution)/shard_map/ppermute | solution.py:243
  44.7 4.2 %collective-permute-start.18 = (bf16[32,768]{1,0:T(8,128)(2,1)S(1)}, bf16[32,768]{1,0:T(8,128)(2,1)S(1)}, u32[]{:S(2)}, u32[]{:S(2)}) collective-permute-start(bf16[32,768]{1,0:T(8,128)(2,1)S(1)} %get-tuple-element.40), channel_id=1, source_target_pairs={{0,2},{1,3},{2,0},{3,1},{4,6},{5,7},{6,4},{7,5},{8,10},{9,11},{10,... | collective-permute-start | bytes 147464 | tf_op jit(solution)/shard_map/ppermute | solution.py:243

commit v15 on v12

--- a/solution.py
+++ b/solution.py
@@ -110,7 +110,7 @@
         out_specs=[ANY] * len(values),
         input_output_aliases={k: k for k in range(len(values))},
         compiler_params=pltpu.CompilerParams(vmem_limit_bytes=1 << 20),
-        cost_estimate=pl.CostEstimate(flops=5 * 10**9, bytes_accessed=10**5, transcendentals=0),
+        cost_estimate=pl.CostEstimate(flops=37 * 10**8, bytes_accessed=10**5, transcendentals=0),
         name="gate",
     )(*values, *others)
 
@@ -276,7 +276,7 @@
         join_kernel,
         out_shape=sent,
         compiler_params=PARAMS,
-        cost_estimate=pl.CostEstimate(flops=40*10**8, bytes_accessed=10**5, transcendentals=0),
+        cost_estimate=pl.CostEstimate(flops=35 * 10**8, bytes_accessed=10**5, transcendentals=0),
         name="join",
     )(own, *swaps(parts, "help"))
     lifters = [lifter] + [swap(lifter, "shard", INNER * d) for d in range(1, planes)]
@@ -292,7 +292,7 @@
         out_shape=jax.ShapeDtypeStruct((planes * rank, width), BF16),
         in_specs=[VMEM] * planes + [ANY],
         compiler_params=PARAMS,
-        cost_estimate=pl.CostEstimate(flops=25 * 10**8, bytes_accessed=10**5, transcendentals=0),
+        cost_estimate=pl.CostEstimate(flops=25*10**8, bytes_accessed=10**5, transcendentals=0),
         name="stack",
     )(*lifters, far)
     theirs = swap(mine, "help", 1)

time: 49.3 us -> 49.9 us (1.012)
  starting transfers between devices: 20.4 us -> 22 us
  waiting for transfers between devices: 21.2 us -> 20.2 us
    ppermute x17, waiting for transfers between devices: 18.5 us -> 16.4 us  [swap(): lax.ppermute(value, axis, [(i, i ^ d) for i in range(lax.axis_size(axis))])]
    ppermute x1, waiting for transfers between devices: 0.9 us -> 2.85 us  [shards(): across = lax.ppermute(near, axes, one)]
    ppermute x1, waiting for transfers between devices: 1.82 us -> 0.01 us  [shards(): far = lax.ppermute(packed, axes, one)]
    ppermute x1, waiting for transfers between devices: 0.01 us -> 0.98 us  [shards(): near, = gate([lax.ppermute(packed, axes, two)], lifters[-1])]
    ppermute x17, starting transfers between devices: 16.4 us -> 17.1 us  [swap(): lax.ppermute(value, axis, [(i, i ^ d) for i in range(lax.axis_size(axis))])]
  transfers between devices with their start and end apart: 20 -> 20, of which waited for: 14 -> 12; matrix products, arithmetic and copies ran while one was open for 0% -> 0% of each run, Pallas kernels for 4% -> 4%
where the time goes in v15:
time: 49.9 us; the launch traced here: 49.7 us
  starting transfers between devices  22 us (44%)
  waiting for transfers between devices  20.2 us (40%)
  Pallas kernels  6.09 us (12%)
  between operations  0.73 us (1%)
  other arithmetic  0.67 us (1%)
    ppermute x17, starting transfers between devices, swap(): lax.ppermute(value, axis, [(i, i ^ d) for i in range(lax.axis_size(axis))])  17.1 us
    ppermute x17, waiting for transfers between devices, swap(): lax.ppermute(value, axis, [(i, i ^ d) for i in range(lax.axis_size(axis))])  16.4 us
    ppermute x1, waiting for transfers between devices, shards(): across = lax.ppermute(near, axes, one)  2.85 us
    ppermute x1, starting transfers between devices, shards(): near, = gate([lax.ppermute(packed, axes, two)], lifters[-1])  2.01 us
    pallas_call x1, Pallas kernels, shards(): pl.pallas_call(functools.partial(lift_kernel, helpers), out_shape=[jax.Sh...  1.92 us
    pallas_call x1, Pallas kernels, shards(): pl.pallas_call(functools.partial(score_kernel, planes, helpers, 3), out_s...  1.81 us
    pallas_call x1, Pallas kernels, shards(): pl.pallas_call(functools.partial(sketch_kernel, helpers), out_shape=[jax....  1.54 us
    ppermute x1, starting transfers between devices, shards(): far = lax.ppermute(packed, axes, one)  1.49 us
  transfers between devices with their start and end apart: 20, of which 12 were waited for; matrix products, arithmetic and copies ran while one was open for 0% of the time, Pallas kernels for 4%

profile of v15, /device:TPU:0, one launch (start us, length us, event | category | flops | bytes accessed | tf_op | source)
XLA Modules:
  0.0 49.7 jit_solution(9154253836167075109)
XLA Ops:
  0.6 1.9 %lift.1 = (bf16[1552,128]{1,0:T(8,128)(2,1)S(1)}, s32[1,1024]{1,0:T(1,128)S(1)}, f32[8,128]{1,0:T(8,128)S(1)}, f32[32,768]{1,0:T(8,128)S(1)}, f32[32,768]{1,0:T(...) custom-call(bf16[256,768]{1,0:T(8,128)(2,1)} %refs_0_.1, s32[2,256]{1,0:T(2,128)} %bitcast.4, ...), custom_call_target="tpu_custom_call" | custom-call | tf_op jit(solution)/shard_map/lift/pallas_call | solution.py:253
  2.6 0.5 %collective-permute-start.2 = (f32[32,768]{1,0:T(8,128)S(1)}, f32[32,768]{1,0:T(8,128)S(1)}, u32[]{:S(2)}, u32[]{:S(2)}) collective-permute-start(f32[32,768]{1,0:T(8,128)S(1)} %get-tuple-element.27), channel_id=1, source_target_pairs={{0,1},{1,0},{2,3},{3,2},{4,5},{5,4},{6,7},{7,6},{8,9},{9,8},{10,11... | collective-permute-start | bytes 294920 | tf_op jit(solution)/shard_map/ppermute | solution.py:236
  3.1 2.6 %collective-permute-start = (bf16[32,768]{1,0:T(8,128)(2,1)S(1)}, bf16[32,768]{1,0:T(8,128)(2,1)S(1)}, u32[]{:S(2)}, u32[]{:S(2)}) collective-permute-start(bf16[32,768]{1,0:T(8,128)(2,1)S(1)} %get-tuple-element.25), channel_id=1, source_target_pairs={{0,3},{1,2},{2,1},{3,0},{4,7},{5,6},{6,5},{7,4},{8,11},{9,10},{10,... | collective-permute-start | bytes 147464 | tf_op jit(solution)/shard_map/ppermute | solution.py:236
  5.7 0.0 collective-permute-start.1
  5.7 2.0 %collective-permute-start.8 = (bf16[1552,128]{1,0:T(8,128)(2,1)S(1)}, bf16[1552,128]{1,0:T(8,128)(2,1)S(1)}, u32[]{:S(2)}, u32[]{:S(2)}) collective-permute-start(bf16[1552,128]{1,0:T(8,128)(2,1)S(1)} %get-tuple-element.28.refs_0_), channel_id=1, source_target_pairs={{0,4},{1,3},{2,6},{3,1},{4,0},{5,7},{6,2},{7,5},{8,12},{9,11},{10,... | collective-permute-start | bytes 1191944 | tf_op jit(solution)/shard_map/ppermute | solution.py:287
  7.7 1.5 %collective-permute-start.6 = (bf16[1552,128]{1,0:T(8,128)(2,1)S(1)}, bf16[1552,128]{1,0:T(8,128)(2,1)S(1)}, u32[]{:S(2)}, u32[]{:S(2)}) collective-permute-start(bf16[1552,128]{1,0:T(8,128)(2,1)S(1)} %get-tuple-element.28.refs_0_), channel_id=1, source_target_pairs={{0,2},{1,5},{2,0},{3,7},{4,6},{5,1},{6,4},{7,3},{8,10},{9,13},{10,... | collective-permute-start | bytes 1191944 | tf_op jit(solution)/shard_map/ppermute | solution.py:286
  9.2 0.0 collective-permute-done.refs_1_
  9.2 1.1 %collective-permute-done.1.refs_2_ = bf16[32,768]{1,0:T(8,128)(2,1)S(1)} collective-permute-done((bf16[32,768]{1,0:T(8,128)(2,1)S(1)}, bf16[32,768]{1,0:T(8,128)(2,1)S(1)}, u32[]{:S(2)}, u32[]{:S(2)}) %collective-permute-start.1) | collective-permute-done | bytes 49184 | tf_op jit(solution)/shard_map/ppermute | solution.py:236
  10.3 0.0 collective-permute-done.2.refs_3_
  10.3 3.7 %collective-permute-start.5 = (bf16[32,768]{1,0:T(8,128)(2,1)S(1)}, bf16[32,768]{1,0:T(8,128)(2,1)S(1)}, u32[]{:S(2)}, u32[]{:S(2)}) collective-permute-start(bf16[32,768]{1,0:T(8,128)(2,1)S(1)} %join.1.refs_0_), channel_id=1, source_target_pairs={{0,24},{4,28},{8,16},{12,20},{16,8},{20,12},{24,0},{28,4},{1,25},{... | collective-permute-start | bytes 147464 | tf_op jit(solution)/shard_map/ppermute | solution.py:236
  14.0 0.0 collective-permute-start.3
  14.0 0.8 %collective-permute-start.4 = (bf16[32,768]{1,0:T(8,128)(2,1)S(1)}, bf16[32,768]{1,0:T(8,128)(2,1)S(1)}, u32[]{:S(2)}, u32[]{:S(2)}) collective-permute-start(bf16[32,768]{1,0:T(8,128)(2,1)S(1)} %join.1.refs_0_), channel_id=1, source_target_pairs={{0,16},{4,20},{8,24},{12,28},{16,0},{20,4},{24,8},{28,12},{1,17},{... | collective-permute-start | bytes 147464 | tf_op jit(solution)/shard_map/ppermute | solution.py:236
  14.8 1.6 %collective-permute-done.5.refs_3_.refs_1_ = bf16[32,768]{1,0:T(8,128)(2,1)S(1)} collective-permute-done((bf16[32,768]{1,0:T(8,128)(2,1)S(1)}, bf16[32,768]{1,0:T(8,128)(2,1)S(1)}, u32[]{:S(2)}, u32[]{:S(2)}) %collective-permute-start.5) | collective-permute-done | bytes 49184 | tf_op jit(solution)/shard_map/ppermute | solution.py:236
  16.4 1.0 %collective-permute-done.8.refs_0_ = bf16[1552,128]{1,0:T(8,128)(2,1)S(1)} collective-permute-done((bf16[1552,128]{1,0:T(8,128)(2,1)S(1)}, bf16[1552,128]{1,0:T(8,128)(2,1)S(1)}, u32[]{:S(2)}, u32[]{:S(2)}) %collective-permute-start.8) | collective-permute-done | bytes 397344 | tf_op jit(solution)/shard_map/ppermute | solution.py:287
  17.4 1.3 %collective-permute-start.9 = (bf16[1552,128]{1,0:T(8,128)(2,1)S(1)}, bf16[1552,128]{1,0:T(8,128)(2,1)S(1)}, u32[]{:S(2)}, u32[]{:S(2)}) collective-permute-start(bf16[1552,128]{1,0:T(8,128)(2,1)S(1)} %gate.1.refs_1_), channel_id=1, source_target_pairs={{0,2},{1,5},{2,0},{3,7},{4,6},{5,1},{6,4},{7,3},{8,10},{9,13},{10,... | collective-permute-start | bytes 1191944 | tf_op jit(solution)/shard_map/ppermute | solution.py:288
  18.7 0.0 collective-permute-done.3.refs_1_
  18.7 0.3 collective-permute-done.4.refs_2_
  19.0 0.0 collective-permute-done.6.refs_4_.refs_2_
  19.0 0.1 collective-permute-start.7
  19.1 1.4 %collective-permute-done.7.theirs_ref = bf16[128,768]{1,0:T(8,128)(2,1)S(1)} collective-permute-done((bf16[128,768]{1,0:T(8,128)(2,1)S(1)}, bf16[128,768]{1,0:T(8,128)(2,1)S(1)}, u32[]{:S(2)}, u32[]{:S(2)}) %collective-permute-start.7) | collective-permute-done | bytes 196640 | tf_op jit(solution)/shard_map/ppermute | solution.py:236
  20.5 1.8 %score.1.refs_1_ = f32[256,896]{1,0:T(8,128)S(1)} custom-call(bf16[128,768]{1,0:T(8,128)(2,1)S(1)} %stack.1.mine_ref, bf16[128,768]{1,0:T(8,128)(2,1)S(1)} %collective-permute-done.7.theirs_ref, bf16[1552,128]{1,0:T(8,128)(2,1)S(1)} %get-tuple-element.28.refs_0_, bf16[1552,128]{1,0:T(8,128)(2,1)S(1)} %gate.1.refs_1_, ...), custom_call_target="tpu_custom_call" | custom-call | tf_op jit(solution)/shard_map/score/pallas_call | solution.py:301
  22.3 0.0 copy-start
  22.3 2.8 %collective-permute-done.9.refs_0_ = bf16[1552,128]{1,0:T(8,128)(2,1)S(1)} collective-permute-done((bf16[1552,128]{1,0:T(8,128)(2,1)S(1)}, bf16[1552,128]{1,0:T(8,128)(2,1)S(1)}, u32[]{:S(2)}, u32[]{:S(2)}) %collective-permute-start.9) | collective-permute-done | bytes 397344 | tf_op jit(solution)/shard_map/ppermute | solution.py:288
  25.2 0.6 %score_last.1 = (f32[128,896]{1,0:T(8,128)S(1)}, bf16[128,896]{1,0:T(8,128)(2,1)S(1)}) custom-call(bf16[128,768]{1,0:T(8,128)(2,1)S(1)} %stack.1.mine_ref, bf16[128,768]{1,0:T(8,128)(2,1)S(1)} %collective-permute-done.7.theirs_ref, bf16[1552,128]{1,0:T(8,128)(2,1)S(1)} %collective-permute-done.9.refs_0_, f32[256,896]{1,0:T(8,128)S(1)} %score.1.refs_1_), custom_call_target="tpu_custom_call" | custom-call | tf_op jit(solution)/shard_map/score_last/pallas_call | solution.py:307
  25.8 0.1 collective-permute-start.10
  25.9 1.5 %collective-permute-done.10.theirs_ref = bf16[128,896]{1,0:T(8,128)(2,1)S(1)} collective-permute-done((bf16[128,896]{1,0:T(8,128)(2,1)S(1)}, bf16[128,896]{1,0:T(8,128)(2,1)S(1)}, u32[]{:S(2)}, u32[]{:S(2)}) %collective-permute-start.10) | collective-permute-done | bytes 229408 | tf_op jit(solution)/shard_map/ppermute | solution.py:236
  27.4 0.1 fold.1
  27.5 4.6 %collective-permute-start.11 = (bf16[208,128]{1,0:T(8,128)(2,1)S(1)}, bf16[208,128]{1,0:T(8,128)(2,1)S(1)}, u32[]{:S(2)}, u32[]{:S(2)}) collective-permute-start(bf16[208,128]{1,0:T(8,128)(2,1)S(1)} %get-tuple-element.32), channel_id=1, source_target_pairs={{0,24},{4,28},{8,16},{12,20},{16,8},{20,12},{24,0},{28,4},{1,25},{... | collective-permute-start | bytes 159752 | tf_op jit(solution)/shard_map/ppermute | solution.py:236
  32.0 0.0 collective-permute-start.12
  32.0 0.6 %collective-permute-start.13 = (bf16[208,128]{1,0:T(8,128)(2,1)S(1)}, bf16[208,128]{1,0:T(8,128)(2,1)S(1)}, u32[]{:S(2)}, u32[]{:S(2)}) collective-permute-start(bf16[208,128]{1,0:T(8,128)(2,1)S(1)} %get-tuple-element.34), channel_id=1, source_target_pairs={{0,8},{4,12},{8,0},{12,4},{16,24},{20,28},{24,16},{28,20},{1,9},{5... | collective-permute-start | bytes 159752 | tf_op jit(solution)/shard_map/ppermute | solution.py:236
  32.7 1.6 %collective-permute-done.11.refs_0_ = bf16[208,128]{1,0:T(8,128)(2,1)S(1)} collective-permute-done((bf16[208,128]{1,0:T(8,128)(2,1)S(1)}, bf16[208,128]{1,0:T(8,128)(2,1)S(1)}, u32[]{:S(2)}, u32[]{:S(2)}) %collective-permute-start.11) | collective-permute-done | bytes 53280 | tf_op jit(solution)/shard_map/ppermute | solution.py:236
  34.3 2.8 %collective-permute-done.12.refs_1_ = bf16[208,128]{1,0:T(8,128)(2,1)S(1)} collective-permute-done((bf16[208,128]{1,0:T(8,128)(2,1)S(1)}, bf16[208,128]{1,0:T(8,128)(2,1)S(1)}, u32[]{:S(2)}, u32[]{:S(2)}) %collective-permute-start.12) | collective-permute-done | bytes 53280 | tf_op jit(solution)/shard_map/ppermute | solution.py:236
  37.1 0.0 collective-permute-done.13.refs_2_
  37.1 0.1 scale.1
  37.2 0.1 collective-permute-start.14
  37.3 0.7 %collective-permute-start.15 = (bf16[32,768]{1,0:T(8,128)(2,1)S(1)}, bf16[32,768]{1,0:T(8,128)(2,1)S(1)}, u32[]{:S(2)}, u32[]{:S(2)}) collective-permute-start(bf16[32,768]{1,0:T(8,128)(2,1)S(1)} %get-tuple-element.36), channel_id=1, source_target_pairs={{0,2},{1,3},{2,0},{3,1},{4,6},{5,7},{6,4},{7,5},{8,10},{9,11},{10,... | collective-permute-start | bytes 147464 | tf_op jit(solution)/shard_map/ppermute | solution.py:236
  37.9 1.2 %collective-permute-start.16 = (bf16[32,768]{1,0:T(8,128)(2,1)S(1)}, bf16[32,768]{1,0:T(8,128)(2,1)S(1)}, u32[]{:S(2)}, u32[]{:S(2)}) collective-permute-start(bf16[32,768]{1,0:T(8,128)(2,1)S(1)} %get-tuple-element.36), channel_id=1, source_target_pairs={{0,3},{1,2},{2,1},{3,0},{4,7},{5,6},{6,5},{7,4},{8,11},{9,10},{10,... | collective-permute-start | bytes 147464 | tf_op jit(solution)/shard_map/ppermute | solution.py:236
  39.1 2.8 %collective-permute-done.15.refs_2_ = bf16[32,768]{1,0:T(8,128)(2,1)S(1)} collective-permute-done((bf16[32,768]{1,0:T(8,128)(2,1)S(1)}, bf16[32,768]{1,0:T(8,128)(2,1)S(1)}, u32[]{:S(2)}, u32[]{:S(2)}) %collective-permute-start.15) | collective-permute-done | bytes 49184 | tf_op jit(solution)/shard_map/ppermute | solution.py:236
  41.9 0.0 collective-permute-done.16.refs_3_
  42.0 0.0 collective-permute-done.14.refs_1_
  42.0 0.0 copy-done
  42.0 1.5 %sketch.1 = (f32[32,1024]{1,0:T(8,128)}, f32[32,768]{1,0:T(8,128)S(1)}, f32[32,768]{1,0:T(8,128)S(1)}, bf16[32,768]{1,0:T(8,128)(2,1)S(1)}, bf16[32,768]{1,0:T(8,128)(2,1)S(1)}) custom-call(s32[1,1024]{1,0:T(1,128)S(1)} %get-tuple-element.22.mark_ref, f32[8,128]{1,0:T(8,128)S(1)} %get-tuple-element.23.resident_ref, bf16[1024,768]{1,0:T(8,128)(2,1)S(1)} %copy-done, ...), custom_call_target="tpu_custom_call" | custom-call | tf_op jit(solution)/shard_map/sketch/pallas_call | solution.py:330
  43.5 0.4 collective-permute-start.19
  43.9 0.9 %collective-permute-start.17 = (bf16[32,768]{1,0:T(8,128)(2,1)S(1)}, bf16[32,768]{1,0:T(8,128)(2,1)S(1)}, u32[]{:S(2)}, u32[]{:S(2)}) collective-permute-start(bf16[32,768]{1,0:T(8,128)(2,1)S(1)} %get-tuple-element.39), channel_id=1, source_target_pairs={{0,3},{1,2},{2,1},{3,0},{4,7},{5,6},{6,5},{7,4},{8,11},{9,10},{10,... | collective-permute-start | bytes 147464 | tf_op jit(solution)/shard_map/ppermute | solution.py:236
  44.8 0.9 %collective-permute-start.18 = (bf16[32,768]{1,0:T(8,128)(2,1)S(1)}, bf16[32,768]{1,0:T(8,128)(2,1)S(1)}, u32[]{:S(2)}, u32[]{:S(2)}) collective-permute-start(bf16[32,768]{1,0:T(8,128)(2,1)S(1)} %get-tuple-element.40), channel_id=1, source_target_pairs={{0,2},{1,3},{2,0},{3,1},{4,6},{5,7},{6,4},{7,5},{8,10},{9,11},{10,... | collective-permute-start | bytes 147464 | tf_op jit(solution)/shard_map/ppermute | solution.py:236
  45.7 2.0 %collective-permute-done.17 = bf16[32,768]{1,0:T(8,128)(2,1)S(1)} collective-permute-done((bf16[32,768]{1,0:T(8,128)(2,1)S(1)}, bf16[32,768]{1,0:T(8,128)(2,1)S(1)}, u32[]{:S(2)}, u32[]{:S(2)}) %collective-permute-start.17) | collective-permute-done | bytes 49184 | tf_op jit(solution)/shard_map/ppermute | solution.py:236
  47.7 1.3 %collective-permute-done.18 = bf16[32,768]{1,0:T(8,128)(2,1)S(1)} collective-permute-done((bf16[32,768]{1,0:T(8,128)(2,1)S(1)}, bf16[32,768]{1,0:T(8,128)(2,1)S(1)}, u32[]{:S(2)}, u32[]{:S(2)}) %collective-permute-start.18) | collective-permute-done | bytes 49184 | tf_op jit(solution)/shard_map/ppermute | solution.py:236
  49.0 0.0 collective-permute-done.19
  49.0 0.7 %add_bitcast_fusion = f32[1,32,768]{2,1,0:T(8,128)} fusion(f32[32,768]{1,0:T(8,128)S(1)} %collective-permute-done.19, bf16[32,768]{1,0:T(8,128)(2,1)S(1)} %collective-permute-done.18, f32[32,768]{1,0:T(8,128)S(1)} %get-tuple-element.38, bf16[32,768]{1,0:T(8,128)(2,1)S(1)} %collective-permute-done.17), kind=kLoop, calls=%fused_computation | loop fusion | flops 122880 | bytes 393216 | tf_op jit(solution)/shard_map/broadcast_in_dim | solution.py:340
  (3 shorter events, 0.0 us)
Async XLA Ops:
  2.6 7.7 %collective-permute-start.2 = (f32[32,768]{1,0:T(8,128)S(1)}, f32[32,768]{1,0:T(8,128)S(1)}, u32[]{:S(2)}, u32[]{:S(2)}) collective-permute-start(f32[32,768]{1,0:T(8,128)S(1)} %get-tuple-element.27), channel_id=1, source_target_pairs={{0,1},{1,0},{2,3},{3,2},{4,5},{5,4},{6,7},{7,6},{8,9},{9,8},{10,11... | collective-permute-start | bytes 294920 | tf_op jit(solution)/shard_map/ppermute | solution.py:236
  3.1 6.2 %collective-permute-start = (bf16[32,768]{1,0:T(8,128)(2,1)S(1)}, bf16[32,768]{1,0:T(8,128)(2,1)S(1)}, u32[]{:S(2)}, u32[]{:S(2)}) collective-permute-start(bf16[32,768]{1,0:T(8,128)(2,1)S(1)} %get-tuple-element.25), channel_id=1, source_target_pairs={{0,3},{1,2},{2,1},{3,0},{4,7},{5,6},{6,5},{7,4},{8,11},{9,10},{10,... | collective-permute-start | bytes 147464 | tf_op jit(solution)/shard_map/ppermute | solution.py:236
  5.7 4.6 %collective-permute-start.1 = (bf16[32,768]{1,0:T(8,128)(2,1)S(1)}, bf16[32,768]{1,0:T(8,128)(2,1)S(1)}, u32[]{:S(2)}, u32[]{:S(2)}) collective-permute-start(bf16[32,768]{1,0:T(8,128)(2,1)S(1)} %get-tuple-element.26), channel_id=1, source_target_pairs={{0,2},{1,3},{2,0},{3,1},{4,6},{5,7},{6,4},{7,5},{8,10},{9,11},{10,... | collective-permute-start | bytes 147464 | tf_op jit(solution)/shard_map/ppermute | solution.py:236
  5.7 11.6 %collective-permute-start.8 = (bf16[1552,128]{1,0:T(8,128)(2,1)S(1)}, bf16[1552,128]{1,0:T(8,128)(2,1)S(1)}, u32[]{:S(2)}, u32[]{:S(2)}) collective-permute-start(bf16[1552,128]{1,0:T(8,128)(2,1)S(1)} %get-tuple-element.28.refs_0_), channel_id=1, source_target_pairs={{0,4},{1,3},{2,6},{3,1},{4,0},{5,7},{6,2},{7,5},{8,12},{9,11},{10,... | collective-permute-start | bytes 1191944 | tf_op jit(solution)/shard_map/ppermute | solution.py:287
  7.7 11.2 %collective-permute-start.6 = (bf16[1552,128]{1,0:T(8,128)(2,1)S(1)}, bf16[1552,128]{1,0:T(8,128)(2,1)S(1)}, u32[]{:S(2)}, u32[]{:S(2)}) collective-permute-start(bf16[1552,128]{1,0:T(8,128)(2,1)S(1)} %get-tuple-element.28.refs_0_), channel_id=1, source_target_pairs={{0,2},{1,5},{2,0},{3,7},{4,6},{5,1},{6,4},{7,3},{8,10},{9,13},{10,... | collective-permute-start | bytes 1191944 | tf_op jit(solution)/shard_map/ppermute | solution.py:286
  10.3 6.1 %collective-permute-start.5 = (bf16[32,768]{1,0:T(8,128)(2,1)S(1)}, bf16[32,768]{1,0:T(8,128)(2,1)S(1)}, u32[]{:S(2)}, u32[]{:S(2)}) collective-permute-start(bf16[32,768]{1,0:T(8,128)(2,1)S(1)} %join.1.refs_0_), channel_id=1, source_target_pairs={{0,24},{4,28},{8,16},{12,20},{16,8},{20,12},{24,0},{28,4},{1,25},{... | collective-permute-start | bytes 147464 | tf_op jit(solution)/shard_map/ppermute | solution.py:236
  14.0 4.7 %collective-permute-start.3 = (bf16[32,768]{1,0:T(8,128)(2,1)S(1)}, bf16[32,768]{1,0:T(8,128)(2,1)S(1)}, u32[]{:S(2)}, u32[]{:S(2)}) collective-permute-start(bf16[32,768]{1,0:T(8,128)(2,1)S(1)} %join.1.refs_0_), channel_id=1, source_target_pairs={{0,8},{4,12},{8,0},{12,4},{16,24},{20,28},{24,16},{28,20},{1,9},{5... | collective-permute-start | bytes 147464 | tf_op jit(solution)/shard_map/ppermute | solution.py:236
  14.0 5.0 %collective-permute-start.4 = (bf16[32,768]{1,0:T(8,128)(2,1)S(1)}, bf16[32,768]{1,0:T(8,128)(2,1)S(1)}, u32[]{:S(2)}, u32[]{:S(2)}) collective-permute-start(bf16[32,768]{1,0:T(8,128)(2,1)S(1)} %join.1.refs_0_), channel_id=1, source_target_pairs={{0,16},{4,20},{8,24},{12,28},{16,0},{20,4},{24,8},{28,12},{1,17},{... | collective-permute-start | bytes 147464 | tf_op jit(solution)/shard_map/ppermute | solution.py:236
  17.4 7.8 %collective-permute-start.9 = (bf16[1552,128]{1,0:T(8,128)(2,1)S(1)}, bf16[1552,128]{1,0:T(8,128)(2,1)S(1)}, u32[]{:S(2)}, u32[]{:S(2)}) collective-permute-start(bf16[1552,128]{1,0:T(8,128)(2,1)S(1)} %gate.1.refs_1_), channel_id=1, source_target_pairs={{0,2},{1,5},{2,0},{3,7},{4,6},{5,1},{6,4},{7,3},{8,10},{9,13},{10,... | collective-permute-start | bytes 1191944 | tf_op jit(solution)/shard_map/ppermute | solution.py:288
  19.0 1.5 %collective-permute-start.7 = (bf16[128,768]{1,0:T(8,128)(2,1)S(1)}, bf16[128,768]{1,0:T(8,128)(2,1)S(1)}, u32[]{:S(2)}, u32[]{:S(2)}) collective-permute-start(bf16[128,768]{1,0:T(8,128)(2,1)S(1)} %stack.1.mine_ref), channel_id=1, source_target_pairs={{0,1},{1,0},{2,3},{3,2},{4,5},{5,4},{6,7},{7,6},{8,9},{9,8},{10,11... | collective-permute-start | bytes 589832 | tf_op jit(solution)/shard_map/ppermute | solution.py:236
  22.3 19.6 %copy-start = (bf16[1024,768]{1,0:T(8,128)(2,1)S(1)}, bf16[1024,768]{1,0:T(8,128)(2,1)}, u32[]{:S(2)}) copy-start(bf16[1024,768]{1,0:T(8,128)(2,1)} %points_ref.1) | copy-start | bytes 4718596
  25.8 1.6 %collective-permute-start.10 = (bf16[128,896]{1,0:T(8,128)(2,1)S(1)}, bf16[128,896]{1,0:T(8,128)(2,1)S(1)}, u32[]{:S(2)}, u32[]{:S(2)}) collective-permute-start(bf16[128,896]{1,0:T(8,128)(2,1)S(1)} %get-tuple-element.30), channel_id=1, source_target_pairs={{0,1},{1,0},{2,3},{3,2},{4,5},{5,4},{6,7},{7,6},{8,9},{9,8},{10,11... | collective-permute-start | bytes 688136 | tf_op jit(solution)/shard_map/ppermute | solution.py:236
  27.5 6.8 %collective-permute-start.11 = (bf16[208,128]{1,0:T(8,128)(2,1)S(1)}, bf16[208,128]{1,0:T(8,128)(2,1)S(1)}, u32[]{:S(2)}, u32[]{:S(2)}) collective-permute-start(bf16[208,128]{1,0:T(8,128)(2,1)S(1)} %get-tuple-element.32), channel_id=1, source_target_pairs={{0,24},{4,28},{8,16},{12,20},{16,8},{20,12},{24,0},{28,4},{1,25},{... | collective-permute-start | bytes 159752 | tf_op jit(solution)/shard_map/ppermute | solution.py:236
  32.0 5.1 %collective-permute-start.12 = (bf16[208,128]{1,0:T(8,128)(2,1)S(1)}, bf16[208,128]{1,0:T(8,128)(2,1)S(1)}, u32[]{:S(2)}, u32[]{:S(2)}) collective-permute-start(bf16[208,128]{1,0:T(8,128)(2,1)S(1)} %get-tuple-element.33), channel_id=1, source_target_pairs={{0,16},{4,20},{8,24},{12,28},{16,0},{20,4},{24,8},{28,12},{1,17},{... | collective-permute-start | bytes 159752 | tf_op jit(solution)/shard_map/ppermute | solution.py:236
  32.0 5.1 %collective-permute-start.13 = (bf16[208,128]{1,0:T(8,128)(2,1)S(1)}, bf16[208,128]{1,0:T(8,128)(2,1)S(1)}, u32[]{:S(2)}, u32[]{:S(2)}) collective-permute-start(bf16[208,128]{1,0:T(8,128)(2,1)S(1)} %get-tuple-element.34), channel_id=1, source_target_pairs={{0,8},{4,12},{8,0},{12,4},{16,24},{20,28},{24,16},{28,20},{1,9},{5... | collective-permute-start | bytes 159752 | tf_op jit(solution)/shard_map/ppermute | solution.py:236
  37.2 4.8 %collective-permute-start.14 = (f32[32,768]{1,0:T(8,128)S(1)}, f32[32,768]{1,0:T(8,128)S(1)}, u32[]{:S(2)}, u32[]{:S(2)}) collective-permute-start(f32[32,768]{1,0:T(8,128)S(1)} %get-tuple-element.35.refs_0_), channel_id=1, source_target_pairs={{0,1},{1,0},{2,3},{3,2},{4,5},{5,4},{6,7},{7,6},{8,9},{9,8},{10,11... | collective-permute-start | bytes 294920 | tf_op jit(solution)/shard_map/ppermute | solution.py:236
  37.3 4.7 %collective-permute-start.15 = (bf16[32,768]{1,0:T(8,128)(2,1)S(1)}, bf16[32,768]{1,0:T(8,128)(2,1)S(1)}, u32[]{:S(2)}, u32[]{:S(2)}) collective-permute-start(bf16[32,768]{1,0:T(8,128)(2,1)S(1)} %get-tuple-element.36), channel_id=1, source_target_pairs={{0,2},{1,3},{2,0},{3,1},{4,6},{5,7},{6,4},{7,5},{8,10},{9,11},{10,... | collective-permute-start | bytes 147464 | tf_op jit(solution)/shard_map/ppermute | solution.py:236
  37.9 4.0 %collective-permute-start.16 = (bf16[32,768]{1,0:T(8,128)(2,1)S(1)}, bf16[32,768]{1,0:T(8,128)(2,1)S(1)}, u32[]{:S(2)}, u32[]{:S(2)}) collective-permute-start(bf16[32,768]{1,0:T(8,128)(2,1)S(1)} %get-tuple-element.36), channel_id=1, source_target_pairs={{0,3},{1,2},{2,1},{3,0},{4,7},{5,6},{6,5},{7,4},{8,11},{9,10},{10,... | collective-permute-start | bytes 147464 | tf_op jit(solution)/shard_map/ppermute | solution.py:236
  43.5 5.5 %collective-permute-start.19 = (f32[32,768]{1,0:T(8,128)S(1)}, f32[32,768]{1,0:T(8,128)S(1)}, u32[]{:S(2)}, u32[]{:S(2)}) collective-permute-start(f32[32,768]{1,0:T(8,128)S(1)} %get-tuple-element.41), channel_id=1, source_target_pairs={{0,1},{1,0},{2,3},{3,2},{4,5},{5,4},{6,7},{7,6},{8,9},{9,8},{10,11... | collective-permute-start | bytes 294920 | tf_op jit(solution)/shard_map/ppermute | solution.py:236
  43.9 3.8 %collective-permute-start.17 = (bf16[32,768]{1,0:T(8,128)(2,1)S(1)}, bf16[32,768]{1,0:T(8,128)(2,1)S(1)}, u32[]{:S(2)}, u32[]{:S(2)}) collective-permute-start(bf16[32,768]{1,0:T(8,128)(2,1)S(1)} %get-tuple-element.39), channel_id=1, source_target_pairs={{0,3},{1,2},{2,1},{3,0},{4,7},{5,6},{6,5},{7,4},{8,11},{9,10},{10,... | collective-permute-start | bytes 147464 | tf_op jit(solution)/shard_map/ppermute | solution.py:236
  44.8 4.2 %collective-permute-start.18 = (bf16[32,768]{1,0:T(8,128)(2,1)S(1)}, bf16[32,768]{1,0:T(8,128)(2,1)S(1)}, u32[]{:S(2)}, u32[]{:S(2)}) collective-permute-start(bf16[32,768]{1,0:T(8,128)(2,1)S(1)} %get-tuple-element.40), channel_id=1, source_target_pairs={{0,2},{1,3},{2,0},{3,1},{4,6},{5,7},{6,4},{7,5},{8,10},{9,11},{10,... | collective-permute-start | bytes 147464 | tf_op jit(solution)/shard_map/ppermute | solution.py:236

commit v16 on v12

--- a/solution.py
+++ b/solution.py
@@ -276,13 +276,13 @@
         join_kernel,
         out_shape=sent,
         compiler_params=PARAMS,
-        cost_estimate=pl.CostEstimate(flops=40*10**8, bytes_accessed=10**5, transcendentals=0),
+        cost_estimate=pl.CostEstimate(flops=4 * 10**9, bytes_accessed=10**5, transcendentals=0),
         name="join",
     )(own, *swaps(parts, "help"))
     lifters = [lifter] + [swap(lifter, "shard", INNER * d) for d in range(1, planes)]
     index, axes = range(groups * helpers), ("shard", "help")
-    one = [(i, i ^ (2 if i % 2 == 0 else helpers)) for i in index]
-    two = [(i, i ^ (helpers if i % 2 == 0 else 2)) for i in index]
+    one = [(i, i ^ (helpers if i % 2 == 0 else 2)) for i in index]
+    two = [(i, i ^ (2 if i % 2 == 0 else helpers)) for i in index]
     far = lax.ppermute(packed, axes, one)
     (near,) = gate([lax.ppermute(packed, axes, two)], lifters[-1])
     across = lax.ppermute(near, axes, one)

time: 49.3 us -> 48.9 us (level)
  waiting for transfers between devices: 21.2 us -> 19.8 us
  starting transfers between devices: 20.4 us -> 21.4 us
    ppermute x17, waiting for transfers between devices: 18.5 us -> 17.6 us  [swap(): lax.ppermute(value, axis, [(i, i ^ d) for i in range(lax.axis_size(axis))])]
    ppermute x1, starting transfers between devices: 0.98 us -> 1.5 us  [shards(): across = lax.ppermute(near, axes, one)]
    ppermute x1, starting transfers between devices: 1.01 us -> 1.52 us  [shards(): far = lax.ppermute(packed, axes, one)]
    ppermute x1, waiting for transfers between devices: 1.82 us -> 1.31 us  [shards(): far = lax.ppermute(packed, axes, one)]
  transfers between devices with their start and end apart: 20 -> 20, of which waited for: 14 -> 13; matrix products, arithmetic and copies ran while one was open for 0% -> 0% of each run, Pallas kernels for 4% -> 4%
where the time goes in v16:
time: 48.9 us; the launch traced here: 48.7 us
  starting transfers between devices  21.4 us (44%)
  waiting for transfers between devices  19.8 us (40%)
  Pallas kernels  6.09 us (12%)
  between operations  0.72 us (1%)
  other arithmetic  0.67 us (1%)
    ppermute x17, waiting for transfers between devices, swap(): lax.ppermute(value, axis, [(i, i ^ d) for i in range(lax.axis_size(axis))])  17.6 us
    ppermute x17, starting transfers between devices, swap(): lax.ppermute(value, axis, [(i, i ^ d) for i in range(lax.axis_size(axis))])  16.4 us
    ppermute x1, starting transfers between devices, shards(): near, = gate([lax.ppermute(packed, axes, two)], lifters[-1])  1.98 us
    pallas_call x1, Pallas kernels, shards(): pl.pallas_call(functools.partial(lift_kernel, helpers), out_shape=[jax.Sh...  1.92 us
    pallas_call x1, Pallas kernels, shards(): pl.pallas_call(functools.partial(score_kernel, planes, helpers, 3), out_s...  1.81 us
    pallas_call x1, Pallas kernels, shards(): pl.pallas_call(functools.partial(sketch_kernel, helpers), out_shape=[jax....  1.54 us
    ppermute x1, starting transfers between devices, shards(): far = lax.ppermute(packed, axes, one)  1.52 us
    ppermute x1, starting transfers between devices, shards(): across = lax.ppermute(near, axes, one)  1.5 us
  transfers between devices with their start and end apart: 20, of which 13 were waited for; matrix products, arithmetic and copies ran while one was open for 0% of the time, Pallas kernels for 4%

profile of v16, /device:TPU:0, one launch (start us, length us, event | category | flops | bytes accessed | tf_op | source)
XLA Modules:
  0.0 48.7 jit_solution(5395833535764737396)
XLA Ops:
  0.6 1.9 %lift.1 = (bf16[1552,128]{1,0:T(8,128)(2,1)S(1)}, s32[1,1024]{1,0:T(1,128)S(1)}, f32[8,128]{1,0:T(8,128)S(1)}, f32[32,768]{1,0:T(8,128)S(1)}, f32[32,768]{1,0:T(...) custom-call(bf16[256,768]{1,0:T(8,128)(2,1)} %refs_0_.1, s32[2,256]{1,0:T(2,128)} %bitcast.4, ...), custom_call_target="tpu_custom_call" | custom-call | tf_op jit(solution)/shard_map/lift/pallas_call | solution.py:253
  2.6 0.5 %collective-permute-start.2 = (f32[32,768]{1,0:T(8,128)S(1)}, f32[32,768]{1,0:T(8,128)S(1)}, u32[]{:S(2)}, u32[]{:S(2)}) collective-permute-start(f32[32,768]{1,0:T(8,128)S(1)} %get-tuple-element.27), channel_id=1, source_target_pairs={{0,1},{1,0},{2,3},{3,2},{4,5},{5,4},{6,7},{7,6},{8,9},{9,8},{10,11... | collective-permute-start | bytes 294920 | tf_op jit(solution)/shard_map/ppermute | solution.py:236
  3.1 2.6 %collective-permute-start = (bf16[32,768]{1,0:T(8,128)(2,1)S(1)}, bf16[32,768]{1,0:T(8,128)(2,1)S(1)}, u32[]{:S(2)}, u32[]{:S(2)}) collective-permute-start(bf16[32,768]{1,0:T(8,128)(2,1)S(1)} %get-tuple-element.25), channel_id=1, source_target_pairs={{0,3},{1,2},{2,1},{3,0},{4,7},{5,6},{6,5},{7,4},{8,11},{9,10},{10,... | collective-permute-start | bytes 147464 | tf_op jit(solution)/shard_map/ppermute | solution.py:236
  5.7 0.0 collective-permute-start.1
  5.7 2.0 %collective-permute-start.8 = (bf16[1552,128]{1,0:T(8,128)(2,1)S(1)}, bf16[1552,128]{1,0:T(8,128)(2,1)S(1)}, u32[]{:S(2)}, u32[]{:S(2)}) collective-permute-start(bf16[1552,128]{1,0:T(8,128)(2,1)S(1)} %get-tuple-element.28.refs_0_), channel_id=1, source_target_pairs={{0,2},{1,5},{2,0},{3,7},{4,6},{5,1},{6,4},{7,3},{8,10},{9,13},{10,... | collective-permute-start | bytes 1191944 | tf_op jit(solution)/shard_map/ppermute | solution.py:287
  7.7 0.0 collective-permute-done.refs_1_
  7.8 2.0 %collective-permute-done.1.refs_2_ = bf16[32,768]{1,0:T(8,128)(2,1)S(1)} collective-permute-done((bf16[32,768]{1,0:T(8,128)(2,1)S(1)}, bf16[32,768]{1,0:T(8,128)(2,1)S(1)}, u32[]{:S(2)}, u32[]{:S(2)}) %collective-permute-start.1) | collective-permute-done | bytes 49184 | tf_op jit(solution)/shard_map/ppermute | solution.py:236
  9.8 0.0 collective-permute-done.2.refs_3_
  9.8 3.7 %collective-permute-start.5 = (bf16[32,768]{1,0:T(8,128)(2,1)S(1)}, bf16[32,768]{1,0:T(8,128)(2,1)S(1)}, u32[]{:S(2)}, u32[]{:S(2)}) collective-permute-start(bf16[32,768]{1,0:T(8,128)(2,1)S(1)} %join.1.refs_0_), channel_id=1, source_target_pairs={{0,24},{4,28},{8,16},{12,20},{16,8},{20,12},{24,0},{28,4},{1,25},{... | collective-permute-start | bytes 147464 | tf_op jit(solution)/shard_map/ppermute | solution.py:236
  13.5 1.5 %collective-permute-start.6 = (bf16[1552,128]{1,0:T(8,128)(2,1)S(1)}, bf16[1552,128]{1,0:T(8,128)(2,1)S(1)}, u32[]{:S(2)}, u32[]{:S(2)}) collective-permute-start(bf16[1552,128]{1,0:T(8,128)(2,1)S(1)} %get-tuple-element.28.refs_0_), channel_id=1, source_target_pairs={{0,4},{1,3},{2,6},{3,1},{4,0},{5,7},{6,2},{7,5},{8,12},{9,11},{10,... | collective-permute-start | bytes 1191944 | tf_op jit(solution)/shard_map/ppermute | solution.py:286
  15.0 0.0 collective-permute-start.3
  15.0 0.8 %collective-permute-start.4 = (bf16[32,768]{1,0:T(8,128)(2,1)S(1)}, bf16[32,768]{1,0:T(8,128)(2,1)S(1)}, u32[]{:S(2)}, u32[]{:S(2)}) collective-permute-start(bf16[32,768]{1,0:T(8,128)(2,1)S(1)} %join.1.refs_0_), channel_id=1, source_target_pairs={{0,16},{4,20},{8,24},{12,28},{16,0},{20,4},{24,8},{28,12},{1,17},{... | collective-permute-start | bytes 147464 | tf_op jit(solution)/shard_map/ppermute | solution.py:236
  15.8 0.0 collective-permute-done.5.refs_3_.refs_1_
  15.8 0.0 collective-permute-done.8.refs_0_
  15.8 1.5 %collective-permute-start.9 = (bf16[1552,128]{1,0:T(8,128)(2,1)S(1)}, bf16[1552,128]{1,0:T(8,128)(2,1)S(1)}, u32[]{:S(2)}, u32[]{:S(2)}) collective-permute-start(bf16[1552,128]{1,0:T(8,128)(2,1)S(1)} %gate.1.refs_1_), channel_id=1, source_target_pairs={{0,4},{1,3},{2,6},{3,1},{4,0},{5,7},{6,2},{7,5},{8,12},{9,11},{10,... | collective-permute-start | bytes 1191944 | tf_op jit(solution)/shard_map/ppermute | solution.py:288
  17.3 1.8 %collective-permute-done.3.refs_1_ = bf16[32,768]{1,0:T(8,128)(2,1)S(1)} collective-permute-done((bf16[32,768]{1,0:T(8,128)(2,1)S(1)}, bf16[32,768]{1,0:T(8,128)(2,1)S(1)}, u32[]{:S(2)}, u32[]{:S(2)}) %collective-permute-start.3) | collective-permute-done | bytes 49184 | tf_op jit(solution)/shard_map/ppermute | solution.py:236
  19.1 0.9 %collective-permute-done.4.refs_2_ = bf16[32,768]{1,0:T(8,128)(2,1)S(1)} collective-permute-done((bf16[32,768]{1,0:T(8,128)(2,1)S(1)}, bf16[32,768]{1,0:T(8,128)(2,1)S(1)}, u32[]{:S(2)}, u32[]{:S(2)}) %collective-permute-start.4) | collective-permute-done | bytes 49184 | tf_op jit(solution)/shard_map/ppermute | solution.py:236
  20.0 1.3 %collective-permute-done.6.refs_4_.refs_2_ = bf16[1552,128]{1,0:T(8,128)(2,1)S(1)} collective-permute-done((bf16[1552,128]{1,0:T(8,128)(2,1)S(1)}, bf16[1552,128]{1,0:T(8,128)(2,1)S(1)}, u32[]{:S(2)}, u32[]{:S(2)}) %collective-permute-start.6) | collective-permute-done | bytes 397344 | tf_op jit(solution)/shard_map/ppermute | solution.py:286
  21.3 0.1 collective-permute-start.7
  21.4 1.4 %collective-permute-done.7.theirs_ref = bf16[128,768]{1,0:T(8,128)(2,1)S(1)} collective-permute-done((bf16[128,768]{1,0:T(8,128)(2,1)S(1)}, bf16[128,768]{1,0:T(8,128)(2,1)S(1)}, u32[]{:S(2)}, u32[]{:S(2)}) %collective-permute-start.7) | collective-permute-done | bytes 196640 | tf_op jit(solution)/shard_map/ppermute | solution.py:236
  22.8 1.8 %score.1.refs_1_ = f32[256,896]{1,0:T(8,128)S(1)} custom-call(bf16[128,768]{1,0:T(8,128)(2,1)S(1)} %stack.1.mine_ref, bf16[128,768]{1,0:T(8,128)(2,1)S(1)} %collective-permute-done.7.theirs_ref, bf16[1552,128]{1,0:T(8,128)(2,1)S(1)} %get-tuple-element.28.refs_0_, bf16[1552,128]{1,0:T(8,128)(2,1)S(1)} %gate.1.refs_1_, ...), custom_call_target="tpu_custom_call" | custom-call | tf_op jit(solution)/shard_map/score/pallas_call | solution.py:301
  24.6 0.0 copy-start
  24.7 0.9 %collective-permute-done.9.refs_0_ = bf16[1552,128]{1,0:T(8,128)(2,1)S(1)} collective-permute-done((bf16[1552,128]{1,0:T(8,128)(2,1)S(1)}, bf16[1552,128]{1,0:T(8,128)(2,1)S(1)}, u32[]{:S(2)}, u32[]{:S(2)}) %collective-permute-start.9) | collective-permute-done | bytes 397344 | tf_op jit(solution)/shard_map/ppermute | solution.py:288
  25.6 0.6 %score_last.1 = (f32[128,896]{1,0:T(8,128)S(1)}, bf16[128,896]{1,0:T(8,128)(2,1)S(1)}) custom-call(bf16[128,768]{1,0:T(8,128)(2,1)S(1)} %stack.1.mine_ref, bf16[128,768]{1,0:T(8,128)(2,1)S(1)} %collective-permute-done.7.theirs_ref, bf16[1552,128]{1,0:T(8,128)(2,1)S(1)} %collective-permute-done.9.refs_0_, f32[256,896]{1,0:T(8,128)S(1)} %score.1.refs_1_), custom_call_target="tpu_custom_call" | custom-call | tf_op jit(solution)/shard_map/score_last/pallas_call | solution.py:307
  26.2 0.1 collective-permute-start.10
  26.3 1.5 %collective-permute-done.10.theirs_ref = bf16[128,896]{1,0:T(8,128)(2,1)S(1)} collective-permute-done((bf16[128,896]{1,0:T(8,128)(2,1)S(1)}, bf16[128,896]{1,0:T(8,128)(2,1)S(1)}, u32[]{:S(2)}, u32[]{:S(2)}) %collective-permute-start.10) | collective-permute-done | bytes 229408 | tf_op jit(solution)/shard_map/ppermute | solution.py:236
  27.8 0.1 fold.1
  27.8 2.5 %collective-permute-start.11 = (bf16[208,128]{1,0:T(8,128)(2,1)S(1)}, bf16[208,128]{1,0:T(8,128)(2,1)S(1)}, u32[]{:S(2)}, u32[]{:S(2)}) collective-permute-start(bf16[208,128]{1,0:T(8,128)(2,1)S(1)} %get-tuple-element.32), channel_id=1, source_target_pairs={{0,24},{4,28},{8,16},{12,20},{16,8},{20,12},{24,0},{28,4},{1,25},{... | collective-permute-start | bytes 159752 | tf_op jit(solution)/shard_map/ppermute | solution.py:236
  30.3 0.0 collective-permute-start.12
  30.3 2.0 %collective-permute-start.13 = (bf16[208,128]{1,0:T(8,128)(2,1)S(1)}, bf16[208,128]{1,0:T(8,128)(2,1)S(1)}, u32[]{:S(2)}, u32[]{:S(2)}) collective-permute-start(bf16[208,128]{1,0:T(8,128)(2,1)S(1)} %get-tuple-element.34), channel_id=1, source_target_pairs={{0,8},{4,12},{8,0},{12,4},{16,24},{20,28},{24,16},{28,20},{1,9},{5... | collective-permute-start | bytes 159752 | tf_op jit(solution)/shard_map/ppermute | solution.py:236
  32.3 1.9 %collective-permute-done.11.refs_0_ = bf16[208,128]{1,0:T(8,128)(2,1)S(1)} collective-permute-done((bf16[208,128]{1,0:T(8,128)(2,1)S(1)}, bf16[208,128]{1,0:T(8,128)(2,1)S(1)}, u32[]{:S(2)}, u32[]{:S(2)}) %collective-permute-start.11) | collective-permute-done | bytes 53280 | tf_op jit(solution)/shard_map/ppermute | solution.py:236
  34.2 1.6 %collective-permute-done.12.refs_1_ = bf16[208,128]{1,0:T(8,128)(2,1)S(1)} collective-permute-done((bf16[208,128]{1,0:T(8,128)(2,1)S(1)}, bf16[208,128]{1,0:T(8,128)(2,1)S(1)}, u32[]{:S(2)}, u32[]{:S(2)}) %collective-permute-start.12) | collective-permute-done | bytes 53280 | tf_op jit(solution)/shard_map/ppermute | solution.py:236
  35.8 0.0 collective-permute-done.13.refs_2_
  35.8 0.1 scale.1
  35.9 0.1 collective-permute-start.14
  36.0 1.4 %collective-permute-start.15 = (bf16[32,768]{1,0:T(8,128)(2,1)S(1)}, bf16[32,768]{1,0:T(8,128)(2,1)S(1)}, u32[]{:S(2)}, u32[]{:S(2)}) collective-permute-start(bf16[32,768]{1,0:T(8,128)(2,1)S(1)} %get-tuple-element.36), channel_id=1, source_target_pairs={{0,2},{1,3},{2,0},{3,1},{4,6},{5,7},{6,4},{7,5},{8,10},{9,11},{10,... | collective-permute-start | bytes 147464 | tf_op jit(solution)/shard_map/ppermute | solution.py:236
  37.5 0.4 collective-permute-start.16
  37.9 2.3 %collective-permute-done.15.refs_2_ = bf16[32,768]{1,0:T(8,128)(2,1)S(1)} collective-permute-done((bf16[32,768]{1,0:T(8,128)(2,1)S(1)}, bf16[32,768]{1,0:T(8,128)(2,1)S(1)}, u32[]{:S(2)}, u32[]{:S(2)}) %collective-permute-start.15) | collective-permute-done | bytes 49184 | tf_op jit(solution)/shard_map/ppermute | solution.py:236
  40.2 1.0 %collective-permute-done.16.refs_3_ = bf16[32,768]{1,0:T(8,128)(2,1)S(1)} collective-permute-done((bf16[32,768]{1,0:T(8,128)(2,1)S(1)}, bf16[32,768]{1,0:T(8,128)(2,1)S(1)}, u32[]{:S(2)}, u32[]{:S(2)}) %collective-permute-start.16) | collective-permute-done | bytes 49184 | tf_op jit(solution)/shard_map/ppermute | solution.py:236
  41.1 0.0 collective-permute-done.14.refs_1_
  41.2 0.0 copy-done
  41.2 1.5 %sketch.1 = (f32[32,1024]{1,0:T(8,128)}, f32[32,768]{1,0:T(8,128)S(1)}, f32[32,768]{1,0:T(8,128)S(1)}, bf16[32,768]{1,0:T(8,128)(2,1)S(1)}, bf16[32,768]{1,0:T(8,128)(2,1)S(1)}) custom-call(s32[1,1024]{1,0:T(1,128)S(1)} %get-tuple-element.22.mark_ref, f32[8,128]{1,0:T(8,128)S(1)} %get-tuple-element.23.resident_ref, bf16[1024,768]{1,0:T(8,128)(2,1)S(1)} %copy-done, ...), custom_call_target="tpu_custom_call" | custom-call | tf_op jit(solution)/shard_map/sketch/pallas_call | solution.py:330
  42.7 0.2 collective-permute-start.19
  42.9 0.9 %collective-permute-start.17 = (bf16[32,768]{1,0:T(8,128)(2,1)S(1)}, bf16[32,768]{1,0:T(8,128)(2,1)S(1)}, u32[]{:S(2)}, u32[]{:S(2)}) collective-permute-start(bf16[32,768]{1,0:T(8,128)(2,1)S(1)} %get-tuple-element.39), channel_id=1, source_target_pairs={{0,3},{1,2},{2,1},{3,0},{4,7},{5,6},{6,5},{7,4},{8,11},{9,10},{10,... | collective-permute-start | bytes 147464 | tf_op jit(solution)/shard_map/ppermute | solution.py:236
  43.9 1.0 %collective-permute-start.18 = (bf16[32,768]{1,0:T(8,128)(2,1)S(1)}, bf16[32,768]{1,0:T(8,128)(2,1)S(1)}, u32[]{:S(2)}, u32[]{:S(2)}) collective-permute-start(bf16[32,768]{1,0:T(8,128)(2,1)S(1)} %get-tuple-element.40), channel_id=1, source_target_pairs={{0,2},{1,3},{2,0},{3,1},{4,6},{5,7},{6,4},{7,5},{8,10},{9,11},{10,... | collective-permute-start | bytes 147464 | tf_op jit(solution)/shard_map/ppermute | solution.py:236
  44.9 1.5 %collective-permute-done.17 = bf16[32,768]{1,0:T(8,128)(2,1)S(1)} collective-permute-done((bf16[32,768]{1,0:T(8,128)(2,1)S(1)}, bf16[32,768]{1,0:T(8,128)(2,1)S(1)}, u32[]{:S(2)}, u32[]{:S(2)}) %collective-permute-start.17) | collective-permute-done | bytes 49184 | tf_op jit(solution)/shard_map/ppermute | solution.py:236
  46.4 1.6 %collective-permute-done.18 = bf16[32,768]{1,0:T(8,128)(2,1)S(1)} collective-permute-done((bf16[32,768]{1,0:T(8,128)(2,1)S(1)}, bf16[32,768]{1,0:T(8,128)(2,1)S(1)}, u32[]{:S(2)}, u32[]{:S(2)}) %collective-permute-start.18) | collective-permute-done | bytes 49184 | tf_op jit(solution)/shard_map/ppermute | solution.py:236
  48.0 0.0 collective-permute-done.19
  48.0 0.7 %add_bitcast_fusion = f32[1,32,768]{2,1,0:T(8,128)} fusion(f32[32,768]{1,0:T(8,128)S(1)} %collective-permute-done.19, bf16[32,768]{1,0:T(8,128)(2,1)S(1)} %collective-permute-done.18, f32[32,768]{1,0:T(8,128)S(1)} %get-tuple-element.38, bf16[32,768]{1,0:T(8,128)(2,1)S(1)} %collective-permute-done.17), kind=kLoop, calls=%fused_computation | loop fusion | flops 122880 | bytes 393216 | tf_op jit(solution)/shard_map/broadcast_in_dim | solution.py:340
  (3 shorter events, 0.0 us)
Async XLA Ops:
  2.6 7.2 %collective-permute-start.2 = (f32[32,768]{1,0:T(8,128)S(1)}, f32[32,768]{1,0:T(8,128)S(1)}, u32[]{:S(2)}, u32[]{:S(2)}) collective-permute-start(f32[32,768]{1,0:T(8,128)S(1)} %get-tuple-element.27), channel_id=1, source_target_pairs={{0,1},{1,0},{2,3},{3,2},{4,5},{5,4},{6,7},{7,6},{8,9},{9,8},{10,11... | collective-permute-start | bytes 294920 | tf_op jit(solution)/shard_map/ppermute | solution.py:236
  3.1 4.7 %collective-permute-start = (bf16[32,768]{1,0:T(8,128)(2,1)S(1)}, bf16[32,768]{1,0:T(8,128)(2,1)S(1)}, u32[]{:S(2)}, u32[]{:S(2)}) collective-permute-start(bf16[32,768]{1,0:T(8,128)(2,1)S(1)} %get-tuple-element.25), channel_id=1, source_target_pairs={{0,3},{1,2},{2,1},{3,0},{4,7},{5,6},{6,5},{7,4},{8,11},{9,10},{10,... | collective-permute-start | bytes 147464 | tf_op jit(solution)/shard_map/ppermute | solution.py:236
  5.7 4.1 %collective-permute-start.1 = (bf16[32,768]{1,0:T(8,128)(2,1)S(1)}, bf16[32,768]{1,0:T(8,128)(2,1)S(1)}, u32[]{:S(2)}, u32[]{:S(2)}) collective-permute-start(bf16[32,768]{1,0:T(8,128)(2,1)S(1)} %get-tuple-element.26), channel_id=1, source_target_pairs={{0,2},{1,3},{2,0},{3,1},{4,6},{5,7},{6,4},{7,5},{8,10},{9,11},{10,... | collective-permute-start | bytes 147464 | tf_op jit(solution)/shard_map/ppermute | solution.py:236
  5.7 10.1 %collective-permute-start.8 = (bf16[1552,128]{1,0:T(8,128)(2,1)S(1)}, bf16[1552,128]{1,0:T(8,128)(2,1)S(1)}, u32[]{:S(2)}, u32[]{:S(2)}) collective-permute-start(bf16[1552,128]{1,0:T(8,128)(2,1)S(1)} %get-tuple-element.28.refs_0_), channel_id=1, source_target_pairs={{0,2},{1,5},{2,0},{3,7},{4,6},{5,1},{6,4},{7,3},{8,10},{9,13},{10,... | collective-permute-start | bytes 1191944 | tf_op jit(solution)/shard_map/ppermute | solution.py:287
  9.8 6.0 %collective-permute-start.5 = (bf16[32,768]{1,0:T(8,128)(2,1)S(1)}, bf16[32,768]{1,0:T(8,128)(2,1)S(1)}, u32[]{:S(2)}, u32[]{:S(2)}) collective-permute-start(bf16[32,768]{1,0:T(8,128)(2,1)S(1)} %join.1.refs_0_), channel_id=1, source_target_pairs={{0,24},{4,28},{8,16},{12,20},{16,8},{20,12},{24,0},{28,4},{1,25},{... | collective-permute-start | bytes 147464 | tf_op jit(solution)/shard_map/ppermute | solution.py:236
  13.5 7.8 %collective-permute-start.6 = (bf16[1552,128]{1,0:T(8,128)(2,1)S(1)}, bf16[1552,128]{1,0:T(8,128)(2,1)S(1)}, u32[]{:S(2)}, u32[]{:S(2)}) collective-permute-start(bf16[1552,128]{1,0:T(8,128)(2,1)S(1)} %get-tuple-element.28.refs_0_), channel_id=1, source_target_pairs={{0,4},{1,3},{2,6},{3,1},{4,0},{5,7},{6,2},{7,5},{8,12},{9,11},{10,... | collective-permute-start | bytes 1191944 | tf_op jit(solution)/shard_map/ppermute | solution.py:286
  15.0 4.1 %collective-permute-start.3 = (bf16[32,768]{1,0:T(8,128)(2,1)S(1)}, bf16[32,768]{1,0:T(8,128)(2,1)S(1)}, u32[]{:S(2)}, u32[]{:S(2)}) collective-permute-start(bf16[32,768]{1,0:T(8,128)(2,1)S(1)} %join.1.refs_0_), channel_id=1, source_target_pairs={{0,8},{4,12},{8,0},{12,4},{16,24},{20,28},{24,16},{28,20},{1,9},{5... | collective-permute-start | bytes 147464 | tf_op jit(solution)/shard_map/ppermute | solution.py:236
  15.0 5.0 %collective-permute-start.4 = (bf16[32,768]{1,0:T(8,128)(2,1)S(1)}, bf16[32,768]{1,0:T(8,128)(2,1)S(1)}, u32[]{:S(2)}, u32[]{:S(2)}) collective-permute-start(bf16[32,768]{1,0:T(8,128)(2,1)S(1)} %join.1.refs_0_), channel_id=1, source_target_pairs={{0,16},{4,20},{8,24},{12,28},{16,0},{20,4},{24,8},{28,12},{1,17},{... | collective-permute-start | bytes 147464 | tf_op jit(solution)/shard_map/ppermute | solution.py:236
  15.8 9.8 %collective-permute-start.9 = (bf16[1552,128]{1,0:T(8,128)(2,1)S(1)}, bf16[1552,128]{1,0:T(8,128)(2,1)S(1)}, u32[]{:S(2)}, u32[]{:S(2)}) collective-permute-start(bf16[1552,128]{1,0:T(8,128)(2,1)S(1)} %gate.1.refs_1_), channel_id=1, source_target_pairs={{0,4},{1,3},{2,6},{3,1},{4,0},{5,7},{6,2},{7,5},{8,12},{9,11},{10,... | collective-permute-start | bytes 1191944 | tf_op jit(solution)/shard_map/ppermute | solution.py:288
  21.3 1.5 %collective-permute-start.7 = (bf16[128,768]{1,0:T(8,128)(2,1)S(1)}, bf16[128,768]{1,0:T(8,128)(2,1)S(1)}, u32[]{:S(2)}, u32[]{:S(2)}) collective-permute-start(bf16[128,768]{1,0:T(8,128)(2,1)S(1)} %stack.1.mine_ref), channel_id=1, source_target_pairs={{0,1},{1,0},{2,3},{3,2},{4,5},{5,4},{6,7},{7,6},{8,9},{9,8},{10,11... | collective-permute-start | bytes 589832 | tf_op jit(solution)/shard_map/ppermute | solution.py:236
  24.6 16.5 %copy-start = (bf16[1024,768]{1,0:T(8,128)(2,1)S(1)}, bf16[1024,768]{1,0:T(8,128)(2,1)}, u32[]{:S(2)}) copy-start(bf16[1024,768]{1,0:T(8,128)(2,1)} %points_ref.1) | copy-start | bytes 4718596
  26.2 1.6 %collective-permute-start.10 = (bf16[128,896]{1,0:T(8,128)(2,1)S(1)}, bf16[128,896]{1,0:T(8,128)(2,1)S(1)}, u32[]{:S(2)}, u32[]{:S(2)}) collective-permute-start(bf16[128,896]{1,0:T(8,128)(2,1)S(1)} %get-tuple-element.30), channel_id=1, source_target_pairs={{0,1},{1,0},{2,3},{3,2},{4,5},{5,4},{6,7},{7,6},{8,9},{9,8},{10,11... | collective-permute-start | bytes 688136 | tf_op jit(solution)/shard_map/ppermute | solution.py:236
  27.8 6.4 %collective-permute-start.11 = (bf16[208,128]{1,0:T(8,128)(2,1)S(1)}, bf16[208,128]{1,0:T(8,128)(2,1)S(1)}, u32[]{:S(2)}, u32[]{:S(2)}) collective-permute-start(bf16[208,128]{1,0:T(8,128)(2,1)S(1)} %get-tuple-element.32), channel_id=1, source_target_pairs={{0,24},{4,28},{8,16},{12,20},{16,8},{20,12},{24,0},{28,4},{1,25},{... | collective-permute-start | bytes 159752 | tf_op jit(solution)/shard_map/ppermute | solution.py:236
  30.3 5.5 %collective-permute-start.12 = (bf16[208,128]{1,0:T(8,128)(2,1)S(1)}, bf16[208,128]{1,0:T(8,128)(2,1)S(1)}, u32[]{:S(2)}, u32[]{:S(2)}) collective-permute-start(bf16[208,128]{1,0:T(8,128)(2,1)S(1)} %get-tuple-element.33), channel_id=1, source_target_pairs={{0,16},{4,20},{8,24},{12,28},{16,0},{20,4},{24,8},{28,12},{1,17},{... | collective-permute-start | bytes 159752 | tf_op jit(solution)/shard_map/ppermute | solution.py:236
  30.3 5.5 %collective-permute-start.13 = (bf16[208,128]{1,0:T(8,128)(2,1)S(1)}, bf16[208,128]{1,0:T(8,128)(2,1)S(1)}, u32[]{:S(2)}, u32[]{:S(2)}) collective-permute-start(bf16[208,128]{1,0:T(8,128)(2,1)S(1)} %get-tuple-element.34), channel_id=1, source_target_pairs={{0,8},{4,12},{8,0},{12,4},{16,24},{20,28},{24,16},{28,20},{1,9},{5... | collective-permute-start | bytes 159752 | tf_op jit(solution)/shard_map/ppermute | solution.py:236
  35.9 5.2 %collective-permute-start.14 = (f32[32,768]{1,0:T(8,128)S(1)}, f32[32,768]{1,0:T(8,128)S(1)}, u32[]{:S(2)}, u32[]{:S(2)}) collective-permute-start(f32[32,768]{1,0:T(8,128)S(1)} %get-tuple-element.35.refs_0_), channel_id=1, source_target_pairs={{0,1},{1,0},{2,3},{3,2},{4,5},{5,4},{6,7},{7,6},{8,9},{9,8},{10,11... | collective-permute-start | bytes 294920 | tf_op jit(solution)/shard_map/ppermute | solution.py:236
  36.0 4.2 %collective-permute-start.15 = (bf16[32,768]{1,0:T(8,128)(2,1)S(1)}, bf16[32,768]{1,0:T(8,128)(2,1)S(1)}, u32[]{:S(2)}, u32[]{:S(2)}) collective-permute-start(bf16[32,768]{1,0:T(8,128)(2,1)S(1)} %get-tuple-element.36), channel_id=1, source_target_pairs={{0,2},{1,3},{2,0},{3,1},{4,6},{5,7},{6,4},{7,5},{8,10},{9,11},{10,... | collective-permute-start | bytes 147464 | tf_op jit(solution)/shard_map/ppermute | solution.py:236
  37.5 3.7 %collective-permute-start.16 = (bf16[32,768]{1,0:T(8,128)(2,1)S(1)}, bf16[32,768]{1,0:T(8,128)(2,1)S(1)}, u32[]{:S(2)}, u32[]{:S(2)}) collective-permute-start(bf16[32,768]{1,0:T(8,128)(2,1)S(1)} %get-tuple-element.36), channel_id=1, source_target_pairs={{0,3},{1,2},{2,1},{3,0},{4,7},{5,6},{6,5},{7,4},{8,11},{9,10},{10,... | collective-permute-start | bytes 147464 | tf_op jit(solution)/shard_map/ppermute | solution.py:236
  42.7 5.3 %collective-permute-start.19 = (f32[32,768]{1,0:T(8,128)S(1)}, f32[32,768]{1,0:T(8,128)S(1)}, u32[]{:S(2)}, u32[]{:S(2)}) collective-permute-start(f32[32,768]{1,0:T(8,128)S(1)} %get-tuple-element.41), channel_id=1, source_target_pairs={{0,1},{1,0},{2,3},{3,2},{4,5},{5,4},{6,7},{7,6},{8,9},{9,8},{10,11... | collective-permute-start | bytes 294920 | tf_op jit(solution)/shard_map/ppermute | solution.py:236
  42.9 3.5 %collective-permute-start.17 = (bf16[32,768]{1,0:T(8,128)(2,1)S(1)}, bf16[32,768]{1,0:T(8,128)(2,1)S(1)}, u32[]{:S(2)}, u32[]{:S(2)}) collective-permute-start(bf16[32,768]{1,0:T(8,128)(2,1)S(1)} %get-tuple-element.39), channel_id=1, source_target_pairs={{0,3},{1,2},{2,1},{3,0},{4,7},{5,6},{6,5},{7,4},{8,11},{9,10},{10,... | collective-permute-start | bytes 147464 | tf_op jit(solution)/shard_map/ppermute | solution.py:236
  43.9 4.2 %collective-permute-start.18 = (bf16[32,768]{1,0:T(8,128)(2,1)S(1)}, bf16[32,768]{1,0:T(8,128)(2,1)S(1)}, u32[]{:S(2)}, u32[]{:S(2)}) collective-permute-start(bf16[32,768]{1,0:T(8,128)(2,1)S(1)} %get-tuple-element.40), channel_id=1, source_target_pairs={{0,2},{1,3},{2,0},{3,1},{4,6},{5,7},{6,4},{7,5},{8,10},{9,11},{10,... | collective-permute-start | bytes 147464 | tf_op jit(solution)/shard_map/ppermute | solution.py:236

commit v17 on v13

--- a/solution.py
+++ b/solution.py
@@ -283,11 +283,11 @@
     )(own, *swaps(parts, "help"))
     lifters = [lifter] + [swap(lifter, "shard", INNER * d) for d in range(1, planes)]
     index, axes = range(groups * helpers), ("shard", "help")
-    one = [(i, i ^ (2 if i % 2 == 0 else helpers)) for i in index]
-    two = [(i, i ^ (helpers if i % 2 == 0 else 2)) for i in index]
+    one = [(i, i ^ (helpers if i % 2 == 0 else 2)) for i in index]
+    two = [(i, i ^ (2 if i % 2 == 0 else helpers)) for i in index]
     far = lax.ppermute(packed, axes, one)
     (near,) = gate([lax.ppermute(packed, axes, two)], lifters[-1])
-    cut = width // LANES * 2 // 3 * count
+    cut = width // LANES // 2 * count
     across = [lax.ppermute(near[:cut], axes, one), lax.ppermute(far[cut:], axes, two)]
 
     mine = pl.pallas_call(

time: 50 us -> 50.7 us (1.014)
  starting transfers between devices: 22 us -> 22.8 us
    ppermute x1, waiting for transfers between devices: 0.01 us -> 2.89 us  [shards(): lax.ppermute(near[:cut], axes, one)]
    ppermute x1, waiting for transfers between devices: 1.82 us -> 0.01 us  [shards(): far = lax.ppermute(packed, axes, one)]
    ppermute x1, waiting for transfers between devices: 1.66 us -> 0.01 us  [shards(): lax.ppermute(far[cut:], axes, two)]
    ppermute x1, starting transfers between devices: 1.01 us -> 2.01 us  [shards(): far = lax.ppermute(packed, axes, one)]
    ppermute x1, starting transfers between devices: 1.04 us -> 1.59 us  [shards(): lax.ppermute(near[:cut], axes, one)]
    ppermute x1, starting transfers between devices: 2.01 us -> 1.49 us  [shards(): near, = gate([lax.ppermute(packed, axes, two)], lifters[-1])]
    ppermute x1, starting transfers between devices: 1.59 us -> 1.07 us  [shards(): lax.ppermute(far[cut:], axes, two)]
  transfers between devices with their start and end apart: 21 -> 21, of which waited for: 13 -> 12; matrix products, arithmetic and copies ran while one was open for 0% -> 0% of each run, Pallas kernels for 4% -> 4%
where the time goes in v17:
time: 50.7 us; the launch traced here: 50.4 us
  starting transfers between devices  22.8 us (45%)
  waiting for transfers between devices  20.1 us (40%)
  Pallas kernels  6.09 us (12%)
  between operations  0.73 us (1%)
  other arithmetic  0.67 us (1%)
    ppermute x17, waiting for transfers between devices, swap(): lax.ppermute(value, axis, [(i, i ^ d) for i in range(lax.axis_size(axis))])  17.2 us
    ppermute x17, starting transfers between devices, swap(): lax.ppermute(value, axis, [(i, i ^ d) for i in range(lax.axis_size(axis))])  16.7 us
    ppermute x1, waiting for transfers between devices, shards(): lax.ppermute(near[:cut], axes, one)  2.89 us
    ppermute x1, starting transfers between devices, shards(): far = lax.ppermute(packed, axes, one)  2.01 us
    pallas_call x1, Pallas kernels, shards(): pl.pallas_call(functools.partial(lift_kernel, helpers), out_shape=[jax.Sh...  1.92 us
    pallas_call x1, Pallas kernels, shards(): pl.pallas_call(functools.partial(score_kernel, planes, helpers, 3, 1), ou...  1.81 us
    ppermute x1, starting transfers between devices, shards(): lax.ppermute(near[:cut], axes, one)  1.59 us
    pallas_call x1, Pallas kernels, shards(): pl.pallas_call(functools.partial(sketch_kernel, helpers), out_shape=[jax....  1.54 us
  transfers between devices with their start and end apart: 21, of which 12 were waited for; matrix products, arithmetic and copies ran while one was open for 0% of the time, Pallas kernels for 4%

profile of v17, /device:TPU:0, one launch (start us, length us, event | category | flops | bytes accessed | tf_op | source)
XLA Modules:
  0.0 50.4 jit_solution(18404232871610865558)
XLA Ops:
  0.6 1.9 %lift.1 = (bf16[1552,128]{1,0:T(8,128)(2,1)S(1)}, s32[1,1024]{1,0:T(1,128)S(1)}, f32[8,128]{1,0:T(8,128)S(1)}, f32[32,768]{1,0:T(8,128)S(1)}, f32[32,768]{1,0:T(...) custom-call(bf16[256,768]{1,0:T(8,128)(2,1)} %refs_0_.1, s32[2,256]{1,0:T(2,128)} %bitcast.4, ...), custom_call_target="tpu_custom_call" | custom-call | tf_op jit(solution)/shard_map/lift/pallas_call | solution.py:255
  2.6 0.5 %collective-permute-start.2 = (f32[32,768]{1,0:T(8,128)S(1)}, f32[32,768]{1,0:T(8,128)S(1)}, u32[]{:S(2)}, u32[]{:S(2)}) collective-permute-start(f32[32,768]{1,0:T(8,128)S(1)} %get-tuple-element.27), channel_id=1, source_target_pairs={{0,1},{1,0},{2,3},{3,2},{4,5},{5,4},{6,7},{7,6},{8,9},{9,8},{10,11... | collective-permute-start | bytes 294920 | tf_op jit(solution)/shard_map/ppermute | solution.py:238
  3.1 2.6 %collective-permute-start = (bf16[32,768]{1,0:T(8,128)(2,1)S(1)}, bf16[32,768]{1,0:T(8,128)(2,1)S(1)}, u32[]{:S(2)}, u32[]{:S(2)}) collective-permute-start(bf16[32,768]{1,0:T(8,128)(2,1)S(1)} %get-tuple-element.25), channel_id=1, source_target_pairs={{0,3},{1,2},{2,1},{3,0},{4,7},{5,6},{6,5},{7,4},{8,11},{9,10},{10,... | collective-permute-start | bytes 147464 | tf_op jit(solution)/shard_map/ppermute | solution.py:238
  5.7 0.0 collective-permute-start.1
  5.7 2.0 %collective-permute-start.6 = (bf16[1552,128]{1,0:T(8,128)(2,1)S(1)}, bf16[1552,128]{1,0:T(8,128)(2,1)S(1)}, u32[]{:S(2)}, u32[]{:S(2)}) collective-permute-start(bf16[1552,128]{1,0:T(8,128)(2,1)S(1)} %get-tuple-element.28.refs_0_), channel_id=1, source_target_pairs={{0,4},{1,3},{2,6},{3,1},{4,0},{5,7},{6,2},{7,5},{8,12},{9,11},{10,... | collective-permute-start | bytes 1191944 | tf_op jit(solution)/shard_map/ppermute | solution.py:288
  7.7 1.5 %collective-permute-start.8 = (bf16[1552,128]{1,0:T(8,128)(2,1)S(1)}, bf16[1552,128]{1,0:T(8,128)(2,1)S(1)}, u32[]{:S(2)}, u32[]{:S(2)}) collective-permute-start(bf16[1552,128]{1,0:T(8,128)(2,1)S(1)} %get-tuple-element.28.refs_0_), channel_id=1, source_target_pairs={{0,2},{1,5},{2,0},{3,7},{4,6},{5,1},{6,4},{7,3},{8,10},{9,13},{10,... | collective-permute-start | bytes 1191944 | tf_op jit(solution)/shard_map/ppermute | solution.py:289
  9.2 0.0 collective-permute-done.refs_1_
  9.2 1.1 %collective-permute-done.1.refs_2_ = bf16[32,768]{1,0:T(8,128)(2,1)S(1)} collective-permute-done((bf16[32,768]{1,0:T(8,128)(2,1)S(1)}, bf16[32,768]{1,0:T(8,128)(2,1)S(1)}, u32[]{:S(2)}, u32[]{:S(2)}) %collective-permute-start.1) | collective-permute-done | bytes 49184 | tf_op jit(solution)/shard_map/ppermute | solution.py:238
  10.3 0.0 collective-permute-done.2.refs_3_
  10.3 3.7 %collective-permute-start.5 = (bf16[32,768]{1,0:T(8,128)(2,1)S(1)}, bf16[32,768]{1,0:T(8,128)(2,1)S(1)}, u32[]{:S(2)}, u32[]{:S(2)}) collective-permute-start(bf16[32,768]{1,0:T(8,128)(2,1)S(1)} %join.1.refs_0_), channel_id=1, source_target_pairs={{0,24},{4,28},{8,16},{12,20},{16,8},{20,12},{24,0},{28,4},{1,25},{... | collective-permute-start | bytes 147464 | tf_op jit(solution)/shard_map/ppermute | solution.py:238
  14.0 0.0 collective-permute-start.3
  14.0 0.8 %collective-permute-start.4 = (bf16[32,768]{1,0:T(8,128)(2,1)S(1)}, bf16[32,768]{1,0:T(8,128)(2,1)S(1)}, u32[]{:S(2)}, u32[]{:S(2)}) collective-permute-start(bf16[32,768]{1,0:T(8,128)(2,1)S(1)} %join.1.refs_0_), channel_id=1, source_target_pairs={{0,16},{4,20},{8,24},{12,28},{16,0},{20,4},{24,8},{28,12},{1,17},{... | collective-permute-start | bytes 147464 | tf_op jit(solution)/shard_map/ppermute | solution.py:238
  14.8 1.6 %collective-permute-done.5.refs_3_.refs_1_ = bf16[32,768]{1,0:T(8,128)(2,1)S(1)} collective-permute-done((bf16[32,768]{1,0:T(8,128)(2,1)S(1)}, bf16[32,768]{1,0:T(8,128)(2,1)S(1)}, u32[]{:S(2)}, u32[]{:S(2)}) %collective-permute-start.5) | collective-permute-done | bytes 49184 | tf_op jit(solution)/shard_map/ppermute | solution.py:238
  16.4 1.7 %collective-permute-done.3.refs_1_ = bf16[32,768]{1,0:T(8,128)(2,1)S(1)} collective-permute-done((bf16[32,768]{1,0:T(8,128)(2,1)S(1)}, bf16[32,768]{1,0:T(8,128)(2,1)S(1)}, u32[]{:S(2)}, u32[]{:S(2)}) %collective-permute-start.3) | collective-permute-done | bytes 49184 | tf_op jit(solution)/shard_map/ppermute | solution.py:238
  18.1 0.9 %collective-permute-done.4.refs_2_ = bf16[32,768]{1,0:T(8,128)(2,1)S(1)} collective-permute-done((bf16[32,768]{1,0:T(8,128)(2,1)S(1)}, bf16[32,768]{1,0:T(8,128)(2,1)S(1)}, u32[]{:S(2)}, u32[]{:S(2)}) %collective-permute-start.4) | collective-permute-done | bytes 49184 | tf_op jit(solution)/shard_map/ppermute | solution.py:238
  19.0 0.0 collective-permute-done.6.refs_4_.refs_2_
  19.0 0.1 collective-permute-start.7
  19.1 1.1 %collective-permute-start.10 = (bf16[784,128]{1,0:T(8,128)(2,1)S(1)}, bf16[784,128]{1,0:T(8,128)(2,1)S(1)}, u32[]{:S(2)}, u32[]{:S(2)}) collective-permute-start(bf16[784,128]{1,0:T(8,128)(2,1)S(1)} %slice.9), channel_id=1, source_target_pairs={{0,2},{1,5},{2,0},{3,7},{4,6},{5,1},{6,4},{7,3},{8,10},{9,13},{10,... | collective-permute-start | bytes 602120 | tf_op jit(solution)/shard_map/ppermute | solution.py:291
  20.2 0.0 collective-permute-done.8.refs_0_
  20.2 1.6 %collective-permute-start.9 = (bf16[768,128]{1,0:T(8,128)(2,1)S(1)}, bf16[768,128]{1,0:T(8,128)(2,1)S(1)}, u32[]{:S(2)}, u32[]{:S(2)}) collective-permute-start(bf16[768,128]{1,0:T(8,128)(2,1)S(1)} %slice.8), channel_id=1, source_target_pairs={{0,4},{1,3},{2,6},{3,1},{4,0},{5,7},{6,2},{7,5},{8,12},{9,11},{10,... | collective-permute-start | bytes 589832 | tf_op jit(solution)/shard_map/ppermute | solution.py:291
  21.8 0.0 collective-permute-done.7.theirs_ref
  21.8 1.8 %score.1.refs_2_ = f32[256,896]{1,0:T(8,128)S(1)} custom-call(bf16[128,768]{1,0:T(8,128)(2,1)S(1)} %stack.1.mine_ref, bf16[128,768]{1,0:T(8,128)(2,1)S(1)} %collective-permute-done.7.theirs_ref, bf16[1552,128]{1,0:T(8,128)(2,1)S(1)} %get-tuple-element.28.refs_0_, bf16[1552,128]{1,0:T(8,128)(2,1)S(1)} %gate.1.refs_1_, ...), custom_call_target="tpu_custom_call" | custom-call | tf_op jit(solution)/shard_map/score/pallas_call | solution.py:304
  23.6 0.0 copy-start
  23.6 2.9 %collective-permute-done.9.refs_0_ = bf16[768,128]{1,0:T(8,128)(2,1)S(1)} collective-permute-done((bf16[768,128]{1,0:T(8,128)(2,1)S(1)}, bf16[768,128]{1,0:T(8,128)(2,1)S(1)}, u32[]{:S(2)}, u32[]{:S(2)}) %collective-permute-start.9) | collective-permute-done | bytes 196640 | tf_op jit(solution)/shard_map/ppermute | solution.py:291
  26.5 0.0 collective-permute-done.10.refs_1_
  26.5 0.6 %score_last.1 = (f32[128,896]{1,0:T(8,128)S(1)}, bf16[128,896]{1,0:T(8,128)(2,1)S(1)}) custom-call(bf16[128,768]{1,0:T(8,128)(2,1)S(1)} %stack.1.mine_ref, bf16[128,768]{1,0:T(8,128)(2,1)S(1)} %collective-permute-done.7.theirs_ref, bf16[768,128]{1,0:T(8,128)(2,1)S(1)} %collective-permute-done.9.refs_0_, ...), custom_call_target="tpu_custom_call" | custom-call | tf_op jit(solution)/shard_map/score_last/pallas_call | solution.py:310
  27.2 0.4 collective-permute-start.11
  27.5 1.2 %collective-permute-done.11.theirs_ref = bf16[128,896]{1,0:T(8,128)(2,1)S(1)} collective-permute-done((bf16[128,896]{1,0:T(8,128)(2,1)S(1)}, bf16[128,896]{1,0:T(8,128)(2,1)S(1)}, u32[]{:S(2)}, u32[]{:S(2)}) %collective-permute-start.11) | collective-permute-done | bytes 229408 | tf_op jit(solution)/shard_map/ppermute | solution.py:238
  28.7 0.1 fold.1
  28.8 3.0 %collective-permute-start.12 = (bf16[208,128]{1,0:T(8,128)(2,1)S(1)}, bf16[208,128]{1,0:T(8,128)(2,1)S(1)}, u32[]{:S(2)}, u32[]{:S(2)}) collective-permute-start(bf16[208,128]{1,0:T(8,128)(2,1)S(1)} %get-tuple-element.32), channel_id=1, source_target_pairs={{0,24},{4,28},{8,16},{12,20},{16,8},{20,12},{24,0},{28,4},{1,25},{... | collective-permute-start | bytes 159752 | tf_op jit(solution)/shard_map/ppermute | solution.py:238
  31.7 0.6 %collective-permute-start.13 = (bf16[208,128]{1,0:T(8,128)(2,1)S(1)}, bf16[208,128]{1,0:T(8,128)(2,1)S(1)}, u32[]{:S(2)}, u32[]{:S(2)}) collective-permute-start(bf16[208,128]{1,0:T(8,128)(2,1)S(1)} %get-tuple-element.33), channel_id=1, source_target_pairs={{0,16},{4,20},{8,24},{12,28},{16,0},{20,4},{24,8},{28,12},{1,17},{... | collective-permute-start | bytes 159752 | tf_op jit(solution)/shard_map/ppermute | solution.py:238
  32.3 0.9 %collective-permute-start.14 = (bf16[208,128]{1,0:T(8,128)(2,1)S(1)}, bf16[208,128]{1,0:T(8,128)(2,1)S(1)}, u32[]{:S(2)}, u32[]{:S(2)}) collective-permute-start(bf16[208,128]{1,0:T(8,128)(2,1)S(1)} %get-tuple-element.34), channel_id=1, source_target_pairs={{0,8},{4,12},{8,0},{12,4},{16,24},{20,28},{24,16},{28,20},{1,9},{5... | collective-permute-start | bytes 159752 | tf_op jit(solution)/shard_map/ppermute | solution.py:238
  33.2 2.1 %collective-permute-done.12.refs_0_ = bf16[208,128]{1,0:T(8,128)(2,1)S(1)} collective-permute-done((bf16[208,128]{1,0:T(8,128)(2,1)S(1)}, bf16[208,128]{1,0:T(8,128)(2,1)S(1)}, u32[]{:S(2)}, u32[]{:S(2)}) %collective-permute-start.12) | collective-permute-done | bytes 53280 | tf_op jit(solution)/shard_map/ppermute | solution.py:238
  35.4 2.4 %collective-permute-done.13.refs_1_ = bf16[208,128]{1,0:T(8,128)(2,1)S(1)} collective-permute-done((bf16[208,128]{1,0:T(8,128)(2,1)S(1)}, bf16[208,128]{1,0:T(8,128)(2,1)S(1)}, u32[]{:S(2)}, u32[]{:S(2)}) %collective-permute-start.13) | collective-permute-done | bytes 53280 | tf_op jit(solution)/shard_map/ppermute | solution.py:238
  37.8 0.0 collective-permute-done.14.refs_2_
  37.8 0.1 scale.1
  37.9 0.1 collective-permute-start.15
  37.9 1.1 %collective-permute-start.16 = (bf16[32,768]{1,0:T(8,128)(2,1)S(1)}, bf16[32,768]{1,0:T(8,128)(2,1)S(1)}, u32[]{:S(2)}, u32[]{:S(2)}) collective-permute-start(bf16[32,768]{1,0:T(8,128)(2,1)S(1)} %get-tuple-element.36), channel_id=1, source_target_pairs={{0,2},{1,3},{2,0},{3,1},{4,6},{5,7},{6,4},{7,5},{8,10},{9,11},{10,... | collective-permute-start | bytes 147464 | tf_op jit(solution)/shard_map/ppermute | solution.py:238
  39.0 0.8 %collective-permute-start.17 = (bf16[32,768]{1,0:T(8,128)(2,1)S(1)}, bf16[32,768]{1,0:T(8,128)(2,1)S(1)}, u32[]{:S(2)}, u32[]{:S(2)}) collective-permute-start(bf16[32,768]{1,0:T(8,128)(2,1)S(1)} %get-tuple-element.36), channel_id=1, source_target_pairs={{0,3},{1,2},{2,1},{3,0},{4,7},{5,6},{6,5},{7,4},{8,11},{9,10},{10,... | collective-permute-start | bytes 147464 | tf_op jit(solution)/shard_map/ppermute | solution.py:238
  39.8 2.5 %collective-permute-done.16.refs_2_ = bf16[32,768]{1,0:T(8,128)(2,1)S(1)} collective-permute-done((bf16[32,768]{1,0:T(8,128)(2,1)S(1)}, bf16[32,768]{1,0:T(8,128)(2,1)S(1)}, u32[]{:S(2)}, u32[]{:S(2)}) %collective-permute-start.16) | collective-permute-done | bytes 49184 | tf_op jit(solution)/shard_map/ppermute | solution.py:238
  42.3 0.6 %collective-permute-done.17.refs_3_ = bf16[32,768]{1,0:T(8,128)(2,1)S(1)} collective-permute-done((bf16[32,768]{1,0:T(8,128)(2,1)S(1)}, bf16[32,768]{1,0:T(8,128)(2,1)S(1)}, u32[]{:S(2)}, u32[]{:S(2)}) %collective-permute-start.17) | collective-permute-done | bytes 49184 | tf_op jit(solution)/shard_map/ppermute | solution.py:238
  42.9 0.0 collective-permute-done.15.refs_1_
  42.9 0.0 copy-done
  42.9 1.5 %sketch.1 = (f32[32,1024]{1,0:T(8,128)}, f32[32,768]{1,0:T(8,128)S(1)}, f32[32,768]{1,0:T(8,128)S(1)}, bf16[32,768]{1,0:T(8,128)(2,1)S(1)}, bf16[32,768]{1,0:T(8,128)(2,1)S(1)}) custom-call(s32[1,1024]{1,0:T(1,128)S(1)} %get-tuple-element.22.mark_ref, f32[8,128]{1,0:T(8,128)S(1)} %get-tuple-element.23.resident_ref, bf16[1024,768]{1,0:T(8,128)(2,1)S(1)} %copy-done, ...), custom_call_target="tpu_custom_call" | custom-call | tf_op jit(solution)/shard_map/sketch/pallas_call | solution.py:333
  44.4 0.2 collective-permute-start.20
  44.6 1.0 %collective-permute-start.18 = (bf16[32,768]{1,0:T(8,128)(2,1)S(1)}, bf16[32,768]{1,0:T(8,128)(2,1)S(1)}, u32[]{:S(2)}, u32[]{:S(2)}) collective-permute-start(bf16[32,768]{1,0:T(8,128)(2,1)S(1)} %get-tuple-element.39), channel_id=1, source_target_pairs={{0,3},{1,2},{2,1},{3,0},{4,7},{5,6},{6,5},{7,4},{8,11},{9,10},{10,... | collective-permute-start | bytes 147464 | tf_op jit(solution)/shard_map/ppermute | solution.py:238
  45.6 1.0 %collective-permute-start.19 = (bf16[32,768]{1,0:T(8,128)(2,1)S(1)}, bf16[32,768]{1,0:T(8,128)(2,1)S(1)}, u32[]{:S(2)}, u32[]{:S(2)}) collective-permute-start(bf16[32,768]{1,0:T(8,128)(2,1)S(1)} %get-tuple-element.40), channel_id=1, source_target_pairs={{0,2},{1,3},{2,0},{3,1},{4,6},{5,7},{6,4},{7,5},{8,10},{9,11},{10,... | collective-permute-start | bytes 147464 | tf_op jit(solution)/shard_map/ppermute | solution.py:238
  46.6 1.5 %collective-permute-done.18 = bf16[32,768]{1,0:T(8,128)(2,1)S(1)} collective-permute-done((bf16[32,768]{1,0:T(8,128)(2,1)S(1)}, bf16[32,768]{1,0:T(8,128)(2,1)S(1)}, u32[]{:S(2)}, u32[]{:S(2)}) %collective-permute-start.18) | collective-permute-done | bytes 49184 | tf_op jit(solution)/shard_map/ppermute | solution.py:238
  48.2 1.6 %collective-permute-done.19 = bf16[32,768]{1,0:T(8,128)(2,1)S(1)} collective-permute-done((bf16[32,768]{1,0:T(8,128)(2,1)S(1)}, bf16[32,768]{1,0:T(8,128)(2,1)S(1)}, u32[]{:S(2)}, u32[]{:S(2)}) %collective-permute-start.19) | collective-permute-done | bytes 49184 | tf_op jit(solution)/shard_map/ppermute | solution.py:238
  49.8 0.0 collective-permute-done.20
  49.8 0.7 %add_bitcast_fusion = f32[1,32,768]{2,1,0:T(8,128)} fusion(f32[32,768]{1,0:T(8,128)S(1)} %collective-permute-done.20, bf16[32,768]{1,0:T(8,128)(2,1)S(1)} %collective-permute-done.19, f32[32,768]{1,0:T(8,128)S(1)} %get-tuple-element.38, bf16[32,768]{1,0:T(8,128)(2,1)S(1)} %collective-permute-done.18), kind=kLoop, calls=%fused_computation | loop fusion | flops 122880 | bytes 393216 | tf_op jit(solution)/shard_map/broadcast_in_dim | solution.py:343
  (5 shorter events, 0.1 us)
Async XLA Ops:
  2.6 7.7 %collective-permute-start.2 = (f32[32,768]{1,0:T(8,128)S(1)}, f32[32,768]{1,0:T(8,128)S(1)}, u32[]{:S(2)}, u32[]{:S(2)}) collective-permute-start(f32[32,768]{1,0:T(8,128)S(1)} %get-tuple-element.27), channel_id=1, source_target_pairs={{0,1},{1,0},{2,3},{3,2},{4,5},{5,4},{6,7},{7,6},{8,9},{9,8},{10,11... | collective-permute-start | bytes 294920 | tf_op jit(solution)/shard_map/ppermute | solution.py:238
  3.1 6.2 %collective-permute-start = (bf16[32,768]{1,0:T(8,128)(2,1)S(1)}, bf16[32,768]{1,0:T(8,128)(2,1)S(1)}, u32[]{:S(2)}, u32[]{:S(2)}) collective-permute-start(bf16[32,768]{1,0:T(8,128)(2,1)S(1)} %get-tuple-element.25), channel_id=1, source_target_pairs={{0,3},{1,2},{2,1},{3,0},{4,7},{5,6},{6,5},{7,4},{8,11},{9,10},{10,... | collective-permute-start | bytes 147464 | tf_op jit(solution)/shard_map/ppermute | solution.py:238
  5.7 4.6 %collective-permute-start.1 = (bf16[32,768]{1,0:T(8,128)(2,1)S(1)}, bf16[32,768]{1,0:T(8,128)(2,1)S(1)}, u32[]{:S(2)}, u32[]{:S(2)}) collective-permute-start(bf16[32,768]{1,0:T(8,128)(2,1)S(1)} %get-tuple-element.26), channel_id=1, source_target_pairs={{0,2},{1,3},{2,0},{3,1},{4,6},{5,7},{6,4},{7,5},{8,10},{9,11},{10,... | collective-permute-start | bytes 147464 | tf_op jit(solution)/shard_map/ppermute | solution.py:238
  5.7 13.2 %collective-permute-start.6 = (bf16[1552,128]{1,0:T(8,128)(2,1)S(1)}, bf16[1552,128]{1,0:T(8,128)(2,1)S(1)}, u32[]{:S(2)}, u32[]{:S(2)}) collective-permute-start(bf16[1552,128]{1,0:T(8,128)(2,1)S(1)} %get-tuple-element.28.refs_0_), channel_id=1, source_target_pairs={{0,4},{1,3},{2,6},{3,1},{4,0},{5,7},{6,2},{7,5},{8,12},{9,11},{10,... | collective-permute-start | bytes 1191944 | tf_op jit(solution)/shard_map/ppermute | solution.py:288
  7.7 12.4 %collective-permute-start.8 = (bf16[1552,128]{1,0:T(8,128)(2,1)S(1)}, bf16[1552,128]{1,0:T(8,128)(2,1)S(1)}, u32[]{:S(2)}, u32[]{:S(2)}) collective-permute-start(bf16[1552,128]{1,0:T(8,128)(2,1)S(1)} %get-tuple-element.28.refs_0_), channel_id=1, source_target_pairs={{0,2},{1,5},{2,0},{3,7},{4,6},{5,1},{6,4},{7,3},{8,10},{9,13},{10,... | collective-permute-start | bytes 1191944 | tf_op jit(solution)/shard_map/ppermute | solution.py:289
  10.3 6.1 %collective-permute-start.5 = (bf16[32,768]{1,0:T(8,128)(2,1)S(1)}, bf16[32,768]{1,0:T(8,128)(2,1)S(1)}, u32[]{:S(2)}, u32[]{:S(2)}) collective-permute-start(bf16[32,768]{1,0:T(8,128)(2,1)S(1)} %join.1.refs_0_), channel_id=1, source_target_pairs={{0,24},{4,28},{8,16},{12,20},{16,8},{20,12},{24,0},{28,4},{1,25},{... | collective-permute-start | bytes 147464 | tf_op jit(solution)/shard_map/ppermute | solution.py:238
  14.0 4.1 %collective-permute-start.3 = (bf16[32,768]{1,0:T(8,128)(2,1)S(1)}, bf16[32,768]{1,0:T(8,128)(2,1)S(1)}, u32[]{:S(2)}, u32[]{:S(2)}) collective-permute-start(bf16[32,768]{1,0:T(8,128)(2,1)S(1)} %join.1.refs_0_), channel_id=1, source_target_pairs={{0,8},{4,12},{8,0},{12,4},{16,24},{20,28},{24,16},{28,20},{1,9},{5... | collective-permute-start | bytes 147464 | tf_op jit(solution)/shard_map/ppermute | solution.py:238
  14.0 5.0 %collective-permute-start.4 = (bf16[32,768]{1,0:T(8,128)(2,1)S(1)}, bf16[32,768]{1,0:T(8,128)(2,1)S(1)}, u32[]{:S(2)}, u32[]{:S(2)}) collective-permute-start(bf16[32,768]{1,0:T(8,128)(2,1)S(1)} %join.1.refs_0_), channel_id=1, source_target_pairs={{0,16},{4,20},{8,24},{12,28},{16,0},{20,4},{24,8},{28,12},{1,17},{... | collective-permute-start | bytes 147464 | tf_op jit(solution)/shard_map/ppermute | solution.py:238
  19.0 2.8 %collective-permute-start.7 = (bf16[128,768]{1,0:T(8,128)(2,1)S(1)}, bf16[128,768]{1,0:T(8,128)(2,1)S(1)}, u32[]{:S(2)}, u32[]{:S(2)}) collective-permute-start(bf16[128,768]{1,0:T(8,128)(2,1)S(1)} %stack.1.mine_ref), channel_id=1, source_target_pairs={{0,1},{1,0},{2,3},{3,2},{4,5},{5,4},{6,7},{7,6},{8,9},{9,8},{10,11... | collective-permute-start | bytes 589832 | tf_op jit(solution)/shard_map/ppermute | solution.py:238
  19.1 7.4 %collective-permute-start.10 = (bf16[784,128]{1,0:T(8,128)(2,1)S(1)}, bf16[784,128]{1,0:T(8,128)(2,1)S(1)}, u32[]{:S(2)}, u32[]{:S(2)}) collective-permute-start(bf16[784,128]{1,0:T(8,128)(2,1)S(1)} %slice.9), channel_id=1, source_target_pairs={{0,2},{1,5},{2,0},{3,7},{4,6},{5,1},{6,4},{7,3},{8,10},{9,13},{10,... | collective-permute-start | bytes 602120 | tf_op jit(solution)/shard_map/ppermute | solution.py:291
  20.2 6.3 %collective-permute-start.9 = (bf16[768,128]{1,0:T(8,128)(2,1)S(1)}, bf16[768,128]{1,0:T(8,128)(2,1)S(1)}, u32[]{:S(2)}, u32[]{:S(2)}) collective-permute-start(bf16[768,128]{1,0:T(8,128)(2,1)S(1)} %slice.8), channel_id=1, source_target_pairs={{0,4},{1,3},{2,6},{3,1},{4,0},{5,7},{6,2},{7,5},{8,12},{9,11},{10,... | collective-permute-start | bytes 589832 | tf_op jit(solution)/shard_map/ppermute | solution.py:291
  23.6 19.3 %copy-start = (bf16[1024,768]{1,0:T(8,128)(2,1)S(1)}, bf16[1024,768]{1,0:T(8,128)(2,1)}, u32[]{:S(2)}) copy-start(bf16[1024,768]{1,0:T(8,128)(2,1)} %points_ref.1) | copy-start | bytes 4718596
  27.2 1.6 %collective-permute-start.11 = (bf16[128,896]{1,0:T(8,128)(2,1)S(1)}, bf16[128,896]{1,0:T(8,128)(2,1)S(1)}, u32[]{:S(2)}, u32[]{:S(2)}) collective-permute-start(bf16[128,896]{1,0:T(8,128)(2,1)S(1)} %get-tuple-element.30), channel_id=1, source_target_pairs={{0,1},{1,0},{2,3},{3,2},{4,5},{5,4},{6,7},{7,6},{8,9},{9,8},{10,11... | collective-permute-start | bytes 688136 | tf_op jit(solution)/shard_map/ppermute | solution.py:238
  28.8 6.6 %collective-permute-start.12 = (bf16[208,128]{1,0:T(8,128)(2,1)S(1)}, bf16[208,128]{1,0:T(8,128)(2,1)S(1)}, u32[]{:S(2)}, u32[]{:S(2)}) collective-permute-start(bf16[208,128]{1,0:T(8,128)(2,1)S(1)} %get-tuple-element.32), channel_id=1, source_target_pairs={{0,24},{4,28},{8,16},{12,20},{16,8},{20,12},{24,0},{28,4},{1,25},{... | collective-permute-start | bytes 159752 | tf_op jit(solution)/shard_map/ppermute | solution.py:238
  31.7 6.0 %collective-permute-start.13 = (bf16[208,128]{1,0:T(8,128)(2,1)S(1)}, bf16[208,128]{1,0:T(8,128)(2,1)S(1)}, u32[]{:S(2)}, u32[]{:S(2)}) collective-permute-start(bf16[208,128]{1,0:T(8,128)(2,1)S(1)} %get-tuple-element.33), channel_id=1, source_target_pairs={{0,16},{4,20},{8,24},{12,28},{16,0},{20,4},{24,8},{28,12},{1,17},{... | collective-permute-start | bytes 159752 | tf_op jit(solution)/shard_map/ppermute | solution.py:238
  32.3 5.4 %collective-permute-start.14 = (bf16[208,128]{1,0:T(8,128)(2,1)S(1)}, bf16[208,128]{1,0:T(8,128)(2,1)S(1)}, u32[]{:S(2)}, u32[]{:S(2)}) collective-permute-start(bf16[208,128]{1,0:T(8,128)(2,1)S(1)} %get-tuple-element.34), channel_id=1, source_target_pairs={{0,8},{4,12},{8,0},{12,4},{16,24},{20,28},{24,16},{28,20},{1,9},{5... | collective-permute-start | bytes 159752 | tf_op jit(solution)/shard_map/ppermute | solution.py:238
  37.9 5.0 %collective-permute-start.15 = (f32[32,768]{1,0:T(8,128)S(1)}, f32[32,768]{1,0:T(8,128)S(1)}, u32[]{:S(2)}, u32[]{:S(2)}) collective-permute-start(f32[32,768]{1,0:T(8,128)S(1)} %get-tuple-element.35.refs_0_), channel_id=1, source_target_pairs={{0,1},{1,0},{2,3},{3,2},{4,5},{5,4},{6,7},{7,6},{8,9},{9,8},{10,11... | collective-permute-start | bytes 294920 | tf_op jit(solution)/shard_map/ppermute | solution.py:238
  37.9 4.3 %collective-permute-start.16 = (bf16[32,768]{1,0:T(8,128)(2,1)S(1)}, bf16[32,768]{1,0:T(8,128)(2,1)S(1)}, u32[]{:S(2)}, u32[]{:S(2)}) collective-permute-start(bf16[32,768]{1,0:T(8,128)(2,1)S(1)} %get-tuple-element.36), channel_id=1, source_target_pairs={{0,2},{1,3},{2,0},{3,1},{4,6},{5,7},{6,4},{7,5},{8,10},{9,11},{10,... | collective-permute-start | bytes 147464 | tf_op jit(solution)/shard_map/ppermute | solution.py:238
  39.0 3.9 %collective-permute-start.17 = (bf16[32,768]{1,0:T(8,128)(2,1)S(1)}, bf16[32,768]{1,0:T(8,128)(2,1)S(1)}, u32[]{:S(2)}, u32[]{:S(2)}) collective-permute-start(bf16[32,768]{1,0:T(8,128)(2,1)S(1)} %get-tuple-element.36), channel_id=1, source_target_pairs={{0,3},{1,2},{2,1},{3,0},{4,7},{5,6},{6,5},{7,4},{8,11},{9,10},{10,... | collective-permute-start | bytes 147464 | tf_op jit(solution)/shard_map/ppermute | solution.py:238
  44.4 5.3 %collective-permute-start.20 = (f32[32,768]{1,0:T(8,128)S(1)}, f32[32,768]{1,0:T(8,128)S(1)}, u32[]{:S(2)}, u32[]{:S(2)}) collective-permute-start(f32[32,768]{1,0:T(8,128)S(1)} %get-tuple-element.41), channel_id=1, source_target_pairs={{0,1},{1,0},{2,3},{3,2},{4,5},{5,4},{6,7},{7,6},{8,9},{9,8},{10,11... | collective-permute-start | bytes 294920 | tf_op jit(solution)/shard_map/ppermute | solution.py:238
  44.6 3.5 %collective-permute-start.18 = (bf16[32,768]{1,0:T(8,128)(2,1)S(1)}, bf16[32,768]{1,0:T(8,128)(2,1)S(1)}, u32[]{:S(2)}, u32[]{:S(2)}) collective-permute-start(bf16[32,768]{1,0:T(8,128)(2,1)S(1)} %get-tuple-element.39), channel_id=1, source_target_pairs={{0,3},{1,2},{2,1},{3,0},{4,7},{5,6},{6,5},{7,4},{8,11},{9,10},{10,... | collective-permute-start | bytes 147464 | tf_op jit(solution)/shard_map/ppermute | solution.py:238
  45.6 4.1 %collective-permute-start.19 = (bf16[32,768]{1,0:T(8,128)(2,1)S(1)}, bf16[32,768]{1,0:T(8,128)(2,1)S(1)}, u32[]{:S(2)}, u32[]{:S(2)}) collective-permute-start(bf16[32,768]{1,0:T(8,128)(2,1)S(1)} %get-tuple-element.40), channel_id=1, source_target_pairs={{0,2},{1,3},{2,0},{3,1},{4,6},{5,7},{6,4},{7,5},{8,10},{9,11},{10,... | collective-permute-start | bytes 147464 | tf_op jit(solution)/shard_map/ppermute | solution.py:238

commit v18 on v16

--- a/solution.py
+++ b/solution.py
@@ -11,7 +11,7 @@
 BF16 = jnp.bfloat16
 LANES = 128
 TILE = 16
-CHUNKS = 4
+CHUNKS = 2
 INNER = 2
 
 ANY = pl.BlockSpec(memory_space=pl.ANY)

time: 48.9 us -> 49 us (level)
  no operation moved by 1% of the time
where the time goes in v18:
time: 49 us; the launch traced here: 48.7 us
  starting transfers between devices  21.4 us (44%)
  waiting for transfers between devices  19.8 us (40%)
  Pallas kernels  6.1 us (12%)
  between operations  0.72 us (1%)
  other arithmetic  0.67 us (1%)
    ppermute x17, waiting for transfers between devices, swap(): lax.ppermute(value, axis, [(i, i ^ d) for i in range(lax.axis_size(axis))])  17.6 us
    ppermute x17, starting transfers between devices, swap(): lax.ppermute(value, axis, [(i, i ^ d) for i in range(lax.axis_size(axis))])  16.4 us
    ppermute x1, starting transfers between devices, shards(): near, = gate([lax.ppermute(packed, axes, two)], lifters[-1])  1.98 us
    pallas_call x1, Pallas kernels, shards(): pl.pallas_call(functools.partial(lift_kernel, helpers), out_shape=[jax.Sh...  1.93 us
    pallas_call x1, Pallas kernels, shards(): pl.pallas_call(functools.partial(score_kernel, planes, helpers, 3), out_s...  1.81 us
    pallas_call x1, Pallas kernels, shards(): pl.pallas_call(functools.partial(sketch_kernel, helpers), out_shape=[jax....  1.54 us
    ppermute x1, starting transfers between devices, shards(): far = lax.ppermute(packed, axes, one)  1.52 us
    ppermute x1, starting transfers between devices, shards(): across = lax.ppermute(near, axes, one)  1.5 us
  transfers between devices with their start and end apart: 20, of which 13 were waited for; matrix products, arithmetic and copies ran while one was open for 0% of the time, Pallas kernels for 4%

profile of v18, /device:TPU:0, one launch (start us, length us, event | category | flops | bytes accessed | tf_op | source)
XLA Modules:
  0.0 48.7 jit_solution(10060965970769968351)
XLA Ops:
  0.6 1.9 %lift.1 = (bf16[1552,128]{1,0:T(8,128)(2,1)S(1)}, s32[1,1024]{1,0:T(1,128)S(1)}, f32[8,128]{1,0:T(8,128)S(1)}, f32[32,768]{1,0:T(8,128)S(1)}, f32[32,768]{1,0:T(...) custom-call(bf16[256,768]{1,0:T(8,128)(2,1)} %refs_0_.1, s32[2,256]{1,0:T(2,128)} %bitcast.4, ...), custom_call_target="tpu_custom_call" | custom-call | tf_op jit(solution)/shard_map/lift/pallas_call | solution.py:253
  2.6 0.5 %collective-permute-start.2 = (f32[32,768]{1,0:T(8,128)S(1)}, f32[32,768]{1,0:T(8,128)S(1)}, u32[]{:S(2)}, u32[]{:S(2)}) collective-permute-start(f32[32,768]{1,0:T(8,128)S(1)} %get-tuple-element.27), channel_id=1, source_target_pairs={{0,1},{1,0},{2,3},{3,2},{4,5},{5,4},{6,7},{7,6},{8,9},{9,8},{10,11... | collective-permute-start | bytes 294920 | tf_op jit(solution)/shard_map/ppermute | solution.py:236
  3.1 2.6 %collective-permute-start = (bf16[32,768]{1,0:T(8,128)(2,1)S(1)}, bf16[32,768]{1,0:T(8,128)(2,1)S(1)}, u32[]{:S(2)}, u32[]{:S(2)}) collective-permute-start(bf16[32,768]{1,0:T(8,128)(2,1)S(1)} %get-tuple-element.25), channel_id=1, source_target_pairs={{0,3},{1,2},{2,1},{3,0},{4,7},{5,6},{6,5},{7,4},{8,11},{9,10},{10,... | collective-permute-start | bytes 147464 | tf_op jit(solution)/shard_map/ppermute | solution.py:236
  5.7 0.0 collective-permute-start.1
  5.7 2.0 %collective-permute-start.8 = (bf16[1552,128]{1,0:T(8,128)(2,1)S(1)}, bf16[1552,128]{1,0:T(8,128)(2,1)S(1)}, u32[]{:S(2)}, u32[]{:S(2)}) collective-permute-start(bf16[1552,128]{1,0:T(8,128)(2,1)S(1)} %get-tuple-element.28.refs_0_), channel_id=1, source_target_pairs={{0,2},{1,5},{2,0},{3,7},{4,6},{5,1},{6,4},{7,3},{8,10},{9,13},{10,... | collective-permute-start | bytes 1191944 | tf_op jit(solution)/shard_map/ppermute | solution.py:287
  7.7 0.0 collective-permute-done.refs_1_
  7.8 2.0 %collective-permute-done.1.refs_2_ = bf16[32,768]{1,0:T(8,128)(2,1)S(1)} collective-permute-done((bf16[32,768]{1,0:T(8,128)(2,1)S(1)}, bf16[32,768]{1,0:T(8,128)(2,1)S(1)}, u32[]{:S(2)}, u32[]{:S(2)}) %collective-permute-start.1) | collective-permute-done | bytes 49184 | tf_op jit(solution)/shard_map/ppermute | solution.py:236
  9.8 0.0 collective-permute-done.2.refs_3_
  9.8 3.7 %collective-permute-start.5 = (bf16[32,768]{1,0:T(8,128)(2,1)S(1)}, bf16[32,768]{1,0:T(8,128)(2,1)S(1)}, u32[]{:S(2)}, u32[]{:S(2)}) collective-permute-start(bf16[32,768]{1,0:T(8,128)(2,1)S(1)} %join.1.refs_0_), channel_id=1, source_target_pairs={{0,24},{4,28},{8,16},{12,20},{16,8},{20,12},{24,0},{28,4},{1,25},{... | collective-permute-start | bytes 147464 | tf_op jit(solution)/shard_map/ppermute | solution.py:236
  13.5 1.5 %collective-permute-start.6 = (bf16[1552,128]{1,0:T(8,128)(2,1)S(1)}, bf16[1552,128]{1,0:T(8,128)(2,1)S(1)}, u32[]{:S(2)}, u32[]{:S(2)}) collective-permute-start(bf16[1552,128]{1,0:T(8,128)(2,1)S(1)} %get-tuple-element.28.refs_0_), channel_id=1, source_target_pairs={{0,4},{1,3},{2,6},{3,1},{4,0},{5,7},{6,2},{7,5},{8,12},{9,11},{10,... | collective-permute-start | bytes 1191944 | tf_op jit(solution)/shard_map/ppermute | solution.py:286
  15.0 0.0 collective-permute-start.3
  15.0 0.8 %collective-permute-start.4 = (bf16[32,768]{1,0:T(8,128)(2,1)S(1)}, bf16[32,768]{1,0:T(8,128)(2,1)S(1)}, u32[]{:S(2)}, u32[]{:S(2)}) collective-permute-start(bf16[32,768]{1,0:T(8,128)(2,1)S(1)} %join.1.refs_0_), channel_id=1, source_target_pairs={{0,16},{4,20},{8,24},{12,28},{16,0},{20,4},{24,8},{28,12},{1,17},{... | collective-permute-start | bytes 147464 | tf_op jit(solution)/shard_map/ppermute | solution.py:236
  15.8 0.0 collective-permute-done.5.refs_3_.refs_1_
  15.8 0.0 collective-permute-done.8.refs_0_
  15.8 1.5 %collective-permute-start.9 = (bf16[1552,128]{1,0:T(8,128)(2,1)S(1)}, bf16[1552,128]{1,0:T(8,128)(2,1)S(1)}, u32[]{:S(2)}, u32[]{:S(2)}) collective-permute-start(bf16[1552,128]{1,0:T(8,128)(2,1)S(1)} %gate.1.refs_1_), channel_id=1, source_target_pairs={{0,4},{1,3},{2,6},{3,1},{4,0},{5,7},{6,2},{7,5},{8,12},{9,11},{10,... | collective-permute-start | bytes 1191944 | tf_op jit(solution)/shard_map/ppermute | solution.py:288
  17.3 1.8 %collective-permute-done.3.refs_1_ = bf16[32,768]{1,0:T(8,128)(2,1)S(1)} collective-permute-done((bf16[32,768]{1,0:T(8,128)(2,1)S(1)}, bf16[32,768]{1,0:T(8,128)(2,1)S(1)}, u32[]{:S(2)}, u32[]{:S(2)}) %collective-permute-start.3) | collective-permute-done | bytes 49184 | tf_op jit(solution)/shard_map/ppermute | solution.py:236
  19.1 0.9 %collective-permute-done.4.refs_2_ = bf16[32,768]{1,0:T(8,128)(2,1)S(1)} collective-permute-done((bf16[32,768]{1,0:T(8,128)(2,1)S(1)}, bf16[32,768]{1,0:T(8,128)(2,1)S(1)}, u32[]{:S(2)}, u32[]{:S(2)}) %collective-permute-start.4) | collective-permute-done | bytes 49184 | tf_op jit(solution)/shard_map/ppermute | solution.py:236
  20.0 1.3 %collective-permute-done.6.refs_4_.refs_2_ = bf16[1552,128]{1,0:T(8,128)(2,1)S(1)} collective-permute-done((bf16[1552,128]{1,0:T(8,128)(2,1)S(1)}, bf16[1552,128]{1,0:T(8,128)(2,1)S(1)}, u32[]{:S(2)}, u32[]{:S(2)}) %collective-permute-start.6) | collective-permute-done | bytes 397344 | tf_op jit(solution)/shard_map/ppermute | solution.py:286
  21.3 0.1 collective-permute-start.7
  21.4 1.4 %collective-permute-done.7.theirs_ref = bf16[128,768]{1,0:T(8,128)(2,1)S(1)} collective-permute-done((bf16[128,768]{1,0:T(8,128)(2,1)S(1)}, bf16[128,768]{1,0:T(8,128)(2,1)S(1)}, u32[]{:S(2)}, u32[]{:S(2)}) %collective-permute-start.7) | collective-permute-done | bytes 196640 | tf_op jit(solution)/shard_map/ppermute | solution.py:236
  22.8 1.8 %score.1.refs_1_ = f32[256,896]{1,0:T(8,128)S(1)} custom-call(bf16[128,768]{1,0:T(8,128)(2,1)S(1)} %stack.1.mine_ref, bf16[128,768]{1,0:T(8,128)(2,1)S(1)} %collective-permute-done.7.theirs_ref, bf16[1552,128]{1,0:T(8,128)(2,1)S(1)} %get-tuple-element.28.refs_0_, bf16[1552,128]{1,0:T(8,128)(2,1)S(1)} %gate.1.refs_1_, ...), custom_call_target="tpu_custom_call" | custom-call | tf_op jit(solution)/shard_map/score/pallas_call | solution.py:301
  24.7 0.0 copy-start
  24.7 0.9 %collective-permute-done.9.refs_0_ = bf16[1552,128]{1,0:T(8,128)(2,1)S(1)} collective-permute-done((bf16[1552,128]{1,0:T(8,128)(2,1)S(1)}, bf16[1552,128]{1,0:T(8,128)(2,1)S(1)}, u32[]{:S(2)}, u32[]{:S(2)}) %collective-permute-start.9) | collective-permute-done | bytes 397344 | tf_op jit(solution)/shard_map/ppermute | solution.py:288
  25.6 0.6 %score_last.1 = (f32[128,896]{1,0:T(8,128)S(1)}, bf16[128,896]{1,0:T(8,128)(2,1)S(1)}) custom-call(bf16[128,768]{1,0:T(8,128)(2,1)S(1)} %stack.1.mine_ref, bf16[128,768]{1,0:T(8,128)(2,1)S(1)} %collective-permute-done.7.theirs_ref, bf16[1552,128]{1,0:T(8,128)(2,1)S(1)} %collective-permute-done.9.refs_0_, f32[256,896]{1,0:T(8,128)S(1)} %score.1.refs_1_), custom_call_target="tpu_custom_call" | custom-call | tf_op jit(solution)/shard_map/score_last/pallas_call | solution.py:307
  26.2 0.1 collective-permute-start.10
  26.3 1.5 %collective-permute-done.10.theirs_ref = bf16[128,896]{1,0:T(8,128)(2,1)S(1)} collective-permute-done((bf16[128,896]{1,0:T(8,128)(2,1)S(1)}, bf16[128,896]{1,0:T(8,128)(2,1)S(1)}, u32[]{:S(2)}, u32[]{:S(2)}) %collective-permute-start.10) | collective-permute-done | bytes 229408 | tf_op jit(solution)/shard_map/ppermute | solution.py:236
  27.8 0.1 fold.1
  27.8 2.5 %collective-permute-start.11 = (bf16[208,128]{1,0:T(8,128)(2,1)S(1)}, bf16[208,128]{1,0:T(8,128)(2,1)S(1)}, u32[]{:S(2)}, u32[]{:S(2)}) collective-permute-start(bf16[208,128]{1,0:T(8,128)(2,1)S(1)} %get-tuple-element.32), channel_id=1, source_target_pairs={{0,24},{4,28},{8,16},{12,20},{16,8},{20,12},{24,0},{28,4},{1,25},{... | collective-permute-start | bytes 159752 | tf_op jit(solution)/shard_map/ppermute | solution.py:236
  30.3 0.0 collective-permute-start.12
  30.3 2.0 %collective-permute-start.13 = (bf16[208,128]{1,0:T(8,128)(2,1)S(1)}, bf16[208,128]{1,0:T(8,128)(2,1)S(1)}, u32[]{:S(2)}, u32[]{:S(2)}) collective-permute-start(bf16[208,128]{1,0:T(8,128)(2,1)S(1)} %get-tuple-element.34), channel_id=1, source_target_pairs={{0,8},{4,12},{8,0},{12,4},{16,24},{20,28},{24,16},{28,20},{1,9},{5... | collective-permute-start | bytes 159752 | tf_op jit(solution)/shard_map/ppermute | solution.py:236
  32.3 1.9 %collective-permute-done.11.refs_0_ = bf16[208,128]{1,0:T(8,128)(2,1)S(1)} collective-permute-done((bf16[208,128]{1,0:T(8,128)(2,1)S(1)}, bf16[208,128]{1,0:T(8,128)(2,1)S(1)}, u32[]{:S(2)}, u32[]{:S(2)}) %collective-permute-start.11) | collective-permute-done | bytes 53280 | tf_op jit(solution)/shard_map/ppermute | solution.py:236
  34.2 1.6 %collective-permute-done.12.refs_1_ = bf16[208,128]{1,0:T(8,128)(2,1)S(1)} collective-permute-done((bf16[208,128]{1,0:T(8,128)(2,1)S(1)}, bf16[208,128]{1,0:T(8,128)(2,1)S(1)}, u32[]{:S(2)}, u32[]{:S(2)}) %collective-permute-start.12) | collective-permute-done | bytes 53280 | tf_op jit(solution)/shard_map/ppermute | solution.py:236
  35.9 0.0 collective-permute-done.13.refs_2_
  35.9 0.1 scale.1
  35.9 0.1 collective-permute-start.14
  36.0 1.4 %collective-permute-start.15 = (bf16[32,768]{1,0:T(8,128)(2,1)S(1)}, bf16[32,768]{1,0:T(8,128)(2,1)S(1)}, u32[]{:S(2)}, u32[]{:S(2)}) collective-permute-start(bf16[32,768]{1,0:T(8,128)(2,1)S(1)} %get-tuple-element.36), channel_id=1, source_target_pairs={{0,2},{1,3},{2,0},{3,1},{4,6},{5,7},{6,4},{7,5},{8,10},{9,11},{10,... | collective-permute-start | bytes 147464 | tf_op jit(solution)/shard_map/ppermute | solution.py:236
  37.5 0.4 collective-permute-start.16
  37.9 2.3 %collective-permute-done.15.refs_2_ = bf16[32,768]{1,0:T(8,128)(2,1)S(1)} collective-permute-done((bf16[32,768]{1,0:T(8,128)(2,1)S(1)}, bf16[32,768]{1,0:T(8,128)(2,1)S(1)}, u32[]{:S(2)}, u32[]{:S(2)}) %collective-permute-start.15) | collective-permute-done | bytes 49184 | tf_op jit(solution)/shard_map/ppermute | solution.py:236
  40.2 1.0 %collective-permute-done.16.refs_3_ = bf16[32,768]{1,0:T(8,128)(2,1)S(1)} collective-permute-done((bf16[32,768]{1,0:T(8,128)(2,1)S(1)}, bf16[32,768]{1,0:T(8,128)(2,1)S(1)}, u32[]{:S(2)}, u32[]{:S(2)}) %collective-permute-start.16) | collective-permute-done | bytes 49184 | tf_op jit(solution)/shard_map/ppermute | solution.py:236
  41.2 0.0 collective-permute-done.14.refs_1_
  41.2 0.0 copy-done
  41.2 1.5 %sketch.1 = (f32[32,1024]{1,0:T(8,128)}, f32[32,768]{1,0:T(8,128)S(1)}, f32[32,768]{1,0:T(8,128)S(1)}, bf16[32,768]{1,0:T(8,128)(2,1)S(1)}, bf16[32,768]{1,0:T(8,128)(2,1)S(1)}) custom-call(s32[1,1024]{1,0:T(1,128)S(1)} %get-tuple-element.22.mark_ref, f32[8,128]{1,0:T(8,128)S(1)} %get-tuple-element.23.resident_ref, bf16[1024,768]{1,0:T(8,128)(2,1)S(1)} %copy-done, ...), custom_call_target="tpu_custom_call" | custom-call | tf_op jit(solution)/shard_map/sketch/pallas_call | solution.py:330
  42.7 0.2 collective-permute-start.19
  42.9 0.9 %collective-permute-start.17 = (bf16[32,768]{1,0:T(8,128)(2,1)S(1)}, bf16[32,768]{1,0:T(8,128)(2,1)S(1)}, u32[]{:S(2)}, u32[]{:S(2)}) collective-permute-start(bf16[32,768]{1,0:T(8,128)(2,1)S(1)} %get-tuple-element.39), channel_id=1, source_target_pairs={{0,3},{1,2},{2,1},{3,0},{4,7},{5,6},{6,5},{7,4},{8,11},{9,10},{10,... | collective-permute-start | bytes 147464 | tf_op jit(solution)/shard_map/ppermute | solution.py:236
  43.9 1.0 %collective-permute-start.18 = (bf16[32,768]{1,0:T(8,128)(2,1)S(1)}, bf16[32,768]{1,0:T(8,128)(2,1)S(1)}, u32[]{:S(2)}, u32[]{:S(2)}) collective-permute-start(bf16[32,768]{1,0:T(8,128)(2,1)S(1)} %get-tuple-element.40), channel_id=1, source_target_pairs={{0,2},{1,3},{2,0},{3,1},{4,6},{5,7},{6,4},{7,5},{8,10},{9,11},{10,... | collective-permute-start | bytes 147464 | tf_op jit(solution)/shard_map/ppermute | solution.py:236
  44.9 1.5 %collective-permute-done.17 = bf16[32,768]{1,0:T(8,128)(2,1)S(1)} collective-permute-done((bf16[32,768]{1,0:T(8,128)(2,1)S(1)}, bf16[32,768]{1,0:T(8,128)(2,1)S(1)}, u32[]{:S(2)}, u32[]{:S(2)}) %collective-permute-start.17) | collective-permute-done | bytes 49184 | tf_op jit(solution)/shard_map/ppermute | solution.py:236
  46.5 1.6 %collective-permute-done.18 = bf16[32,768]{1,0:T(8,128)(2,1)S(1)} collective-permute-done((bf16[32,768]{1,0:T(8,128)(2,1)S(1)}, bf16[32,768]{1,0:T(8,128)(2,1)S(1)}, u32[]{:S(2)}, u32[]{:S(2)}) %collective-permute-start.18) | collective-permute-done | bytes 49184 | tf_op jit(solution)/shard_map/ppermute | solution.py:236
  48.0 0.0 collective-permute-done.19
  48.0 0.7 %add_bitcast_fusion = f32[1,32,768]{2,1,0:T(8,128)} fusion(f32[32,768]{1,0:T(8,128)S(1)} %collective-permute-done.19, bf16[32,768]{1,0:T(8,128)(2,1)S(1)} %collective-permute-done.18, f32[32,768]{1,0:T(8,128)S(1)} %get-tuple-element.38, bf16[32,768]{1,0:T(8,128)(2,1)S(1)} %collective-permute-done.17), kind=kLoop, calls=%fused_computation | loop fusion | flops 122880 | bytes 393216 | tf_op jit(solution)/shard_map/broadcast_in_dim | solution.py:340
  (3 shorter events, 0.0 us)
Async XLA Ops:
  2.6 7.2 %collective-permute-start.2 = (f32[32,768]{1,0:T(8,128)S(1)}, f32[32,768]{1,0:T(8,128)S(1)}, u32[]{:S(2)}, u32[]{:S(2)}) collective-permute-start(f32[32,768]{1,0:T(8,128)S(1)} %get-tuple-element.27), channel_id=1, source_target_pairs={{0,1},{1,0},{2,3},{3,2},{4,5},{5,4},{6,7},{7,6},{8,9},{9,8},{10,11... | collective-permute-start | bytes 294920 | tf_op jit(solution)/shard_map/ppermute | solution.py:236
  3.1 4.7 %collective-permute-start = (bf16[32,768]{1,0:T(8,128)(2,1)S(1)}, bf16[32,768]{1,0:T(8,128)(2,1)S(1)}, u32[]{:S(2)}, u32[]{:S(2)}) collective-permute-start(bf16[32,768]{1,0:T(8,128)(2,1)S(1)} %get-tuple-element.25), channel_id=1, source_target_pairs={{0,3},{1,2},{2,1},{3,0},{4,7},{5,6},{6,5},{7,4},{8,11},{9,10},{10,... | collective-permute-start | bytes 147464 | tf_op jit(solution)/shard_map/ppermute | solution.py:236
  5.7 4.1 %collective-permute-start.1 = (bf16[32,768]{1,0:T(8,128)(2,1)S(1)}, bf16[32,768]{1,0:T(8,128)(2,1)S(1)}, u32[]{:S(2)}, u32[]{:S(2)}) collective-permute-start(bf16[32,768]{1,0:T(8,128)(2,1)S(1)} %get-tuple-element.26), channel_id=1, source_target_pairs={{0,2},{1,3},{2,0},{3,1},{4,6},{5,7},{6,4},{7,5},{8,10},{9,11},{10,... | collective-permute-start | bytes 147464 | tf_op jit(solution)/shard_map/ppermute | solution.py:236
  5.7 10.1 %collective-permute-start.8 = (bf16[1552,128]{1,0:T(8,128)(2,1)S(1)}, bf16[1552,128]{1,0:T(8,128)(2,1)S(1)}, u32[]{:S(2)}, u32[]{:S(2)}) collective-permute-start(bf16[1552,128]{1,0:T(8,128)(2,1)S(1)} %get-tuple-element.28.refs_0_), channel_id=1, source_target_pairs={{0,2},{1,5},{2,0},{3,7},{4,6},{5,1},{6,4},{7,3},{8,10},{9,13},{10,... | collective-permute-start | bytes 1191944 | tf_op jit(solution)/shard_map/ppermute | solution.py:287
  9.8 6.0 %collective-permute-start.5 = (bf16[32,768]{1,0:T(8,128)(2,1)S(1)}, bf16[32,768]{1,0:T(8,128)(2,1)S(1)}, u32[]{:S(2)}, u32[]{:S(2)}) collective-permute-start(bf16[32,768]{1,0:T(8,128)(2,1)S(1)} %join.1.refs_0_), channel_id=1, source_target_pairs={{0,24},{4,28},{8,16},{12,20},{16,8},{20,12},{24,0},{28,4},{1,25},{... | collective-permute-start | bytes 147464 | tf_op jit(solution)/shard_map/ppermute | solution.py:236
  13.5 7.8 %collective-permute-start.6 = (bf16[1552,128]{1,0:T(8,128)(2,1)S(1)}, bf16[1552,128]{1,0:T(8,128)(2,1)S(1)}, u32[]{:S(2)}, u32[]{:S(2)}) collective-permute-start(bf16[1552,128]{1,0:T(8,128)(2,1)S(1)} %get-tuple-element.28.refs_0_), channel_id=1, source_target_pairs={{0,4},{1,3},{2,6},{3,1},{4,0},{5,7},{6,2},{7,5},{8,12},{9,11},{10,... | collective-permute-start | bytes 1191944 | tf_op jit(solution)/shard_map/ppermute | solution.py:286
  15.0 4.1 %collective-permute-start.3 = (bf16[32,768]{1,0:T(8,128)(2,1)S(1)}, bf16[32,768]{1,0:T(8,128)(2,1)S(1)}, u32[]{:S(2)}, u32[]{:S(2)}) collective-permute-start(bf16[32,768]{1,0:T(8,128)(2,1)S(1)} %join.1.refs_0_), channel_id=1, source_target_pairs={{0,8},{4,12},{8,0},{12,4},{16,24},{20,28},{24,16},{28,20},{1,9},{5... | collective-permute-start | bytes 147464 | tf_op jit(solution)/shard_map/ppermute | solution.py:236
  15.0 5.0 %collective-permute-start.4 = (bf16[32,768]{1,0:T(8,128)(2,1)S(1)}, bf16[32,768]{1,0:T(8,128)(2,1)S(1)}, u32[]{:S(2)}, u32[]{:S(2)}) collective-permute-start(bf16[32,768]{1,0:T(8,128)(2,1)S(1)} %join.1.refs_0_), channel_id=1, source_target_pairs={{0,16},{4,20},{8,24},{12,28},{16,0},{20,4},{24,8},{28,12},{1,17},{... | collective-permute-start | bytes 147464 | tf_op jit(solution)/shard_map/ppermute | solution.py:236
  15.8 9.8 %collective-permute-start.9 = (bf16[1552,128]{1,0:T(8,128)(2,1)S(1)}, bf16[1552,128]{1,0:T(8,128)(2,1)S(1)}, u32[]{:S(2)}, u32[]{:S(2)}) collective-permute-start(bf16[1552,128]{1,0:T(8,128)(2,1)S(1)} %gate.1.refs_1_), channel_id=1, source_target_pairs={{0,4},{1,3},{2,6},{3,1},{4,0},{5,7},{6,2},{7,5},{8,12},{9,11},{10,... | collective-permute-start | bytes 1191944 | tf_op jit(solution)/shard_map/ppermute | solution.py:288
  21.3 1.5 %collective-permute-start.7 = (bf16[128,768]{1,0:T(8,128)(2,1)S(1)}, bf16[128,768]{1,0:T(8,128)(2,1)S(1)}, u32[]{:S(2)}, u32[]{:S(2)}) collective-permute-start(bf16[128,768]{1,0:T(8,128)(2,1)S(1)} %stack.1.mine_ref), channel_id=1, source_target_pairs={{0,1},{1,0},{2,3},{3,2},{4,5},{5,4},{6,7},{7,6},{8,9},{9,8},{10,11... | collective-permute-start | bytes 589832 | tf_op jit(solution)/shard_map/ppermute | solution.py:236
  24.7 16.5 %copy-start = (bf16[1024,768]{1,0:T(8,128)(2,1)S(1)}, bf16[1024,768]{1,0:T(8,128)(2,1)}, u32[]{:S(2)}) copy-start(bf16[1024,768]{1,0:T(8,128)(2,1)} %points_ref.1) | copy-start | bytes 4718596
  26.2 1.6 %collective-permute-start.10 = (bf16[128,896]{1,0:T(8,128)(2,1)S(1)}, bf16[128,896]{1,0:T(8,128)(2,1)S(1)}, u32[]{:S(2)}, u32[]{:S(2)}) collective-permute-start(bf16[128,896]{1,0:T(8,128)(2,1)S(1)} %get-tuple-element.30), channel_id=1, source_target_pairs={{0,1},{1,0},{2,3},{3,2},{4,5},{5,4},{6,7},{7,6},{8,9},{9,8},{10,11... | collective-permute-start | bytes 688136 | tf_op jit(solution)/shard_map/ppermute | solution.py:236
  27.8 6.4 %collective-permute-start.11 = (bf16[208,128]{1,0:T(8,128)(2,1)S(1)}, bf16[208,128]{1,0:T(8,128)(2,1)S(1)}, u32[]{:S(2)}, u32[]{:S(2)}) collective-permute-start(bf16[208,128]{1,0:T(8,128)(2,1)S(1)} %get-tuple-element.32), channel_id=1, source_target_pairs={{0,24},{4,28},{8,16},{12,20},{16,8},{20,12},{24,0},{28,4},{1,25},{... | collective-permute-start | bytes 159752 | tf_op jit(solution)/shard_map/ppermute | solution.py:236
  30.3 5.5 %collective-permute-start.12 = (bf16[208,128]{1,0:T(8,128)(2,1)S(1)}, bf16[208,128]{1,0:T(8,128)(2,1)S(1)}, u32[]{:S(2)}, u32[]{:S(2)}) collective-permute-start(bf16[208,128]{1,0:T(8,128)(2,1)S(1)} %get-tuple-element.33), channel_id=1, source_target_pairs={{0,16},{4,20},{8,24},{12,28},{16,0},{20,4},{24,8},{28,12},{1,17},{... | collective-permute-start | bytes 159752 | tf_op jit(solution)/shard_map/ppermute | solution.py:236
  30.3 5.5 %collective-permute-start.13 = (bf16[208,128]{1,0:T(8,128)(2,1)S(1)}, bf16[208,128]{1,0:T(8,128)(2,1)S(1)}, u32[]{:S(2)}, u32[]{:S(2)}) collective-permute-start(bf16[208,128]{1,0:T(8,128)(2,1)S(1)} %get-tuple-element.34), channel_id=1, source_target_pairs={{0,8},{4,12},{8,0},{12,4},{16,24},{20,28},{24,16},{28,20},{1,9},{5... | collective-permute-start | bytes 159752 | tf_op jit(solution)/shard_map/ppermute | solution.py:236
  35.9 5.2 %collective-permute-start.14 = (f32[32,768]{1,0:T(8,128)S(1)}, f32[32,768]{1,0:T(8,128)S(1)}, u32[]{:S(2)}, u32[]{:S(2)}) collective-permute-start(f32[32,768]{1,0:T(8,128)S(1)} %get-tuple-element.35.refs_0_), channel_id=1, source_target_pairs={{0,1},{1,0},{2,3},{3,2},{4,5},{5,4},{6,7},{7,6},{8,9},{9,8},{10,11... | collective-permute-start | bytes 294920 | tf_op jit(solution)/shard_map/ppermute | solution.py:236
  36.0 4.2 %collective-permute-start.15 = (bf16[32,768]{1,0:T(8,128)(2,1)S(1)}, bf16[32,768]{1,0:T(8,128)(2,1)S(1)}, u32[]{:S(2)}, u32[]{:S(2)}) collective-permute-start(bf16[32,768]{1,0:T(8,128)(2,1)S(1)} %get-tuple-element.36), channel_id=1, source_target_pairs={{0,2},{1,3},{2,0},{3,1},{4,6},{5,7},{6,4},{7,5},{8,10},{9,11},{10,... | collective-permute-start | bytes 147464 | tf_op jit(solution)/shard_map/ppermute | solution.py:236
  37.5 3.7 %collective-permute-start.16 = (bf16[32,768]{1,0:T(8,128)(2,1)S(1)}, bf16[32,768]{1,0:T(8,128)(2,1)S(1)}, u32[]{:S(2)}, u32[]{:S(2)}) collective-permute-start(bf16[32,768]{1,0:T(8,128)(2,1)S(1)} %get-tuple-element.36), channel_id=1, source_target_pairs={{0,3},{1,2},{2,1},{3,0},{4,7},{5,6},{6,5},{7,4},{8,11},{9,10},{10,... | collective-permute-start | bytes 147464 | tf_op jit(solution)/shard_map/ppermute | solution.py:236
  42.7 5.3 %collective-permute-start.19 = (f32[32,768]{1,0:T(8,128)S(1)}, f32[32,768]{1,0:T(8,128)S(1)}, u32[]{:S(2)}, u32[]{:S(2)}) collective-permute-start(f32[32,768]{1,0:T(8,128)S(1)} %get-tuple-element.41), channel_id=1, source_target_pairs={{0,1},{1,0},{2,3},{3,2},{4,5},{5,4},{6,7},{7,6},{8,9},{9,8},{10,11... | collective-permute-start | bytes 294920 | tf_op jit(solution)/shard_map/ppermute | solution.py:236
  42.9 3.5 %collective-permute-start.17 = (bf16[32,768]{1,0:T(8,128)(2,1)S(1)}, bf16[32,768]{1,0:T(8,128)(2,1)S(1)}, u32[]{:S(2)}, u32[]{:S(2)}) collective-permute-start(bf16[32,768]{1,0:T(8,128)(2,1)S(1)} %get-tuple-element.39), channel_id=1, source_target_pairs={{0,3},{1,2},{2,1},{3,0},{4,7},{5,6},{6,5},{7,4},{8,11},{9,10},{10,... | collective-permute-start | bytes 147464 | tf_op jit(solution)/shard_map/ppermute | solution.py:236
  43.9 4.2 %collective-permute-start.18 = (bf16[32,768]{1,0:T(8,128)(2,1)S(1)}, bf16[32,768]{1,0:T(8,128)(2,1)S(1)}, u32[]{:S(2)}, u32[]{:S(2)}) collective-permute-start(bf16[32,768]{1,0:T(8,128)(2,1)S(1)} %get-tuple-element.40), channel_id=1, source_target_pairs={{0,2},{1,3},{2,0},{3,1},{4,6},{5,7},{6,4},{7,5},{8,10},{9,11},{10,... | collective-permute-start | bytes 147464 | tf_op jit(solution)/shard_map/ppermute | solution.py:236

commit v19 on v16

--- a/solution.py
+++ b/solution.py
@@ -329,7 +329,7 @@
 
     sketch, regressor, *parts = pl.pallas_call(
         functools.partial(sketch_kernel, helpers),
-        out_shape=[jax.ShapeDtypeStruct((rank, own_points), F32), block, block] + [sent] * (helpers - 2),
+        out_shape=[jax.ShapeDtypeStruct((rank, own_points), F32), block] + [sent] * (helpers - 1),
         out_specs=[HBM] + [VMEM] * helpers,
         scratch_shapes=[pltpu.VMEM((rank, own_points), F32), pltpu.SemaphoreType.DMA],
         compiler_params=PARAMS,

time: 48.9 us -> 48.8 us (level)
  no operation moved by 1% of the time
where the time goes in v19:
time: 48.8 us; the launch traced here: 48.5 us
  starting transfers between devices  21.1 us (43%)
  waiting for transfers between devices  20 us (41%)
  Pallas kernels  6.09 us (12%)
  between operations  0.72 us (1%)
  other arithmetic  0.67 us (1%)
    ppermute x17, waiting for transfers between devices, swap(): lax.ppermute(value, axis, [(i, i ^ d) for i in range(lax.axis_size(axis))])  17.7 us
    ppermute x17, starting transfers between devices, swap(): lax.ppermute(value, axis, [(i, i ^ d) for i in range(lax.axis_size(axis))])  16.1 us
    ppermute x1, starting transfers between devices, shards(): near, = gate([lax.ppermute(packed, axes, two)], lifters[-1])  1.98 us
    pallas_call x1, Pallas kernels, shards(): pl.pallas_call(functools.partial(lift_kernel, helpers), out_shape=[jax.Sh...  1.92 us
    pallas_call x1, Pallas kernels, shards(): pl.pallas_call(functools.partial(score_kernel, planes, helpers, 3), out_s...  1.81 us
    pallas_call x1, Pallas kernels, shards(): pl.pallas_call(functools.partial(sketch_kernel, helpers), out_shape=[jax....  1.54 us
    ppermute x1, starting transfers between devices, shards(): far = lax.ppermute(packed, axes, one)  1.52 us
    ppermute x1, starting transfers between devices, shards(): across = lax.ppermute(near, axes, one)  1.5 us
  transfers between devices with their start and end apart: 20, of which 13 were waited for; matrix products, arithmetic and copies ran while one was open for 0% of the time, Pallas kernels for 4%

profile of v19, /device:TPU:0, one launch (start us, length us, event | category | flops | bytes accessed | tf_op | source)
XLA Modules:
  0.0 48.5 jit_solution(15070875987533533437)
XLA Ops:
  0.6 1.9 %lift.1 = (bf16[1552,128]{1,0:T(8,128)(2,1)S(1)}, s32[1,1024]{1,0:T(1,128)S(1)}, f32[8,128]{1,0:T(8,128)S(1)}, f32[32,768]{1,0:T(8,128)S(1)}, f32[32,768]{1,0:T(...) custom-call(bf16[256,768]{1,0:T(8,128)(2,1)} %refs_0_.1, s32[2,256]{1,0:T(2,128)} %bitcast.4, ...), custom_call_target="tpu_custom_call" | custom-call | tf_op jit(solution)/shard_map/lift/pallas_call | solution.py:253
  2.6 0.5 %collective-permute-start.2 = (f32[32,768]{1,0:T(8,128)S(1)}, f32[32,768]{1,0:T(8,128)S(1)}, u32[]{:S(2)}, u32[]{:S(2)}) collective-permute-start(f32[32,768]{1,0:T(8,128)S(1)} %get-tuple-element.27), channel_id=1, source_target_pairs={{0,1},{1,0},{2,3},{3,2},{4,5},{5,4},{6,7},{7,6},{8,9},{9,8},{10,11... | collective-permute-start | bytes 294920 | tf_op jit(solution)/shard_map/ppermute | solution.py:236
  3.1 2.6 %collective-permute-start = (bf16[32,768]{1,0:T(8,128)(2,1)S(1)}, bf16[32,768]{1,0:T(8,128)(2,1)S(1)}, u32[]{:S(2)}, u32[]{:S(2)}) collective-permute-start(bf16[32,768]{1,0:T(8,128)(2,1)S(1)} %get-tuple-element.25), channel_id=1, source_target_pairs={{0,3},{1,2},{2,1},{3,0},{4,7},{5,6},{6,5},{7,4},{8,11},{9,10},{10,... | collective-permute-start | bytes 147464 | tf_op jit(solution)/shard_map/ppermute | solution.py:236
  5.7 0.0 collective-permute-start.1
  5.7 2.0 %collective-permute-start.8 = (bf16[1552,128]{1,0:T(8,128)(2,1)S(1)}, bf16[1552,128]{1,0:T(8,128)(2,1)S(1)}, u32[]{:S(2)}, u32[]{:S(2)}) collective-permute-start(bf16[1552,128]{1,0:T(8,128)(2,1)S(1)} %get-tuple-element.28.refs_0_), channel_id=1, source_target_pairs={{0,2},{1,5},{2,0},{3,7},{4,6},{5,1},{6,4},{7,3},{8,10},{9,13},{10,... | collective-permute-start | bytes 1191944 | tf_op jit(solution)/shard_map/ppermute | solution.py:287
  7.7 0.0 collective-permute-done.refs_1_
  7.8 2.0 %collective-permute-done.1.refs_2_ = bf16[32,768]{1,0:T(8,128)(2,1)S(1)} collective-permute-done((bf16[32,768]{1,0:T(8,128)(2,1)S(1)}, bf16[32,768]{1,0:T(8,128)(2,1)S(1)}, u32[]{:S(2)}, u32[]{:S(2)}) %collective-permute-start.1) | collective-permute-done | bytes 49184 | tf_op jit(solution)/shard_map/ppermute | solution.py:236
  9.8 0.0 collective-permute-done.2.refs_3_
  9.8 3.7 %collective-permute-start.5 = (bf16[32,768]{1,0:T(8,128)(2,1)S(1)}, bf16[32,768]{1,0:T(8,128)(2,1)S(1)}, u32[]{:S(2)}, u32[]{:S(2)}) collective-permute-start(bf16[32,768]{1,0:T(8,128)(2,1)S(1)} %join.1.refs_0_), channel_id=1, source_target_pairs={{0,24},{4,28},{8,16},{12,20},{16,8},{20,12},{24,0},{28,4},{1,25},{... | collective-permute-start | bytes 147464 | tf_op jit(solution)/shard_map/ppermute | solution.py:236
  13.5 1.5 %collective-permute-start.6 = (bf16[1552,128]{1,0:T(8,128)(2,1)S(1)}, bf16[1552,128]{1,0:T(8,128)(2,1)S(1)}, u32[]{:S(2)}, u32[]{:S(2)}) collective-permute-start(bf16[1552,128]{1,0:T(8,128)(2,1)S(1)} %get-tuple-element.28.refs_0_), channel_id=1, source_target_pairs={{0,4},{1,3},{2,6},{3,1},{4,0},{5,7},{6,2},{7,5},{8,12},{9,11},{10,... | collective-permute-start | bytes 1191944 | tf_op jit(solution)/shard_map/ppermute | solution.py:286
  15.0 0.0 collective-permute-start.3
  15.0 0.8 %collective-permute-start.4 = (bf16[32,768]{1,0:T(8,128)(2,1)S(1)}, bf16[32,768]{1,0:T(8,128)(2,1)S(1)}, u32[]{:S(2)}, u32[]{:S(2)}) collective-permute-start(bf16[32,768]{1,0:T(8,128)(2,1)S(1)} %join.1.refs_0_), channel_id=1, source_target_pairs={{0,16},{4,20},{8,24},{12,28},{16,0},{20,4},{24,8},{28,12},{1,17},{... | collective-permute-start | bytes 147464 | tf_op jit(solution)/shard_map/ppermute | solution.py:236
  15.8 0.0 collective-permute-done.5.refs_3_.refs_1_
  15.8 0.0 collective-permute-done.8.refs_0_
  15.8 1.5 %collective-permute-start.9 = (bf16[1552,128]{1,0:T(8,128)(2,1)S(1)}, bf16[1552,128]{1,0:T(8,128)(2,1)S(1)}, u32[]{:S(2)}, u32[]{:S(2)}) collective-permute-start(bf16[1552,128]{1,0:T(8,128)(2,1)S(1)} %gate.1.refs_1_), channel_id=1, source_target_pairs={{0,4},{1,3},{2,6},{3,1},{4,0},{5,7},{6,2},{7,5},{8,12},{9,11},{10,... | collective-permute-start | bytes 1191944 | tf_op jit(solution)/shard_map/ppermute | solution.py:288
  17.3 1.8 %collective-permute-done.3.refs_1_ = bf16[32,768]{1,0:T(8,128)(2,1)S(1)} collective-permute-done((bf16[32,768]{1,0:T(8,128)(2,1)S(1)}, bf16[32,768]{1,0:T(8,128)(2,1)S(1)}, u32[]{:S(2)}, u32[]{:S(2)}) %collective-permute-start.3) | collective-permute-done | bytes 49184 | tf_op jit(solution)/shard_map/ppermute | solution.py:236
  19.1 0.9 %collective-permute-done.4.refs_2_ = bf16[32,768]{1,0:T(8,128)(2,1)S(1)} collective-permute-done((bf16[32,768]{1,0:T(8,128)(2,1)S(1)}, bf16[32,768]{1,0:T(8,128)(2,1)S(1)}, u32[]{:S(2)}, u32[]{:S(2)}) %collective-permute-start.4) | collective-permute-done | bytes 49184 | tf_op jit(solution)/shard_map/ppermute | solution.py:236
  20.0 1.3 %collective-permute-done.6.refs_4_.refs_2_ = bf16[1552,128]{1,0:T(8,128)(2,1)S(1)} collective-permute-done((bf16[1552,128]{1,0:T(8,128)(2,1)S(1)}, bf16[1552,128]{1,0:T(8,128)(2,1)S(1)}, u32[]{:S(2)}, u32[]{:S(2)}) %collective-permute-start.6) | collective-permute-done | bytes 397344 | tf_op jit(solution)/shard_map/ppermute | solution.py:286
  21.3 0.1 collective-permute-start.7
  21.4 1.4 %collective-permute-done.7.theirs_ref = bf16[128,768]{1,0:T(8,128)(2,1)S(1)} collective-permute-done((bf16[128,768]{1,0:T(8,128)(2,1)S(1)}, bf16[128,768]{1,0:T(8,128)(2,1)S(1)}, u32[]{:S(2)}, u32[]{:S(2)}) %collective-permute-start.7) | collective-permute-done | bytes 196640 | tf_op jit(solution)/shard_map/ppermute | solution.py:236
  22.8 1.8 %score.1.refs_1_ = f32[256,896]{1,0:T(8,128)S(1)} custom-call(bf16[128,768]{1,0:T(8,128)(2,1)S(1)} %stack.1.mine_ref, bf16[128,768]{1,0:T(8,128)(2,1)S(1)} %collective-permute-done.7.theirs_ref, bf16[1552,128]{1,0:T(8,128)(2,1)S(1)} %get-tuple-element.28.refs_0_, bf16[1552,128]{1,0:T(8,128)(2,1)S(1)} %gate.1.refs_1_, ...), custom_call_target="tpu_custom_call" | custom-call | tf_op jit(solution)/shard_map/score/pallas_call | solution.py:301
  24.6 0.0 copy-start
  24.7 0.9 %collective-permute-done.9.refs_0_ = bf16[1552,128]{1,0:T(8,128)(2,1)S(1)} collective-permute-done((bf16[1552,128]{1,0:T(8,128)(2,1)S(1)}, bf16[1552,128]{1,0:T(8,128)(2,1)S(1)}, u32[]{:S(2)}, u32[]{:S(2)}) %collective-permute-start.9) | collective-permute-done | bytes 397344 | tf_op jit(solution)/shard_map/ppermute | solution.py:288
  25.6 0.6 %score_last.1 = (f32[128,896]{1,0:T(8,128)S(1)}, bf16[128,896]{1,0:T(8,128)(2,1)S(1)}) custom-call(bf16[128,768]{1,0:T(8,128)(2,1)S(1)} %stack.1.mine_ref, bf16[128,768]{1,0:T(8,128)(2,1)S(1)} %collective-permute-done.7.theirs_ref, bf16[1552,128]{1,0:T(8,128)(2,1)S(1)} %collective-permute-done.9.refs_0_, f32[256,896]{1,0:T(8,128)S(1)} %score.1.refs_1_), custom_call_target="tpu_custom_call" | custom-call | tf_op jit(solution)/shard_map/score_last/pallas_call | solution.py:307
  26.2 0.1 collective-permute-start.10
  26.3 1.5 %collective-permute-done.10.theirs_ref = bf16[128,896]{1,0:T(8,128)(2,1)S(1)} collective-permute-done((bf16[128,896]{1,0:T(8,128)(2,1)S(1)}, bf16[128,896]{1,0:T(8,128)(2,1)S(1)}, u32[]{:S(2)}, u32[]{:S(2)}) %collective-permute-start.10) | collective-permute-done | bytes 229408 | tf_op jit(solution)/shard_map/ppermute | solution.py:236
  27.8 0.1 fold.1
  27.8 2.5 %collective-permute-start.11 = (bf16[208,128]{1,0:T(8,128)(2,1)S(1)}, bf16[208,128]{1,0:T(8,128)(2,1)S(1)}, u32[]{:S(2)}, u32[]{:S(2)}) collective-permute-start(bf16[208,128]{1,0:T(8,128)(2,1)S(1)} %get-tuple-element.32), channel_id=1, source_target_pairs={{0,24},{4,28},{8,16},{12,20},{16,8},{20,12},{24,0},{28,4},{1,25},{... | collective-permute-start | bytes 159752 | tf_op jit(solution)/shard_map/ppermute | solution.py:236
  30.3 0.0 collective-permute-start.12
  30.3 2.0 %collective-permute-start.13 = (bf16[208,128]{1,0:T(8,128)(2,1)S(1)}, bf16[208,128]{1,0:T(8,128)(2,1)S(1)}, u32[]{:S(2)}, u32[]{:S(2)}) collective-permute-start(bf16[208,128]{1,0:T(8,128)(2,1)S(1)} %get-tuple-element.34), channel_id=1, source_target_pairs={{0,8},{4,12},{8,0},{12,4},{16,24},{20,28},{24,16},{28,20},{1,9},{5... | collective-permute-start | bytes 159752 | tf_op jit(solution)/shard_map/ppermute | solution.py:236
  32.3 1.9 %collective-permute-done.11.refs_0_ = bf16[208,128]{1,0:T(8,128)(2,1)S(1)} collective-permute-done((bf16[208,128]{1,0:T(8,128)(2,1)S(1)}, bf16[208,128]{1,0:T(8,128)(2,1)S(1)}, u32[]{:S(2)}, u32[]{:S(2)}) %collective-permute-start.11) | collective-permute-done | bytes 53280 | tf_op jit(solution)/shard_map/ppermute | solution.py:236
  34.2 1.6 %collective-permute-done.12.refs_1_ = bf16[208,128]{1,0:T(8,128)(2,1)S(1)} collective-permute-done((bf16[208,128]{1,0:T(8,128)(2,1)S(1)}, bf16[208,128]{1,0:T(8,128)(2,1)S(1)}, u32[]{:S(2)}, u32[]{:S(2)}) %collective-permute-start.12) | collective-permute-done | bytes 53280 | tf_op jit(solution)/shard_map/ppermute | solution.py:236
  35.8 0.0 collective-permute-done.13.refs_2_
  35.8 0.1 scale.1
  35.9 0.1 collective-permute-start.14
  36.0 1.4 %collective-permute-start.15 = (bf16[32,768]{1,0:T(8,128)(2,1)S(1)}, bf16[32,768]{1,0:T(8,128)(2,1)S(1)}, u32[]{:S(2)}, u32[]{:S(2)}) collective-permute-start(bf16[32,768]{1,0:T(8,128)(2,1)S(1)} %get-tuple-element.36), channel_id=1, source_target_pairs={{0,2},{1,3},{2,0},{3,1},{4,6},{5,7},{6,4},{7,5},{8,10},{9,11},{10,... | collective-permute-start | bytes 147464 | tf_op jit(solution)/shard_map/ppermute | solution.py:236
  37.5 0.4 collective-permute-start.16
  37.9 2.3 %collective-permute-done.15.refs_2_ = bf16[32,768]{1,0:T(8,128)(2,1)S(1)} collective-permute-done((bf16[32,768]{1,0:T(8,128)(2,1)S(1)}, bf16[32,768]{1,0:T(8,128)(2,1)S(1)}, u32[]{:S(2)}, u32[]{:S(2)}) %collective-permute-start.15) | collective-permute-done | bytes 49184 | tf_op jit(solution)/shard_map/ppermute | solution.py:236
  40.2 1.0 %collective-permute-done.16.refs_3_ = bf16[32,768]{1,0:T(8,128)(2,1)S(1)} collective-permute-done((bf16[32,768]{1,0:T(8,128)(2,1)S(1)}, bf16[32,768]{1,0:T(8,128)(2,1)S(1)}, u32[]{:S(2)}, u32[]{:S(2)}) %collective-permute-start.16) | collective-permute-done | bytes 49184 | tf_op jit(solution)/shard_map/ppermute | solution.py:236
  41.1 0.0 collective-permute-done.14.refs_1_
  41.2 0.0 copy-done
  41.2 1.5 %sketch.1 = (f32[32,1024]{1,0:T(8,128)}, f32[32,768]{1,0:T(8,128)S(1)}, bf16[32,768]{1,0:T(8,128)(2,1)S(1)}, bf16[32,768]{1,0:T(8,128)(2,1)S(1)}, bf16[32,768]{1,0:T(8,128)(2,1)S(1)}) custom-call(s32[1,1024]{1,0:T(1,128)S(1)} %get-tuple-element.22.mark_ref, f32[8,128]{1,0:T(8,128)S(1)} %get-tuple-element.23.resident_ref, bf16[1024,768]{1,0:T(8,128)(2,1)S(1)} %copy-done, ...), custom_call_target="tpu_custom_call" | custom-call | tf_op jit(solution)/shard_map/sketch/pallas_call | solution.py:330
  42.7 0.9 %collective-permute-start.17 = (bf16[32,768]{1,0:T(8,128)(2,1)S(1)}, bf16[32,768]{1,0:T(8,128)(2,1)S(1)}, u32[]{:S(2)}, u32[]{:S(2)}) collective-permute-start(bf16[32,768]{1,0:T(8,128)(2,1)S(1)} %get-tuple-element.39), channel_id=1, source_target_pairs={{0,3},{1,2},{2,1},{3,0},{4,7},{5,6},{6,5},{7,4},{8,11},{9,10},{10,... | collective-permute-start | bytes 147464 | tf_op jit(solution)/shard_map/ppermute | solution.py:236
  43.6 0.9 %collective-permute-start.18 = (bf16[32,768]{1,0:T(8,128)(2,1)S(1)}, bf16[32,768]{1,0:T(8,128)(2,1)S(1)}, u32[]{:S(2)}, u32[]{:S(2)}) collective-permute-start(bf16[32,768]{1,0:T(8,128)(2,1)S(1)} %get-tuple-element.40), channel_id=1, source_target_pairs={{0,2},{1,3},{2,0},{3,1},{4,6},{5,7},{6,4},{7,5},{8,10},{9,11},{10,... | collective-permute-start | bytes 147464 | tf_op jit(solution)/shard_map/ppermute | solution.py:236
  44.6 0.1 collective-permute-start.19
  44.6 1.8 %collective-permute-done.17 = bf16[32,768]{1,0:T(8,128)(2,1)S(1)} collective-permute-done((bf16[32,768]{1,0:T(8,128)(2,1)S(1)}, bf16[32,768]{1,0:T(8,128)(2,1)S(1)}, u32[]{:S(2)}, u32[]{:S(2)}) %collective-permute-start.17) | collective-permute-done | bytes 49184 | tf_op jit(solution)/shard_map/ppermute | solution.py:236
  46.5 1.4 %collective-permute-done.18 = bf16[32,768]{1,0:T(8,128)(2,1)S(1)} collective-permute-done((bf16[32,768]{1,0:T(8,128)(2,1)S(1)}, bf16[32,768]{1,0:T(8,128)(2,1)S(1)}, u32[]{:S(2)}, u32[]{:S(2)}) %collective-permute-start.18) | collective-permute-done | bytes 49184 | tf_op jit(solution)/shard_map/ppermute | solution.py:236
  47.9 0.0 collective-permute-done.19
  47.9 0.7 %add_bitcast_fusion = f32[1,32,768]{2,1,0:T(8,128)} fusion(bf16[32,768]{1,0:T(8,128)(2,1)S(1)} %collective-permute-done.19, bf16[32,768]{1,0:T(8,128)(2,1)S(1)} %collective-permute-done.18, f32[32,768]{1,0:T(8,128)S(1)} %get-tuple-element.38, bf16[32,768]{1,0:T(8,128)(2,1)S(1)} %collective-permute-done.17), kind=kLoop, calls=%fused_computation | loop fusion | flops 147456 | bytes 344064 | tf_op jit(solution)/shard_map/broadcast_in_dim | solution.py:340
  (3 shorter events, 0.0 us)
Async XLA Ops:
  2.6 7.2 %collective-permute-start.2 = (f32[32,768]{1,0:T(8,128)S(1)}, f32[32,768]{1,0:T(8,128)S(1)}, u32[]{:S(2)}, u32[]{:S(2)}) collective-permute-start(f32[32,768]{1,0:T(8,128)S(1)} %get-tuple-element.27), channel_id=1, source_target_pairs={{0,1},{1,0},{2,3},{3,2},{4,5},{5,4},{6,7},{7,6},{8,9},{9,8},{10,11... | collective-permute-start | bytes 294920 | tf_op jit(solution)/shard_map/ppermute | solution.py:236
  3.1 4.7 %collective-permute-start = (bf16[32,768]{1,0:T(8,128)(2,1)S(1)}, bf16[32,768]{1,0:T(8,128)(2,1)S(1)}, u32[]{:S(2)}, u32[]{:S(2)}) collective-permute-start(bf16[32,768]{1,0:T(8,128)(2,1)S(1)} %get-tuple-element.25), channel_id=1, source_target_pairs={{0,3},{1,2},{2,1},{3,0},{4,7},{5,6},{6,5},{7,4},{8,11},{9,10},{10,... | collective-permute-start | bytes 147464 | tf_op jit(solution)/shard_map/ppermute | solution.py:236
  5.7 4.1 %collective-permute-start.1 = (bf16[32,768]{1,0:T(8,128)(2,1)S(1)}, bf16[32,768]{1,0:T(8,128)(2,1)S(1)}, u32[]{:S(2)}, u32[]{:S(2)}) collective-permute-start(bf16[32,768]{1,0:T(8,128)(2,1)S(1)} %get-tuple-element.26), channel_id=1, source_target_pairs={{0,2},{1,3},{2,0},{3,1},{4,6},{5,7},{6,4},{7,5},{8,10},{9,11},{10,... | collective-permute-start | bytes 147464 | tf_op jit(solution)/shard_map/ppermute | solution.py:236
  5.7 10.1 %collective-permute-start.8 = (bf16[1552,128]{1,0:T(8,128)(2,1)S(1)}, bf16[1552,128]{1,0:T(8,128)(2,1)S(1)}, u32[]{:S(2)}, u32[]{:S(2)}) collective-permute-start(bf16[1552,128]{1,0:T(8,128)(2,1)S(1)} %get-tuple-element.28.refs_0_), channel_id=1, source_target_pairs={{0,2},{1,5},{2,0},{3,7},{4,6},{5,1},{6,4},{7,3},{8,10},{9,13},{10,... | collective-permute-start | bytes 1191944 | tf_op jit(solution)/shard_map/ppermute | solution.py:287
  9.8 6.0 %collective-permute-start.5 = (bf16[32,768]{1,0:T(8,128)(2,1)S(1)}, bf16[32,768]{1,0:T(8,128)(2,1)S(1)}, u32[]{:S(2)}, u32[]{:S(2)}) collective-permute-start(bf16[32,768]{1,0:T(8,128)(2,1)S(1)} %join.1.refs_0_), channel_id=1, source_target_pairs={{0,24},{4,28},{8,16},{12,20},{16,8},{20,12},{24,0},{28,4},{1,25},{... | collective-permute-start | bytes 147464 | tf_op jit(solution)/shard_map/ppermute | solution.py:236
  13.5 7.8 %collective-permute-start.6 = (bf16[1552,128]{1,0:T(8,128)(2,1)S(1)}, bf16[1552,128]{1,0:T(8,128)(2,1)S(1)}, u32[]{:S(2)}, u32[]{:S(2)}) collective-permute-start(bf16[1552,128]{1,0:T(8,128)(2,1)S(1)} %get-tuple-element.28.refs_0_), channel_id=1, source_target_pairs={{0,4},{1,3},{2,6},{3,1},{4,0},{5,7},{6,2},{7,5},{8,12},{9,11},{10,... | collective-permute-start | bytes 1191944 | tf_op jit(solution)/shard_map/ppermute | solution.py:286
  15.0 4.1 %collective-permute-start.3 = (bf16[32,768]{1,0:T(8,128)(2,1)S(1)}, bf16[32,768]{1,0:T(8,128)(2,1)S(1)}, u32[]{:S(2)}, u32[]{:S(2)}) collective-permute-start(bf16[32,768]{1,0:T(8,128)(2,1)S(1)} %join.1.refs_0_), channel_id=1, source_target_pairs={{0,8},{4,12},{8,0},{12,4},{16,24},{20,28},{24,16},{28,20},{1,9},{5... | collective-permute-start | bytes 147464 | tf_op jit(solution)/shard_map/ppermute | solution.py:236
  15.0 5.0 %collective-permute-start.4 = (bf16[32,768]{1,0:T(8,128)(2,1)S(1)}, bf16[32,768]{1,0:T(8,128)(2,1)S(1)}, u32[]{:S(2)}, u32[]{:S(2)}) collective-permute-start(bf16[32,768]{1,0:T(8,128)(2,1)S(1)} %join.1.refs_0_), channel_id=1, source_target_pairs={{0,16},{4,20},{8,24},{12,28},{16,0},{20,4},{24,8},{28,12},{1,17},{... | collective-permute-start | bytes 147464 | tf_op jit(solution)/shard_map/ppermute | solution.py:236
  15.8 9.8 %collective-permute-start.9 = (bf16[1552,128]{1,0:T(8,128)(2,1)S(1)}, bf16[1552,128]{1,0:T(8,128)(2,1)S(1)}, u32[]{:S(2)}, u32[]{:S(2)}) collective-permute-start(bf16[1552,128]{1,0:T(8,128)(2,1)S(1)} %gate.1.refs_1_), channel_id=1, source_target_pairs={{0,4},{1,3},{2,6},{3,1},{4,0},{5,7},{6,2},{7,5},{8,12},{9,11},{10,... | collective-permute-start | bytes 1191944 | tf_op jit(solution)/shard_map/ppermute | solution.py:288
  21.3 1.5 %collective-permute-start.7 = (bf16[128,768]{1,0:T(8,128)(2,1)S(1)}, bf16[128,768]{1,0:T(8,128)(2,1)S(1)}, u32[]{:S(2)}, u32[]{:S(2)}) collective-permute-start(bf16[128,768]{1,0:T(8,128)(2,1)S(1)} %stack.1.mine_ref), channel_id=1, source_target_pairs={{0,1},{1,0},{2,3},{3,2},{4,5},{5,4},{6,7},{7,6},{8,9},{9,8},{10,11... | collective-permute-start | bytes 589832 | tf_op jit(solution)/shard_map/ppermute | solution.py:236
  24.6 16.5 %copy-start = (bf16[1024,768]{1,0:T(8,128)(2,1)S(1)}, bf16[1024,768]{1,0:T(8,128)(2,1)}, u32[]{:S(2)}) copy-start(bf16[1024,768]{1,0:T(8,128)(2,1)} %points_ref.1) | copy-start | bytes 4718596
  26.2 1.6 %collective-permute-start.10 = (bf16[128,896]{1,0:T(8,128)(2,1)S(1)}, bf16[128,896]{1,0:T(8,128)(2,1)S(1)}, u32[]{:S(2)}, u32[]{:S(2)}) collective-permute-start(bf16[128,896]{1,0:T(8,128)(2,1)S(1)} %get-tuple-element.30), channel_id=1, source_target_pairs={{0,1},{1,0},{2,3},{3,2},{4,5},{5,4},{6,7},{7,6},{8,9},{9,8},{10,11... | collective-permute-start | bytes 688136 | tf_op jit(solution)/shard_map/ppermute | solution.py:236
  27.8 6.4 %collective-permute-start.11 = (bf16[208,128]{1,0:T(8,128)(2,1)S(1)}, bf16[208,128]{1,0:T(8,128)(2,1)S(1)}, u32[]{:S(2)}, u32[]{:S(2)}) collective-permute-start(bf16[208,128]{1,0:T(8,128)(2,1)S(1)} %get-tuple-element.32), channel_id=1, source_target_pairs={{0,24},{4,28},{8,16},{12,20},{16,8},{20,12},{24,0},{28,4},{1,25},{... | collective-permute-start | bytes 159752 | tf_op jit(solution)/shard_map/ppermute | solution.py:236
  30.3 5.5 %collective-permute-start.12 = (bf16[208,128]{1,0:T(8,128)(2,1)S(1)}, bf16[208,128]{1,0:T(8,128)(2,1)S(1)}, u32[]{:S(2)}, u32[]{:S(2)}) collective-permute-start(bf16[208,128]{1,0:T(8,128)(2,1)S(1)} %get-tuple-element.33), channel_id=1, source_target_pairs={{0,16},{4,20},{8,24},{12,28},{16,0},{20,4},{24,8},{28,12},{1,17},{... | collective-permute-start | bytes 159752 | tf_op jit(solution)/shard_map/ppermute | solution.py:236
  30.3 5.5 %collective-permute-start.13 = (bf16[208,128]{1,0:T(8,128)(2,1)S(1)}, bf16[208,128]{1,0:T(8,128)(2,1)S(1)}, u32[]{:S(2)}, u32[]{:S(2)}) collective-permute-start(bf16[208,128]{1,0:T(8,128)(2,1)S(1)} %get-tuple-element.34), channel_id=1, source_target_pairs={{0,8},{4,12},{8,0},{12,4},{16,24},{20,28},{24,16},{28,20},{1,9},{5... | collective-permute-start | bytes 159752 | tf_op jit(solution)/shard_map/ppermute | solution.py:236
  35.9 5.2 %collective-permute-start.14 = (f32[32,768]{1,0:T(8,128)S(1)}, f32[32,768]{1,0:T(8,128)S(1)}, u32[]{:S(2)}, u32[]{:S(2)}) collective-permute-start(f32[32,768]{1,0:T(8,128)S(1)} %get-tuple-element.35.refs_0_), channel_id=1, source_target_pairs={{0,1},{1,0},{2,3},{3,2},{4,5},{5,4},{6,7},{7,6},{8,9},{9,8},{10,11... | collective-permute-start | bytes 294920 | tf_op jit(solution)/shard_map/ppermute | solution.py:236
  36.0 4.2 %collective-permute-start.15 = (bf16[32,768]{1,0:T(8,128)(2,1)S(1)}, bf16[32,768]{1,0:T(8,128)(2,1)S(1)}, u32[]{:S(2)}, u32[]{:S(2)}) collective-permute-start(bf16[32,768]{1,0:T(8,128)(2,1)S(1)} %get-tuple-element.36), channel_id=1, source_target_pairs={{0,2},{1,3},{2,0},{3,1},{4,6},{5,7},{6,4},{7,5},{8,10},{9,11},{10,... | collective-permute-start | bytes 147464 | tf_op jit(solution)/shard_map/ppermute | solution.py:236
  37.5 3.7 %collective-permute-start.16 = (bf16[32,768]{1,0:T(8,128)(2,1)S(1)}, bf16[32,768]{1,0:T(8,128)(2,1)S(1)}, u32[]{:S(2)}, u32[]{:S(2)}) collective-permute-start(bf16[32,768]{1,0:T(8,128)(2,1)S(1)} %get-tuple-element.36), channel_id=1, source_target_pairs={{0,3},{1,2},{2,1},{3,0},{4,7},{5,6},{6,5},{7,4},{8,11},{9,10},{10,... | collective-permute-start | bytes 147464 | tf_op jit(solution)/shard_map/ppermute | solution.py:236
  42.7 3.8 %collective-permute-start.17 = (bf16[32,768]{1,0:T(8,128)(2,1)S(1)}, bf16[32,768]{1,0:T(8,128)(2,1)S(1)}, u32[]{:S(2)}, u32[]{:S(2)}) collective-permute-start(bf16[32,768]{1,0:T(8,128)(2,1)S(1)} %get-tuple-element.39), channel_id=1, source_target_pairs={{0,3},{1,2},{2,1},{3,0},{4,7},{5,6},{6,5},{7,4},{8,11},{9,10},{10,... | collective-permute-start | bytes 147464 | tf_op jit(solution)/shard_map/ppermute | solution.py:236
  43.6 4.2 %collective-permute-start.18 = (bf16[32,768]{1,0:T(8,128)(2,1)S(1)}, bf16[32,768]{1,0:T(8,128)(2,1)S(1)}, u32[]{:S(2)}, u32[]{:S(2)}) collective-permute-start(bf16[32,768]{1,0:T(8,128)(2,1)S(1)} %get-tuple-element.40), channel_id=1, source_target_pairs={{0,2},{1,3},{2,0},{3,1},{4,6},{5,7},{6,4},{7,5},{8,10},{9,11},{10,... | collective-permute-start | bytes 147464 | tf_op jit(solution)/shard_map/ppermute | solution.py:236
  44.6 3.3 %collective-permute-start.19 = (bf16[32,768]{1,0:T(8,128)(2,1)S(1)}, bf16[32,768]{1,0:T(8,128)(2,1)S(1)}, u32[]{:S(2)}, u32[]{:S(2)}) collective-permute-start(bf16[32,768]{1,0:T(8,128)(2,1)S(1)} %get-tuple-element.41), channel_id=1, source_target_pairs={{0,1},{1,0},{2,3},{3,2},{4,5},{5,4},{6,7},{7,6},{8,9},{9,8},{10,11... | collective-permute-start | bytes 147464 | tf_op jit(solution)/shard_map/ppermute | solution.py:236
